TPU v7x, 128 devices: a whole 4x4x4 slice. The times are simulated.
128 devices in a mesh: tok: 16 (over y, z_hi, core), br: 8 (over z_lo, x).
Axes of the slice: x: 4, y: 4, z: 4 (z_hi: 2, z_lo: 2; z = z_hi * 2 + z_lo), core: 2. Of those that a mesh axis runs over, the one named last changes fastest.
Arguments:
- tokens: bfloat16 [16384, 2048], P(('tok', 'br')), may hold values from -6 to 6
- norm_gain: float32 [2048], replicated, may hold values from 0.1 to 1.9
- norm_bias: float32 [2048], replicated, may hold values from -3 to 3
- qkv_weight: bfloat16 [3, 2048, 2048], P(None, 'tok', 'br'), may hold values from -0.125 to 0.125
- qkv_bias: bfloat16 [3, 32, 64], P(None, 'br', 'tok'), may hold values from -3 to 3
- out_weight: bfloat16 [2048, 2048], P('br', 'tok'), may hold values from -1.5 to 1.5
- gate_weight: bfloat16 [2048, 5632], P('tok', 'br'), may hold values from -0.125 to 0.125
- up_weight: bfloat16 [2048, 5632], P('tok', 'br'), may hold values from -0.125 to 0.125
- down_weight: bfloat16 [5632, 2048], P('br', 'tok'), may hold values from -0.078125 to 0.078125
- cotangent: bfloat16 [16384, 2048], P(('tok', 'br')), may hold values from -6 to 6
- block_map: int32 [32], replicated, may hold values from 0 to 31, as said below
- lengths: int32 [10], replicated, may hold values from 256 to 4096, as said below
Outputs:
- out: bfloat16 [16384, 2048], P(('tok', 'br'))
- grad_tokens: float32 [16384, 2048], P(('tok', 'br'))
- grad_gain: float32 [2048], P(('tok', 'br'))
- grad_bias: float32 [2048], P(('tok', 'br'))
- grad_qkv: float32 [3, 2048, 2048], P(None, 'tok', 'br')
- grad_qkv_bias: float32 [3, 32, 64], P(None, 'br', 'tok')
- grad_out: float32 [2048, 2048], P('br', 'tok')
- grad_gate: float32 [2048, 5632], P('tok', 'br')
- grad_up: float32 [2048, 5632], P('tok', 'br')
- grad_down: float32 [5632, 2048], P('br', 'tok')
Inputs may be any that keep to these rules, and one draw needn't show every extreme that they name: `block_map`: a permutation of the 32 block numbers. `lengths`: each long row is its whole capacity 8 * 512; every short row is at most its capacity 2 * 512.
All inputs are finite; a program needn't handle non-finite values.
Results may differ from a plain program's by a relative error of at most 0.03.
Values may be sent and summed in bfloat16 or wider, within the bound.
A program may use at most 192 MiB of HBM per device.

v0:
```python
import math

import jax
import jax.numpy as jnp
from jax import lax
from jax.sharding import PartitionSpec as P

HD = 64
ROT = 16
BLK = 512
LB = 8


EPSILON = 1e-05
ROPE_BASE = 10000.0
MASKED = -1e30


def rotate(values, positions, turning):
    half_rot = ROT // 2
    frequency = ROPE_BASE ** (-(jnp.arange(half_rot).astype(jnp.float32) * 2.0 / ROT))
    angles = positions[:, None] * frequency[None, :]
    cosine = jnp.cos(angles)[:, None, :]
    sine_part = turning * jnp.sin(angles)[:, None, :]
    front_half = values[..., :half_rot]
    back_half = values[..., half_rot:ROT]
    return jnp.concatenate(
        [
            front_half * cosine - back_half * sine_part,
            back_half * cosine + front_half * sine_part,
            values[..., ROT:],
        ],
        axis=-1,
    )


def contract_rows(left, right):
    return lax.dot_general(
        left, right, (((0,), (0,)), ((), ())), preferred_element_type=jnp.float32
    )


def contract_last(left, right):
    return lax.dot_general(
        left, right, (((1,), (1,)), ((), ())), preferred_element_type=jnp.float32
    )


def block_rows(blocks, long_blocks):
    is_long = blocks < long_blocks
    long_rows = long_blocks // LB
    row_of = jnp.where(is_long, blocks // LB, long_rows + (blocks - long_blocks) // 2)
    start_of = jnp.where(is_long, blocks % LB * BLK, (blocks - long_blocks) % 2 * BLK)
    in_block = jnp.arange(BLK, dtype=jnp.int32)
    token_row = (row_of[:, None] + 0 * in_block[None, :]).reshape(-1)
    token_pos = (start_of[:, None] + in_block[None, :]).reshape(-1)
    return (token_row, token_pos)


def keep_same(state_in):
    return state_in


def guarded(allowed, update, state_in):
    return lax.cond(jnp.any(allowed), update, keep_same, state_in)


def pair_mask(query_row, query_pos, key_row, key_pos, key_limit):
    return (
        (key_row[None, :] == query_row[:, None])
        & (key_pos[None, :] <= query_pos[:, None])
        & (key_pos[None, :] < key_limit[None, :])
    )


def add_rows(whole, piece, slot):
    current = lax.dynamic_slice_in_dim(whole, slot * BLK, BLK, 0)
    return lax.dynamic_update_slice_in_dim(whole, current + piece, slot * BLK, 0)


def body(
    tokens,
    norm_gain,
    norm_bias,
    qkv_weight,
    qkv_bias,
    out_weight,
    gate_weight,
    up_weight,
    down_weight,
    cotangent,
    block_map,
    lengths,
):
    tok_count = lax.axis_size("tok")
    tok_index = lax.axis_index("tok")
    total_blocks = block_map.shape[0]
    long_blocks = total_blocks // 2
    per_device = total_blocks // tok_count
    group_rows = per_device * BLK
    score_scale = 1.0 / math.sqrt(HD)
    residual = tokens.astype(jnp.float32)
    centred = residual - jnp.mean(residual, axis=-1, keepdims=True)
    inverse = lax.rsqrt(jnp.mean(centred * centred, axis=-1, keepdims=True) + EPSILON)
    normed = centred * inverse
    shifted = (normed * norm_gain + norm_bias).astype(jnp.bfloat16)
    group_normed, group_grad = (
        lax.all_gather(shifted, "br", axis=0, tiled=True),
        lax.all_gather(cotangent, "br", axis=0, tiled=True),
    )
    qkv_full, bias_full, out_full, gate_full, up_full, down_full = (
        lax.all_gather(qkv_weight, "tok", axis=1, tiled=True),
        lax.all_gather(qkv_bias, "tok", axis=2, tiled=True),
        lax.all_gather(out_weight, "tok", axis=1, tiled=True),
        lax.all_gather(gate_weight, "tok", axis=0, tiled=True),
        lax.all_gather(up_weight, "tok", axis=0, tiled=True),
        lax.all_gather(down_weight, "tok", axis=1, tiled=True),
    )
    local_heads = bias_full.shape[1]
    local_width = local_heads * HD
    all_rows, all_pos = block_rows(block_map, long_blocks)
    row_table = jnp.arange(lengths.shape[0], dtype=jnp.int32)
    all_limit = jnp.sum(
        jnp.where(all_rows[:, None] == row_table[None, :], lengths[None, :], 0), axis=1
    )
    my_blocks = lax.dynamic_slice_in_dim(block_map, tok_index * per_device, per_device)
    my_rows, my_pos = block_rows(my_blocks, long_blocks)
    my_angles = my_pos.astype(jnp.float32)
    slot_table = jnp.arange(total_blocks, dtype=jnp.int32)
    joined_parts = [
        jnp.dot(group_normed, qkv_full[member], preferred_element_type=jnp.float32)
        + bias_full[member].reshape(-1).astype(jnp.float32)
        for member in range(3)
    ]
    queries = rotate(joined_parts[0].reshape(group_rows, local_heads, HD), my_angles, 1.0).astype(
        jnp.bfloat16
    )
    key_rows = (
        rotate(joined_parts[1].reshape(group_rows, local_heads, HD), my_angles, 1.0)
        .astype(jnp.bfloat16)
        .reshape(group_rows, local_width)
    )
    value_rows = joined_parts[2].astype(jnp.bfloat16)
    all_keys, all_values = (
        lax.all_gather(key_rows, "tok", axis=0, tiled=True),
        lax.all_gather(value_rows, "tok", axis=0, tiled=True),
    )

    def sweep(step, carry, global_block):
        is_long = global_block < long_blocks
        first = jnp.where(
            is_long, global_block // LB * LB, long_blocks + (global_block - long_blocks) // 2 * 2
        )
        count = jnp.where(is_long, LB, 2)

        def row_slot(state, offset):
            block = jnp.minimum(first + offset, total_blocks - 1)
            slot = jnp.sum(jnp.where(block_map == block, slot_table, 0))
            return step(state, slot, offset < count)

        return lax.scan(row_slot, carry, jnp.arange(LB, dtype=jnp.int32))

    def slot_info(slot):
        return (
            lax.dynamic_slice_in_dim(all_rows, slot * BLK, BLK),
            lax.dynamic_slice_in_dim(all_pos, slot * BLK, BLK),
            lax.dynamic_slice_in_dim(all_limit, slot * BLK, BLK),
        )

    def slot_keys(slot):
        key_piece = lax.dynamic_slice_in_dim(all_keys, slot * BLK, BLK, 0).reshape(
            BLK, local_heads, HD
        )
        value_piece = lax.dynamic_slice_in_dim(all_values, slot * BLK, BLK, 0).reshape(
            BLK, local_heads, HD
        )
        return (key_piece, value_piece)

    def piece_scores(query_block, allowed, key_piece):
        raw = (
            jnp.einsum("qhd,khd->hqk", query_block, key_piece, preferred_element_type=jnp.float32)
            * score_scale
        )
        return jnp.where(allowed[None], raw, MASKED)

    def score_grads(
        query_block, grad_block, key_piece, value_piece, allowed, log_total, delta_heads
    ):
        scores = piece_scores(query_block, allowed, key_piece)
        probabilities = jnp.exp(scores - log_total[..., None])
        grad_probs = jnp.einsum(
            "qhd,khd->hqk", grad_block, value_piece, preferred_element_type=jnp.float32
        )
        grad_scores = (probabilities * (grad_probs - delta_heads[..., None])).astype(jnp.bfloat16)
        return (probabilities, grad_scores)

    def query_slices(block_index):
        query_block = lax.dynamic_slice_in_dim(queries, block_index * BLK, BLK, 0)
        query_row = lax.dynamic_slice_in_dim(my_rows, block_index * BLK, BLK)
        query_pos = lax.dynamic_slice_in_dim(my_pos, block_index * BLK, BLK)
        return (query_block, query_row, query_pos)

    def forward_block(block_index):
        query_block, query_row, query_pos = query_slices(block_index)
        global_block = my_blocks[block_index]

        def stats_step(state_in, slot, valid):
            allowed = pair_mask(query_row, query_pos, *slot_info(slot)) & valid

            def update(state_now):
                running_max, running_sum = state_now
                key_piece, unused_values = slot_keys(slot)
                scores = piece_scores(query_block, allowed, key_piece)
                new_max = jnp.maximum(running_max, jnp.max(scores, axis=-1))
                new_sum = running_sum * jnp.exp(running_max - new_max) + jnp.sum(
                    jnp.exp(scores - new_max[..., None]), axis=-1
                )
                return (new_max, new_sum)

            return (guarded(allowed, update, state_in), None)

        start_state = (
            jnp.full((local_heads, BLK), MASKED, jnp.float32),
            jnp.zeros((local_heads, BLK), jnp.float32),
        )
        (running_max, running_sum), unused_stats = sweep(stats_step, start_state, global_block)
        log_total = running_max + jnp.log(running_sum)

        def value_step(weighted, slot, valid):
            allowed = pair_mask(query_row, query_pos, *slot_info(slot)) & valid

            def update(weighted_now):
                key_piece, value_piece = slot_keys(slot)
                scores = piece_scores(query_block, allowed, key_piece)
                weights = jnp.exp(scores - log_total[..., None]).astype(jnp.bfloat16)
                return weighted_now + jnp.einsum(
                    "hqk,khd->qhd", weights, value_piece, preferred_element_type=jnp.float32
                )

            return (guarded(allowed, update, weighted), None)

        weighted, unused_values = sweep(
            value_step, jnp.zeros((BLK, local_heads, HD), jnp.float32), global_block
        )
        return (weighted, log_total)

    attended, log_totals = lax.map(forward_block, jnp.arange(per_device))
    mixed = attended.reshape(group_rows, local_width).astype(jnp.bfloat16)
    gate_pre = jnp.dot(group_normed, gate_full, preferred_element_type=jnp.float32)
    up_pre = jnp.dot(group_normed, up_full, preferred_element_type=jnp.float32)
    sigmoid_gate = jax.nn.sigmoid(gate_pre)
    hidden = (gate_pre * sigmoid_gate * up_pre).astype(jnp.bfloat16)
    branches = jnp.dot(mixed, out_full, preferred_element_type=jnp.float32) + jnp.dot(
        hidden, down_full, preferred_element_type=jnp.float32
    )
    summed = lax.psum_scatter(
        branches.astype(jnp.bfloat16), "br", scatter_dimension=0, tiled=True
    ).astype(jnp.float32)
    result = (residual + summed).astype(jnp.bfloat16)
    grad_down = contract_rows(hidden, group_grad)
    grad_hidden = contract_last(group_grad, down_full)
    grad_gate_pre = (
        grad_hidden * up_pre * sigmoid_gate * (1.0 + gate_pre * (1.0 - sigmoid_gate))
    ).astype(jnp.bfloat16)
    grad_up_pre = (grad_hidden * gate_pre * sigmoid_gate).astype(jnp.bfloat16)
    grad_gate = contract_rows(group_normed, grad_gate_pre)
    grad_up = contract_rows(group_normed, grad_up_pre)
    grad_shifted = contract_last(grad_gate_pre, gate_full) + contract_last(grad_up_pre, up_full)
    grad_out = contract_rows(mixed, group_grad)
    grad_mixed = contract_last(group_grad, out_full).astype(jnp.bfloat16)
    grad_blocks = grad_mixed.reshape(per_device, BLK, local_heads, HD)
    row_delta = jnp.sum(grad_blocks.astype(jnp.float32) * attended, axis=-1)
    total_rows = tok_count * group_rows

    def backward_block(grads_in, packed):
        block_index, grad_block, delta_block, log_total = packed
        query_block, query_row, query_pos = query_slices(block_index)
        delta_heads = jnp.transpose(delta_block)

        def key_step(state_in, slot, valid):
            allowed = pair_mask(query_row, query_pos, *slot_info(slot)) & valid

            def update(state_now):
                grad_query, key_acc, value_acc = state_now
                key_piece, value_piece = slot_keys(slot)
                probabilities, grad_scores = score_grads(
                    query_block, grad_block, key_piece, value_piece, allowed, log_total, delta_heads
                )
                grad_value_piece = jnp.einsum(
                    "hqk,qhd->khd",
                    probabilities.astype(jnp.bfloat16),
                    grad_block,
                    preferred_element_type=jnp.float32,
                )
                new_query = (
                    grad_query
                    + jnp.einsum(
                        "hqk,khd->qhd", grad_scores, key_piece, preferred_element_type=jnp.float32
                    )
                    * score_scale
                )
                grad_key_piece = (
                    jnp.einsum(
                        "hqk,qhd->khd", grad_scores, query_block, preferred_element_type=jnp.float32
                    )
                    * score_scale
                )
                key_acc = add_rows(key_acc, grad_key_piece.reshape(BLK, local_width), slot)
                value_acc = add_rows(value_acc, grad_value_piece.reshape(BLK, local_width), slot)
                return (new_query, key_acc, value_acc)

            return (guarded(allowed, update, state_in), None)

        start_state = (jnp.zeros((BLK, local_heads, HD), jnp.float32), grads_in[0], grads_in[1])
        (grad_query, key_acc, value_acc), unused_steps = sweep(
            key_step, start_state, my_blocks[block_index]
        )
        return ((key_acc, value_acc), grad_query)

    zero_rows = jnp.zeros((total_rows, local_width), jnp.float32)
    (key_grads, value_grads), query_grads = lax.scan(
        backward_block,
        (zero_rows, zero_rows),
        (jnp.arange(per_device), grad_blocks, row_delta, log_totals),
    )
    my_key_grads, my_value_grads = (
        lax.psum_scatter(
            key_grads.astype(jnp.bfloat16), "tok", scatter_dimension=0, tiled=True
        ).astype(jnp.float32),
        lax.psum_scatter(
            value_grads.astype(jnp.bfloat16), "tok", scatter_dimension=0, tiled=True
        ).astype(jnp.float32),
    )
    grad_queries = rotate(
        query_grads.reshape(group_rows, local_heads, HD), my_angles, -1.0
    ).reshape(group_rows, local_width)
    grad_keys = rotate(my_key_grads.reshape(group_rows, local_heads, HD), my_angles, -1.0).reshape(
        group_rows, local_width
    )
    grad_joined = jnp.stack([grad_queries, grad_keys, my_value_grads]).astype(jnp.bfloat16)
    grad_qkv = jnp.stack([contract_rows(group_normed, grad_joined[member]) for member in range(3)])
    grad_qkv_bias = jnp.sum(grad_joined.astype(jnp.float32), axis=1).reshape(3, local_heads, HD)
    for member in range(3):
        grad_shifted = grad_shifted + contract_last(grad_joined[member], qkv_full[member])
    grad_qkv, grad_qkv_bias, grad_out, grad_gate, grad_up, grad_down = (
        lax.psum_scatter(
            grad_qkv.astype(jnp.bfloat16), "tok", scatter_dimension=1, tiled=True
        ).astype(jnp.float32),
        lax.psum_scatter(
            grad_qkv_bias.astype(jnp.bfloat16), "tok", scatter_dimension=2, tiled=True
        ).astype(jnp.float32),
        lax.psum_scatter(
            grad_out.astype(jnp.bfloat16), "tok", scatter_dimension=1, tiled=True
        ).astype(jnp.float32),
        lax.psum_scatter(
            grad_gate.astype(jnp.bfloat16), "tok", scatter_dimension=0, tiled=True
        ).astype(jnp.float32),
        lax.psum_scatter(
            grad_up.astype(jnp.bfloat16), "tok", scatter_dimension=0, tiled=True
        ).astype(jnp.float32),
        lax.psum_scatter(
            grad_down.astype(jnp.bfloat16), "tok", scatter_dimension=1, tiled=True
        ).astype(jnp.float32),
    )
    my_grad_shifted = lax.psum_scatter(
        grad_shifted.astype(jnp.bfloat16), "br", scatter_dimension=0, tiled=True
    ).astype(jnp.float32)
    gain_part = jnp.sum(my_grad_shifted * normed, axis=0)
    bias_part = jnp.sum(my_grad_shifted, axis=0)
    grad_normed = my_grad_shifted * norm_gain
    grad_tokens = cotangent.astype(jnp.float32) + inverse * (
        grad_normed
        - jnp.mean(grad_normed, axis=-1, keepdims=True)
        - normed * jnp.mean(grad_normed * normed, axis=-1, keepdims=True)
    )
    grad_gain, grad_bias = (
        lax.psum_scatter(gain_part, ("tok", "br"), scatter_dimension=0, tiled=True),
        lax.psum_scatter(bias_part, ("tok", "br"), scatter_dimension=0, tiled=True),
    )
    return (
        result,
        grad_tokens,
        grad_gain,
        grad_bias,
        grad_qkv,
        grad_qkv_bias,
        grad_out,
        grad_gate,
        grad_up,
        grad_down,
    )


def solution(mesh):
    in_specs = (
        P(("tok", "br"), None),
        P(),
        P(),
        P(None, "tok", "br"),
        P(None, "br", "tok"),
        P("br", "tok"),
        P("tok", "br"),
        P("tok", "br"),
        P("br", "tok"),
        P(("tok", "br"), None),
        P(),
        P(),
    )
    out_specs = (
        P(("tok", "br"), None),
        P(("tok", "br"), None),
        P(("tok", "br")),
        P(("tok", "br")),
        P(None, "tok", "br"),
        P(None, "br", "tok"),
        P("br", "tok"),
        P("tok", "br"),
        P("tok", "br"),
        P("br", "tok"),
    )
    return jax.shard_map(body, mesh=mesh, in_specs=in_specs, out_specs=out_specs, check_vma=False)
```

profile of v0, /device:TPU:1, one launch (start us, length us, event | category | flops | bytes accessed | tf_op | source)
XLA Modules:
  0.0 1643.7 jit_solution(8439705770616027520)
XLA Ops:
  15.5 26.7 %all_gather.32 = bf16[3,4,64]{1,0,2:T(4,128)(2,1)S(1)} all-gather(bf16[3,4,4]{1,0,2:T(4,128)(2,1)S(1)} %copy.108), channel_id=1, replica_groups=mesh['tok'=16,'br'=8] {'tok'}, dimensions={2}, use_global_device_ids=true | all-gather | bytes 1632 | tf_op jit(solution)/shard_map/all_gather | solution.py:113
  42.5 24.1 %all-gather.12.cloned.1.call-done = bf16[3,2048,256]{2,1,0:T(8,128)(2,1)} async-done(((bf16[3,128,256]{2,1,0:T(8,128)(2,1)}), bf16[3,2048,256]{2,1,0:T(8,128)(2,1)}) %all-gather.12.cloned.1.call-update) | async-done | bytes 3145744 | tf_op jit(solution)/shard_map/all_gather | solution.py:112
  66.6 53.0 %all-gather.10.cloned.1.call-done = bf16[1024,2048]{1,0:T(8,128)(2,1)} async-done(((bf16[128,2048]{1,0:T(8,128)(2,1)}), bf16[1024,2048]{1,0:T(8,128)(2,1)}) %all-gather.10.cloned.1.call-update) | async-done | bytes 4194320 | tf_op jit(solution)/shard_map/all_gather | solution.py:108
  136.0 30.5 %all-gather.18.cloned.1.call-done = bf16[256,2048]{1,0:T(8,128)(2,1)} async-done(((bf16[256,128]{1,0:T(8,128)(2,1)}), bf16[256,2048]{1,0:T(8,128)(2,1)}) %all-gather.18.cloned.1.call-update) | async-done | bytes 1048592 | tf_op jit(solution)/shard_map/all_gather | solution.py:114
  166.5 52.3 %all-gather.26.cloned.1.call-done = bf16[1024,2048]{1,0:T(8,128)(2,1)} async-done(((bf16[128,2048]{1,0:T(8,128)(2,1)}), bf16[1024,2048]{1,0:T(8,128)(2,1)}) %all-gather.26.cloned.1.call-update) | async-done | bytes 4194320 | tf_op jit(solution)/shard_map/all_gather | solution.py:109
  223.4 69.7 %all-gather.16.cloned.1.call-done = bf16[16384,256]{1,0:T(8,128)(2,1)} async-done(((bf16[1024,256]{1,0:T(8,128)(2,1)}), bf16[16384,256]{1,0:T(8,128)(2,1)}) %all-gather.16.cloned.1.call-update) | async-done | bytes 8388624 | tf_op jit(solution)/shard_map/all_gather | solution.py:146
  293.1 12.0 copy.112
  305.1 61.4 %all-gather.14.cloned.1.call-done = bf16[16384,256]{0,1:T(8,128)(2,1)} async-done(((bf16[1024,256]{0,1:T(8,128)(2,1)}), bf16[16384,256]{0,1:T(8,128)(2,1)}) %all-gather.14.cloned.1.call-update) | async-done | bytes 8388624 | tf_op jit(solution)/shard_map/all_gather | solution.py:145
  366.5 247.4 %while.125 = (s32[]{:T(128)}, f32[2,512,4,64]{1,3,2,0:T(8,128)}, f32[2,4,512]{2,1,0:T(4,128)S(1)}, s32[2]{0:T(128)S(1)}, s32[2]{0:T(128)S(1)}, /*index=5*/s32[10...) while((s32[]{:T(128)}, f32[2,512,4,64]{1,3,2,0:T(8,128)}, ...), condition=%wide.region_18.19_spmd.clone.clone, body=%wide.region_3.18_spmd.clone.clone.sunk | while | flops 417488128 | bytes 16335822 | solution.py:247
  374.5 46.8 %while.127 = (s32[]{:T(128)}, f32[4,512]{1,0:T(4,128)S(1)}, f32[4,512]{1,0:T(4,128)S(1)}, s32[8]{0:T(128)S(1)}, s32[]{:T(128)}, /*index=5*/s32[32]{0:T(128)S(1)}...) while((s32[]{:T(128)}, f32[4,512]{1,0:T(4,128)S(1)}, ...), condition=%wide.region_11.11_spmd, body=%wide.region_4.10_spmd.sunk | while | flops 143135328 | bytes 10350265 | solution.py:161
  421.4 47.1 %while.128 = (s32[]{:T(128)}, f32[512,4,64]{0,2,1:T(8,128)S(1)}, s32[8]{0:T(128)S(1)}, s32[]{:T(128)}, s32[32]{0:T(128)S(1)}, /*index=5*/s32[32]{0:T(128)S(1)}, ...) while((s32[]{:T(128)}, f32[512,4,64]{0,2,1:T(8,128)S(1)}, ...), condition=%wide.region_17.17_spmd, body=%wide.region_12.16_spmd.sunk | while | flops 274334304 | bytes 3436201 | solution.py:161
  477.5 67.9 %while.127 = (s32[]{:T(128)}, f32[4,512]{1,0:T(4,128)S(1)}, f32[4,512]{1,0:T(4,128)S(1)}, s32[8]{0:T(128)S(1)}, s32[]{:T(128)}, /*index=5*/s32[32]{0:T(128)S(1)}...) while((s32[]{:T(128)}, f32[4,512]{1,0:T(4,128)S(1)}, ...), condition=%wide.region_11.11_spmd, body=%wide.region_4.10_spmd.sunk | while | flops 143135328 | bytes 10350265 | solution.py:161
  545.4 67.6 %while.128 = (s32[]{:T(128)}, f32[512,4,64]{0,2,1:T(8,128)S(1)}, s32[8]{0:T(128)S(1)}, s32[]{:T(128)}, s32[32]{0:T(128)S(1)}, /*index=5*/s32[32]{0:T(128)S(1)}, ...) while((s32[]{:T(128)}, f32[512,4,64]{0,2,1:T(8,128)S(1)}, ...), condition=%wide.region_17.17_spmd, body=%wide.region_12.16_spmd.sunk | while | flops 274334304 | bytes 3436201 | solution.py:161
  616.3 7.7 broadcast_in_dim.105
  624.0 7.7 broadcast_in_dim.105.clone
  631.7 216.3 %while.122 = (s32[]{:T(128)}, f32[16384,256]{0,1:T(8,128)}, f32[16384,256]{0,1:T(8,128)}, f32[2,512,4,64]{1,0,3,2:T(2,128)}, s32[2]{0:T(128)S(1)}, /*index=5*/s3...) while((s32[]{:T(128)}, f32[16384,256]{0,1:T(8,128)}, ...), condition=%wide.region_28.29_spmd.clone, body=%wide.region_21.28_spmd.clone.sunk | while | flops 683819712 | bytes 31954124 | solution.py:321
  640.3 59.7 %while.126 = (s32[]{:T(128)}, f32[512,4,64]{0,2,1:T(8,128)S(1)}, f32[16384,256]{0,1:T(8,128)}, f32[16384,256]{0,1:T(8,128)}, s32[8]{0:T(128)S(1)}, /*index=5*/s3...) while((s32[]{:T(128)}, f32[512,4,64]{0,2,1:T(8,128)S(1)}, ...), condition=%wide.region_27.27_spmd, body=%wide.region_22.26_spmd.sunk | while | flops 683803264 | bytes 27832096 | solution.py:161
  645.3 9.8 conditional.8
  660.1 9.7 conditional.8
  700.6 10.4 dynamic_update_slice.41
  719.1 118.0 %while.126 = (s32[]{:T(128)}, f32[512,4,64]{0,2,1:T(8,128)S(1)}, f32[16384,256]{0,1:T(8,128)}, f32[16384,256]{0,1:T(8,128)}, s32[8]{0:T(128)S(1)}, /*index=5*/s3...) while((s32[]{:T(128)}, f32[512,4,64]{0,2,1:T(8,128)S(1)}, ...), condition=%wide.region_27.27_spmd, body=%wide.region_22.26_spmd.sunk | while | flops 683803264 | bytes 27832096 | solution.py:161
  724.1 9.8 conditional.8
  738.9 9.7 conditional.8
  753.6 9.8 conditional.8
  768.4 9.7 conditional.8
  783.1 9.8 conditional.8
  797.9 9.8 conditional.8
  812.6 9.7 conditional.8
  827.4 9.7 conditional.8
  837.6 10.4 dynamic_update_slice.41
  848.0 8.9 convert_element_type.187
  857.0 8.9 convert_element_type.188
  872.0 7.9 fusion.68
  879.9 9.8 multiply_convert_fusion
  905.8 7.4 convolution_convert_fusion.2
  925.2 79.6 %reduce-scatter.21.cloned.1.call-done = bf16[1024,256]{0,1:T(8,128)(2,1)} async-done(((bf16[16384,256]{0,1:T(8,128)(2,1)}), bf16[1024,256]{0,1:T(8,128)(2,1)}) %reduce-scatter.21.cloned.1.call-update) | async-done | bytes 524304 | tf_op jit(solution)/shard_map/reduce_scatter | solution.py:327
  1007.2 103.3 %reduce-scatter.23.cloned.1.call-done = bf16[1024,256]{0,1:T(8,128)(2,1)} async-done(((bf16[16384,256]{0,1:T(8,128)(2,1)}), bf16[1024,256]{0,1:T(8,128)(2,1)}) %reduce-scatter.23.cloned.1.call-update) | async-done | bytes 524304 | tf_op jit(solution)/shard_map/reduce_scatter | solution.py:330
  1119.4 9.1 fusion.70
  1143.5 14.4 add_convert_fusion
  1158.3 5.9 fusion.69
  1169.3 18.8 %reduce-scatter.31.cloned.1.call-done = bf16[128,704]{1,0:T(8,128)(2,1)} async-done(((bf16[2048,704]{1,0:T(8,128)(2,1)}), bf16[128,704]{1,0:T(8,128)(2,1)}) %reduce-scatter.31.cloned.1.call-update) | async-done | bytes 180240
  1190.0 76.2 %reduce-scatter.33.cloned.1.call-done = bf16[128,704]{1,0:T(8,128)(2,1)} async-done(((bf16[2048,704]{1,0:T(8,128)(2,1)}), bf16[128,704]{1,0:T(8,128)(2,1)}) %reduce-scatter.33.cloned.1.call-update) | async-done | bytes 180240
  1268.1 76.1 %reduce-scatter.35.cloned.1.call-done = bf16[128,704]{1,0:T(8,128)(2,1)} async-done(((bf16[2048,704]{1,0:T(8,128)(2,1)}), bf16[128,704]{1,0:T(8,128)(2,1)}) %reduce-scatter.35.cloned.1.call-update) | async-done | bytes 180240
  1346.0 67.2 %reduce-scatter.29.cloned.1.call-done = bf16[128,256]{1,0:T(8,128)(2,1)} async-done(((bf16[2048,256]{1,0:T(8,128)(2,1)}), bf16[128,256]{1,0:T(8,128)(2,1)}) %reduce-scatter.29.cloned.1.call-update) | async-done | bytes 65552
  1415.2 35.1 %all-reduce.2 = bf16[3,4,64]{2,1,0:T(4,128)(2,1)S(1)} all-reduce(bf16[3,4,64]{2,1,0:T(4,128)(2,1)S(1)} %convert_element_type.192), channel_id=9, replica_groups=mesh['tok'=16,'br'=8] {'tok'}, use_global_device_ids=true, to_apply=%region_40.41.clone | all-reduce | flops 768 | bytes 3072
  1451.0 41.7 %reduce-scatter.27.cloned.1.call-done = bf16[3,128,256]{2,1,0:T(8,128)(2,1)} async-done(((bf16[3,2048,256]{2,1,0:T(8,128)(2,1)}), bf16[3,128,256]{2,1,0:T(8,128)(2,1)}) %reduce-scatter.27.cloned.1.call-update) | async-done | bytes 196624 | tf_op jit(solution)/shard_map/reduce_scatter | solution.py:346
  1494.5 53.6 %reduce-scatter.25.cloned.1.call-done = bf16[128,2048]{1,0:T(8,128)(2,1)} async-done(((bf16[1024,2048]{1,0:T(8,128)(2,1)}), bf16[128,2048]{1,0:T(8,128)(2,1)}) %reduce-scatter.25.cloned.1.call-update) | async-done | bytes 524304 | tf_op jit(solution)/shard_map/reduce_scatter | solution.py:365
  1549.6 82.9 %all-reduce.3 = (f32[2048]{0:T(1024)S(1)}, f32[2048]{0:T(1024)S(1)}) all-reduce(f32[2048]{0:T(1024)S(1)} %get-tuple-element.1239, f32[2048]{0:T(1024)S(1)} %get-tuple-element.1242), channel_id=6, replica_groups=mesh['tok'=16,'br'=8] {'tok','br'}, use_global_device_ids=true, to_apply=%region_35.36.clone | all-reduce | flops 4096 | bytes 32768
  (682 shorter events, 452.0 us)
Async XLA Ops:
  7.2 59.4 %all-gather.12.cloned.1.call-start = ((), (), s32[]{:S(2)}) async-start(), calls=%async_computation.10 | async-start | bytes 3342336 | tf_op jit(solution)/shard_map/all_gather | solution.py:112
  7.9 111.7 %all-gather.10.cloned.1.call-start = ((), (), s32[]{:S(2)}) async-start(), calls=%async_computation.9 | async-start | bytes 4718592 | tf_op jit(solution)/shard_map/all_gather | solution.py:108
  9.2 1.3 copy-start.14
  10.5 0.5 copy-start.16
  13.3 153.2 %all-gather.18.cloned.1.call-start = ((), (), s32[]{:S(2)}) async-start(), calls=%async_computation.13 | async-start | bytes 1114112 | tf_op jit(solution)/shard_map/all_gather | solution.py:114
  14.1 204.8 %all-gather.26.cloned.1.call-start = ((), (), s32[]{:S(2)}) async-start(), calls=%async_computation.18 | async-start | bytes 4718592 | tf_op jit(solution)/shard_map/all_gather | solution.py:109
  14.7 278.4 %all-gather.16.cloned.1.call-start = ((), (), s32[]{:S(2)}) async-start(), calls=%async_computation.12 | async-start | bytes 8912896 | tf_op jit(solution)/shard_map/all_gather | solution.py:146
  42.5 81.7 %copy-start.4 = (s32[32]{0:T(128)S(1)}, s32[32]{0:T(128)}, u32[]{:S(2)}) copy-start(s32[32]{0:T(128)} %param.38) | copy-start | bytes 388
  66.6 59.0 %copy-start.2 = (bf16[3,2048,256]{2,1,0:T(8,128)(2,1)S(1)}, bf16[3,2048,256]{2,1,0:T(8,128)(2,1)}, u32[]{:S(2)}) copy-start(bf16[3,2048,256]{2,1,0:T(8,128)(2,1)} %all-gather.12.cloned.1.call-done) | copy-start | bytes 9437188
  124.1 242.3 %all-gather.14.cloned.1.call-start = ((), (), s32[]{:S(2)}) async-start(), calls=%async_computation.11 | async-start | bytes 8912896 | tf_op jit(solution)/shard_map/all_gather | solution.py:145
  125.6 5.0 copy-start.10
  125.6 3.7 copy-start.19
  129.3 5.2 copy-start.18
  130.6 1.2 copy-start.9
  131.8 734.2 %all-gather.20.cloned.1.call-start = ((), (), s32[]{:S(2)}) async-start(), calls=%async_computation.14 | async-start | bytes 3063808 | tf_op jit(solution)/shard_map/all_gather | solution.py:115
  132.6 739.4 %all-gather.22.cloned.1.call-start = ((), (), s32[]{:S(2)}) async-start(), calls=%async_computation.15 | async-start | bytes 3063808 | tf_op jit(solution)/shard_map/all_gather | solution.py:116
  133.3 746.5 %all-gather.24.cloned.1.call-start = ((), (), s32[]{:S(2)}) async-start(), calls=%async_computation.16 | async-start | bytes 3063808 | tf_op jit(solution)/shard_map/all_gather | solution.py:117
  134.1 870.8 %reduce-scatter.21.cloned.1.call-start = ((), (), s32[]{:S(2)}) async-start(), calls=%async_computation.19 | async-start | bytes 8912896 | tf_op jit(solution)/shard_map/reduce_scatter | solution.py:327
  857.0 253.6 %reduce-scatter.23.cloned.1.call-start = ((), (), s32[]{:S(2)}) async-start(), calls=%async_computation.20 | async-start | bytes 8912896 | tf_op jit(solution)/shard_map/reduce_scatter | solution.py:330
  866.0 322.2 %reduce-scatter.31.cloned.1.call-start = ((), (), s32[]{:S(2)}) async-start(), calls=%async_computation.24 | async-start | bytes 3342336
  879.9 10.9 copy-start.20
  889.7 1.1 copy-start.25
  897.0 369.3 %reduce-scatter.33.cloned.1.call-start = ((), (), s32[]{:S(2)}) async-start(), calls=%async_computation.25 | async-start | bytes 3342336
  905.6 438.6 %reduce-scatter.35.cloned.1.call-start = ((), (), s32[]{:S(2)}) async-start(), calls=%async_computation.26 | async-start | bytes 3342336
  913.2 5.0 copy-start.1
  913.2 5.1 copy-start.8
  918.2 495.0 %reduce-scatter.29.cloned.1.call-start = ((), (), s32[]{:S(2)}) async-start(), calls=%async_computation.23 | async-start | bytes 1114112
  923.8 83.2 %copy-start.11 = (f32[1024,8]{0,1:T(8,128)S(1)}, f32[1024,8]{0,1:T(8,128)}, u32[]{:S(2)}) copy-start(f32[1024,8]{0,1:T(8,128)} %copy-done.10) | copy-start | bytes 98308
  923.8 83.2 %copy-start.12 = (f32[1024,8]{0,1:T(8,128)S(1)}, f32[1024,8]{0,1:T(8,128)}, u32[]{:S(2)}) copy-start(f32[1024,8]{0,1:T(8,128)} %get-tuple-element.1457) | copy-start | bytes 98308
  925.2 567.6 %reduce-scatter.27.cloned.1.call-start = ((), (), s32[]{:S(2)}) async-start(), calls=%async_computation.22 | async-start | bytes 3342336 | tf_op jit(solution)/shard_map/reduce_scatter | solution.py:346
  1110.5 3.8 copy-start.21
  1119.1 428.9 %reduce-scatter.25.cloned.1.call-start = ((), (), s32[]{:S(2)}) async-start(), calls=%async_computation.21 | async-start | bytes 4718592 | tf_op jit(solution)/shard_map/reduce_scatter | solution.py:365
  1119.4 9.2 copy-start.22
  1119.4 9.2 copy-start.24
  1128.5 5.8 copy-start.3
  1139.0 4.6 copy-start.5
  1158.0 475.7 %reduce-scatter.19.cloned.1.call-start = ((), (), s32[]{:S(2)}) async-start(), calls=%async_computation.17 | async-start | bytes 4718592 | tf_op jit(solution)/shard_map/reduce_scatter | solution.py:256
  1158.3 5.9 copy-start.7
  1167.4 0.7 copy-start.23
  1167.4 380.6 %copy-start = (bf16[128,2048]{1,0:T(8,128)(2,1)S(1)}, bf16[128,2048]{1,0:T(8,128)(2,1)}, u32[]{:S(2)}) copy-start(bf16[128,2048]{1,0:T(8,128)(2,1)} %param.28) | copy-start | bytes 1572868
  1167.4 380.6 %copy-start.13 = (f32[2048]{0:T(1024)S(1)}, f32[2048]{0:T(1024)}, u32[]{:S(2)}) copy-start(f32[2048]{0:T(1024)} %param.29) | copy-start | bytes 24580
  1167.4 380.6 %copy-start.15 = (f32[128]{0:T(128)S(1)}, f32[128]{0:T(128)}, u32[]{:S(2)}) copy-start(f32[128]{0:T(128)} %copy-done.14) | copy-start | bytes 1540
  1167.4 380.6 %copy-start.17 = (f32[128]{0:T(128)S(1)}, f32[128]{0:T(128)}, u32[]{:S(2)}) copy-start(f32[128]{0:T(128)} %copy-done.16) | copy-start | bytes 1540
  1167.5 466.2 %copy-start.6 = (bf16[128,2048]{1,0:T(8,128)(2,1)S(1)}, bf16[128,2048]{1,0:T(8,128)(2,1)}, u32[]{:S(2)}) copy-start(bf16[128,2048]{1,0:T(8,128)(2,1)} %param.37) | copy-start | bytes 1572868
Sparse Core Ops, SparseCore 0:
  10.5 56.0 all-gather.11
  68.8 50.7 all-gather.9
  121.9 44.6 all-gather.17
  168.0 50.7 all-gather.25
  221.1 71.9 all-gather.15
  296.0 70.4 all-gather.13
  368.7 50.8 all-gather.19
  421.8 51.7 all-gather.21
  475.9 51.6 all-gather.23
  857.1 147.7 reduce-scatter.20
  1009.2 101.2 reduce-scatter.22
  1114.4 73.7 reduce-scatter.30
  1192.2 74.0 reduce-scatter.32
  1270.1 74.0 reduce-scatter.34
  1348.4 64.7 reduce-scatter.28
  1417.6 75.0 reduce-scatter.26
  1495.1 52.8 reduce-scatter.24
  1550.4 52.7 reduce-scatter.18
where the time goes:
time: 1660 us; the launch traced here: 1640 us
  waiting for transfers between devices  812 us (49%)
  matrix products  185 us (11%)
  loops' own time  173 us (10%)
  other arithmetic  157 us (9%)
  local copies, waits for them, and re-layouts  155 us (9%)
  blocking collectives  145 us (9%)
    unnamed x22, waiting for transfers between devices  242 us
    another operation x6, loops' own time, sweep(): return lax.scan(row_slot, carry, jnp.arange(LB, dtype=jnp.int32))  125 us
    unnamed x2, blocking collectives  118 us
    reduce_scatter x1, waiting for transfers between devices, body(): lax.psum_scatter(value_grads.astype(jnp.bfloat16), 'tok', scatter_dimensi...  103 us
    reduce_scatter x1, waiting for transfers between devices, body(): lax.psum_scatter(key_grads.astype(jnp.bfloat16), 'tok', scatter_dimension...  79.6 us
    all_gather x1, waiting for transfers between devices, body(): lax.all_gather(value_rows, 'tok', axis=0, tiled=True)  69.7 us
    all_gather x1, waiting for transfers between devices, body(): lax.all_gather(key_rows, 'tok', axis=0, tiled=True)  61.4 us
    reduce_scatter x1, waiting for transfers between devices, body(): lax.psum_scatter(grad_shifted.astype(jnp.bfloat16), 'br', scatter_dimensi...  53.6 us
  transfers between devices with their start and end apart: 18, of which 14 were waited for; matrix products, arithmetic and copies ran while one was open for 30% of the time, Pallas kernels for 0%

commit v1 on v0

v1 whole, which is shorter than its diff:
```python
import functools

import jax
import jax.numpy as jnp
from jax import lax
from jax.experimental import pallas as pl
from jax.experimental.pallas import tpu as pltpu
from jax.sharding import PartitionSpec as P

HD = 64
ROT = 16
BLK = 512
LB = 8
EPSILON = 1e-05
ROPE_BASE = 10000.0
MASKED = -1e30
BF = jnp.bfloat16
F32 = jnp.float32
NN = (((1,), (0,)), ((), ()))
NT = (((1,), (1,)), ((), ()))
TN = (((0,), (0,)), ((), ()))
VMEM = pl.BlockSpec(memory_space=pltpu.VMEM)
SMEM = pl.BlockSpec(memory_space=pltpu.SMEM)


def dot(left, right, dims):
    return lax.dot_general(left, right, dims, preferred_element_type=F32)


def block_info(block, long_blocks):
    is_long = block < long_blocks
    place = jnp.where(is_long, block % LB, (block - long_blocks) % 2)
    return is_long, place, block - place


def lane_half(packed, half, upper):
    piece = packed[:, half * HD : (half + 1) * HD]
    zero = jnp.zeros_like(piece)
    return jnp.concatenate([zero, piece] if upper else [piece, zero], axis=1)


def allowed_pairs(place, step, limit):
    key_pos = step * BLK + lax.broadcasted_iota(jnp.int32, (BLK, BLK), 0)
    query_pos = place * BLK + lax.broadcasted_iota(jnp.int32, (BLK, BLK), 1)
    return (key_pos <= query_pos) & (key_pos < limit)


def attn_fwd_kernel(long_blocks, qblk, qlim, kslot, q_ref, kv_ref, ot_ref, lse_ref, o_ref):
    def pack(i, unused):
        packed = q_ref[i]
        for half in range(2):
            slot = 2 * i + half
            is_long, place, first = block_info(qblk[slot], long_blocks)
            limit = qlim[slot]
            queries = lane_half(packed, half, False) * jnp.asarray(0.125, BF)

            def step(j, carry, masked):
                top, total, acc = carry
                rows = pl.ds(pl.multiple_of(kslot[first + j] * BLK, BLK), BLK)
                kv = kv_ref[rows, :]
                scores = dot(kv, queries, NT)
                if masked:
                    scores = jnp.where(allowed_pairs(place, j, limit), scores, MASKED)
                new_top = jnp.maximum(top, jnp.max(scores, axis=0, keepdims=True))
                fade = jnp.exp(top - new_top)
                probs = jnp.exp(scores - new_top)
                total = total * fade + jnp.sum(probs, axis=0, keepdims=True)
                acc = acc * fade + dot(kv, probs.astype(BF), TN)
                return new_top, total, acc

            free = jnp.where(is_long, place, 0)
            carry = (
                jnp.full((1, BLK), MASKED, F32),
                jnp.zeros((1, BLK), F32),
                jnp.zeros((2 * HD, BLK), F32),
            )
            carry = lax.fori_loop(0, free, lambda j, c: step(j, c, False), carry)
            top, total, acc = lax.fori_loop(free, place + 1, lambda j, c: step(j, c, True), carry)
            lse_ref[slot] = top + jnp.log(total)
            ot_ref[i, half * HD : (half + 1) * HD, :] = acc[HD:, :] / total
        o_ref[i] = jnp.transpose(ot_ref[i]).astype(BF)
        return unused

    lax.fori_loop(0, q_ref.shape[0], pack, 0)


def attn_fwd(qblk, qlim, kslot, q, kv, long_blocks):
    n = q.shape[0]
    return pl.pallas_call(
        functools.partial(attn_fwd_kernel, long_blocks),
        out_shape=(
            jax.ShapeDtypeStruct((n, 2 * HD, BLK), F32),
            jax.ShapeDtypeStruct((2 * n, 1, BLK), F32),
            jax.ShapeDtypeStruct((n, BLK, 2 * HD), BF),
        ),
        in_specs=[SMEM, SMEM, SMEM, VMEM, VMEM],
        out_specs=(VMEM, VMEM, VMEM),
        compiler_params=pltpu.CompilerParams(vmem_limit_bytes=48 * 2**20),
        cost_estimate=pl.CostEstimate(
            flops=int(20e9), bytes_accessed=8 * 2**20, transcendentals=8 * 2**20
        ),
        name="attn_fwd",
    )(qblk, qlim, kslot, q, kv)


def attn_bwd_kernel(
    long_blocks, qblk, qlim, kslot, q_ref, do_ref, kv_ref, ot_ref, lse_ref, dq_ref, dkv_ref, acc, dqt
):
    acc[...] = jnp.zeros_like(acc)

    def pack(i, unused):
        q_packed = q_ref[i]
        d_packed = do_ref[i]
        d_turned = jnp.transpose(d_packed.astype(F32))
        for half in range(2):
            slot = 2 * i + half
            is_long, place, first = block_info(qblk[slot], long_blocks)
            limit = qlim[slot]
            queries = lane_half(q_packed, half, False) * jnp.asarray(0.125, BF)
            grads = lane_half(d_packed, half, True)
            both = jnp.concatenate([queries, grads], axis=0)
            lanes = slice(half * HD, (half + 1) * HD)
            delta = jnp.sum(d_turned[lanes] * ot_ref[i, lanes, :], axis=0, keepdims=True)
            lse = lse_ref[slot]

            def step(j, total, masked):
                rows = pl.ds(pl.multiple_of(kslot[first + j] * BLK, BLK), BLK)
                kv = kv_ref[rows, :]
                scores = dot(kv, queries, NT)
                if masked:
                    scores = jnp.where(allowed_pairs(place, j, limit), scores, MASKED)
                probs = jnp.exp(scores - lse)
                ds = (probs * (dot(kv, grads, NT) - delta)).astype(BF)
                acc[rows, :] += dot(jnp.concatenate([ds, probs.astype(BF)], axis=1), both, NN)
                return total + dot(kv, ds, TN)

            free = jnp.where(is_long, place, 0)
            total = lax.fori_loop(
                0, free, lambda j, c: step(j, c, False), jnp.zeros((2 * HD, BLK), F32)
            )
            total = lax.fori_loop(free, place + 1, lambda j, c: step(j, c, True), total)
            dqt[lanes, :] = total[:HD, :] * 0.125
        dq_ref[i] = jnp.transpose(dqt[...]).astype(BF)
        return unused

    lax.fori_loop(0, q_ref.shape[0], pack, 0)

    def finish(i, unused):
        rows = pl.ds(pl.multiple_of(i * BLK, BLK), BLK)
        dkv_ref[rows, :] = acc[rows, :].astype(BF)
        return unused

    lax.fori_loop(0, kv_ref.shape[0] // BLK, finish, 0)


def attn_bwd(qblk, qlim, kslot, q, do, kv, ot, lse, long_blocks):
    n = q.shape[0]
    return pl.pallas_call(
        functools.partial(attn_bwd_kernel, long_blocks),
        out_shape=(
            jax.ShapeDtypeStruct((n, BLK, 2 * HD), BF),
            jax.ShapeDtypeStruct(kv.shape, BF),
        ),
        in_specs=[SMEM, SMEM, SMEM, VMEM, VMEM, VMEM, VMEM, VMEM],
        out_specs=(VMEM, VMEM),
        scratch_shapes=[pltpu.VMEM(kv.shape, F32), pltpu.VMEM((2 * HD, BLK), F32)],
        compiler_params=pltpu.CompilerParams(vmem_limit_bytes=56 * 2**20),
        cost_estimate=pl.CostEstimate(
            flops=int(30e9), bytes_accessed=12 * 2**20, transcendentals=8 * 2**20
        ),
        name="attn_bwd",
    )(qblk, qlim, kslot, q, do, kv, ot, lse)


def turn(values, cos, sin, copies):
    width = values.shape[1]
    lane = lax.broadcasted_iota(jnp.int32, values.shape, 1) % HD
    partner = jnp.where(
        lane < ROT // 2,
        pltpu.roll(values, width - ROT // 2, 1),
        pltpu.roll(values, ROT // 2, 1),
    )
    cos = jnp.concatenate([cos] * copies, axis=1)
    sin = jnp.concatenate([sin] * copies, axis=1)
    return values * cos + partner * sin


def project_kernel(heads, x_ref, w_ref, b_ref, cq, sq, ck, sk, q_ref, kv_ref):
    width = heads * HD
    parts = []
    for slot in range(2):
        joined = dot(x_ref[slot], w_ref[...], NN) + b_ref[...]
        parts.append(
            turn(joined[:, :width], cq[slot], sq[slot], heads // 2).astype(BF)
        )
        kv = turn(joined[:, width:], ck[slot], sk[slot], heads).astype(BF)
        for head in range(heads):
            kv_ref[head, slot] = kv[:, head * 2 * HD : (head + 1) * 2 * HD]
    for head in range(heads):
        lanes = slice(head * HD, (head + 1) * HD)
        q_ref[head] = jnp.concatenate([parts[0][:, lanes], parts[1][:, lanes]], axis=1)


def project(x, w, bias, tables, heads):
    tile = 256
    width = 3 * heads * HD
    depth = x.shape[1]
    table = pl.BlockSpec((2, tile, 2 * HD), lambda i: (0, i, 0))
    return pl.pallas_call(
        functools.partial(project_kernel, heads),
        grid=(BLK // tile,),
        out_shape=(
            jax.ShapeDtypeStruct((heads, BLK, 2 * HD), BF),
            jax.ShapeDtypeStruct((heads, 2, BLK, 2 * HD), BF),
        ),
        in_specs=[
            pl.BlockSpec((2, tile, depth), lambda i: (0, i, 0)),
            pl.BlockSpec((depth, width), lambda i: (0, 0)),
            pl.BlockSpec((1, width), lambda i: (0, 0)),
            table,
            table,
            table,
            table,
        ],
        out_specs=(
            pl.BlockSpec((heads, tile, 2 * HD), lambda i: (0, i, 0)),
            pl.BlockSpec((heads, 2, tile, 2 * HD), lambda i: (0, 0, i, 0)),
        ),
        compiler_params=pltpu.CompilerParams(vmem_limit_bytes=40 * 2**20),
        name="project",
    )(x.reshape(2, BLK, depth), w, bias, *tables)


def unturn_kernel(heads, dq_ref, dkv_ref, cq, sq, ck, sk, out_ref, sum_ref):
    width = heads * HD
    sums = jnp.zeros((1, 3 * width), F32)
    for slot in range(2):
        lanes = slice(slot * HD, (slot + 1) * HD)
        q = jnp.concatenate([dq_ref[head][:, lanes] for head in range(heads)], axis=1)
        q = turn(q.astype(F32), cq[slot], -sq[slot], heads // 2).astype(BF)
        kv = jnp.concatenate([dkv_ref[head, slot] for head in range(heads)], axis=1)
        kv = turn(kv.astype(F32), ck[slot], -sk[slot], heads).astype(BF)
        both = jnp.concatenate([q, kv], axis=1)
        out_ref[slot] = both
        sums += jnp.sum(both.astype(F32), axis=0, keepdims=True)

    @pl.when(pl.program_id(0) == 0)
    def _():
        sum_ref[...] = jnp.zeros_like(sum_ref)

    sum_ref[...] += sums


def unturn(dq, dkv, tables, heads):
    tile = 256
    width = 3 * heads * HD
    table = pl.BlockSpec((2, tile, 2 * HD), lambda i: (0, i, 0))
    out, sums = pl.pallas_call(
        functools.partial(unturn_kernel, heads),
        grid=(BLK // tile,),
        out_shape=(
            jax.ShapeDtypeStruct((2, BLK, width), BF),
            jax.ShapeDtypeStruct((1, width), F32),
        ),
        in_specs=[
            pl.BlockSpec((heads, tile, 2 * HD), lambda i: (0, i, 0)),
            pl.BlockSpec((heads, 2, tile, 2 * HD), lambda i: (0, 0, i, 0)),
            table,
            table,
            table,
            table,
        ],
        out_specs=(
            pl.BlockSpec((2, tile, width), lambda i: (0, i, 0)),
            pl.BlockSpec((1, width), lambda i: (0, 0)),
        ),
        compiler_params=pltpu.CompilerParams(vmem_limit_bytes=40 * 2**20),
        name="unturn",
    )(dq, dkv, *tables)
    return out.reshape(2 * BLK, width), sums


def tok_perm(dy, dz, dc):
    pairs = []
    for t in range(16):
        y, z, c = t // 4, (t // 2) % 2, t % 2
        pairs.append((t, ((y + dy) % 4) * 4 + (z ^ dz) * 2 + (c ^ dc)))
    return pairs


def pick(array, index):
    return lax.dynamic_index_in_dim(array, index, 0, keepdims=False)


def spread_heads(by_head, y):
    parts = [pick(by_head, y)]
    for d in range(1, 4):
        parts.append(lax.ppermute(pick(by_head, (y + d) % 4), "tok", tok_perm(d, 0, 0)))
    return parts


def return_heads(parts, y):
    back = [parts[0]]
    for d in range(1, 4):
        back.append(lax.ppermute(parts[d], "tok", tok_perm(4 - d, 0, 0)))
    stacked = jnp.stack(back + back)
    return lax.dynamic_slice_in_dim(stacked, (4 - y) % 4, 4, 0)


def rotary_tables(positions, long_shape):
    half = ROT // 2
    frequency = ROPE_BASE ** (-(jnp.arange(half).astype(F32) * 2.0 / ROT))
    angles = positions.astype(F32)[:, None] * frequency[None, :]
    cos, sin = jnp.cos(angles), jnp.sin(angles)
    rows = positions.shape[0]
    one = jnp.ones((rows, HD - ROT), F32)
    zero = jnp.zeros((rows, HD - ROT), F32)
    cos64 = jnp.concatenate([cos, cos, one], axis=1)
    sin64 = jnp.concatenate([-sin, sin, zero], axis=1)
    tables = (
        jnp.concatenate([cos64, cos64], axis=1),
        jnp.concatenate([sin64, sin64], axis=1),
        jnp.concatenate([cos64, jnp.ones((rows, HD), F32)], axis=1),
        jnp.concatenate([sin64, jnp.zeros((rows, HD), F32)], axis=1),
    )
    return tuple(t.reshape(2, BLK, 2 * HD) for t in tables)


def body(
    tokens,
    norm_gain,
    norm_bias,
    qkv_weight,
    qkv_bias,
    out_weight,
    gate_weight,
    up_weight,
    down_weight,
    cotangent,
    block_map,
    lengths,
):
    tok = lax.axis_index("tok")
    y, z, c = tok // 4, (tok // 2) % 2, tok % 2
    total_blocks = block_map.shape[0]
    long_blocks = total_blocks // 2
    rows = tokens.shape[0]
    depth = tokens.shape[1]
    wrows = qkv_weight.shape[1]
    heads = qkv_bias.shape[1]
    width = heads * HD
    hidden_width = gate_weight.shape[1]
    main = hidden_width // 128 * 128
    tail = hidden_width - main

    residual = tokens.astype(F32)
    centred = residual - jnp.mean(residual, axis=-1, keepdims=True)
    inverse = lax.rsqrt(jnp.mean(centred * centred, axis=-1, keepdims=True) + EPSILON)
    normed = centred * inverse
    shifted = (normed * norm_gain + norm_bias).astype(BF)

    kv_shard = jnp.stack(
        [w.reshape(wrows, heads, HD) for w in (qkv_weight[1], qkv_weight[2])], axis=2
    ).reshape(wrows, 2 * width)
    bias_row = jnp.pad(qkv_bias.reshape(1, -1), ((0, wrows - 1), (0, 128 - qkv_bias.size)))
    qkv_shard = jnp.concatenate([qkv_weight[0], kv_shard, bias_row], axis=1)
    gu_shard = jnp.concatenate(
        [gate_weight[:, :main], up_weight[:, :main], gate_weight[:, main:], up_weight[:, main:]],
        axis=1,
    )
    do_shard = jnp.concatenate(
        [
            jnp.transpose(down_weight),
            jnp.zeros((wrows, 128 - tail), BF),
            jnp.transpose(out_weight),
        ],
        axis=1,
    )
    qkv_full = lax.all_gather(qkv_shard, "tok", axis=0, tiled=True)
    x = lax.all_gather(shifted, "br", axis=0, tiled=True)
    grad = lax.all_gather(cotangent, "br", axis=0, tiled=True)
    do_full = lax.all_gather(do_shard, "tok", axis=0, tiled=True)
    gu_full = lax.all_gather(gu_shard, "tok", axis=0, tiled=True)

    bias = qkv_full.reshape(16, wrows, -1)[:, 0, 3 * width : 3 * width + qkv_bias.size]
    bias = jnp.transpose(bias.reshape(16, 3, heads, 4), (1, 2, 0, 3)).reshape(3, heads, HD)
    bias = jnp.concatenate(
        [bias[0].reshape(1, width), jnp.stack([bias[1], bias[2]], axis=1).reshape(1, 2 * width)],
        axis=1,
    ).astype(F32)

    slot_table = jnp.arange(total_blocks, dtype=jnp.int32)
    slot_of = jnp.sum(
        jnp.where(block_map[None, :] == slot_table[:, None], slot_table[None, :], 0), axis=1
    )
    owner = slot_of // 2
    key_index = (((owner // 2) % 2 ^ z) * 2 + (owner % 2 ^ c)) * 4 + (y - owner // 4) % 4
    key_slot = (key_index * 2 + slot_of % 2).astype(jnp.int32)
    from_tok = ((y - jnp.arange(4, dtype=jnp.int32)) % 4) * 4 + z * 2 + c
    my_queries = jnp.stack([2 * from_tok, 2 * from_tok + 1], axis=1).reshape(-1)
    query_block = jnp.sum(
        jnp.where(my_queries[:, None] == slot_table[None, :], block_map[None, :], 0), axis=1
    ).astype(jnp.int32)
    query_row = jnp.where(
        query_block < long_blocks,
        query_block // LB,
        long_blocks // LB + (query_block - long_blocks) // 2,
    )
    row_table = jnp.arange(lengths.shape[0], dtype=jnp.int32)
    query_limit = jnp.sum(
        jnp.where(query_row[:, None] == row_table[None, :], lengths[None, :], 0), axis=1
    ).astype(jnp.int32)

    my_blocks = lax.dynamic_slice_in_dim(block_map, tok * 2, 2)
    my_start = (
        jnp.where(my_blocks < long_blocks, my_blocks % LB, (my_blocks - long_blocks) % 2) * BLK
    )
    positions = (my_start[:, None] + jnp.arange(BLK, dtype=jnp.int32)[None, :]).reshape(-1)
    tables = rotary_tables(positions, long_blocks)

    q_heads, kv_heads = project(x, qkv_full, bias, tables, heads)
    joined = jnp.concatenate([q_heads, kv_heads.reshape(heads, 2 * BLK, 2 * HD)], axis=1)
    parts = jnp.stack(spread_heads(joined, y))
    q_all = parts[:, :BLK]
    kv_mine = parts[:, BLK:]
    kv_core = lax.ppermute(kv_mine, "tok", tok_perm(0, 0, 1))
    kv_far = lax.ppermute(kv_mine, "tok", tok_perm(0, 1, 0))
    kv_diag = lax.ppermute(kv_far, "tok", tok_perm(0, 0, 1))
    kv_all = jnp.stack([kv_mine, kv_core, kv_far, kv_diag]).reshape(-1, 2 * HD)

    turned, lse, o_parts = attn_fwd(query_block, query_limit, key_slot, q_all, kv_all, long_blocks)

    def to_heads(flat):
        split = flat.reshape(2, BLK, heads, HD)
        return jnp.transpose(split, (2, 1, 0, 3)).reshape(heads, BLK, 2 * HD)

    def from_heads(packed):
        split = packed.reshape(heads, BLK, 2, HD)
        return jnp.transpose(split, (2, 1, 0, 3)).reshape(2 * BLK, width)

    mixed = from_heads(return_heads([o_parts[d] for d in range(4)], y))

    down_width = do_full.shape[1] - width
    down_full = do_full[:, :down_width]
    out_full = do_full[:, down_width:]
    grad_mixed = dot(grad, out_full, NN).astype(BF)
    do_all = jnp.stack(spread_heads(to_heads(grad_mixed), y))

    both = dot(x, gu_full, NN)
    grad_hidden = dot(grad, down_full, NN)
    ends = both[:, 2 * main :]
    gate = jnp.concatenate([both[:, :main], ends[:, :tail]], axis=1)
    up = jnp.concatenate([both[:, main : 2 * main], ends[:, tail:]], axis=1)
    gh = grad_hidden[:, :hidden_width]
    sig = jax.nn.sigmoid(gate)
    hidden = (gate * sig * up).astype(BF)
    hidden = jnp.pad(hidden, ((0, 0), (0, down_width - hidden_width)))
    grad_gate = (gh * up * sig * (1.0 + gate * (1.0 - sig))).astype(BF)
    grad_up = (gh * gate * sig).astype(BF)
    grad_both = jnp.concatenate(
        [grad_gate[:, :main], grad_up[:, :main], grad_gate[:, main:], grad_up[:, main:]], axis=1
    )
    branches = (dot(hidden, down_full, NT) + dot(mixed, out_full, NT)).astype(BF)
    summed = lax.psum_scatter(branches, "br", scatter_dimension=0, tiled=True)
    result = (residual + summed.astype(F32)).astype(BF)
    grad_do = jnp.concatenate([dot(grad, hidden, TN), dot(grad, mixed, TN)], axis=1).astype(BF)
    grad_gu = dot(x, grad_both, TN).astype(BF)
    grad_do = lax.psum_scatter(grad_do, "tok", scatter_dimension=0, tiled=True)
    grad_gu = lax.psum_scatter(grad_gu, "tok", scatter_dimension=0, tiled=True)

    dq_parts, dkv_all = attn_bwd(
        query_block, query_limit, key_slot, q_all, do_all, kv_all, turned, lse, long_blocks
    )
    dkv = dkv_all.reshape(2, 2, 4 * 2 * BLK, 2 * HD)
    near = dkv[:, 0].astype(F32) + lax.ppermute(dkv[:, 1], "tok", tok_perm(0, 0, 1)).astype(F32)
    far = lax.ppermute(near[1].astype(BF), "tok", tok_perm(0, 1, 0))
    mine = (near[0] + far.astype(F32)).astype(BF).reshape(4, 2 * BLK, 2 * HD)
    back = return_heads([jnp.concatenate([dq_parts[d], mine[d]], axis=0) for d in range(4)], y)
    dq_heads = back[:, :BLK]
    dkv_heads = back[:, BLK:].reshape(heads, 2, BLK, 2 * HD)
    grad_joined, bias_sums = unturn(dq_heads, dkv_heads, tables, heads)
    grad_shifted = (
        dot(grad_both, gu_full, NT) + dot(grad_joined, qkv_full[:, : 3 * width], NT)
    ).astype(BF)
    my_grad_shifted = lax.psum_scatter(
        grad_shifted, "br", scatter_dimension=0, tiled=True
    ).astype(F32)
    grad_qkv = dot(x, grad_joined, TN).astype(BF)
    qsum = bias_sums[0, :width].reshape(1, heads, HD)
    kvsum = jnp.transpose(bias_sums[0, width:].reshape(heads, 2, HD), (1, 0, 2))
    bsum = jnp.concatenate([qsum, kvsum], axis=0).reshape(3, heads, 16, 4)
    bsum = jnp.transpose(bsum, (2, 0, 1, 3)).reshape(16, 1, qkv_bias.size).astype(BF)
    bsum = jnp.pad(bsum, ((0, 0), (0, wrows - 1), (0, 128 - qkv_bias.size)))
    grad_qkv = jnp.concatenate([grad_qkv, bsum.reshape(16 * wrows, 128)], axis=1)
    grad_qkv = lax.psum_scatter(grad_qkv, "tok", scatter_dimension=0, tiled=True).astype(F32)

    grad_bias_out = grad_qkv[0, 3 * width : 3 * width + qkv_bias.size].reshape(qkv_bias.shape)
    gkv = grad_qkv[:, width : 3 * width].reshape(wrows, heads, 2, HD)
    grad_qkv_out = jnp.stack(
        [
            grad_qkv[:, :width],
            gkv[:, :, 0].reshape(wrows, width),
            gkv[:, :, 1].reshape(wrows, width),
        ]
    )
    grad_do = grad_do.astype(F32)
    grad_gu = grad_gu.astype(F32)
    grad_down_out = jnp.transpose(grad_do[:, :hidden_width])
    grad_out_out = jnp.transpose(grad_do[:, down_width:])
    grad_gate_out = jnp.concatenate(
        [grad_gu[:, :main], grad_gu[:, 2 * main : 2 * main + tail]], axis=1
    )
    grad_up_out = jnp.concatenate(
        [grad_gu[:, main : 2 * main], grad_gu[:, 2 * main + tail :]], axis=1
    )

    gain_part = jnp.sum(my_grad_shifted * normed, axis=0)
    bias_part = jnp.sum(my_grad_shifted, axis=0)
    grad_normed = my_grad_shifted * norm_gain
    grad_tokens = cotangent.astype(F32) + inverse * (
        grad_normed
        - jnp.mean(grad_normed, axis=-1, keepdims=True)
        - normed * jnp.mean(grad_normed * normed, axis=-1, keepdims=True)
    )
    grad_gain, grad_bias = (
        lax.psum_scatter(gain_part, ("tok", "br"), scatter_dimension=0, tiled=True),
        lax.psum_scatter(bias_part, ("tok", "br"), scatter_dimension=0, tiled=True),
    )
    return (
        result,
        grad_tokens,
        grad_gain,
        grad_bias,
        grad_qkv_out,
        grad_bias_out,
        grad_out_out,
        grad_gate_out,
        grad_up_out,
        grad_down_out,
    )


def solution(mesh):
    in_specs = (
        P(("tok", "br"), None),
        P(),
        P(),
        P(None, "tok", "br"),
        P(None, "br", "tok"),
        P("br", "tok"),
        P("tok", "br"),
        P("tok", "br"),
        P("br", "tok"),
        P(("tok", "br"), None),
        P(),
        P(),
    )
    out_specs = (
        P(("tok", "br"), None),
        P(("tok", "br"), None),
        P(("tok", "br")),
        P(("tok", "br")),
        P(None, "tok", "br"),
        P(None, "br", "tok"),
        P("br", "tok"),
        P("tok", "br"),
        P("tok", "br"),
        P("br", "tok"),
    )
    return jax.shard_map(body, mesh=mesh, in_specs=in_specs, out_specs=out_specs, check_vma=False)
```

time: 1660 us -> 782 us (0.47)
  waiting for transfers between devices: 812 us -> 409 us
  loops' own time: 173 us -> 0 us
  other arithmetic: 157 us -> 40.3 us
  matrix products: 185 us -> 73.5 us
  local copies, waits for them, and re-layouts: 155 us -> 60.6 us
  Pallas kernels: 0 us -> 65.6 us
  blocking collectives: 145 us -> 82.9 us
  starting transfers between devices: 1.54 us -> 30.1 us
    unnamed x22 -> x12, waiting for transfers between devices: 242 us -> 51.8 us
    another operation x56 -> x0, loops' own time: 173 us -> none  [the longest x6 125 us: sweep(): return lax.scan(row_slot, carry, jnp.arange(LB, dtype=jnp.int32))]
    reduce_scatter x5 -> x3, waiting for transfers between devices: 278 us -> 139 us  [the longest x1 87.6 us: body(): grad_gu = lax.psum_scatter(grad_gu, 'tok', scatter_dimension=0, tiled=True)]
    all_gather x9 -> x5, waiting for transfers between devices: 291 us -> 169 us  [the longest x1 61 us: body(): do_full = lax.all_gather(do_shard, 'tok', axis=0, tiled=True)]
    dot_general x91 -> x11, matrix products: 185 us -> 73.5 us  [dot(): return lax.dot_general(left, right, dims, preferred_element_type=F32)]
    dynamic_slice x160 -> x6, local copies, waits for them, and re-layouts: 77 us -> 0.66 us  [the longest x4 0.4 us: pick(): return lax.dynamic_index_in_dim(array, index, 0, keepdims=False)]
    pallas_call x0 -> x4, Pallas kernels: none -> 65.6 us  [the longest x1 33.3 us: attn_bwd(): pl.pallas_call(functools.partial(attn_bwd_kernel, long_blocks), out_shape...]
    reduce_or x48 -> x0, other arithmetic: 48.8 us -> none  [guarded(): return lax.cond(jnp.any(allowed), update, keep_same, state_in)]
  transfers between devices with their start and end apart: 18 -> 27, of which waited for: 14 -> 13; matrix products, arithmetic and copies ran while one was open for 30% -> 19% of each run, Pallas kernels for 0% -> 8%
where the time goes in v1:
time: 782 us; the launch traced here: 777 us
  waiting for transfers between devices  409 us (52%)
  blocking collectives  82.9 us (11%)
  matrix products  73.5 us (9%)
  Pallas kernels  65.6 us (8%)
  local copies, waits for them, and re-layouts  60.6 us (8%)
  other arithmetic  40.3 us (5%)
  starting transfers between devices  30.1 us (4%)
  between operations  15.9 us (2%)
    reduce_scatter x1, waiting for transfers between devices, body(): grad_gu = lax.psum_scatter(grad_gu, 'tok', scatter_dimension=0, tiled=True)  87.6 us
    unnamed x1, blocking collectives  82.9 us
    dot_general x11, matrix products, dot(): return lax.dot_general(left, right, dims, preferred_element_type=F32)  73.5 us
    all_gather x1, waiting for transfers between devices, body(): do_full = lax.all_gather(do_shard, 'tok', axis=0, tiled=True)  61 us
    unnamed x12, waiting for transfers between devices  51.8 us
    reduce_scatter x1, waiting for transfers between devices, body(): lax.psum_scatter(grad_shifted, 'br', scatter_dimension=0, tiled=True)  51.8 us
    all_gather x1, waiting for transfers between devices, body(): x = lax.all_gather(shifted, 'br', axis=0, tiled=True)  51.4 us
    all_gather x1, waiting for transfers between devices, body(): qkv_full = lax.all_gather(qkv_shard, 'tok', axis=0, tiled=True)  44.6 us
  transfers between devices with their start and end apart: 27, of which 13 were waited for; matrix products, arithmetic and copies ran while one was open for 19% of the time, Pallas kernels for 8%

profile of v1, /device:TPU:1, one launch (start us, length us, event | category | flops | bytes accessed | tf_op | source)
XLA Modules:
  0.0 777.4 jit_solution(5684694161007478935)
XLA Ops:
  24.4 44.6 %all-gather.12.cloned.1.call-done.w_ref = bf16[2048,896]{1,0:T(8,128)(2,1)} async-done(((bf16[128,896]{1,0:T(8,128)(2,1)}), bf16[2048,896]{1,0:T(8,128)(2,1)}) %all-gather.12.cloned.1.call-update) | async-done | bytes 3670032 | tf_op jit(solution)/shard_map/all_gather | solution.py:379
  70.6 51.4 %all-gather.6.cloned.1.call-done = bf16[1024,2048]{1,0:T(8,128)(2,1)} async-done(((bf16[128,2048]{1,0:T(8,128)(2,1)}), bf16[1024,2048]{1,0:T(8,128)(2,1)}) %all-gather.6.cloned.1.call-update) | async-done | bytes 4194320 | tf_op jit(solution)/shard_map/all_gather | solution.py:380
  122.0 2.2 copy-done
  126.2 4.9 project.1
  133.4 2.4 collective-permute-start.1
  137.4 6.3 collective-permute-done
  143.7 9.4 %collective-permute-done.1 = bf16[1536,128]{1,0:T(8,128)(2,1)S(1)} collective-permute-done((bf16[1536,128]{1,0:T(8,128)(2,1)}, bf16[1536,128]{1,0:T(8,128)(2,1)S(1)}, u32[]{:S(2)}, u32[]{:S(2)}) %collective-permute-start.1) | collective-permute-done | bytes 393248 | tf_op jit(solution)/shard_map/ppermute | solution.py:298
  153.1 2.1 pad_maximum_fusion.5
  155.3 2.6 collective-permute-start.4
  161.1 2.3 fusion.88
  163.4 11.7 %all-gather.14.cloned.1.call-done = bf16[1024,2048]{1,0:T(8,128)(2,1)} async-done(((bf16[128,2048]{1,0:T(8,128)(2,1)}), bf16[1024,2048]{1,0:T(8,128)(2,1)}) %all-gather.14.cloned.1.call-update) | async-done | bytes 4194320 | tf_op jit(solution)/shard_map/all_gather | solution.py:381
  175.1 61.0 %all-gather.10.cloned.1.call-done = bf16[2048,1024]{0,1:T(8,128)(2,1)} async-done(((bf16[128,1024]{0,1:T(8,128)(2,1)}), bf16[2048,1024]{0,1:T(8,128)(2,1)}) %all-gather.10.cloned.1.call-update) | async-done | bytes 4194320 | tf_op jit(solution)/shard_map/all_gather | solution.py:382
  236.1 4.6 fusion.21
  244.4 2.3 collective-permute-start.10
  246.9 8.3 %fusion.9 = f32[1024,768]{1,0:T(8,128)} fusion(bf16[1024,2048]{1,0:T(8,128)(2,1)} %all-gather.14.cloned.1.call-done, bf16[2048,1024]{0,1:T(8,128)(2,1)} %all-gather.10.cloned.1.call-done), kind=kOutput, calls=%fused_computation.33 | convolution fusion | flops 3221225472 | bytes 10485760 | tf_op jit(solution)/shard_map/dot_general | solution.py:27
  257.1 3.7 pad_maximum_fusion
  260.9 24.8 %attn_fwd.1 = (f32[4,128,512]{2,1,0:T(8,128)S(1)}, f32[8,1,512]{2,1,0:T(1,128)S(1)}, bf16[4,512,128]{2,1,0:T(8,128)(2,1)S(1)}) custom-call(s32[8]{0:T(128)S(1)} %select_reduce_fusion.2.qblk, s32[8]{0:T(128)S(1)} %select_reduce_fusion.1.qlim, s32[32]{0:T(128)S(1)} %fusion.52.kslot, bf16[4,512,128]{2,1,0:T(8,128)(2,1)S(1)} %pad_maximum_fusion.8.q_ref, ...), custom_call_target="tpu_custom_call" | custom-call | flops 20000000000 | bytes 8388608 | tf_op jit(solution)/shard_map/attn_fwd/pallas_call | solution.py:89
  288.0 2.5 collective-permute-start.7
  290.6 33.3 %attn_bwd.1 = (bf16[4,512,128]{2,1,0:T(8,128)(2,1)}, bf16[16384,128]{1,0:T(8,128)(2,1)}) custom-call(s32[8]{0:T(128)} %copy-done.7, s32[8]{0:T(128)} %copy-done.8, s32[32]{0:T(128)} %copy-done.4, bf16[4,512,128]{2,1,0:T(8,128)(2,1)} %copy-done.3, bf16[4,512,128]{2,1,0:T(8,128)(2,1)} %pad_maximum_fusion.9.do_ref, bf16[16384,128]{1,0:T(8,128)(2,1)} %bitcast.166, ...), custom_call_target="tpu_custom_call" | custom-call | flops 30000001024 | bytes 12582912 | tf_op jit(solution)/shard_map/attn_bwd/pallas_call | solution.py:158
  324.0 3.1 slice_bitcast_fusion.1
  327.1 9.0 %collective-permute-start.12 = (bf16[2,4096,128]{2,1,0:T(8,128)(2,1)}, bf16[2,4096,128]{2,1,0:T(8,128)(2,1)}, u32[]{:S(2)}, u32[]{:S(2)}) collective-permute-start(bf16[2,4096,128]{2,1,0:T(8,128)(2,1)} %slice_bitcast_fusion.1), channel_id=1, source_target_pairs={{0,8},{8,0},{16,24},{24,16},{32,40},{40,32},{48,56},{56,48},{64,72... | collective-permute-start | bytes 6291464 | tf_op jit(solution)/shard_map/ppermute | solution.py:475
  338.6 4.4 fusion.6
  343.1 10.6 %fusion.71 = f32[1024,1408]{1,0:T(8,128)S(1)} fusion(bf16[1024,2048]{1,0:T(8,128)(2,1)} %all-gather.6.cloned.1.call-done, bf16[2048,1408]{0,1:T(8,128)(2,1)} %all-gather.8.cloned.1.call-done), kind=kOutput, calls=%fused_computation.217 | convolution fusion | flops 5905580032 | bytes 15728640 | tf_op jit(solution)/shard_map/dot_general | solution.py:27
  355.7 3.2 multiply_convert_fusion
  358.9 2.7 convert_add_fusion
  363.8 3.7 fusion.1
  367.6 2.4 pad_maximum_fusion.1
  370.0 6.4 copy.111
  376.5 13.7 %collective-permute-done.13 = bf16[4096,128]{1,0:T(8,128)(2,1)} collective-permute-done((bf16[4096,128]{1,0:T(8,128)(2,1)S(1)}, bf16[4096,128]{1,0:T(8,128)(2,1)}, u32[]{:S(2)}, u32[]{:S(2)}) %collective-permute-start.13) | collective-permute-done | bytes 1048608 | tf_op jit(solution)/shard_map/ppermute | solution.py:476
  390.2 2.2 fusion.8
  393.2 2.1 collective-permute-start.15
  395.6 6.8 collective-permute-done.14
  404.4 10.5 %collective-permute-done.16 = bf16[1536,128]{1,0:T(8,128)(2,1)S(1)} collective-permute-done((bf16[1536,128]{1,0:T(8,128)(2,1)S(1)}, bf16[1536,128]{1,0:T(8,128)(2,1)S(1)}, u32[]{:S(2)}, u32[]{:S(2)}) %collective-permute-start.16) | collective-permute-done | bytes 393248 | tf_op jit(solution)/shard_map/ppermute | solution.py:305
  415.4 2.6 unturn.1
  420.4 6.2 convolution_convert_fusion.2
  426.5 2.1 pad_maximum_fusion.2
  428.6 6.0 copy.109
  439.2 5.0 concatenate.105
  444.1 11.0 %convolution_convert_fusion = bf16[2048,1408]{1,0:T(8,128)(2,1)} fusion(bf16[1024,2048]{1,0:T(8,128)(2,1)} %all-gather.6.cloned.1.call-done, bf16[1024,1408]{1,0:T(8,128)(2,1)} %concatenate.105), kind=kOutput, calls=%fused_computation.2 | convolution fusion | flops 5908463616 | bytes 12845056 | tf_op jit(solution)/shard_map/dot_general | solution.py:27
  455.4 9.7 %fusion.72 = f32[1024,2048]{1,0:T(8,128)S(1)} fusion(bf16[1024,1408]{1,0:T(8,128)(2,1)} %concatenate.105, bf16[2048,1408]{0,1:T(8,128)(2,1)} %all-gather.8.cloned.1.call-done), kind=kOutput, calls=%fused_computation.218 | convolution fusion | flops 5905580032 | bytes 17039360 | tf_op jit(solution)/shard_map/dot_general | solution.py:27
  465.1 5.1 add_convert_fusion
  471.7 5.4 fusion.4
  477.2 4.6 add_convert_fusion.1
  484.4 51.0 %reduce-scatter.16.cloned.1.call-done = bf16[128,896]{1,0:T(8,128)(2,1)} async-done(((bf16[2048,896]{1,0:T(8,128)(2,1)}), bf16[128,896]{1,0:T(8,128)(2,1)}) %reduce-scatter.16.cloned.1.call-update) | async-done | bytes 229392
  538.4 87.6 %reduce-scatter.14.cloned.1.call-done = bf16[128,1408]{1,0:T(8,128)(2,1)} async-done(((bf16[2048,1408]{1,0:T(8,128)(2,1)}), bf16[128,1408]{1,0:T(8,128)(2,1)}) %reduce-scatter.14.cloned.1.call-update) | async-done | bytes 360464 | tf_op jit(solution)/shard_map/reduce_scatter | solution.py:469
  629.9 51.8 %reduce-scatter.12.cloned.1.call-done = bf16[128,2048]{1,0:T(8,128)(2,1)} async-done(((bf16[1024,2048]{1,0:T(8,128)(2,1)}), bf16[128,2048]{1,0:T(8,128)(2,1)}) %reduce-scatter.12.cloned.1.call-update) | async-done | bytes 524304 | tf_op jit(solution)/shard_map/reduce_scatter | solution.py:485
  683.2 82.9 %all-reduce.5 = (f32[2048]{0:T(1024)S(1)}, f32[2048]{0:T(1024)S(1)}) all-reduce(f32[2048]{0:T(1024)S(1)} %get-tuple-element.68, f32[2048]{0:T(1024)S(1)} %get-tuple-element.71), channel_id=4, replica_groups=mesh['tok'=16,'br'=8] {'tok','br'}, use_global_device_ids=true, to_apply=%region_10.11.clone | all-reduce | flops 4096 | bytes 32768
  767.3 2.9 fusion.26
  (270 shorter events, 66.4 us)
Async XLA Ops:
  7.2 7.7 copy-start.31
  7.2 7.7 copy-start.34
  7.2 61.7 %all-gather.12.cloned.1.call-start = ((), (), s32[]{:S(2)}) async-start(), calls=%async_computation.8 | async-start | bytes 3899392 | tf_op jit(solution)/shard_map/all_gather | solution.py:379
  9.1 6.8 slice-start
  9.2 6.8 slice-start.1
  10.2 6.9 copy-start.42
  10.2 111.8 %all-gather.6.cloned.1.call-start = ((), (), s32[]{:S(2)}) async-start(), calls=%async_computation.5 | async-start | bytes 4718592 | tf_op jit(solution)/shard_map/all_gather | solution.py:380
  11.5 7.7 copy-start.35
  14.1 161.0 %all-gather.14.cloned.1.call-start = ((), (), s32[]{:S(2)}) async-start(), calls=%async_computation.10 | async-start | bytes 4718592 | tf_op jit(solution)/shard_map/all_gather | solution.py:381
  14.8 221.3 %all-gather.10.cloned.1.call-start = ((), (), s32[]{:S(2)}) async-start(), calls=%async_computation.7 | async-start | bytes 4456448 | tf_op jit(solution)/shard_map/all_gather | solution.py:382
  15.9 327.2 %all-gather.8.cloned.1.call-start = ((), (), s32[]{:S(2)}) async-start(), calls=%async_computation.6 | async-start | bytes 6127616 | tf_op jit(solution)/shard_map/all_gather | solution.py:383
  16.8 465.0 %reduce-scatter.18.cloned.1.call-start = ((), (), s32[]{:S(2)}) async-start(), calls=%async_computation.14 | async-start | bytes 4456448
  131.1 26.7 %copy-start.41 = (s32[10]{0:T(128)S(1)}, s32[10]{0:T(128)}, u32[]{:S(2)}) copy-start(s32[10]{0:T(128)} %param.23) | copy-start | bytes 124
  132.2 11.5 %collective-permute-start = (bf16[1536,128]{1,0:T(8,128)(2,1)}, bf16[1536,128]{1,0:T(8,128)(2,1)S(1)}, u32[]{:S(2)}, u32[]{:S(2)}) collective-permute-start(bf16[1536,128]{1,0:T(8,128)(2,1)} %get-tuple-element.82), channel_id=1, source_target_pairs={{0,32},{8,40},{16,48},{24,56},{32,64},{40,72},{48,80},{56,88},{64,... | collective-permute-start | bytes 1179656 | tf_op jit(solution)/shard_map/ppermute | solution.py:298
  133.4 19.7 %collective-permute-start.1 = (bf16[1536,128]{1,0:T(8,128)(2,1)}, bf16[1536,128]{1,0:T(8,128)(2,1)S(1)}, u32[]{:S(2)}, u32[]{:S(2)}) collective-permute-start(bf16[1536,128]{1,0:T(8,128)(2,1)} %get-tuple-element.83), channel_id=1, source_target_pairs={{0,64},{8,72},{16,80},{24,88},{32,96},{40,104},{48,112},{56,120},{... | collective-permute-start | bytes 1179656 | tf_op jit(solution)/shard_map/ppermute | solution.py:298
  135.8 17.3 %collective-permute-start.2 = (bf16[1536,128]{1,0:T(8,128)(2,1)}, bf16[1536,128]{1,0:T(8,128)(2,1)}, u32[]{:S(2)}, u32[]{:S(2)}) collective-permute-start(bf16[1536,128]{1,0:T(8,128)(2,1)} %get-tuple-element.84), channel_id=1, source_target_pairs={{0,96},{8,104},{16,112},{24,120},{32,0},{40,8},{48,16},{56,24},{64... | collective-permute-start | bytes 1179656 | tf_op jit(solution)/shard_map/ppermute | solution.py:298
  137.3 123.5 %copy-start.7 = (s32[8]{0:T(128)}, s32[8]{0:T(128)S(1)}, u32[]{:S(2)}) copy-start(s32[8]{0:T(128)S(1)} %select_reduce_fusion.2.qblk) | copy-start | bytes 100
  155.3 86.9 %collective-permute-start.4 = (bf16[4,1024,128]{2,1,0:T(8,128)(2,1)}, bf16[4,1024,128]{2,1,0:T(8,128)(2,1)}, u32[]{:S(2)}, u32[]{:S(2)}) collective-permute-start(bf16[4,1024,128]{2,1,0:T(8,128)(2,1)} %pad_maximum_fusion.5), channel_id=1, source_target_pairs={{0,16},{8,24},{16,0},{24,8},{32,48},{40,56},{48,32},{56,40},{64,80... | collective-permute-start | bytes 3145736 | tf_op jit(solution)/shard_map/ppermute | solution.py:427
  158.0 102.9 %copy-start.8 = (s32[8]{0:T(128)}, s32[8]{0:T(128)S(1)}, u32[]{:S(2)}) copy-start(s32[8]{0:T(128)S(1)} %select_reduce_fusion.1.qlim) | copy-start | bytes 100
  158.2 102.7 %copy-start.4 = (s32[32]{0:T(128)}, s32[32]{0:T(128)S(1)}, u32[]{:S(2)}) copy-start(s32[32]{0:T(128)S(1)} %fusion.52.kslot) | copy-start | bytes 388
  158.2 98.9 %collective-permute-start.3 = (bf16[4,1024,128]{2,1,0:T(8,128)(2,1)}, bf16[4,1024,128]{2,1,0:T(8,128)(2,1)}, u32[]{:S(2)}, u32[]{:S(2)}) collective-permute-start(bf16[4,1024,128]{2,1,0:T(8,128)(2,1)} %pad_maximum_fusion.5), channel_id=1, source_target_pairs={{0,8},{8,0},{16,24},{24,16},{32,40},{40,32},{48,56},{56,48},{64,72... | collective-permute-start | bytes 3145736 | tf_op jit(solution)/shard_map/ppermute | solution.py:426
  161.0 99.9 %copy-start.3 = (bf16[4,512,128]{2,1,0:T(8,128)(2,1)}, bf16[4,512,128]{2,1,0:T(8,128)(2,1)S(1)}, u32[]{:S(2)}) copy-start(bf16[4,512,128]{2,1,0:T(8,128)(2,1)S(1)} %pad_maximum_fusion.8.q_ref) | copy-start | bytes 1572868
  242.2 14.9 %collective-permute-start.5 = (bf16[4,1024,128]{2,1,0:T(8,128)(2,1)}, bf16[4,1024,128]{2,1,0:T(8,128)(2,1)}, u32[]{:S(2)}, u32[]{:S(2)}) collective-permute-start(bf16[4,1024,128]{2,1,0:T(8,128)(2,1)} %collective-permute-done.4), channel_id=1, source_target_pairs={{0,8},{8,0},{16,24},{24,16},{32,40},{40,32},{48,56},{56,48},{64,72... | collective-permute-start | bytes 3145736 | tf_op jit(solution)/shard_map/ppermute | solution.py:428
  243.4 11.9 %collective-permute-start.9 = (bf16[512,128]{1,0:T(8,128)(2,1)S(1)}, bf16[512,128]{1,0:T(8,128)(2,1)S(1)}, u32[]{:S(2)}, u32[]{:S(2)}) collective-permute-start(bf16[512,128]{1,0:T(8,128)(2,1)S(1)} %bitcast.191), channel_id=1, source_target_pairs={{0,32},{8,40},{16,48},{24,56},{32,64},{40,72},{48,80},{56,88},{64,... | collective-permute-start | bytes 393224 | tf_op jit(solution)/shard_map/ppermute | solution.py:298
  244.4 11.0 %collective-permute-start.10 = (bf16[512,128]{1,0:T(8,128)(2,1)S(1)}, bf16[512,128]{1,0:T(8,128)(2,1)S(1)}, u32[]{:S(2)}, u32[]{:S(2)}) collective-permute-start(bf16[512,128]{1,0:T(8,128)(2,1)S(1)} %bitcast.190), channel_id=1, source_target_pairs={{0,64},{8,72},{16,80},{24,88},{32,96},{40,104},{48,112},{56,120},{... | collective-permute-start | bytes 393224 | tf_op jit(solution)/shard_map/ppermute | solution.py:298
  246.7 8.7 %collective-permute-start.11 = (bf16[512,128]{1,0:T(8,128)(2,1)S(1)}, bf16[512,128]{1,0:T(8,128)(2,1)}, u32[]{:S(2)}, u32[]{:S(2)}) collective-permute-start(bf16[512,128]{1,0:T(8,128)(2,1)S(1)} %bitcast.189), channel_id=1, source_target_pairs={{0,96},{8,104},{16,112},{24,120},{32,0},{40,8},{48,16},{56,24},{64... | collective-permute-start | bytes 393224 | tf_op jit(solution)/shard_map/ppermute | solution.py:298
  286.7 50.1 %collective-permute-start.8 = (bf16[512,128]{1,0:T(8,128)(2,1)S(1)}, bf16[512,128]{1,0:T(8,128)(2,1)S(1)}, u32[]{:S(2)}, u32[]{:S(2)}) collective-permute-start(bf16[512,128]{1,0:T(8,128)(2,1)S(1)} %get-tuple-element.99), channel_id=1, source_target_pairs={{0,32},{8,40},{16,48},{24,56},{32,64},{40,72},{48,80},{56,88},{64,... | collective-permute-start | bytes 393224 | tf_op jit(solution)/shard_map/ppermute | solution.py:305
  288.0 48.8 %collective-permute-start.7 = (bf16[512,128]{1,0:T(8,128)(2,1)S(1)}, bf16[512,128]{1,0:T(8,128)(2,1)S(1)}, u32[]{:S(2)}, u32[]{:S(2)}) collective-permute-start(bf16[512,128]{1,0:T(8,128)(2,1)S(1)} %get-tuple-element.101), channel_id=1, source_target_pairs={{0,64},{8,72},{16,80},{24,88},{32,96},{40,104},{48,112},{56,120},{... | collective-permute-start | bytes 393224 | tf_op jit(solution)/shard_map/ppermute | solution.py:305
  290.5 46.2 %collective-permute-start.6 = (bf16[512,128]{1,0:T(8,128)(2,1)S(1)}, bf16[512,128]{1,0:T(8,128)(2,1)S(1)}, u32[]{:S(2)}, u32[]{:S(2)}) collective-permute-start(bf16[512,128]{1,0:T(8,128)(2,1)S(1)} %get-tuple-element.102), channel_id=1, source_target_pairs={{0,96},{8,104},{16,112},{24,120},{32,0},{40,8},{48,16},{56,24},{64... | collective-permute-start | bytes 393224 | tf_op jit(solution)/shard_map/ppermute | solution.py:305
  324.0 12.1 %copy-start.29 = (bf16[4,512,128]{2,1,0:T(8,128)(2,1)S(1)}, bf16[4,512,128]{2,1,0:T(8,128)(2,1)}, u32[]{:S(2)}) copy-start(bf16[4,512,128]{2,1,0:T(8,128)(2,1)} %get-tuple-element.24) | copy-start | bytes 1572868
  327.1 31.9 %collective-permute-start.12 = (bf16[2,4096,128]{2,1,0:T(8,128)(2,1)}, bf16[2,4096,128]{2,1,0:T(8,128)(2,1)}, u32[]{:S(2)}, u32[]{:S(2)}) collective-permute-start(bf16[2,4096,128]{2,1,0:T(8,128)(2,1)} %slice_bitcast_fusion.1), channel_id=1, source_target_pairs={{0,8},{8,0},{16,24},{24,16},{32,40},{40,32},{48,56},{56,48},{64,72... | collective-permute-start | bytes 6291464 | tf_op jit(solution)/shard_map/ppermute | solution.py:475
  363.7 26.5 %collective-permute-start.13 = (bf16[4096,128]{1,0:T(8,128)(2,1)S(1)}, bf16[4096,128]{1,0:T(8,128)(2,1)}, u32[]{:S(2)}, u32[]{:S(2)}) collective-permute-start(bf16[4096,128]{1,0:T(8,128)(2,1)S(1)} %fusion.31), channel_id=1, source_target_pairs={{0,16},{8,24},{16,0},{24,8},{32,48},{40,56},{48,32},{56,40},{64,80... | collective-permute-start | bytes 3145736 | tf_op jit(solution)/shard_map/ppermute | solution.py:476
  376.4 159.0 %reduce-scatter.16.cloned.1.call-start = ((), (), s32[]{:S(2)}) async-start(), calls=%async_computation.13 | async-start | bytes 3899392
  376.5 16.0 %copy-start.30 = (bf16[512,128]{1,0:T(8,128)(2,1)S(1)}, bf16[512,128]{1,0:T(8,128)(2,1)}, u32[]{:S(2)}) copy-start(bf16[512,128]{1,0:T(8,128)(2,1)} %get-tuple-element.93) | copy-start | bytes 393220
  392.6 9.9 %collective-permute-start.14 = (bf16[1536,128]{1,0:T(8,128)(2,1)S(1)}, bf16[1536,128]{1,0:T(8,128)(2,1)S(1)}, u32[]{:S(2)}, u32[]{:S(2)}) collective-permute-start(bf16[1536,128]{1,0:T(8,128)(2,1)S(1)} %pad_maximum_fusion.10), channel_id=1, source_target_pairs={{0,96},{8,104},{16,112},{24,120},{32,0},{40,8},{48,16},{56,24},{64... | collective-permute-start | bytes 1179656 | tf_op jit(solution)/shard_map/ppermute | solution.py:305
  393.2 11.1 %collective-permute-start.15 = (bf16[1536,128]{1,0:T(8,128)(2,1)S(1)}, bf16[1536,128]{1,0:T(8,128)(2,1)S(1)}, u32[]{:S(2)}, u32[]{:S(2)}) collective-permute-start(bf16[1536,128]{1,0:T(8,128)(2,1)S(1)} %pad_maximum_fusion.11), channel_id=1, source_target_pairs={{0,64},{8,72},{16,80},{24,88},{32,96},{40,104},{48,112},{56,120},{... | collective-permute-start | bytes 1179656 | tf_op jit(solution)/shard_map/ppermute | solution.py:305
  395.3 19.6 %collective-permute-start.16 = (bf16[1536,128]{1,0:T(8,128)(2,1)S(1)}, bf16[1536,128]{1,0:T(8,128)(2,1)S(1)}, u32[]{:S(2)}, u32[]{:S(2)}) collective-permute-start(bf16[1536,128]{1,0:T(8,128)(2,1)S(1)} %pad_maximum_fusion.12), channel_id=1, source_target_pairs={{0,32},{8,40},{16,48},{24,56},{32,64},{40,72},{48,80},{56,88},{64,... | collective-permute-start | bytes 1179656 | tf_op jit(solution)/shard_map/ppermute | solution.py:305
  434.7 191.3 %reduce-scatter.14.cloned.1.call-start = ((), (), s32[]{:S(2)}) async-start(), calls=%async_computation.12 | async-start | bytes 6127616 | tf_op jit(solution)/shard_map/reduce_scatter | solution.py:469
  455.1 10.0 %copy-start.6 = (bf16[2,512,768]{2,1,0:T(8,128)(2,1)S(1)}, bf16[2,512,768]{2,1,0:T(8,128)(2,1)}, u32[]{:S(2)}) copy-start(bf16[2,512,768]{2,1,0:T(8,128)(2,1)} %copy-done.5) | copy-start | bytes 4718596
  455.1 226.5 %reduce-scatter.12.cloned.1.call-start = ((), (), s32[]{:S(2)}) async-start(), calls=%async_computation.11 | async-start | bytes 4718592 | tf_op jit(solution)/shard_map/reduce_scatter | solution.py:485
  455.4 9.7 %copy-start.2 = (bf16[2048,896]{1,0:T(8,128)(2,1)S(1)}, bf16[2048,896]{1,0:T(8,128)(2,1)}, u32[]{:S(2)}) copy-start(bf16[2048,896]{1,0:T(8,128)(2,1)} %all-gather.12.cloned.1.call-done.w_ref) | copy-start | bytes 11010052
  470.2 6.9 copy-start.24
  470.3 297.0 %reduce-scatter.10.cloned.1.call-start = ((), (), s32[]{:S(2)}) async-start(), calls=%async_computation.9 | async-start | bytes 4718592 | tf_op jit(solution)/shard_map/reduce_scatter | solution.py:464
  536.6 145.0 %copy-start.12 = (bf16[128,2048]{1,0:T(8,128)(2,1)S(1)}, bf16[128,2048]{1,0:T(8,128)(2,1)}, u32[]{:S(2)}) copy-start(bf16[128,2048]{1,0:T(8,128)(2,1)} %param.12) | copy-start | bytes 1572868
  536.6 145.0 %copy-start.33 = (f32[2048]{0:T(1024)S(1)}, f32[2048]{0:T(1024)}, u32[]{:S(2)}) copy-start(f32[2048]{0:T(1024)} %param.13) | copy-start | bytes 24580
  536.6 145.0 %copy-start.36 = (f32[128]{0:T(128)S(1)}, f32[128]{0:T(128)}, u32[]{:S(2)}) copy-start(f32[128]{0:T(128)} %copy-done.35) | copy-start | bytes 1540
  536.6 145.0 %copy-start.39 = (f32[128]{0:T(128)S(1)}, f32[128]{0:T(128)}, u32[]{:S(2)}) copy-start(f32[128]{0:T(128)} %copy-done.38) | copy-start | bytes 1540
  536.7 230.6 %copy-start.25 = (bf16[128,2048]{1,0:T(8,128)(2,1)S(1)}, bf16[128,2048]{1,0:T(8,128)(2,1)}, u32[]{:S(2)}) copy-start(bf16[128,2048]{1,0:T(8,128)(2,1)} %param.21) | copy-start | bytes 1572868
  (26 other events, 81.2 us)
Sparse Core Ops, SparseCore 0:
  11.0 57.8 all-gather.11
  71.2 50.7 all-gather.5
  123.6 51.3 all-gather.13
  177.7 58.3 all-gather.9
  238.8 69.5 all-gather.7
  376.5 78.1 reduce-scatter.17
  459.3 76.0 reduce-scatter.15
  540.1 85.9 reduce-scatter.13
  628.6 52.9 reduce-scatter.11
  684.0 52.8 reduce-scatter.9

commit v2 on v1

--- a/solution.py
+++ b/solution.py
@@ -21,6 +21,7 @@
 TN = (((0,), (0,)), ((), ()))
 VMEM = pl.BlockSpec(memory_space=pltpu.VMEM)
 SMEM = pl.BlockSpec(memory_space=pltpu.SMEM)
+ANY = pl.BlockSpec(memory_space=pl.ANY)
 
 
 def dot(left, right, dims):
@@ -280,29 +281,520 @@
     return out.reshape(2 * BLK, width), sums
 
 
-def tok_perm(dy, dz, dc):
-    pairs = []
-    for t in range(16):
-        y, z, c = t // 4, (t // 2) % 2, t % 2
-        pairs.append((t, ((y + dy) % 4) * 4 + (z ^ dz) * 2 + (c ^ dc)))
-    return pairs
-
-
-def pick(array, index):
-    return lax.dynamic_index_in_dim(array, index, 0, keepdims=False)
-
-
-def spread_heads(by_head, y):
-    parts = [pick(by_head, y)]
-    for d in range(1, 4):
-        parts.append(lax.ppermute(pick(by_head, (y + d) % 4), "tok", tok_perm(d, 0, 0)))
-    return parts
-
-
-def return_heads(parts, y):
-    back = [parts[0]]
-    for d in range(1, 4):
-        back.append(lax.ppermute(parts[d], "tok", tok_perm(4 - d, 0, 0)))
+def coords():
+    tok, br = lax.axis_index("tok"), lax.axis_index("br")
+    return tok // 4, (tok // 2) % 2, tok % 2, br // 4, br % 4
+
+
+def peer(dy=0, dz=0, dc=0, dl=0, dx=0):
+    y, z, c, l, x = coords()
+    tok = ((y + dy) % 4) * 4 + ((z + dz) % 2) * 2 + (c + dc) % 2
+    return tok, ((l + dl) % 2) * 4 + (x + dx) % 4
+
+
+class Links:
+    def __init__(self, send_sems, recv_sems, local_sems):
+        self.sems = (send_sems, recv_sems, local_sems)
+        self.sent, self.locals = [], []
+
+    def greet(self, partners):
+        barrier = pltpu.get_barrier_semaphore()
+        for offsets in partners:
+            pl.semaphore_signal(
+                barrier, inc=1, device_id=peer(**offsets), device_id_type=pl.DeviceIdType.MESH
+            )
+        pl.semaphore_wait(barrier, len(partners))
+
+    def copy(self, number, source, target, offsets):
+        return pltpu.make_async_remote_copy(
+            src_ref=source,
+            dst_ref=target,
+            send_sem=self.sems[0].at[number],
+            recv_sem=self.sems[1].at[number],
+            device_id=peer(**offsets),
+            device_id_type=pl.DeviceIdType.MESH,
+        )
+
+    def send(self, source, target, **offsets):
+        copy = self.copy(len(self.sent), source, target, offsets)
+        copy.start()
+        self.sent.append(copy)
+        return len(self.sent) - 1, offsets
+
+    def arrived(self, ticket, place):
+        self.copy(ticket[0], place, place, ticket[1]).wait_recv()
+
+    def local(self, source, target):
+        copy = pltpu.make_async_copy(source, target, self.sems[2].at[len(self.locals)])
+        copy.start()
+        self.locals.append([copy, True])
+        return len(self.locals) - 1
+
+    def settle(self, number):
+        copy, pending = self.locals[number]
+        if pending:
+            copy.wait()
+        self.locals[number][1] = False
+
+    def close(self):
+        for number in range(len(self.locals)):
+            self.settle(number)
+        for copy in self.sent:
+            copy.wait_send()
+
+
+def in_turn(tasks):
+    tasks = list(tasks)
+    while tasks:
+        for task in list(tasks):
+            try:
+                next(task)
+            except StopIteration:
+                tasks.remove(task)
+
+
+def ring_four(links, own, place, axis, landed):
+    right = links.send(own, place(0, None), **{axis: 1})
+    left = links.send(own, place(0, None), **{axis: -1})
+    yield
+    links.arrived(right, place(-1, None))
+    on_right = links.send(place(-1, 0), place(-1, 0), **{axis: 1})
+    landed(-1)
+    yield
+    links.arrived(left, place(1, None))
+    on_left = links.send(place(1, 1), place(1, 1), **{axis: -1})
+    landed(1)
+    yield
+    links.arrived(on_right, place(2, 0))
+    links.arrived(on_left, place(2, 1))
+    landed(2)
+
+
+def half_of(ref, part):
+    if part is None:
+        return ref
+    rows = ref.shape[0] // 2
+    return ref.at[pl.ds(part * rows, rows)]
+
+
+def gather_br(links, own, whole):
+    unused_y, unused_z, unused_c, l, x = coords()
+
+    def place(dl):
+        return lambda dx, part: half_of(whole.at[(l + dl) % 2, (x + dx) % 4], part)
+
+    links.local(own, place(0)(0, None))
+    across = links.send(own, place(0)(0, None), dl=1)
+    near = ring_four(links, own, place(0), "dx", lambda d: None)
+    next(near)
+    yield
+    links.arrived(across, place(1)(0, None))
+    far = ring_four(links, place(1)(0, None), place(1), "dx", lambda d: None)
+    next(far)
+    for unused in near:
+        yield
+    for unused in far:
+        yield
+
+
+def gather_tok(links, own, whole):
+    y, z, c, unused_l, unused_x = coords()
+    passed = []
+
+    def place(dz, dc=0):
+        return lambda dy, part: half_of(
+            whole.at[(y + dy) % 4, (z + dz) % 2, (c + dc) % 2], part
+        )
+
+    def passer(dz):
+        def landed(dy):
+            ref = place(dz)(dy, None)
+            passed.append((links.send(ref, ref, dc=1), place(dz, 1)(dy, None)))
+
+        return landed
+
+    links.local(own, place(0)(0, None))
+    across = links.send(own, place(0)(0, None), dz=1)
+    near = ring_four(links, own, place(0), "dy", passer(0))
+    next(near)
+    passed.append((links.send(own, place(0)(0, None), dc=1), place(0, 1)(0, None)))
+    yield
+    links.arrived(across, place(1)(0, None))
+    far = ring_four(links, place(1)(0, None), place(1), "dy", passer(1))
+    next(far)
+    passer(1)(0)
+    for unused in near:
+        yield
+    for unused in far:
+        yield
+    for ticket, ref in passed:
+        links.arrived(ticket, ref)
+
+
+def spread_heads(links, joined, queries, pairs):
+    y, z, c, unused_l, unused_x = coords()
+    rows = queries.shape[1]
+    keys = pl.ds(rows, joined.shape[1] - rows)
+    links.local(joined.at[y, pl.ds(0, rows)], queries.at[y])
+    links.local(joined.at[y, keys], pairs.at[y, z, c])
+    order = (1, 3, 2)
+    direct = [
+        links.send(joined.at[(y + d) % 4, keys], pairs.at[y, z, c], dy=d) for d in order
+    ]
+    across = [links.send(joined.at[y, keys], pairs.at[y, z, c], dz=1)]
+    passed = [(links.send(joined.at[y, keys], pairs.at[y, z, c], dc=1), 0, 0)]
+    asked = [
+        links.send(joined.at[(y + d) % 4, pl.ds(0, rows)], queries.at[y], dy=d) for d in order
+    ]
+    yield
+
+    def far(i):
+        dy = 0 if i == 0 else -order[i - 1]
+        ref = pairs.at[(y + dy) % 4, 1 - z, c]
+        links.arrived(across[i], ref)
+        passed.append((links.send(ref, ref, dc=1), dy, 1))
+
+    for i, d in enumerate(order):
+        ref = pairs.at[(y - d) % 4, z, c]
+        links.arrived(direct[i], ref)
+        across.append(links.send(ref, ref, dz=1))
+        passed.append((links.send(ref, ref, dc=1), -d, 0))
+        yield
+        far(i)
+        yield
+    far(3)
+    yield
+    for i, d in enumerate(order):
+        links.arrived(asked[i], queries.at[(y - d) % 4])
+    for ticket, dy, dz in passed:
+        links.arrived(ticket, pairs.at[(y + dy) % 4, (z + dz) % 2, 1 - c])
+
+
+def add_up(target, sources, rows, finish):
+    chunk = 16
+
+    def step(i, unused):
+        here = pl.ds(pl.multiple_of(i * chunk, chunk), chunk)
+        total = sources[0][here, :].astype(F32)
+        for source in sources[1:]:
+            total = total + source[here, :].astype(F32)
+        target[here, :] = finish(total, here).astype(target.dtype)
+        return unused
+
+    lax.fori_loop(0, rows // chunk, step, 0)
+
+
+def plain(total, here):
+    return total
+
+
+def reduce_heads(links, grads, dq, dq_home, grads_home, mine, near, far, total):
+    y, z, c, unused_l, unused_x = coords()
+    order = (1, 3, 2, 0)
+    held, from_core = {}, {}
+    for dz in (1, 0):
+        for d in order:
+            place = ((y + d) % 4, (z + dz) % 2)
+            from_core[d, dz] = links.send(
+                grads.at[place[0], place[1], 1 - c], near.at[place[0], place[1]], dc=1
+            )
+            held[d, dz] = links.local(
+                grads.at[place[0], place[1], c], mine.at[place[0], place[1]]
+            )
+    asked = [links.send(dq.at[(y + d) % 4], dq_home.at[y], dy=d) for d in order[:3]]
+    links.local(dq.at[y], dq_home.at[y])
+    yield
+    rows = mine.shape[2]
+    across = {}
+    for d in order:
+        here = (y + d) % 4
+        links.arrived(from_core[d, 1], near.at[here, 1 - z])
+        links.settle(held[d, 1])
+        add_up(
+            mine.at[here, 1 - z], [mine.at[here, 1 - z], near.at[here, 1 - z]], rows, plain
+        )
+        across[d] = links.send(mine.at[here, 1 - z], far.at[here], dz=1)
+        yield
+    home = {}
+    for d in order:
+        here = (y + d) % 4
+        links.arrived(from_core[d, 0], near.at[here, z])
+        links.settle(held[d, 0])
+        links.arrived(across[d], far.at[here])
+        add_up(
+            total.at[here], [mine.at[here, z], near.at[here, z], far.at[here]], rows, plain
+        )
+        if d:
+            home[d] = links.send(total.at[here], grads_home.at[y], dy=d)
+        else:
+            links.local(total.at[here], grads_home.at[y])
+        yield
+    for i, d in enumerate(order[:3]):
+        links.arrived(asked[i], dq_home.at[(y - d) % 4])
+        links.arrived(home[d], grads_home.at[(y - d) % 4])
+
+
+def reduce_br(links, parts, own, near, out, far, target, finish):
+    unused_y, unused_z, unused_c, l, x = coords()
+    order = (1, 3, 2)
+    tickets = {}
+    held = {}
+    for dl in (1, 0):
+        there = (l + dl) % 2
+        held[dl] = links.local(parts.at[there, x], own.at[there])
+        for i, d in enumerate(order):
+            tickets[dl, i] = links.send(
+                parts.at[there, (x + d) % 4], near.at[i, there], dx=d
+            )
+    yield
+    rows = out.shape[0]
+    for i in range(3):
+        links.arrived(tickets[1, i], near.at[i, 1 - l])
+        yield
+    links.settle(held[1])
+    add_up(out, [own.at[1 - l]] + [near.at[i, 1 - l] for i in range(3)], rows, plain)
+    across = links.send(out, far, dl=1)
+    yield
+    for i in range(3):
+        links.arrived(tickets[0, i], near.at[i, l])
+        yield
+    links.settle(held[0])
+    links.arrived(across, far)
+    add_up(
+        target, [own.at[l]] + [near.at[i, l] for i in range(3)] + [far], rows, finish
+    )
+
+
+def reduce_tok(links, parts, mine, near, side, out, far, target):
+    y, z, c, unused_l, unused_x = coords()
+    order = (1, 3, 2)
+    tickets, held = {}, {}
+    for d in order + (0,):
+        here = (y + d) % 4
+        tickets[d] = links.send(parts.at[here, :, 1 - c], near.at[here], dc=1)
+        held[d] = links.local(parts.at[here, :, c], mine.at[here])
+    yield
+    rows = out.shape[0]
+    sent = {}
+    for i, d in enumerate(order + (0,)):
+        here = (y + d) % 4
+        links.arrived(tickets[d], near.at[here])
+        links.settle(held[d])
+        for k in range(2):
+            add_up(mine.at[here, k], [mine.at[here, k], near.at[here, k]], rows, plain)
+        if d:
+            sent[i] = links.send(mine.at[here], side.at[i], dy=d)
+        yield
+    for i in range(3):
+        links.arrived(sent[i], side.at[i])
+        yield
+    add_up(out, [mine.at[y, 1 - z]] + [side.at[i, 1 - z] for i in range(3)], rows, plain)
+    across = links.send(out, far, dz=1)
+    yield
+    links.arrived(across, far)
+    add_up(target, [mine.at[y, z]] + [side.at[i, z] for i in range(3)] + [far], rows, plain)
+
+
+BR_NEAR = [dict(dl=1), dict(dx=1), dict(dx=-1)]
+BR_ALL = BR_NEAR + [dict(dx=2)]
+TOK_NEAR = [dict(dz=1), dict(dc=1), dict(dy=1), dict(dy=-1)]
+TOK_ALL = TOK_NEAR + [dict(dy=2)]
+
+
+def comm_call(kernel, name, number, args, outs, scratch=(), in_vmem=(), out_vmem=(), copies=48):
+    return pl.pallas_call(
+        kernel,
+        out_shape=tuple(outs),
+        in_specs=[VMEM if i in in_vmem else ANY for i in range(len(args))],
+        out_specs=tuple(VMEM if i in out_vmem else ANY for i in range(len(outs))),
+        scratch_shapes=list(scratch)
+        + [
+            pltpu.SemaphoreType.DMA((copies,)),
+            pltpu.SemaphoreType.DMA((copies,)),
+            pltpu.SemaphoreType.DMA((16,)),
+        ],
+        compiler_params=pltpu.CompilerParams(
+            collective_id=number, has_side_effects=True, vmem_limit_bytes=48 * 2**20
+        ),
+        name=name,
+    )(*args)
+
+
+def start_kernel(s_ref, w_ref, x_out, w_out, *sems):
+    links = Links(*sems)
+    links.greet(BR_NEAR + TOK_NEAR)
+    in_turn([gather_br(links, s_ref, x_out), gather_tok(links, w_ref, w_out)])
+    links.close()
+
+
+def start(shifted, weights):
+    rows, depth = shifted.shape
+    wrows, cols = weights.shape
+    return comm_call(
+        start_kernel,
+        "start",
+        0,
+        (shifted, weights),
+        (
+            jax.ShapeDtypeStruct((2, 4, rows, depth), BF),
+            jax.ShapeDtypeStruct((4, 2, 2, wrows, cols), BF),
+        ),
+    )
+
+
+def heads_kernel(joined, cot, queries, pairs, grad_out, *sems):
+    links = Links(*sems)
+    links.greet(BR_NEAR + TOK_ALL)
+    in_turn([spread_heads(links, joined, queries, pairs), gather_br(links, cot, grad_out)])
+    links.close()
+
+
+def heads_out(joined, cot):
+    rows, depth = cot.shape
+    heads, span, lanes = joined.shape
+    return comm_call(
+        heads_kernel,
+        "heads_out",
+        1,
+        (joined, cot),
+        (
+            jax.ShapeDtypeStruct((4, BLK, lanes), BF),
+            jax.ShapeDtypeStruct((4, 2, 2, span - BLK, lanes), BF),
+            jax.ShapeDtypeStruct((2, 4, rows, depth), BF),
+        ),
+    )
+
+
+def home_kernel(grads, dq, branches, tokens, dq_home, grads_home, result, *rest):
+    mine, near, far, total, own, side, out, cross = rest[:8]
+    links = Links(*rest[8:])
+    links.greet(BR_ALL + TOK_ALL)
+
+    def finish(value, here):
+        return value + tokens[here, :].astype(F32)
+
+    in_turn(
+        [
+            reduce_heads(links, grads, dq, dq_home, grads_home, mine, near, far, total),
+            reduce_br(links, branches, own, side, out, cross, result, finish),
+        ]
+    )
+    links.close()
+
+
+def heads_home(grads, dq, branches, tokens):
+    rows, depth = tokens.shape
+    span, lanes = grads.shape[3:]
+    return comm_call(
+        home_kernel,
+        "heads_home",
+        2,
+        (grads, dq, branches, tokens),
+        (
+            jax.ShapeDtypeStruct(dq.shape, BF),
+            jax.ShapeDtypeStruct((4, span, lanes), BF),
+            jax.ShapeDtypeStruct((rows, depth), BF),
+        ),
+        scratch=[
+            pltpu.VMEM((4, 2, span, lanes), BF),
+            pltpu.VMEM((4, 2, span, lanes), BF),
+            pltpu.VMEM((4, span, lanes), BF),
+            pltpu.VMEM((4, span, lanes), BF),
+            pltpu.VMEM((2, rows, depth), BF),
+            pltpu.VMEM((3, 2, rows, depth), BF),
+            pltpu.VMEM((rows, depth), BF),
+            pltpu.VMEM((rows, depth), BF),
+        ],
+        in_vmem=(3,),
+        out_vmem=(2,),
+    )
+
+
+def last_kernel(grads, weights, shifted, mine_out, *rest):
+    own, side, out, cross, mine, near, edge, wout, wcross = rest[:9]
+    links = Links(*rest[9:])
+    links.greet(BR_ALL + TOK_ALL)
+    in_turn(
+        [
+            reduce_tok(links, weights, mine, near, edge, wout, wcross, mine_out),
+            reduce_br(links, grads, own, side, out, cross, shifted, plain),
+        ]
+    )
+    links.close()
+
+
+def last_sums(grads, weights):
+    rows, depth = grads.shape[2:]
+    wrows, cols = weights.shape[3:]
+    return comm_call(
+        last_kernel,
+        "last_sums",
+        3,
+        (grads, weights),
+        (
+            jax.ShapeDtypeStruct((rows, depth), F32),
+            jax.ShapeDtypeStruct((wrows, cols), F32),
+        ),
+        scratch=[
+            pltpu.VMEM((2, rows, depth), BF),
+            pltpu.VMEM((3, 2, rows, depth), BF),
+            pltpu.VMEM((rows, depth), BF),
+            pltpu.VMEM((rows, depth), BF),
+            pltpu.VMEM((4, 2, wrows, cols), BF),
+            pltpu.VMEM((4, 2, wrows, cols), BF),
+            pltpu.VMEM((3, 2, wrows, cols), BF),
+            pltpu.VMEM((wrows, cols), BF),
+            pltpu.VMEM((wrows, cols), BF),
+        ],
+        out_vmem=(0, 1),
+    )
+
+
+def sides_kernel(parts, result, here, side, *sems):
+    y, z, c, l, x = coords()
+    links = Links(*sems)
+    near = [dict(dl=i // 4, dx=i % 4) for i in range(1, 8)]
+    wide = [dict(dy=i // 4, dz=(i // 2) % 2, dc=i % 2) for i in range(1, 16)]
+    links.greet(near + wide)
+    tickets = []
+    for i, o in enumerate(near):
+        there = ((l + o["dl"]) % 2) * 4 + (x + o["dx"]) % 4
+        tickets.append(links.send(parts.at[there], here.at[i], **o))
+    total = parts[l * 4 + x]
+    for i, ticket in enumerate(tickets):
+        links.arrived(ticket, here.at[i])
+        total = total + here[i]
+    here[7] = total
+    tickets = [links.send(here.at[7], side.at[i], **o) for i, o in enumerate(wide)]
+    for i, ticket in enumerate(tickets):
+        links.arrived(ticket, side.at[i])
+        total = total + side[i]
+    result[...] = total
+    links.close()
+
+
+def sum_sides(parts):
+    return comm_call(
+        sides_kernel,
+        "sum_sides",
+        4,
+        (parts,),
+        (jax.ShapeDtypeStruct(parts.shape[1:], F32),),
+        scratch=[pltpu.VMEM(parts.shape, F32), pltpu.VMEM((15,) + parts.shape[1:], F32)],
+        in_vmem=(0,),
+        out_vmem=(0,),
+    )[0]
+
+
+def tok_perm(dy):
+    return [(t, ((t // 4 + dy) % 4) * 4 + t % 4) for t in range(16)]
+
+
+def swap_heads(parts, y):
+    back = [lax.dynamic_index_in_dim(parts, y, 0, keepdims=False)]
+    for d in (3, 2, 1):
+        piece = lax.dynamic_index_in_dim(parts, (y + d) % 4, 0, keepdims=False)
+        back.append(lax.ppermute(piece, "tok", tok_perm(d)))
     stacked = jnp.stack(back + back)
     return lax.dynamic_slice_in_dim(stacked, (4 - y) % 4, 4, 0)
 
@@ -364,23 +856,27 @@
     ).reshape(wrows, 2 * width)
     bias_row = jnp.pad(qkv_bias.reshape(1, -1), ((0, wrows - 1), (0, 128 - qkv_bias.size)))
     qkv_shard = jnp.concatenate([qkv_weight[0], kv_shard, bias_row], axis=1)
-    gu_shard = jnp.concatenate(
-        [gate_weight[:, :main], up_weight[:, :main], gate_weight[:, main:], up_weight[:, main:]],
-        axis=1,
-    )
-    do_shard = jnp.concatenate(
+    ff_shard = jnp.concatenate(
         [
+            gate_weight[:, :main],
+            up_weight[:, :main],
+            gate_weight[:, main:],
+            up_weight[:, main:],
             jnp.transpose(down_weight),
             jnp.zeros((wrows, 128 - tail), BF),
             jnp.transpose(out_weight),
         ],
         axis=1,
     )
-    qkv_full = lax.all_gather(qkv_shard, "tok", axis=0, tiled=True)
-    x = lax.all_gather(shifted, "br", axis=0, tiled=True)
-    grad = lax.all_gather(cotangent, "br", axis=0, tiled=True)
-    do_full = lax.all_gather(do_shard, "tok", axis=0, tiled=True)
-    gu_full = lax.all_gather(gu_shard, "tok", axis=0, tiled=True)
+    both_width = 2 * hidden_width
+    down_width = main + 128
+    ff_full = lax.all_gather(ff_shard, "tok", axis=0, tiled=True)
+    gu_full = ff_full[:, :both_width]
+    down_full = ff_full[:, both_width : both_width + down_width]
+    out_full = ff_full[:, both_width + down_width :]
+    x, qkv_full = start(shifted, qkv_shard)
+    x = x.reshape(2 * BLK, depth)
+    qkv_full = qkv_full.reshape(16 * wrows, -1)
 
     bias = qkv_full.reshape(16, wrows, -1)[:, 0, 3 * width : 3 * width + qkv_bias.size]
     bias = jnp.transpose(bias.reshape(16, 3, heads, 4), (1, 2, 0, 3)).reshape(3, heads, HD)
@@ -393,10 +889,8 @@
     slot_of = jnp.sum(
         jnp.where(block_map[None, :] == slot_table[:, None], slot_table[None, :], 0), axis=1
     )
-    owner = slot_of // 2
-    key_index = (((owner // 2) % 2 ^ z) * 2 + (owner % 2 ^ c)) * 4 + (y - owner // 4) % 4
-    key_slot = (key_index * 2 + slot_of % 2).astype(jnp.int32)
-    from_tok = ((y - jnp.arange(4, dtype=jnp.int32)) % 4) * 4 + z * 2 + c
+    key_slot = slot_of.astype(jnp.int32)
+    from_tok = jnp.arange(4, dtype=jnp.int32) * 4 + z * 2 + c
     my_queries = jnp.stack([2 * from_tok, 2 * from_tok + 1], axis=1).reshape(-1)
     query_block = jnp.sum(
         jnp.where(my_queries[:, None] == slot_table[None, :], block_map[None, :], 0), axis=1
@@ -420,13 +914,9 @@
 
     q_heads, kv_heads = project(x, qkv_full, bias, tables, heads)
     joined = jnp.concatenate([q_heads, kv_heads.reshape(heads, 2 * BLK, 2 * HD)], axis=1)
-    parts = jnp.stack(spread_heads(joined, y))
-    q_all = parts[:, :BLK]
-    kv_mine = parts[:, BLK:]
-    kv_core = lax.ppermute(kv_mine, "tok", tok_perm(0, 0, 1))
-    kv_far = lax.ppermute(kv_mine, "tok", tok_perm(0, 1, 0))
-    kv_diag = lax.ppermute(kv_far, "tok", tok_perm(0, 0, 1))
-    kv_all = jnp.stack([kv_mine, kv_core, kv_far, kv_diag]).reshape(-1, 2 * HD)
+    q_all, kv_all, grad = heads_out(joined, cotangent)
+    grad = grad.reshape(2 * BLK, depth)
+    kv_all = kv_all.reshape(-1, 2 * HD)
 
     turned, lse, o_parts = attn_fwd(query_block, query_limit, key_slot, q_all, kv_all, long_blocks)
 
@@ -438,13 +928,10 @@
         split = packed.reshape(heads, BLK, 2, HD)
         return jnp.transpose(split, (2, 1, 0, 3)).reshape(2 * BLK, width)
 
-    mixed = from_heads(return_heads([o_parts[d] for d in range(4)], y))
-
-    down_width = do_full.shape[1] - width
-    down_full = do_full[:, :down_width]
-    out_full = do_full[:, down_width:]
+    mixed = from_heads(swap_heads(o_parts, y))
+
     grad_mixed = dot(grad, out_full, NN).astype(BF)
-    do_all = jnp.stack(spread_heads(to_heads(grad_mixed), y))
+    do_all = swap_heads(to_heads(grad_mixed), y)
 
     both = dot(x, gu_full, NN)
     grad_hidden = dot(grad, down_full, NN)
@@ -461,30 +948,30 @@
         [grad_gate[:, :main], grad_up[:, :main], grad_gate[:, main:], grad_up[:, main:]], axis=1
     )
     branches = (dot(hidden, down_full, NT) + dot(mixed, out_full, NT)).astype(BF)
-    summed = lax.psum_scatter(branches, "br", scatter_dimension=0, tiled=True)
-    result = (residual + summed.astype(F32)).astype(BF)
-    grad_do = jnp.concatenate([dot(grad, hidden, TN), dot(grad, mixed, TN)], axis=1).astype(BF)
-    grad_gu = dot(x, grad_both, TN).astype(BF)
-    grad_do = lax.psum_scatter(grad_do, "tok", scatter_dimension=0, tiled=True)
-    grad_gu = lax.psum_scatter(grad_gu, "tok", scatter_dimension=0, tiled=True)
+    grad_ff = jnp.concatenate(
+        [
+            dot(x, grad_both, TN).astype(BF),
+            dot(grad, hidden, TN).astype(BF),
+            dot(grad, mixed, TN).astype(BF),
+        ],
+        axis=1,
+    )
+    grad_ff = lax.psum_scatter(grad_ff, "tok", scatter_dimension=0, tiled=True)
 
     dq_parts, dkv_all = attn_bwd(
         query_block, query_limit, key_slot, q_all, do_all, kv_all, turned, lse, long_blocks
     )
-    dkv = dkv_all.reshape(2, 2, 4 * 2 * BLK, 2 * HD)
-    near = dkv[:, 0].astype(F32) + lax.ppermute(dkv[:, 1], "tok", tok_perm(0, 0, 1)).astype(F32)
-    far = lax.ppermute(near[1].astype(BF), "tok", tok_perm(0, 1, 0))
-    mine = (near[0] + far.astype(F32)).astype(BF).reshape(4, 2 * BLK, 2 * HD)
-    back = return_heads([jnp.concatenate([dq_parts[d], mine[d]], axis=0) for d in range(4)], y)
-    dq_heads = back[:, :BLK]
-    dkv_heads = back[:, BLK:].reshape(heads, 2, BLK, 2 * HD)
+    dq_heads, dkv_heads, result = heads_home(
+        dkv_all.reshape(4, 2, 2, 2 * BLK, 2 * HD),
+        dq_parts,
+        branches.reshape(2, 4, rows, depth),
+        tokens,
+    )
+    dkv_heads = dkv_heads.reshape(heads, 2, BLK, 2 * HD)
     grad_joined, bias_sums = unturn(dq_heads, dkv_heads, tables, heads)
     grad_shifted = (
         dot(grad_both, gu_full, NT) + dot(grad_joined, qkv_full[:, : 3 * width], NT)
     ).astype(BF)
-    my_grad_shifted = lax.psum_scatter(
-        grad_shifted, "br", scatter_dimension=0, tiled=True
-    ).astype(F32)
     grad_qkv = dot(x, grad_joined, TN).astype(BF)
     qsum = bias_sums[0, :width].reshape(1, heads, HD)
     kvsum = jnp.transpose(bias_sums[0, width:].reshape(heads, 2, HD), (1, 0, 2))
@@ -492,7 +979,9 @@
     bsum = jnp.transpose(bsum, (2, 0, 1, 3)).reshape(16, 1, qkv_bias.size).astype(BF)
     bsum = jnp.pad(bsum, ((0, 0), (0, wrows - 1), (0, 128 - qkv_bias.size)))
     grad_qkv = jnp.concatenate([grad_qkv, bsum.reshape(16 * wrows, 128)], axis=1)
-    grad_qkv = lax.psum_scatter(grad_qkv, "tok", scatter_dimension=0, tiled=True).astype(F32)
+    my_grad_shifted, grad_qkv = last_sums(
+        grad_shifted.reshape(2, 4, rows, depth), grad_qkv.reshape(4, 2, 2, wrows, -1)
+    )
 
     grad_bias_out = grad_qkv[0, 3 * width : 3 * width + qkv_bias.size].reshape(qkv_bias.shape)
     gkv = grad_qkv[:, width : 3 * width].reshape(wrows, heads, 2, HD)
@@ -503,16 +992,12 @@
             gkv[:, :, 1].reshape(wrows, width),
         ]
     )
-    grad_do = grad_do.astype(F32)
-    grad_gu = grad_gu.astype(F32)
-    grad_down_out = jnp.transpose(grad_do[:, :hidden_width])
-    grad_out_out = jnp.transpose(grad_do[:, down_width:])
-    grad_gate_out = jnp.concatenate(
-        [grad_gu[:, :main], grad_gu[:, 2 * main : 2 * main + tail]], axis=1
-    )
-    grad_up_out = jnp.concatenate(
-        [grad_gu[:, main : 2 * main], grad_gu[:, 2 * main + tail :]], axis=1
-    )
+    grad_ff = grad_ff.astype(F32)
+    ends = grad_ff[:, 2 * main : both_width]
+    grad_gate_out = jnp.concatenate([grad_ff[:, :main], ends[:, :tail]], axis=1)
+    grad_up_out = jnp.concatenate([grad_ff[:, main : 2 * main], ends[:, tail:]], axis=1)
+    grad_down_out = jnp.transpose(grad_ff[:, both_width : both_width + hidden_width])
+    grad_out_out = jnp.transpose(grad_ff[:, both_width + down_width :])
 
     gain_part = jnp.sum(my_grad_shifted * normed, axis=0)
     bias_part = jnp.sum(my_grad_shifted, axis=0)
@@ -522,10 +1007,11 @@
         - jnp.mean(grad_normed, axis=-1, keepdims=True)
         - normed * jnp.mean(grad_normed * normed, axis=-1, keepdims=True)
     )
-    grad_gain, grad_bias = (
-        lax.psum_scatter(gain_part, ("tok", "br"), scatter_dimension=0, tiled=True),
-        lax.psum_scatter(bias_part, ("tok", "br"), scatter_dimension=0, tiled=True),
-    )
+    sides = jnp.stack([gain_part, bias_part]).reshape(2, 16, 8, 16)
+    sides = jnp.transpose(sides, (2, 0, 1, 3)).reshape(8, 2, 256)
+    sides = sum_sides(jnp.pad(sides, ((0, 0), (0, 6), (0, 0))))
+    sides = lax.dynamic_slice_in_dim(sides[:2].reshape(2, 16, 16), tok, 1, 1)[:, 0]
+    grad_gain, grad_bias = sides[0], sides[1]
     return (
         result,
         grad_tokens,

time: 782 us -> 503 us (0.64)
  waiting for transfers between devices: 409 us -> 6.15 us
  Pallas kernels: 65.6 us -> 309 us
  blocking collectives: 82.9 us -> 0 us
  starting transfers between devices: 30.1 us -> 3.96 us
  other arithmetic: 40.3 us -> 27.1 us
    pallas_call x0 -> x5, Pallas kernels: none -> 253 us  [comm_call(): pl.pallas_call(kernel, out_shape=tuple(outs), in_specs=[VMEM if i in in_v...]
    all_gather x5 -> x1, waiting for transfers between devices: 169 us -> 0.01 us  [body(): ff_full = lax.all_gather(ff_shard, 'tok', axis=0, tiled=True)]
    reduce_scatter x3 -> x0, waiting for transfers between devices: 139 us -> none  [the longest x1 87.6 us: body(): grad_gu = lax.psum_scatter(grad_gu, 'tok', scatter_dimension=0, tiled=True)]
    unnamed x1 -> x0, blocking collectives: 82.9 us -> none
    unnamed x12 -> x3, waiting for transfers between devices: 51.8 us -> 0.03 us
    ppermute x17 -> x6, waiting for transfers between devices: 48.6 us -> 6.11 us  [swap_heads(): back.append(lax.ppermute(piece, 'tok', tok_perm(d)))]
    ppermute x17 -> x6, starting transfers between devices: 29.4 us -> 3.88 us  [swap_heads(): back.append(lax.ppermute(piece, 'tok', tok_perm(d)))]
    concatenate x7 -> x3, other arithmetic: 4.19 us -> 18.2 us  [the longest x1 16.6 us: body(): jnp.concatenate([dot(x, grad_both, TN).astype(BF), dot(grad, hidden, TN)....]
  transfers between devices with their start and end apart: 27 -> 8, of which waited for: 13 -> 3; matrix products, arithmetic and copies ran while one was open for 19% -> 13% of each run, Pallas kernels for 8% -> 62%
where the time goes in v2:
time: 503 us; the launch traced here: 495 us
  Pallas kernels  309 us (61%)
  matrix products  71.3 us (14%)
  local copies, waits for them, and re-layouts  61.9 us (12%)
  other arithmetic  27.1 us (5%)
  between operations  15.7 us (3%)
  waiting for transfers between devices  6.15 us (1%)
    pallas_call x5, Pallas kernels, comm_call(): pl.pallas_call(kernel, out_shape=tuple(outs), in_specs=[VMEM if i in in_v...  253 us
    dot_general x11, matrix products, dot(): return lax.dot_general(left, right, dims, preferred_element_type=F32)  71.3 us
    unnamed x106, local copies, waits for them, and re-layouts  34.5 us
    pallas_call x1, Pallas kernels, attn_bwd(): pl.pallas_call(functools.partial(attn_bwd_kernel, long_blocks), out_shape...  28.3 us
    pallas_call x1, Pallas kernels, attn_fwd(): pl.pallas_call(functools.partial(attn_fwd_kernel, long_blocks), out_shape...  19.9 us
    concatenate x1, other arithmetic, body(): jnp.concatenate([dot(x, grad_both, TN).astype(BF), dot(grad, hidden, TN)....  16.6 us
  transfers between devices with their start and end apart: 8, of which 3 were waited for; matrix products, arithmetic and copies ran while one was open for 13% of the time, Pallas kernels for 62%

profile of v2, /device:TPU:1, one launch (start us, length us, event | category | flops | bytes accessed | tf_op | source)
XLA Modules:
  0.0 495.4 jit_solution(17799172871311114775)
XLA Ops:
  7.3 1.0 slice_dynamic-update-slice_fusion.1
  8.2 0.9 slice_dynamic-update-slice_fusion
  10.6 0.9 bitcast_dynamic-update-slice_fusion
  14.4 0.9 slice_bitcast_fusion.3
  17.5 52.6 %start.1 = (bf16[2,4,128,2048]{3,2,1,0:T(8,128)(2,1)}, bf16[4,2,2,128,896]{4,3,2,1,0:T(8,128)(2,1)S(1)}) custom-call(bf16[128,2048]{1,0:T(8,128)(2,1)S(1)} %fusion.18.s_ref, bf16[128,896]{1,0:T(8,128)(2,1)S(1)} %fusion.28.w_ref), custom_call_target="tpu_custom_call" | custom-call | tf_op jit(solution)/shard_map/start/pallas_call | solution.py:605
  70.1 1.8 copy-done.6
  73.2 1.9 multiply_sine_fusion
  75.1 1.1 concatenate.86.cq
  77.1 2.2 concatenate.87.sq
  79.3 2.0 maximum_maximum_fusion
  81.6 2.2 copy-done.5
  83.8 4.9 project.1
  88.9 52.2 %heads_out.1 = (bf16[4,512,128]{2,1,0:T(8,128)(2,1)S(1)}, bf16[4,2,2,1024,128]{4,3,2,1,0:T(8,128)(2,1)}, bf16[2,4,128,2048]{3,2,1,0:T(8,128)(2,1)}) custom-call(bf16[4,1536,128]{2,1,0:T(8,128)(2,1)S(1)} %pad_maximum_fusion.4.joined, bf16[128,2048]{1,0:T(8,128)(2,1)S(1)} %copy-done.9), custom_call_target="tpu_custom_call" | custom-call | tf_op jit(solution)/shard_map/heads_out/pallas_call | solution.py:605
  141.7 19.9 %attn_fwd.1 = (f32[4,128,512]{2,1,0:T(8,128)S(1)}, f32[8,1,512]{2,1,0:T(1,128)S(1)}, bf16[4,512,128]{2,1,0:T(8,128)(2,1)S(1)}) custom-call(s32[8]{0:T(128)S(1)} %select_reduce_fusion.2.qblk, s32[8]{0:T(128)S(1)} %select_reduce_fusion.1.qlim, s32[32]{0:T(128)S(1)} %select_reduce_fusion.kslot, bf16[4,512,128]{2,1,0:T(8,128)(2,1)S(1)} %get-tuple-element.33.q_ref, ...), custom_call_target="tpu_custom_call" | custom-call | flops 20000000000 | bytes 8388608 | tf_op jit(solution)/shard_map/attn_fwd/pallas_call | solution.py:90
  161.6 1.0 copy-done.18
  163.9 1.2 collective-permute-start.3
  165.9 2.5 collective-permute-done.3
  168.4 2.3 collective-permute-done.4
  170.8 1.3 collective-permute-done.5
  173.1 4.4 convolution_convert_fusion.3
  177.5 10.6 %fusion.2 = f32[1024,1408]{1,0:T(8,128)S(1)} fusion(bf16[1024,2048]{1,0:T(8,128)(2,1)} %bitcast.108, bf16[2048,2432]{0,1:T(8,128)(2,1)} %all-gather.2.cloned.1.call-done), kind=kOutput, calls=%fused_computation.6 | convolution fusion | flops 5905580032 | bytes 15728640 | tf_op jit(solution)/shard_map/dot_general | solution.py:28
  188.6 1.8 copy-done.32
  190.5 6.4 %multiply_convert_fusion = (bf16[1024,704]{1,0:T(8,128)(2,1)S(1)}, bf16[1024,704]{1,0:T(8,128)(2,1)S(1)}, bf16[1024,704]{1,0:T(8,128)(2,1)S(1)}) fusion(f32[1024,64]{1,0:T(8,128)S(1)} %get-tuple-element.57, f32[1024,640]{1,0:T(8,128)S(1)} %get-tuple-element.55, f32[1024,64]{1,0:T(8,128)S(1)} %get-tuple-element.58, f32[1024,640]{1,0:T(8,128)S(1)} %get-tuple-element.56, ...), kind=kOutput, calls=%fused_computation.16 | convolution fusion | flops 2965766144 | bytes 17170432 | tf_op jit(solution)/shard_map/dot_general | solution.py:28
  197.9 1.2 slice.188
  199.8 5.0 %convolution_convert_fusion.1 = bf16[2048,768]{0,1:T(8,128)(2,1)} fusion(bf16[1024,2048]{1,0:T(8,128)(2,1)S(1)} %bitcast.149, bf16[1024,704]{1,0:T(8,128)(2,1)S(1)} %get-tuple-element.54), kind=kOutput, calls=%fused_computation.9 | convolution fusion | flops 3222798336 | bytes 8781824 | tf_op jit(solution)/shard_map/dot_general | solution.py:28
  204.8 5.2 %concatenate.94 = bf16[1024,1408]{1,0:T(8,128)(2,1)} concatenate(bf16[1024,640]{1,0:T(8,128)(2,1)S(1)} %slice.187, bf16[1024,640]{1,0:T(8,128)(2,1)} %slice.188, bf16[1024,64]{1,0:T(8,128)(2,1)} %slice.189, bf16[1024,64]{1,0:T(8,128)(2,1)} %slice.190), dimensions={1} | concatenate | bytes 5767168 | tf_op jit(solution)/shard_map/concatenate | solution.py:947
  210.1 9.2 %convolution_convert_fusion = bf16[2048,1408]{0,1:T(8,128)(2,1)S(1)} fusion(bf16[1024,2048]{1,0:T(8,128)(2,1)} %bitcast.109, bf16[1024,1408]{1,0:T(8,128)(2,1)} %concatenate.94), kind=kOutput, calls=%fused_computation.3 | convolution fusion | flops 5908463616 | bytes 12845056 | tf_op jit(solution)/shard_map/dot_general | solution.py:28
  219.3 16.6 %pad_maximum_fusion = bf16[2048,2432]{0,1:T(8,128)(2,1)} fusion(bf16[2048,256]{0,1:T(8,128)(2,1)S(1)} %copy-done.23, bf16[2048,768]{0,1:T(8,128)(2,1)S(1)} %copy-done.21, bf16[2048,1408]{0,1:T(8,128)(2,1)S(1)} %convolution_convert_fusion), kind=kLoop, calls=%fused_computation | loop fusion | flops 29884416 | bytes 19922944 | tf_op jit(solution)/shard_map/concatenate | solution.py:951
  235.9 13.5 %copy.106 = bf16[2048,2432]{1,0:T(8,128)(2,1)} copy(bf16[2048,2432]{0,1:T(8,128)(2,1)} %pad_maximum_fusion) | data formatting | bytes 19922944
  249.4 3.8 convolution_convert_fusion.4
  254.6 0.9 collective-permute-start.1
  256.3 6.1 %fusion.5 = f32[1024,2048]{1,0:T(8,128)S(1)} fusion(bf16[2048,2432]{0,1:T(8,128)(2,1)} %all-gather.2.cloned.1.call-done, bf16[1024,704]{1,0:T(8,128)(2,1)} %copy-done.35), kind=kOutput, calls=%fused_computation.12 | convolution fusion | flops 3221225472 | bytes 13107200 | tf_op jit(solution)/shard_map/dot_general | solution.py:28
  262.4 8.9 %fusion = f32[1024,2048]{1,0:T(8,128)} fusion(bf16[1024,1408]{1,0:T(8,128)(2,1)S(1)} %copy-done.22, bf16[2048,2432]{0,1:T(8,128)(2,1)S(1)} %bitcast.140), kind=kOutput, calls=%fused_computation.4 | convolution fusion | flops 5905580032 | bytes 17039360 | tf_op jit(solution)/shard_map/dot_general | solution.py:28
  271.3 3.4 add_convert_fusion.1
  275.9 28.3 %attn_bwd.1 = (bf16[4,512,128]{2,1,0:T(8,128)(2,1)}, bf16[16384,128]{1,0:T(8,128)(2,1)}) custom-call(s32[8]{0:T(128)} %copy-done.15, s32[8]{0:T(128)} %copy-done.16, s32[32]{0:T(128)} %copy-done.17, bf16[4,512,128]{2,1,0:T(8,128)(2,1)} %copy-done.14, bf16[4,512,128]{2,1,0:T(8,128)(2,1)} %constant_dynamic-slice_fusion.3.do_ref, bf16[16384,128]{1,0:T(8,128)(2,1)} %bitcast.145, ...), custom_call_target="tpu_custom_call" | custom-call | flops 30000001024 | bytes 12582912 | tf_op jit(solution)/shard_map/attn_bwd/pallas_call | solution.py:159
  304.2 1.1 copy-done.11
  305.3 70.5 %heads_home.1 = (bf16[4,512,128]{2,1,0:T(8,128)(2,1)S(1)}, bf16[4,1024,128]{2,1,0:T(8,128)(2,1)S(1)}, bf16[128,2048]{1,0:T(8,128)(2,1)S(1)}) custom-call(bf16[4,2,2,1024,128]{4,3,2,1,0:T(8,128)(2,1)} %bitcast.120, bf16[4,512,128]{2,1,0:T(8,128)(2,1)S(1)} %copy-done.11, bf16[2,4,128,2048]{3,2,1,0:T(8,128)(2,1)} %bitcast.119, bf16[128,2048]{1,0:T(8,128)(2,1)S(1)} %copy-done), custom_call_target="tpu_custom_call" | custom-call | tf_op jit(solution)/shard_map/heads_home/pallas_call | solution.py:605
  375.8 2.8 unturn.1
  378.6 1.1 copy-done.12
  380.6 6.2 %convolution_convert_fusion.2 = bf16[2048,768]{1,0:T(8,128)(2,1)S(1)} fusion(bf16[1024,2048]{1,0:T(8,128)(2,1)} %bitcast.110, bf16[1024,768]{1,0:T(8,128)(2,1)} %bitcast.117), kind=kOutput, calls=%fused_computation.10 | convolution fusion | flops 3222798336 | bytes 8912896 | tf_op jit(solution)/shard_map/dot_general | solution.py:28
  387.3 1.5 copy-done.8
  389.3 7.3 %add_convert_fusion = bf16[1024,2048]{1,0:T(8,128)(2,1)} fusion(f32[1024,2048]{1,0:T(8,128)} %fusion, bf16[1024,768]{1,0:T(8,128)(2,1)S(1)} %bitcast.118, bf16[2048,896]{1,0:T(8,128)(2,1)S(1)} %bitcast.114), kind=kOutput, calls=%fused_computation.1 | convolution fusion | flops 3225419776 | bytes 17301504 | tf_op jit(solution)/shard_map/dot_general | solution.py:28
  396.6 55.5 %last_sums.1 = (f32[128,2048]{1,0:T(8,128)S(1)}, f32[128,896]{1,0:T(8,128)S(1)}) custom-call(bf16[2,4,128,2048]{3,2,1,0:T(8,128)(2,1)} %bitcast.121, bf16[4,2,2,128,896]{4,3,2,1,0:T(8,128)(2,1)S(1)} %pad_maximum_fusion.1.weights), custom_call_target="tpu_custom_call" | custom-call | tf_op jit(solution)/shard_map/last_sums/pallas_call | solution.py:605
  453.0 22.6 %sum_sides.1 = f32[8,256]{1,0:T(8,128)S(1)} custom-call(f32[8,8,256]{2,1,0:T(8,128)S(1)} %pad.19.parts), custom_call_target="tpu_custom_call" | custom-call | tf_op jit(solution)/shard_map/sum_sides/pallas_call | solution.py:605
  476.5 1.1 copy.102
  478.2 1.0 copy.104
  481.4 1.4 fusion.22
  482.8 1.4 copy.107
  (205 shorter events, 27.9 us)
Async XLA Ops:
  7.2 8.6 %copy-start = (bf16[128,2048]{1,0:T(8,128)(2,1)S(1)}, bf16[128,2048]{1,0:T(8,128)(2,1)}, u32[]{:S(2)}) copy-start(bf16[128,2048]{1,0:T(8,128)(2,1)} %tokens.1) | copy-start | bytes 1572868
  7.2 9.9 %copy-start.27 = (f32[2048]{0:T(1024)S(1)}, f32[2048]{0:T(1024)}, u32[]{:S(2)}) copy-start(f32[2048]{0:T(1024)} %param.14) | copy-start | bytes 24580
  7.2 9.9 %copy-start.25 = (f32[2048]{0:T(1024)S(1)}, f32[2048]{0:T(1024)}, u32[]{:S(2)}) copy-start(f32[2048]{0:T(1024)} %param.13) | copy-start | bytes 24580
  7.2 65.8 %copy-start.33 = (s32[32]{0:T(128)S(1)}, s32[32]{0:T(128)}, u32[]{:S(2)}) copy-start(s32[32]{0:T(128)} %param.22) | copy-start | bytes 388
  7.2 170.3 %all-gather.2.cloned.1.call-start = ((), (), s32[]{:S(2)}) async-start(), calls=%async_computation.1 | async-start | bytes 10584064 | tf_op jit(solution)/shard_map/all_gather | solution.py:873
  12.5 0.8 copy-start.24
  13.3 469.5 %reduce-scatter.4.cloned.1.call-start = ((), (), s32[]{:S(2)}) async-start(), calls=%async_computation.2 | async-start | bytes 10584064
  16.0 0.6 copy-start.28
  16.5 0.5 copy-start.30
  70.1 1.8 copy-start.6
  75.1 1.1 copy-start.20
  79.3 2.4 copy-start.7
  81.2 7.5 %copy-start.1 = (f32[2,512,128]{2,1,0:T(8,128)}, f32[2,512,128]{2,1,0:T(8,128)S(1)}, u32[]{:S(2)}) copy-start(f32[2,512,128]{2,1,0:T(8,128)S(1)} %get-tuple-element.86.ck) | copy-start | bytes 1572868
  81.3 7.5 %copy-start.3 = (f32[2,512,128]{2,1,0:T(8,128)}, f32[2,512,128]{2,1,0:T(8,128)S(1)}, u32[]{:S(2)}) copy-start(f32[2,512,128]{2,1,0:T(8,128)S(1)} %get-tuple-element.87.sk) | copy-start | bytes 1572868
  81.6 2.2 copy-start.5
  83.8 5.1 %copy-start.9 = (bf16[128,2048]{1,0:T(8,128)(2,1)S(1)}, bf16[128,2048]{1,0:T(8,128)(2,1)}, u32[]{:S(2)}) copy-start(bf16[128,2048]{1,0:T(8,128)(2,1)} %cot.1) | copy-start | bytes 1572868
  88.8 52.7 %copy-start.34 = (s32[10]{0:T(128)S(1)}, s32[10]{0:T(128)}, u32[]{:S(2)}) copy-start(s32[10]{0:T(128)} %param.23) | copy-start | bytes 124
  141.1 20.5 %copy-start.14 = (bf16[4,512,128]{2,1,0:T(8,128)(2,1)}, bf16[4,512,128]{2,1,0:T(8,128)(2,1)S(1)}, u32[]{:S(2)}) copy-start(bf16[4,512,128]{2,1,0:T(8,128)(2,1)S(1)} %get-tuple-element.33.q_ref) | copy-start | bytes 1572868
  141.2 20.3 %copy-start.17 = (s32[32]{0:T(128)}, s32[32]{0:T(128)S(1)}, u32[]{:S(2)}) copy-start(s32[32]{0:T(128)S(1)} %select_reduce_fusion.kslot) | copy-start | bytes 388
  141.4 20.1 %copy-start.15 = (s32[8]{0:T(128)}, s32[8]{0:T(128)S(1)}, u32[]{:S(2)}) copy-start(s32[8]{0:T(128)S(1)} %select_reduce_fusion.2.qblk) | copy-start | bytes 100
  141.7 19.9 %copy-start.16 = (s32[8]{0:T(128)}, s32[8]{0:T(128)S(1)}, u32[]{:S(2)}) copy-start(s32[8]{0:T(128)S(1)} %select_reduce_fusion.1.qlim) | copy-start | bytes 100
  161.6 1.0 copy-start.18
  162.6 0.6 copy-start.19
  163.9 4.5 collective-permute-start.3
  165.1 5.6 %collective-permute-start.4 = (bf16[512,128]{1,0:T(8,128)(2,1)}, bf16[512,128]{1,0:T(8,128)(2,1)S(1)}, u32[]{:S(2)}, u32[]{:S(2)}) collective-permute-start(bf16[512,128]{1,0:T(8,128)(2,1)} %get-tuple-element.65), channel_id=1, source_target_pairs={{0,64},{8,72},{16,80},{24,88},{32,96},{40,104},{48,112},{56,120},{... | collective-permute-start | bytes 393224 | tf_op jit(solution)/shard_map/ppermute | solution.py:797
  165.7 6.4 %collective-permute-start.5 = (bf16[512,128]{1,0:T(8,128)(2,1)}, bf16[512,128]{1,0:T(8,128)(2,1)S(1)}, u32[]{:S(2)}, u32[]{:S(2)}) collective-permute-start(bf16[512,128]{1,0:T(8,128)(2,1)} %get-tuple-element.63), channel_id=1, source_target_pairs={{0,32},{8,40},{16,48},{24,56},{32,64},{40,72},{48,80},{56,88},{64,... | collective-permute-start | bytes 393224 | tf_op jit(solution)/shard_map/ppermute | solution.py:797
  188.3 2.2 copy-start.32
  196.9 2.9 copy-start.35
  210.1 9.2 %copy-start.21 = (bf16[2048,768]{0,1:T(8,128)(2,1)S(1)}, bf16[2048,768]{0,1:T(8,128)(2,1)}, u32[]{:S(2)}) copy-start(bf16[2048,768]{0,1:T(8,128)(2,1)} %convolution_convert_fusion.1) | copy-start | bytes 9437188
  210.1 9.2 %copy-start.23 = (bf16[2048,256]{0,1:T(8,128)(2,1)S(1)}, bf16[2048,256]{0,1:T(8,128)(2,1)}, u32[]{:S(2)}) copy-start(bf16[2048,256]{0,1:T(8,128)(2,1)} %convolution_convert_fusion.3) | copy-start | bytes 3145732
  254.1 20.8 %collective-permute-start = (bf16[512,128]{1,0:T(8,128)(2,1)S(1)}, bf16[512,128]{1,0:T(8,128)(2,1)S(1)}, u32[]{:S(2)}, u32[]{:S(2)}) collective-permute-start(bf16[512,128]{1,0:T(8,128)(2,1)S(1)} %bitcast.136), channel_id=1, source_target_pairs={{0,96},{8,104},{16,112},{24,120},{32,0},{40,8},{48,16},{56,24},{64... | collective-permute-start | bytes 393224 | tf_op jit(solution)/shard_map/ppermute | solution.py:797
  254.6 20.3 %collective-permute-start.1 = (bf16[512,128]{1,0:T(8,128)(2,1)S(1)}, bf16[512,128]{1,0:T(8,128)(2,1)S(1)}, u32[]{:S(2)}, u32[]{:S(2)}) collective-permute-start(bf16[512,128]{1,0:T(8,128)(2,1)S(1)} %bitcast.137), channel_id=1, source_target_pairs={{0,64},{8,72},{16,80},{24,88},{32,96},{40,104},{48,112},{56,120},{... | collective-permute-start | bytes 393224 | tf_op jit(solution)/shard_map/ppermute | solution.py:797
  255.6 6.7 %slice-start = ((s8[9961472]{0:T(1024)(128)(4,1)}), s8[4194304]{0:T(1024)(128)(4,1)S(1)}, s32[]{:S(2)}) async-start(s8[9961472]{0:T(1024)(128)(4,1)} %bitcast.139), calls=%async_computation.3 | async-start | bytes 8388608
  255.6 6.7 %copy-start.22 = (bf16[1024,1408]{1,0:T(8,128)(2,1)S(1)}, bf16[1024,1408]{1,0:T(8,128)(2,1)}, u32[]{:S(2)}) copy-start(bf16[1024,1408]{1,0:T(8,128)(2,1)} %concatenate.94) | copy-start | bytes 8650756
  255.6 6.7 %slice-start.1 = ((s8[9961472]{0:T(1024)(128)(4,1)}), s8[4194304]{0:T(1024)(128)(4,1)S(1)}, s32[]{:S(2)}) async-start(s8[9961472]{0:T(1024)(128)(4,1)} %bitcast.139), calls=%async_computation.4 | async-start | bytes 8388608
  255.7 6.7 %slice-start.2 = ((s8[9961472]{0:T(1024)(128)(4,1)}), s8[1572864]{0:T(1024)(128)(4,1)S(1)}, s32[]{:S(2)}) async-start(s8[9961472]{0:T(1024)(128)(4,1)} %bitcast.139), calls=%async_computation.5 | async-start | bytes 3145728
  255.7 19.2 %collective-permute-start.2 = (bf16[512,128]{1,0:T(8,128)(2,1)S(1)}, bf16[512,128]{1,0:T(8,128)(2,1)S(1)}, u32[]{:S(2)}, u32[]{:S(2)}) collective-permute-start(bf16[512,128]{1,0:T(8,128)(2,1)S(1)} %bitcast.138), channel_id=1, source_target_pairs={{0,32},{8,40},{16,48},{24,56},{32,64},{40,72},{48,80},{56,88},{64,... | collective-permute-start | bytes 393224 | tf_op jit(solution)/shard_map/ppermute | solution.py:797
  304.2 1.1 copy-start.11
  305.3 70.5 %copy-start.2 = (f32[2,512,128]{2,1,0:T(8,128)S(1)}, f32[2,512,128]{2,1,0:T(8,128)}, u32[]{:S(2)}) copy-start(f32[2,512,128]{2,1,0:T(8,128)} %copy-done.1) | copy-start | bytes 1572868
  305.3 70.5 %copy-start.4 = (f32[2,512,128]{2,1,0:T(8,128)S(1)}, f32[2,512,128]{2,1,0:T(8,128)}, u32[]{:S(2)}) copy-start(f32[2,512,128]{2,1,0:T(8,128)} %copy-done.3) | copy-start | bytes 1572868
  378.6 1.1 copy-start.12
  386.8 2.0 copy-start.8
  386.8 2.5 copy-start.13
  396.6 55.5 %copy-start.26 = (f32[2048]{0:T(1024)S(1)}, f32[2048]{0:T(1024)}, u32[]{:S(2)}) copy-start(f32[2048]{0:T(1024)} %param.13) | copy-start | bytes 24580
  396.6 55.6 %copy-start.29 = (f32[128]{0:T(128)S(1)}, f32[128]{0:T(128)}, u32[]{:S(2)}) copy-start(f32[128]{0:T(128)} %copy-done.28) | copy-start | bytes 1540
  396.6 55.6 %copy-start.31 = (f32[128]{0:T(128)S(1)}, f32[128]{0:T(128)}, u32[]{:S(2)}) copy-start(f32[128]{0:T(128)} %copy-done.30) | copy-start | bytes 1540
  452.2 29.2 %copy-start.10 = (bf16[128,2048]{1,0:T(8,128)(2,1)S(1)}, bf16[128,2048]{1,0:T(8,128)(2,1)}, u32[]{:S(2)}) copy-start(bf16[128,2048]{1,0:T(8,128)(2,1)} %cot.1) | copy-start | bytes 1572868
Sparse Core Ops, SparseCore 0:
  13.4 112.2 all-gather.1
  249.6 126.0 reduce-scatter.3

commit v3 on v2

--- a/solution.py
+++ b/solution.py
@@ -2,6 +2,7 @@
 
 import jax
 import jax.numpy as jnp
+import numpy as np
 from jax import lax
 from jax.experimental import pallas as pl
 from jax.experimental.pallas import tpu as pltpu
@@ -173,7 +174,7 @@
     )(qblk, qlim, kslot, q, do, kv, ot, lse)
 
 
-def turn(values, cos, sin, copies):
+def turn(values, table, copies, paired, sign):
     width = values.shape[1]
     lane = lax.broadcasted_iota(jnp.int32, values.shape, 1) % HD
     partner = jnp.where(
@@ -181,20 +182,21 @@
         pltpu.roll(values, width - ROT // 2, 1),
         pltpu.roll(values, ROT // 2, 1),
     )
+    cos, sin = table[:, :HD], sign * table[:, HD:]
+    cos = jnp.concatenate([cos, jnp.ones_like(cos) if paired else cos], axis=1)
+    sin = jnp.concatenate([sin, jnp.zeros_like(sin) if paired else sin], axis=1)
     cos = jnp.concatenate([cos] * copies, axis=1)
     sin = jnp.concatenate([sin] * copies, axis=1)
     return values * cos + partner * sin
 
 
-def project_kernel(heads, x_ref, w_ref, b_ref, cq, sq, ck, sk, q_ref, kv_ref):
+def project_kernel(heads, places, x_ref, w_ref, b_ref, t0_ref, t1_ref, q_ref, kv_ref):
     width = heads * HD
     parts = []
-    for slot in range(2):
+    for slot, table in enumerate((t0_ref[...], t1_ref[...])):
         joined = dot(x_ref[slot], w_ref[...], NN) + b_ref[...]
-        parts.append(
-            turn(joined[:, :width], cq[slot], sq[slot], heads // 2).astype(BF)
-        )
-        kv = turn(joined[:, width:], ck[slot], sk[slot], heads).astype(BF)
+        parts.append(turn(joined[:, :width], table, heads // 2, False, 1.0).astype(BF))
+        kv = turn(joined[:, width:], table, heads, True, 1.0).astype(BF)
         for head in range(heads):
             kv_ref[head, slot] = kv[:, head * 2 * HD : (head + 1) * 2 * HD]
     for head in range(heads):
@@ -202,45 +204,51 @@
         q_ref[head] = jnp.concatenate([parts[0][:, lanes], parts[1][:, lanes]], axis=1)
 
 
-def project(x, w, bias, tables, heads):
+def table_specs(tile):
+    return [
+        pl.BlockSpec((None, tile, 2 * HD), lambda i, places: (places[0], i, 0)),
+        pl.BlockSpec((None, tile, 2 * HD), lambda i, places: (places[1], i, 0)),
+    ]
+
+
+def project(places, x, w, bias, table, heads):
     tile = 256
     width = 3 * heads * HD
     depth = x.shape[1]
-    table = pl.BlockSpec((2, tile, 2 * HD), lambda i: (0, i, 0))
     return pl.pallas_call(
         functools.partial(project_kernel, heads),
-        grid=(BLK // tile,),
+        grid_spec=pltpu.PrefetchScalarGridSpec(
+            num_scalar_prefetch=1,
+            grid=(BLK // tile,),
+            in_specs=[
+                pl.BlockSpec((2, tile, depth), lambda i, places: (0, i, 0)),
+                pl.BlockSpec((depth, width), lambda i, places: (0, 0)),
+                pl.BlockSpec((1, width), lambda i, places: (0, 0)),
+            ]
+            + table_specs(tile),
+            out_specs=(
+                pl.BlockSpec((heads, tile, 2 * HD), lambda i, places: (0, i, 0)),
+                pl.BlockSpec((heads, 2, tile, 2 * HD), lambda i, places: (0, 0, i, 0)),
+            ),
+        ),
         out_shape=(
             jax.ShapeDtypeStruct((heads, BLK, 2 * HD), BF),
             jax.ShapeDtypeStruct((heads, 2, BLK, 2 * HD), BF),
         ),
-        in_specs=[
-            pl.BlockSpec((2, tile, depth), lambda i: (0, i, 0)),
-            pl.BlockSpec((depth, width), lambda i: (0, 0)),
-            pl.BlockSpec((1, width), lambda i: (0, 0)),
-            table,
-            table,
-            table,
-            table,
-        ],
-        out_specs=(
-            pl.BlockSpec((heads, tile, 2 * HD), lambda i: (0, i, 0)),
-            pl.BlockSpec((heads, 2, tile, 2 * HD), lambda i: (0, 0, i, 0)),
-        ),
         compiler_params=pltpu.CompilerParams(vmem_limit_bytes=40 * 2**20),
         name="project",
-    )(x.reshape(2, BLK, depth), w, bias, *tables)
-
-
-def unturn_kernel(heads, dq_ref, dkv_ref, cq, sq, ck, sk, out_ref, sum_ref):
+    )(places, x.reshape(2, BLK, depth), w, bias, table, table)
+
+
+def unturn_kernel(heads, places, dq_ref, dkv_ref, t0_ref, t1_ref, out_ref, sum_ref):
     width = heads * HD
     sums = jnp.zeros((1, 3 * width), F32)
-    for slot in range(2):
+    for slot, table in enumerate((t0_ref[...], t1_ref[...])):
         lanes = slice(slot * HD, (slot + 1) * HD)
         q = jnp.concatenate([dq_ref[head][:, lanes] for head in range(heads)], axis=1)
-        q = turn(q.astype(F32), cq[slot], -sq[slot], heads // 2).astype(BF)
+        q = turn(q.astype(F32), table, heads // 2, False, -1.0).astype(BF)
         kv = jnp.concatenate([dkv_ref[head, slot] for head in range(heads)], axis=1)
-        kv = turn(kv.astype(F32), ck[slot], -sk[slot], heads).astype(BF)
+        kv = turn(kv.astype(F32), table, heads, True, -1.0).astype(BF)
         both = jnp.concatenate([q, kv], axis=1)
         out_ref[slot] = both
         sums += jnp.sum(both.astype(F32), axis=0, keepdims=True)
@@ -252,33 +260,165 @@
     sum_ref[...] += sums
 
 
-def unturn(dq, dkv, tables, heads):
+def unturn(places, dq, dkv, table, heads):
     tile = 256
     width = 3 * heads * HD
-    table = pl.BlockSpec((2, tile, 2 * HD), lambda i: (0, i, 0))
     out, sums = pl.pallas_call(
         functools.partial(unturn_kernel, heads),
-        grid=(BLK // tile,),
+        grid_spec=pltpu.PrefetchScalarGridSpec(
+            num_scalar_prefetch=1,
+            grid=(BLK // tile,),
+            in_specs=[
+                pl.BlockSpec((heads, tile, 2 * HD), lambda i, places: (0, i, 0)),
+                pl.BlockSpec((heads, 2, tile, 2 * HD), lambda i, places: (0, 0, i, 0)),
+            ]
+            + table_specs(tile),
+            out_specs=(
+                pl.BlockSpec((2, tile, width), lambda i, places: (0, i, 0)),
+                pl.BlockSpec((1, width), lambda i, places: (0, 0)),
+            ),
+        ),
         out_shape=(
             jax.ShapeDtypeStruct((2, BLK, width), BF),
             jax.ShapeDtypeStruct((1, width), F32),
         ),
-        in_specs=[
-            pl.BlockSpec((heads, tile, 2 * HD), lambda i: (0, i, 0)),
-            pl.BlockSpec((heads, 2, tile, 2 * HD), lambda i: (0, 0, i, 0)),
-            table,
-            table,
-            table,
-            table,
-        ],
-        out_specs=(
-            pl.BlockSpec((2, tile, width), lambda i: (0, i, 0)),
-            pl.BlockSpec((1, width), lambda i: (0, 0)),
-        ),
         compiler_params=pltpu.CompilerParams(vmem_limit_bytes=40 * 2**20),
         name="unturn",
-    )(dq, dkv, *tables)
+    )(places, dq, dkv, table, table)
     return out.reshape(2 * BLK, width), sums
+
+
+def mixed_grad_kernel(heads, g_ref, w0_ref, w1_ref, out_ref):
+    weights = jnp.concatenate([w0_ref[...], w1_ref[...]], axis=1)
+    parts = [dot(g_ref[slot], weights, NN).astype(BF) for slot in range(2)]
+    for head in range(heads):
+        lanes = slice(head * HD, (head + 1) * HD)
+        out_ref[head] = jnp.concatenate([parts[0][:, lanes], parts[1][:, lanes]], axis=1)
+
+
+def mixed_grad(g, weights, first, heads):
+    tile = 256
+    depth = g.shape[2]
+    block = first // 128
+    return pl.pallas_call(
+        functools.partial(mixed_grad_kernel, heads),
+        grid=(BLK // tile,),
+        out_shape=jax.ShapeDtypeStruct((heads, BLK, 2 * HD), BF),
+        in_specs=[
+            pl.BlockSpec((2, tile, depth), lambda i: (0, i, 0)),
+            pl.BlockSpec((depth, 128), lambda i: (0, block)),
+            pl.BlockSpec((depth, 128), lambda i: (0, block + 1)),
+        ],
+        out_specs=pl.BlockSpec((heads, tile, 2 * HD), lambda i: (0, i, 0)),
+        compiler_params=pltpu.CompilerParams(vmem_limit_bytes=40 * 2**20),
+        name="mixed_grad",
+    )(g, weights, weights)
+
+
+def ff_kernel(
+    heads, main, both, down, order, x_ref, g_ref, o_ref, w_ref, a_ref, h_ref, s_ref, *outs
+):
+    rows, depth = x_ref.shape[1:]
+    x = x_ref[...].reshape(2 * rows, depth)
+    g = g_ref[...].reshape(2 * rows, depth)
+    gate_up = dot(x, w_ref[:, :both], NN)
+    gh = dot(g, w_ref[:, both : both + down], NN)
+    ends = gate_up[:, 2 * main :]
+    gate = jnp.concatenate([gate_up[:, :main], ends], axis=1)
+    up = jnp.concatenate([gate_up[:, main : 2 * main], pltpu.roll(ends, HD, 1)], axis=1)
+    sig = jax.nn.sigmoid(gate)
+    silu = gate * sig
+    hidden = (silu * up).astype(BF)
+    d_gate = gh * up * sig * (1.0 + gate * (1.0 - sig))
+    d_up = gh * silu
+    tail = d_gate[:, main:] + pltpu.roll(d_up[:, main:], HD, 1)
+    grads = jnp.concatenate(
+        [d_gate[:, :main].astype(BF), d_up[:, :main].astype(BF), tail.astype(BF)], axis=1
+    )
+    mixed = [
+        jnp.concatenate(
+            [o_ref[head][:, slot * HD : (slot + 1) * HD] for head in range(heads)], axis=1
+        )
+        for slot in range(2)
+    ]
+    held = jnp.concatenate([hidden, jnp.concatenate(mixed, axis=0)], axis=1)
+    a_ref[...] = grads.reshape(2, rows, both)
+    h_ref[...] = held.reshape(2, rows, -1)
+    s_ref[...] = dot(grads, w_ref[:, :both], NT).astype(BF).reshape(2, rows, depth)
+    branches = dot(held, w_ref[:, both:], NT).astype(BF).reshape(2, rows, depth)
+    for i, out in enumerate(outs):
+
+        @pl.when(pl.program_id(0) == i)
+        def _():
+            out[...] = branches
+
+
+def feed_forward(order, x, g, o, w, heads, main, both, down):
+    depth, cols = w.shape
+    rows = BLK // 4
+    kept = cols - both
+
+    def tile(lanes, lead=2):
+        return pl.BlockSpec((lead, rows, lanes), lambda i, order: (0, order[i], 0))
+
+    part = pl.BlockSpec((2, rows, depth), lambda i, order: (0, 0, 0))
+    return pl.pallas_call(
+        functools.partial(ff_kernel, heads, main, both, down),
+        grid_spec=pltpu.PrefetchScalarGridSpec(
+            num_scalar_prefetch=1,
+            grid=(4,),
+            in_specs=[
+                tile(depth),
+                tile(depth),
+                tile(2 * HD, heads),
+                pl.BlockSpec(
+                    (depth, cols), lambda i, order: (0, 0), pipeline_mode=pl.Buffered(1)
+                ),
+            ],
+            out_specs=(tile(both), tile(kept), tile(depth)) + (part,) * 4,
+        ),
+        out_shape=(
+            jax.ShapeDtypeStruct((2, BLK, both), BF),
+            jax.ShapeDtypeStruct((2, BLK, kept), BF),
+            jax.ShapeDtypeStruct((2, BLK, depth), BF),
+        )
+        + (jax.ShapeDtypeStruct((2, rows, depth), BF),) * 4,
+        compiler_params=pltpu.CompilerParams(vmem_limit_bytes=60 * 2**20),
+        cost_estimate=pl.CostEstimate(
+            flops=int(19e9), bytes_accessed=30 * 2**20, transcendentals=2**20
+        ),
+        name="feed_forward",
+    )(order, x, g, o, w)
+
+
+def ff_weights_kernel(x_ref, g_ref, a_ref, h_ref, out_ref):
+    both = a_ref.shape[1]
+    out_ref[:, :both] = dot(x_ref[...], a_ref[...], TN).astype(BF)
+    out_ref[:, both:] = dot(g_ref[...], h_ref[...], TN).astype(BF)
+
+
+def ff_weights(x, g, a, h):
+    rows, depth = x.shape
+    tile = 256
+    cols = a.shape[1] + h.shape[1]
+    strip = pl.BlockSpec((rows, tile), lambda i: (0, i))
+    return pl.pallas_call(
+        ff_weights_kernel,
+        grid=(depth // tile,),
+        out_shape=jax.ShapeDtypeStruct((depth, cols), BF),
+        in_specs=[
+            strip,
+            strip,
+            pl.BlockSpec(a.shape, lambda i: (0, 0), pipeline_mode=pl.Buffered(1)),
+            pl.BlockSpec(h.shape, lambda i: (0, 0), pipeline_mode=pl.Buffered(1)),
+        ],
+        out_specs=pl.BlockSpec((tile, cols), lambda i: (i, 0)),
+        compiler_params=pltpu.CompilerParams(vmem_limit_bytes=48 * 2**20),
+        cost_estimate=pl.CostEstimate(
+            flops=int(10e9), bytes_accessed=24 * 2**20, transcendentals=0
+        ),
+        name="ff_weights",
+    )(x, g, a, h)
 
 
 def coords():
@@ -665,48 +805,30 @@
     )
 
 
-def home_kernel(grads, dq, branches, tokens, dq_home, grads_home, result, *rest):
-    mine, near, far, total, own, side, out, cross = rest[:8]
-    links = Links(*rest[8:])
-    links.greet(BR_ALL + TOK_ALL)
-
-    def finish(value, here):
-        return value + tokens[here, :].astype(F32)
-
-    in_turn(
-        [
-            reduce_heads(links, grads, dq, dq_home, grads_home, mine, near, far, total),
-            reduce_br(links, branches, own, side, out, cross, result, finish),
-        ]
-    )
+def home_kernel(grads, dq, dq_home, grads_home, mine, near, far, total, *sems):
+    links = Links(*sems)
+    links.greet(TOK_ALL)
+    in_turn([reduce_heads(links, grads, dq, dq_home, grads_home, mine, near, far, total)])
     links.close()
 
 
-def heads_home(grads, dq, branches, tokens):
-    rows, depth = tokens.shape
+def heads_home(grads, dq):
     span, lanes = grads.shape[3:]
     return comm_call(
         home_kernel,
         "heads_home",
         2,
-        (grads, dq, branches, tokens),
+        (grads, dq),
         (
             jax.ShapeDtypeStruct(dq.shape, BF),
             jax.ShapeDtypeStruct((4, span, lanes), BF),
-            jax.ShapeDtypeStruct((rows, depth), BF),
         ),
         scratch=[
             pltpu.VMEM((4, 2, span, lanes), BF),
             pltpu.VMEM((4, 2, span, lanes), BF),
             pltpu.VMEM((4, span, lanes), BF),
             pltpu.VMEM((4, span, lanes), BF),
-            pltpu.VMEM((2, rows, depth), BF),
-            pltpu.VMEM((3, 2, rows, depth), BF),
-            pltpu.VMEM((rows, depth), BF),
-            pltpu.VMEM((rows, depth), BF),
         ],
-        in_vmem=(3,),
-        out_vmem=(2,),
     )
 
 
@@ -790,6 +912,10 @@
     return [(t, ((t // 4 + dy) % 4) * 4 + t % 4) for t in range(16)]
 
 
+def br_perm(dl, dx):
+    return [(b, (b // 4 ^ dl) * 4 + (b + dx) % 4) for b in range(8)]
+
+
 def swap_heads(parts, y):
     back = [lax.dynamic_index_in_dim(parts, y, 0, keepdims=False)]
     for d in (3, 2, 1):
@@ -799,23 +925,14 @@
     return lax.dynamic_slice_in_dim(stacked, (4 - y) % 4, 4, 0)
 
 
-def rotary_tables(positions, long_shape):
+def rotary_table():
     half = ROT // 2
-    frequency = ROPE_BASE ** (-(jnp.arange(half).astype(F32) * 2.0 / ROT))
-    angles = positions.astype(F32)[:, None] * frequency[None, :]
-    cos, sin = jnp.cos(angles), jnp.sin(angles)
-    rows = positions.shape[0]
-    one = jnp.ones((rows, HD - ROT), F32)
-    zero = jnp.zeros((rows, HD - ROT), F32)
-    cos64 = jnp.concatenate([cos, cos, one], axis=1)
-    sin64 = jnp.concatenate([-sin, sin, zero], axis=1)
-    tables = (
-        jnp.concatenate([cos64, cos64], axis=1),
-        jnp.concatenate([sin64, sin64], axis=1),
-        jnp.concatenate([cos64, jnp.ones((rows, HD), F32)], axis=1),
-        jnp.concatenate([sin64, jnp.zeros((rows, HD), F32)], axis=1),
-    )
-    return tuple(t.reshape(2, BLK, 2 * HD) for t in tables)
+    frequency = (ROPE_BASE ** (-(np.arange(half) * 2.0 / ROT))).astype(np.float32)
+    angles = np.arange(LB * BLK, dtype=np.float32)[:, None] * frequency[None, :]
+    cos, sin = np.cos(angles), np.sin(angles)
+    one = np.ones((LB * BLK, HD - ROT), np.float32)
+    table = np.concatenate([cos, cos, one, -sin, sin, 0.0 * one], axis=1)
+    return table.astype(np.float32).reshape(LB, BLK, 2 * HD)
 
 
 def body(
@@ -871,9 +988,6 @@
     both_width = 2 * hidden_width
     down_width = main + 128
     ff_full = lax.all_gather(ff_shard, "tok", axis=0, tiled=True)
-    gu_full = ff_full[:, :both_width]
-    down_full = ff_full[:, both_width : both_width + down_width]
-    out_full = ff_full[:, both_width + down_width :]
     x, qkv_full = start(shifted, qkv_shard)
     x = x.reshape(2 * BLK, depth)
     qkv_full = qkv_full.reshape(16 * wrows, -1)
@@ -906,71 +1020,65 @@
     ).astype(jnp.int32)
 
     my_blocks = lax.dynamic_slice_in_dim(block_map, tok * 2, 2)
-    my_start = (
-        jnp.where(my_blocks < long_blocks, my_blocks % LB, (my_blocks - long_blocks) % 2) * BLK
-    )
-    positions = (my_start[:, None] + jnp.arange(BLK, dtype=jnp.int32)[None, :]).reshape(-1)
-    tables = rotary_tables(positions, long_blocks)
-
-    q_heads, kv_heads = project(x, qkv_full, bias, tables, heads)
+    places = jnp.where(my_blocks < long_blocks, my_blocks % LB, (my_blocks - long_blocks) % 2)
+    table = jnp.asarray(rotary_table())
+
+    q_heads, kv_heads = project(places, x, qkv_full, bias, table, heads)
     joined = jnp.concatenate([q_heads, kv_heads.reshape(heads, 2 * BLK, 2 * HD)], axis=1)
     q_all, kv_all, grad = heads_out(joined, cotangent)
-    grad = grad.reshape(2 * BLK, depth)
     kv_all = kv_all.reshape(-1, 2 * HD)
 
     turned, lse, o_parts = attn_fwd(query_block, query_limit, key_slot, q_all, kv_all, long_blocks)
 
-    def to_heads(flat):
-        split = flat.reshape(2, BLK, heads, HD)
-        return jnp.transpose(split, (2, 1, 0, 3)).reshape(heads, BLK, 2 * HD)
-
-    def from_heads(packed):
-        split = packed.reshape(heads, BLK, 2, HD)
-        return jnp.transpose(split, (2, 1, 0, 3)).reshape(2 * BLK, width)
-
-    mixed = from_heads(swap_heads(o_parts, y))
-
-    grad_mixed = dot(grad, out_full, NN).astype(BF)
-    do_all = swap_heads(to_heads(grad_mixed), y)
-
-    both = dot(x, gu_full, NN)
-    grad_hidden = dot(grad, down_full, NN)
-    ends = both[:, 2 * main :]
-    gate = jnp.concatenate([both[:, :main], ends[:, :tail]], axis=1)
-    up = jnp.concatenate([both[:, main : 2 * main], ends[:, tail:]], axis=1)
-    gh = grad_hidden[:, :hidden_width]
-    sig = jax.nn.sigmoid(gate)
-    hidden = (gate * sig * up).astype(BF)
-    hidden = jnp.pad(hidden, ((0, 0), (0, down_width - hidden_width)))
-    grad_gate = (gh * up * sig * (1.0 + gate * (1.0 - sig))).astype(BF)
-    grad_up = (gh * gate * sig).astype(BF)
-    grad_both = jnp.concatenate(
-        [grad_gate[:, :main], grad_up[:, :main], grad_gate[:, main:], grad_up[:, main:]], axis=1
-    )
-    branches = (dot(hidden, down_full, NT) + dot(mixed, out_full, NT)).astype(BF)
-    grad_ff = jnp.concatenate(
-        [
-            dot(x, grad_both, TN).astype(BF),
-            dot(grad, hidden, TN).astype(BF),
-            dot(grad, mixed, TN).astype(BF),
-        ],
-        axis=1,
+    o_heads = swap_heads(o_parts, y)
+    grad = grad.reshape(2, BLK, depth)
+    do_heads = mixed_grad(grad, ff_full, both_width + down_width, heads)
+    o_heads, do_heads = lax.optimization_barrier((o_heads, do_heads))
+    do_all = swap_heads(do_heads, y)
+
+    br = lax.axis_index("br")
+    l, xi = br // 4, br % 4
+    order = ((xi + jnp.array([1, 3, 2, 0], jnp.int32)) % 4).astype(jnp.int32)
+    grad_both, held, grad_x, *branches = feed_forward(
+        order,
+        x.reshape(2, BLK, depth),
+        grad,
+        o_heads,
+        ff_full,
+        heads,
+        main,
+        both_width,
+        down_width,
+    )
+    moved = [
+        lax.ppermute(branches[i], "br", br_perm(0, d)) for i, d in enumerate((1, 3, 2))
+    ]
+    grad_ff = ff_weights(
+        x,
+        grad.reshape(2 * BLK, depth),
+        grad_both.reshape(2 * BLK, -1),
+        held.reshape(2 * BLK, -1),
     )
     grad_ff = lax.psum_scatter(grad_ff, "tok", scatter_dimension=0, tiled=True)
 
     dq_parts, dkv_all = attn_bwd(
         query_block, query_limit, key_slot, q_all, do_all, kv_all, turned, lse, long_blocks
     )
-    dq_heads, dkv_heads, result = heads_home(
+    summed = branches[3].astype(F32)
+    for piece in moved:
+        summed = summed + piece.astype(F32)
+    summed, dq_parts = lax.optimization_barrier((summed, dq_parts))
+    across = lax.dynamic_index_in_dim(summed.astype(BF), 1 - l, 0, keepdims=False)
+    across = lax.ppermute(across, "br", br_perm(1, 0))
+    dq_heads, dkv_heads = heads_home(
         dkv_all.reshape(4, 2, 2, 2 * BLK, 2 * HD),
         dq_parts,
-        branches.reshape(2, 4, rows, depth),
-        tokens,
     )
     dkv_heads = dkv_heads.reshape(heads, 2, BLK, 2 * HD)
-    grad_joined, bias_sums = unturn(dq_heads, dkv_heads, tables, heads)
+    grad_joined, bias_sums = unturn(places, dq_heads, dkv_heads, table, heads)
     grad_shifted = (
-        dot(grad_both, gu_full, NT) + dot(grad_joined, qkv_full[:, : 3 * width], NT)
+        grad_x.reshape(2 * BLK, depth).astype(F32)
+        + dot(grad_joined, qkv_full[:, : 3 * width], NT)
     ).astype(BF)
     grad_qkv = dot(x, grad_joined, TN).astype(BF)
     qsum = bias_sums[0, :width].reshape(1, heads, HD)
@@ -979,6 +1087,9 @@
     bsum = jnp.transpose(bsum, (2, 0, 1, 3)).reshape(16, 1, qkv_bias.size).astype(BF)
     bsum = jnp.pad(bsum, ((0, 0), (0, wrows - 1), (0, 128 - qkv_bias.size)))
     grad_qkv = jnp.concatenate([grad_qkv, bsum.reshape(16 * wrows, 128)], axis=1)
+    across, grad_shifted = lax.optimization_barrier((across, grad_shifted))
+    summed = lax.dynamic_index_in_dim(summed, l, 0, keepdims=False) + across.astype(F32)
+    result = (residual + summed).astype(BF)
     my_grad_shifted, grad_qkv = last_sums(
         grad_shifted.reshape(2, 4, rows, depth), grad_qkv.reshape(4, 2, 2, wrows, -1)
     )

time: 503 us -> 450 us (0.89); the launches traced: 495 us -> 450 us
  matrix products: 71.3 us -> 10.3 us
  Pallas kernels: 309 us -> 339 us
  local copies, waits for them, and re-layouts: 61.9 us -> 45.9 us
  other arithmetic: 27.1 us -> 11.6 us
  waiting for transfers between devices: 6.15 us -> 16.5 us
  starting transfers between devices: 3.96 us -> 11.9 us
    dot_general x11 -> x2, matrix products: 71.3 us -> 10.3 us  [dot(): return lax.dot_general(left, right, dims, preferred_element_type=F32)]
    pallas_call x2 -> x5, Pallas kernels: 7.74 us -> 57.6 us  [the longest x1 31.1 us: feed_forward(): pl.pallas_call(functools.partial(ff_kernel, heads, main, both, down), gri...]
    pallas_call x5, Pallas kernels: 253 us -> 231 us  [comm_call(): pl.pallas_call(kernel, out_shape=tuple(outs), in_specs=[VMEM if i in in_v...]
    concatenate x2 -> x0, other arithmetic: 18.6 us -> none  [the longest x1 16.6 us: body(): jnp.concatenate([dot(x, grad_both, TN).astype(BF), dot(grad, hidden, TN)....]
    ppermute x0 -> x4, waiting for transfers between devices: none -> 10.2 us  [the longest x3 6.28 us: body(): lax.ppermute(branches[i], 'br', br_perm(0, d))]
    concatenate x5 -> x0, local copies, waits for them, and re-layouts: 8.68 us -> none  [the longest x1 5.25 us: body(): jnp.concatenate([grad_gate[:, :main], grad_up[:, :main], grad_gate[:, mai...]
    unnamed x106 -> x90, local copies, waits for them, and re-layouts: 34.5 us -> 29.9 us
  transfers between devices with their start and end apart: 8 -> 12, of which waited for: 3 -> 4; matrix products, arithmetic and copies ran while one was open for 13% -> 9% of each run, Pallas kernels for 62% -> 64%
where the time goes in v3:
time: 450 us
  Pallas kernels  339 us (75%)
  local copies, waits for them, and re-layouts  45.9 us (10%)
  waiting for transfers between devices  16.5 us (4%)
  between operations  14.9 us (3%)
  starting transfers between devices  11.9 us (3%)
  other arithmetic  11.6 us (3%)
  matrix products  10.3 us (2%)
    pallas_call x5, Pallas kernels, comm_call(): pl.pallas_call(kernel, out_shape=tuple(outs), in_specs=[VMEM if i in in_v...  231 us
    pallas_call x1, Pallas kernels, feed_forward(): pl.pallas_call(functools.partial(ff_kernel, heads, main, both, down), gri...  31.1 us
    unnamed x90, local copies, waits for them, and re-layouts  29.9 us
    pallas_call x1, Pallas kernels, attn_bwd(): pl.pallas_call(functools.partial(attn_bwd_kernel, long_blocks), out_shape...  29.6 us
    pallas_call x1, Pallas kernels, attn_fwd(): pl.pallas_call(functools.partial(attn_fwd_kernel, long_blocks), out_shape...  20.7 us
    pallas_call x1, Pallas kernels, ff_weights(): pl.pallas_call(ff_weights_kernel, grid=(depth // tile,), out_shape=jax.Sh...  15.1 us
    dot_general x2, matrix products, dot(): return lax.dot_general(left, right, dims, preferred_element_type=F32)  10.3 us
  transfers between devices with their start and end apart: 12, of which 4 were waited for; matrix products, arithmetic and copies ran while one was open for 9% of the time, Pallas kernels for 64%

profile of v3, /device:TPU:1, one launch (start us, length us, event | category | flops | bytes accessed | tf_op | source)
XLA Modules:
  0.0 450.1 jit_solution(8708495421971207721)
XLA Ops:
  7.3 0.8 slice.103
  8.1 0.9 slice.101
  9.7 0.9 slice.102
  10.9 1.0 copy.105
  12.2 1.1 copy.104
  13.3 1.0 concatenate.53
  16.1 51.5 %start.1 = (bf16[2,4,128,2048]{3,2,1,0:T(8,128)(2,1)}, bf16[4,2,2,128,896]{4,3,2,1,0:T(8,128)(2,1)S(1)}) custom-call(bf16[128,2048]{1,0:T(8,128)(2,1)S(1)} %fusion.9.s_ref, bf16[128,896]{1,0:T(8,128)(2,1)S(1)} %fusion.19.w_ref), custom_call_target="tpu_custom_call" | custom-call | tf_op jit(solution)/shard_map/start/pallas_call | solution.py:745
  67.6 1.9 copy-done.4
  70.5 2.2 copy-done.1
  72.7 2.1 copy-done.5
  74.9 5.3 %project.1 = (bf16[4,512,128]{2,1,0:T(8,128)(2,1)S(1)}, bf16[4,2,512,128]{3,2,1,0:T(8,128)(2,1)S(1)}) custom-call(s32[2]{0:T(128)S(1)} %compare_select_fusion.7.places, bf16[2,512,2048]{2,1,0:T(8,128)(2,1)S(1)} %bitcast.99, bf16[2048,896]{1,0:T(8,128)(2,1)S(1)} %bitcast.105, f32[1,768]{1,0:T(1,128)S(1)} %maximum_convert_fusion.b_ref, ...), custom_call_target="tpu_custom_call" | custom-call | tf_op jit(solution)/shard_map/project/pallas_call | solution.py:218
  80.3 0.9 copy-done.7
  81.3 59.6 %heads_out.1 = (bf16[4,512,128]{2,1,0:T(8,128)(2,1)S(1)}, bf16[4,2,2,1024,128]{4,3,2,1,0:T(8,128)(2,1)}, bf16[2,4,128,2048]{3,2,1,0:T(8,128)(2,1)}) custom-call(bf16[4,1536,128]{2,1,0:T(8,128)(2,1)S(1)} %pad_maximum_fusion.1.joined, bf16[128,2048]{1,0:T(8,128)(2,1)S(1)} %copy-done.7), custom_call_target="tpu_custom_call" | custom-call | tf_op jit(solution)/shard_map/heads_out/pallas_call | solution.py:745
  141.4 20.7 %attn_fwd.1 = (f32[4,128,512]{2,1,0:T(8,128)S(1)}, f32[8,1,512]{2,1,0:T(1,128)S(1)}, bf16[4,512,128]{2,1,0:T(8,128)(2,1)S(1)}) custom-call(s32[8]{0:T(128)S(1)} %select_reduce_fusion.2.qblk, s32[8]{0:T(128)S(1)} %select_reduce_fusion.1.qlim, s32[32]{0:T(128)S(1)} %select_reduce_fusion.kslot, bf16[4,512,128]{2,1,0:T(8,128)(2,1)S(1)} %get-tuple-element.46.q_ref, ...), custom_call_target="tpu_custom_call" | custom-call | flops 20000000000 | bytes 8388608 | tf_op jit(solution)/shard_map/attn_fwd/pallas_call | solution.py:91
  162.1 1.0 copy-done.15
  164.5 1.2 collective-permute-start.2
  165.6 2.3 collective-permute-start.1
  168.0 1.2 collective-permute-start
  169.1 1.2 and_select_fusion.4.order
  170.3 2.9 collective-permute-done
  177.9 1.9 constant_dynamic-slice_fusion.3.o_ref
  179.7 2.2 copy-done.3
  181.9 3.0 mixed_grad.1
  184.9 31.1 %feed_forward.1 = (bf16[2,512,1408]{2,1,0:T(8,128)(2,1)}, bf16[2,512,1024]{2,1,0:T(8,128)(2,1)}, bf16[2,512,2048]{2,1,0:T(8,128)(2,1)}, bf16[2,128,2048]{2,1,0:T...) custom-call(s32[4]{0:T(128)} %and_select_fusion.4.order, ...), custom_call_target="tpu_custom_call" | custom-call | flops 19000000512 | bytes 31457280 | tf_op jit(solution)/shard_map/feed_forward/pallas_call | solution.py:365
  216.1 1.8 copy-done.10
  217.9 1.6 copy-done.11
  219.5 15.1 %ff_weights.1 = bf16[2048,2432]{1,0:T(8,128)(2,1)} custom-call(bf16[1024,2048]{1,0:T(8,128)(2,1)} %bitcast.98, bf16[1024,2048]{1,0:T(8,128)(2,1)} %bitcast.102, bf16[1024,1408]{1,0:T(8,128)(2,1)S(1)} %bitcast.111, bf16[1024,1024]{1,0:T(8,128)(2,1)S(1)} %bitcast.112), custom_call_target="tpu_custom_call" | custom-call | flops 10000000000 | bytes 25165824 | tf_op jit(solution)/shard_map/ff_weights/pallas_call | solution.py:405
  235.3 2.4 collective-permute-start.6
  237.7 1.7 collective-permute-start.7
  239.4 2.7 collective-permute-start.4
  242.8 3.4 collective-permute-done.7
  250.1 1.9 constant_dynamic-slice_fusion.2.do_ref
  252.0 29.6 %attn_bwd.1 = (bf16[4,512,128]{2,1,0:T(8,128)(2,1)}, bf16[16384,128]{1,0:T(8,128)(2,1)}) custom-call(s32[8]{0:T(128)} %copy-done.12, s32[8]{0:T(128)} %copy-done.13, s32[32]{0:T(128)} %copy-done.14, bf16[4,512,128]{2,1,0:T(8,128)(2,1)} %copy-done.9, bf16[4,512,128]{2,1,0:T(8,128)(2,1)} %constant_dynamic-slice_fusion.2.do_ref, bf16[16384,128]{1,0:T(8,128)(2,1)} %bitcast.129, ...), custom_call_target="tpu_custom_call" | custom-call | flops 30000001024 | bytes 12582912 | tf_op jit(solution)/shard_map/attn_bwd/pallas_call | solution.py:160
  281.6 6.3 %collective-permute-done.3 = bf16[2,128,2048]{2,1,0:T(8,128)(2,1)S(1)} collective-permute-done((bf16[2,128,2048]{2,1,0:T(8,128)(2,1)}, bf16[2,128,2048]{2,1,0:T(8,128)(2,1)S(1)}, u32[]{:S(2)}, u32[]{:S(2)}) %collective-permute-start.3) | collective-permute-done | bytes 1048608 | tf_op jit(solution)/shard_map/ppermute | solution.py:1054
  288.9 44.4 %heads_home.1 = (bf16[4,512,128]{2,1,0:T(8,128)(2,1)S(1)}, bf16[4,1024,128]{2,1,0:T(8,128)(2,1)S(1)}) custom-call(bf16[4,2,2,1024,128]{4,3,2,1,0:T(8,128)(2,1)} %bitcast.113, bf16[4,512,128]{2,1,0:T(8,128)(2,1)S(1)} %copy-done.8), custom_call_target="tpu_custom_call" | custom-call | tf_op jit(solution)/shard_map/heads_home/pallas_call | solution.py:745
  333.3 3.1 unturn.1
  336.9 4.9 %convolution_convert_fusion = bf16[2048,768]{1,0:T(8,128)(2,1)} fusion(bf16[1024,2048]{1,0:T(8,128)(2,1)S(1)} %bitcast.100, bf16[1024,768]{1,0:T(8,128)(2,1)S(1)} %bitcast.109), kind=kOutput, calls=%fused_computation.3 | convolution fusion | flops 3222798336 | bytes 8912896 | tf_op jit(solution)/shard_map/dot_general | solution.py:29
  341.9 5.3 %fusion = bf16[1024,2048]{1,0:T(8,128)(2,1)} fusion(bf16[2,512,2048]{2,1,0:T(8,128)(2,1)S(1)} %copy-done.31, bf16[1024,768]{1,0:T(8,128)(2,1)S(1)} %bitcast.110, bf16[2048,896]{1,0:T(8,128)(2,1)S(1)} %bitcast.106), kind=kOutput, calls=%fused_computation.1 | convolution fusion | flops 3227516928 | bytes 13107200 | tf_op jit(solution)/shard_map/dot_general | solution.py:29
  348.1 2.4 pad_maximum_fusion.weights
  350.4 4.0 collective-permute-done.9
  355.2 55.3 %last_sums.1 = (f32[128,2048]{1,0:T(8,128)S(1)}, f32[128,896]{1,0:T(8,128)S(1)}) custom-call(bf16[2,4,128,2048]{3,2,1,0:T(8,128)(2,1)} %bitcast.114, bf16[4,2,2,128,896]{4,3,2,1,0:T(8,128)(2,1)S(1)} %pad_maximum_fusion.weights), custom_call_target="tpu_custom_call" | custom-call | tf_op jit(solution)/shard_map/last_sums/pallas_call | solution.py:745
  412.1 20.5 %sum_sides.1 = f32[8,256]{1,0:T(8,128)S(1)} custom-call(f32[8,8,256]{2,1,0:T(8,128)S(1)} %pad.14.parts), custom_call_target="tpu_custom_call" | custom-call | tf_op jit(solution)/shard_map/sum_sides/pallas_call | solution.py:745
  434.3 3.1 fusion.13
  437.4 1.2 convert_element_type.86
  438.7 1.0 fusion.26
  439.8 0.9 copy.116
  440.7 0.9 copy.115
  441.6 0.9 copy.117
  (170 shorter events, 23.2 us)
Async XLA Ops:
  7.2 7.3 %copy-start.28 = (bf16[3,4,4]{2,1,0:T(4,128)(2,1)S(1)}, bf16[3,4,4]{2,1,0:T(4,128)(2,1)}, u32[]{:S(2)}) copy-start(bf16[3,4,4]{2,1,0:T(4,128)(2,1)} %param.18) | copy-start | bytes 292
  7.2 7.6 %copy-start.23 = (bf16[3,128,256]{2,1,0:T(8,128)(2,1)S(1)}, bf16[3,128,256]{2,1,0:T(8,128)(2,1)}, u32[]{:S(2)}) copy-start(bf16[3,128,256]{2,1,0:T(8,128)(2,1)} %param.17) | copy-start | bytes 589828
  7.2 8.0 %copy-start.17 = (bf16[128,2048]{1,0:T(8,128)(2,1)S(1)}, bf16[128,2048]{1,0:T(8,128)(2,1)}, u32[]{:S(2)}) copy-start(bf16[128,2048]{1,0:T(8,128)(2,1)} %param.14) | copy-start | bytes 1572868
  7.2 172.5 %all-gather.2.cloned.1.call-start = ((), (), s32[]{:S(2)}) async-start(), calls=%async_computation.1 | async-start | bytes 10584064 | tf_op jit(solution)/shard_map/all_gather | solution.py:990
  10.9 4.8 %copy-start.24 = (f32[2048]{0:T(1024)S(1)}, f32[2048]{0:T(1024)}, u32[]{:S(2)}) copy-start(f32[2048]{0:T(1024)} %param.15) | copy-start | bytes 24580
  10.9 4.8 %copy-start.25 = (f32[2048]{0:T(1024)S(1)}, f32[2048]{0:T(1024)}, u32[]{:S(2)}) copy-start(f32[2048]{0:T(1024)} %param.16) | copy-start | bytes 24580
  14.3 56.1 %copy-start.29 = (s32[32]{0:T(128)S(1)}, s32[32]{0:T(128)}, u32[]{:S(2)}) copy-start(s32[32]{0:T(128)} %param.24) | copy-start | bytes 388
  14.3 56.2 %copy-start = (f32[8,512,128]{2,1,0:T(8,128)S(1)}, f32[8,512,128]{2,1,0:T(8,128)}, u32[]{:S(2)}) copy-start(f32[8,512,128]{2,1,0:T(8,128)} %constant.191.clone.t0_ref.t1_ref) | copy-start | bytes 6291460
  14.3 423.1 %reduce-scatter.2.cloned.1.call-start = ((), (), s32[]{:S(2)}) async-start(), calls=%async_computation.2 | async-start | bytes 10584064 | tf_op jit(solution)/shard_map/reduce_scatter | solution.py:1062
  15.7 64.5 %copy-start.26 = (f32[128]{0:T(128)}, f32[128]{0:T(128)S(1)}, u32[]{:S(2)}) copy-start(f32[128]{0:T(128)S(1)} %add_rsqrt_fusion) | copy-start | bytes 1540
  67.6 1.9 copy-start.4
  70.5 2.2 copy-start.1
  72.7 2.1 copy-start.5
  80.2 1.1 copy-start.7
  80.2 61.0 %copy-start.30 = (s32[10]{0:T(128)S(1)}, s32[10]{0:T(128)}, u32[]{:S(2)}) copy-start(s32[10]{0:T(128)} %param.25) | copy-start | bytes 124
  140.8 21.2 %copy-start.9 = (bf16[4,512,128]{2,1,0:T(8,128)(2,1)}, bf16[4,512,128]{2,1,0:T(8,128)(2,1)S(1)}, u32[]{:S(2)}) copy-start(bf16[4,512,128]{2,1,0:T(8,128)(2,1)S(1)} %get-tuple-element.46.q_ref) | copy-start | bytes 1572868
  141.0 21.1 %copy-start.14 = (s32[32]{0:T(128)}, s32[32]{0:T(128)S(1)}, u32[]{:S(2)}) copy-start(s32[32]{0:T(128)S(1)} %select_reduce_fusion.kslot) | copy-start | bytes 388
  141.2 20.9 %copy-start.12 = (s32[8]{0:T(128)}, s32[8]{0:T(128)S(1)}, u32[]{:S(2)}) copy-start(s32[8]{0:T(128)S(1)} %select_reduce_fusion.2.qblk) | copy-start | bytes 100
  141.4 20.7 %copy-start.13 = (s32[8]{0:T(128)}, s32[8]{0:T(128)S(1)}, u32[]{:S(2)}) copy-start(s32[8]{0:T(128)S(1)} %select_reduce_fusion.1.qlim) | copy-start | bytes 100
  162.1 1.0 copy-start.15
  163.1 0.6 copy-start.16
  164.5 10.1 %collective-permute-start.2 = (bf16[512,128]{1,0:T(8,128)(2,1)}, bf16[512,128]{1,0:T(8,128)(2,1)S(1)}, u32[]{:S(2)}, u32[]{:S(2)}) collective-permute-start(bf16[512,128]{1,0:T(8,128)(2,1)} %get-tuple-element.126), channel_id=1, source_target_pairs={{0,32},{8,40},{16,48},{24,56},{32,64},{40,72},{48,80},{56,88},{64,... | collective-permute-start | bytes 393224 | tf_op jit(solution)/shard_map/ppermute | solution.py:923
  165.6 8.2 %collective-permute-start.1 = (bf16[512,128]{1,0:T(8,128)(2,1)}, bf16[512,128]{1,0:T(8,128)(2,1)S(1)}, u32[]{:S(2)}, u32[]{:S(2)}) collective-permute-start(bf16[512,128]{1,0:T(8,128)(2,1)} %get-tuple-element.128), channel_id=1, source_target_pairs={{0,64},{8,72},{16,80},{24,88},{32,96},{40,104},{48,112},{56,120},{... | collective-permute-start | bytes 393224 | tf_op jit(solution)/shard_map/ppermute | solution.py:923
  168.0 5.2 %collective-permute-start = (bf16[512,128]{1,0:T(8,128)(2,1)}, bf16[512,128]{1,0:T(8,128)(2,1)S(1)}, u32[]{:S(2)}, u32[]{:S(2)}) collective-permute-start(bf16[512,128]{1,0:T(8,128)(2,1)} %get-tuple-element.129), channel_id=1, source_target_pairs={{0,96},{8,104},{16,112},{24,120},{32,0},{40,8},{48,16},{56,24},{64... | collective-permute-start | bytes 393224 | tf_op jit(solution)/shard_map/ppermute | solution.py:923
  179.7 2.2 copy-start.3
  216.1 1.8 copy-start.10
  217.9 1.6 copy-start.11
  235.3 6.8 %collective-permute-start.6 = (bf16[512,128]{1,0:T(8,128)(2,1)}, bf16[512,128]{1,0:T(8,128)(2,1)S(1)}, u32[]{:S(2)}, u32[]{:S(2)}) collective-permute-start(bf16[512,128]{1,0:T(8,128)(2,1)} %get-tuple-element.125), channel_id=1, source_target_pairs={{0,96},{8,104},{16,112},{24,120},{32,0},{40,8},{48,16},{56,24},{64... | collective-permute-start | bytes 393224 | tf_op jit(solution)/shard_map/ppermute | solution.py:923
  237.7 9.1 %collective-permute-start.8 = (bf16[512,128]{1,0:T(8,128)(2,1)S(1)}, bf16[512,128]{1,0:T(8,128)(2,1)S(1)}, u32[]{:S(2)}, u32[]{:S(2)}) collective-permute-start(bf16[512,128]{1,0:T(8,128)(2,1)S(1)} %get-tuple-element.122), channel_id=1, source_target_pairs={{0,32},{8,40},{16,48},{24,56},{32,64},{40,72},{48,80},{56,88},{64,... | collective-permute-start | bytes 393224 | tf_op jit(solution)/shard_map/ppermute | solution.py:923
  237.7 8.4 %collective-permute-start.7 = (bf16[512,128]{1,0:T(8,128)(2,1)S(1)}, bf16[512,128]{1,0:T(8,128)(2,1)S(1)}, u32[]{:S(2)}, u32[]{:S(2)}) collective-permute-start(bf16[512,128]{1,0:T(8,128)(2,1)S(1)} %get-tuple-element.124), channel_id=1, source_target_pairs={{0,64},{8,72},{16,80},{24,88},{32,96},{40,104},{48,112},{56,120},{... | collective-permute-start | bytes 393224 | tf_op jit(solution)/shard_map/ppermute | solution.py:923
  239.4 48.5 %collective-permute-start.3 = (bf16[2,128,2048]{2,1,0:T(8,128)(2,1)}, bf16[2,128,2048]{2,1,0:T(8,128)(2,1)S(1)}, u32[]{:S(2)}, u32[]{:S(2)}) collective-permute-start(bf16[2,128,2048]{2,1,0:T(8,128)(2,1)} %get-tuple-element.51), channel_id=1, source_target_pairs={{0,1},{1,2},{2,3},{3,0},{4,5},{5,6},{6,7},{7,4},{8,9},{9,10},{10,1... | collective-permute-start | bytes 3145736 | tf_op jit(solution)/shard_map/ppermute | solution.py:1054
  239.4 48.5 %collective-permute-start.4 = (bf16[2,128,2048]{2,1,0:T(8,128)(2,1)}, bf16[2,128,2048]{2,1,0:T(8,128)(2,1)S(1)}, u32[]{:S(2)}, u32[]{:S(2)}) collective-permute-start(bf16[2,128,2048]{2,1,0:T(8,128)(2,1)} %get-tuple-element.52), channel_id=1, source_target_pairs={{0,3},{1,0},{2,1},{3,2},{4,7},{5,4},{6,5},{7,6},{8,11},{9,8},{10,9... | collective-permute-start | bytes 3145736 | tf_op jit(solution)/shard_map/ppermute | solution.py:1054
  242.1 45.8 %collective-permute-start.5 = (bf16[2,128,2048]{2,1,0:T(8,128)(2,1)}, bf16[2,128,2048]{2,1,0:T(8,128)(2,1)S(1)}, u32[]{:S(2)}, u32[]{:S(2)}) collective-permute-start(bf16[2,128,2048]{2,1,0:T(8,128)(2,1)} %get-tuple-element.53), channel_id=1, source_target_pairs={{0,2},{1,3},{2,0},{3,1},{4,6},{5,7},{6,4},{7,5},{8,10},{9,11},{10,... | collective-permute-start | bytes 3145736 | tf_op jit(solution)/shard_map/ppermute | solution.py:1054
  252.0 35.9 %copy-start.21 = (bf16[2,128,2048]{2,1,0:T(8,128)(2,1)S(1)}, bf16[2,128,2048]{2,1,0:T(8,128)(2,1)}, u32[]{:S(2)}) copy-start(bf16[2,128,2048]{2,1,0:T(8,128)(2,1)} %get-tuple-element.50) | copy-start | bytes 3145732
  287.9 1.0 copy-start.8
  288.6 47.9 %copy-start.19 = (f32[2,128,2048]{2,1,0:T(8,128)}, f32[2,128,2048]{2,1,0:T(8,128)S(1)}, u32[]{:S(2)}) copy-start(f32[2,128,2048]{2,1,0:T(8,128)S(1)} %convert_add_fusion.1) | copy-start | bytes 6291460
  333.3 3.6 copy-start.2
  336.6 17.8 %collective-permute-start.9 = (bf16[128,2048]{1,0:T(8,128)(2,1)S(1)}, bf16[128,2048]{1,0:T(8,128)(2,1)S(1)}, u32[]{:S(2)}, u32[]{:S(2)}) collective-permute-start(bf16[128,2048]{1,0:T(8,128)(2,1)S(1)} %fusion.17), channel_id=1, source_target_pairs={{0,4},{1,5},{2,6},{3,7},{4,0},{5,1},{6,2},{7,3},{8,12},{9,13},{10,... | collective-permute-start | bytes 1572872 | tf_op jit(solution)/shard_map/ppermute | solution.py:1072
  336.9 5.0 %copy-start.6 = (bf16[4,2,2,128,896]{4,3,2,1,0:T(8,128)(2,1)S(1)}, bf16[4,2,2,128,896]{4,3,2,1,0:T(8,128)(2,1)}, u32[]{:S(2)}) copy-start(bf16[4,2,2,128,896]{4,3,2,1,0:T(8,128)(2,1)} %copy-done.4) | copy-start | bytes 11010052
  336.9 5.0 %copy-start.31 = (bf16[2,512,2048]{2,1,0:T(8,128)(2,1)S(1)}, bf16[2,512,2048]{2,1,0:T(8,128)(2,1)}, u32[]{:S(2)}) copy-start(bf16[2,512,2048]{2,1,0:T(8,128)(2,1)} %get-tuple-element.59) | copy-start | bytes 12582916
  354.4 0.8 copy-start.22
  355.2 56.0 %copy-start.18 = (bf16[128,2048]{1,0:T(8,128)(2,1)S(1)}, bf16[128,2048]{1,0:T(8,128)(2,1)}, u32[]{:S(2)}) copy-start(bf16[128,2048]{1,0:T(8,128)(2,1)} %param.14) | copy-start | bytes 1572868
  355.2 56.0 %copy-start.27 = (f32[128]{0:T(128)S(1)}, f32[128]{0:T(128)}, u32[]{:S(2)}) copy-start(f32[128]{0:T(128)} %copy-done.26) | copy-start | bytes 1540
  437.4 2.3 copy-start.20
Sparse Core Ops, SparseCore 0:
  14.4 102.2 all-gather.1
  234.7 132.2 reduce-scatter.1

commit v4 on v2

--- a/solution.py
+++ b/solution.py
@@ -2,6 +2,7 @@
 
 import jax
 import jax.numpy as jnp
+import numpy as np
 from jax import lax
 from jax.experimental import pallas as pl
 from jax.experimental.pallas import tpu as pltpu
@@ -22,6 +23,7 @@
 VMEM = pl.BlockSpec(memory_space=pltpu.VMEM)
 SMEM = pl.BlockSpec(memory_space=pltpu.SMEM)
 ANY = pl.BlockSpec(memory_space=pl.ANY)
+SMALL = pl.CostEstimate(flops=1000, bytes_accessed=1000, transcendentals=0)
 
 
 def dot(left, right, dims):
@@ -48,7 +50,7 @@
 
 def attn_fwd_kernel(long_blocks, qblk, qlim, kslot, q_ref, kv_ref, ot_ref, lse_ref, o_ref):
     def pack(i, unused):
-        packed = q_ref[i]
+        packed = q_ref[i, 0]
         for half in range(2):
             slot = 2 * i + half
             is_long, place, first = block_info(qblk[slot], long_blocks)
@@ -96,22 +98,20 @@
         ),
         in_specs=[SMEM, SMEM, SMEM, VMEM, VMEM],
         out_specs=(VMEM, VMEM, VMEM),
-        compiler_params=pltpu.CompilerParams(vmem_limit_bytes=48 * 2**20),
-        cost_estimate=pl.CostEstimate(
-            flops=int(20e9), bytes_accessed=8 * 2**20, transcendentals=8 * 2**20
-        ),
+        compiler_params=pltpu.CompilerParams(vmem_limit_bytes=60 * 2**20),
+        cost_estimate=SMALL,
         name="attn_fwd",
     )(qblk, qlim, kslot, q, kv)
 
 
 def attn_bwd_kernel(
-    long_blocks, qblk, qlim, kslot, q_ref, do_ref, kv_ref, ot_ref, lse_ref, dq_ref, dkv_ref, acc, dqt
+    long_blocks, qblk, qlim, kslot, q_ref, kv_ref, ot_ref, lse_ref, dq_ref, dkv_ref, acc, dqt
 ):
     acc[...] = jnp.zeros_like(acc)
 
     def pack(i, unused):
-        q_packed = q_ref[i]
-        d_packed = do_ref[i]
+        q_packed = q_ref[i, 0]
+        d_packed = q_ref[i, 1]
         d_turned = jnp.transpose(d_packed.astype(F32))
         for half in range(2):
             slot = 2 * i + half
@@ -154,7 +154,7 @@
     lax.fori_loop(0, kv_ref.shape[0] // BLK, finish, 0)
 
 
-def attn_bwd(qblk, qlim, kslot, q, do, kv, ot, lse, long_blocks):
+def attn_bwd(qblk, qlim, kslot, q, kv, ot, lse, long_blocks):
     n = q.shape[0]
     return pl.pallas_call(
         functools.partial(attn_bwd_kernel, long_blocks),
@@ -162,18 +162,16 @@
             jax.ShapeDtypeStruct((n, BLK, 2 * HD), BF),
             jax.ShapeDtypeStruct(kv.shape, BF),
         ),
-        in_specs=[SMEM, SMEM, SMEM, VMEM, VMEM, VMEM, VMEM, VMEM],
+        in_specs=[SMEM, SMEM, SMEM, VMEM, VMEM, VMEM, VMEM],
         out_specs=(VMEM, VMEM),
         scratch_shapes=[pltpu.VMEM(kv.shape, F32), pltpu.VMEM((2 * HD, BLK), F32)],
-        compiler_params=pltpu.CompilerParams(vmem_limit_bytes=56 * 2**20),
-        cost_estimate=pl.CostEstimate(
-            flops=int(30e9), bytes_accessed=12 * 2**20, transcendentals=8 * 2**20
-        ),
+        compiler_params=pltpu.CompilerParams(vmem_limit_bytes=60 * 2**20),
+        cost_estimate=SMALL,
         name="attn_bwd",
-    )(qblk, qlim, kslot, q, do, kv, ot, lse)
-
-
-def turn(values, cos, sin, copies):
+    )(qblk, qlim, kslot, q, kv, ot, lse)
+
+
+def turn(values, table, copies, paired, sign):
     width = values.shape[1]
     lane = lax.broadcasted_iota(jnp.int32, values.shape, 1) % HD
     partner = jnp.where(
@@ -181,104 +179,218 @@
         pltpu.roll(values, width - ROT // 2, 1),
         pltpu.roll(values, ROT // 2, 1),
     )
+    cos, sin = table[:, :HD], sign * table[:, HD:]
+    cos = jnp.concatenate([cos, jnp.ones_like(cos) if paired else cos], axis=1)
+    sin = jnp.concatenate([sin, jnp.zeros_like(sin) if paired else sin], axis=1)
     cos = jnp.concatenate([cos] * copies, axis=1)
     sin = jnp.concatenate([sin] * copies, axis=1)
     return values * cos + partner * sin
 
 
-def project_kernel(heads, x_ref, w_ref, b_ref, cq, sq, ck, sk, q_ref, kv_ref):
+def project_kernel(
+    heads, places, x_ref, g_ref, w_ref, b_ref, wo_ref, t0_ref, t1_ref, out_ref
+):
     width = heads * HD
-    parts = []
-    for slot in range(2):
-        joined = dot(x_ref[slot], w_ref[...], NN) + b_ref[...]
-        parts.append(
-            turn(joined[:, :width], cq[slot], sq[slot], heads // 2).astype(BF)
-        )
-        kv = turn(joined[:, width:], ck[slot], sk[slot], heads).astype(BF)
+    rows = w_ref.shape[0] // 16
+    corner = b_ref[:8, :].astype(F32)
+    for t in range(1, 16):
+        corner = corner + b_ref[t * rows : t * rows + 8, :].astype(F32)
+    bias = jnp.concatenate([corner[r : r + 1] for r in range(3 * width // 128)], axis=1)
+    parts, grads = [], []
+    tile, depth = x_ref.shape[1:]
+    products = dot(x_ref[...].reshape(2 * tile, depth), w_ref[...], NN) + bias
+    mixed = dot(g_ref[...].reshape(2 * tile, depth), wo_ref[...], NN).astype(BF)
+    for slot, table in enumerate((t0_ref[...], t1_ref[...])):
+        joined = products[slot * tile : (slot + 1) * tile]
+        parts.append(turn(joined[:, :width], table, heads // 2, False, 1.0).astype(BF))
+        grads.append(mixed[slot * tile : (slot + 1) * tile])
+        kv = turn(joined[:, width:], table, heads, True, 1.0).astype(BF)
         for head in range(heads):
-            kv_ref[head, slot] = kv[:, head * 2 * HD : (head + 1) * 2 * HD]
+            out_ref[head, 2 + slot] = kv[:, head * 2 * HD : (head + 1) * 2 * HD]
     for head in range(heads):
         lanes = slice(head * HD, (head + 1) * HD)
-        q_ref[head] = jnp.concatenate([parts[0][:, lanes], parts[1][:, lanes]], axis=1)
-
-
-def project(x, w, bias, tables, heads):
+        for i, pair in enumerate((parts, grads)):
+            out_ref[head, i] = jnp.concatenate([pair[0][:, lanes], pair[1][:, lanes]], axis=1)
+
+
+def project(places, x, g, w, ff, table, heads):
     tile = 256
     width = 3 * heads * HD
-    depth = x.shape[1]
-    table = pl.BlockSpec((2, tile, 2 * HD), lambda i: (0, i, 0))
+    depth = x.shape[2]
+    rows = pl.BlockSpec((2, tile, depth), lambda i, places: (0, i, 0))
     return pl.pallas_call(
         functools.partial(project_kernel, heads),
-        grid=(BLK // tile,),
-        out_shape=(
-            jax.ShapeDtypeStruct((heads, BLK, 2 * HD), BF),
-            jax.ShapeDtypeStruct((heads, 2, BLK, 2 * HD), BF),
+        grid_spec=pltpu.PrefetchScalarGridSpec(
+            num_scalar_prefetch=1,
+            grid=(BLK // tile,),
+            in_specs=[
+                rows,
+                rows,
+                pl.BlockSpec((depth, width), lambda i, places: (0, 0)),
+                pl.BlockSpec((depth, 128), lambda i, places: (0, width // 128)),
+                pl.BlockSpec((depth, heads * HD), lambda i, places: (0, 3)),
+                pl.BlockSpec((None, tile, 2 * HD), lambda i, places: (places[0], i, 0)),
+                pl.BlockSpec((None, tile, 2 * HD), lambda i, places: (places[1], i, 0)),
+            ],
+            out_specs=pl.BlockSpec((heads, 4, tile, 2 * HD), lambda i, places: (0, 0, i, 0)),
         ),
-        in_specs=[
-            pl.BlockSpec((2, tile, depth), lambda i: (0, i, 0)),
-            pl.BlockSpec((depth, width), lambda i: (0, 0)),
-            pl.BlockSpec((1, width), lambda i: (0, 0)),
-            table,
-            table,
-            table,
-            table,
-        ],
-        out_specs=(
-            pl.BlockSpec((heads, tile, 2 * HD), lambda i: (0, i, 0)),
-            pl.BlockSpec((heads, 2, tile, 2 * HD), lambda i: (0, 0, i, 0)),
-        ),
-        compiler_params=pltpu.CompilerParams(vmem_limit_bytes=40 * 2**20),
+        out_shape=jax.ShapeDtypeStruct((heads, 4, BLK, 2 * HD), BF),
+        compiler_params=pltpu.CompilerParams(vmem_limit_bytes=60 * 2**20),
+        cost_estimate=SMALL,
         name="project",
-    )(x.reshape(2, BLK, depth), w, bias, *tables)
-
-
-def unturn_kernel(heads, dq_ref, dkv_ref, cq, sq, ck, sk, out_ref, sum_ref):
+    )(places, x, g, w, w, ff, table, table)
+
+
+def join_kernel(
+    heads,
+    places,
+    dq_ref,
+    dkv_ref,
+    t0_ref,
+    t1_ref,
+    x_ref,
+    g_ref,
+    m_ref,
+    w_ref,
+    s_ref,
+    out_ref,
+    gs_ref,
+    gj,
+    sums,
+):
     width = heads * HD
-    sums = jnp.zeros((1, 3 * width), F32)
-    for slot in range(2):
-        lanes = slice(slot * HD, (slot + 1) * HD)
-        q = jnp.concatenate([dq_ref[head][:, lanes] for head in range(heads)], axis=1)
-        q = turn(q.astype(F32), cq[slot], -sq[slot], heads // 2).astype(BF)
-        kv = jnp.concatenate([dkv_ref[head, slot] for head in range(heads)], axis=1)
-        kv = turn(kv.astype(F32), ck[slot], -sk[slot], heads).astype(BF)
-        both = jnp.concatenate([q, kv], axis=1)
-        out_ref[slot] = both
-        sums += jnp.sum(both.astype(F32), axis=0, keepdims=True)
 
     @pl.when(pl.program_id(0) == 0)
     def _():
-        sum_ref[...] = jnp.zeros_like(sum_ref)
-
-    sum_ref[...] += sums
-
-
-def unturn(dq, dkv, tables, heads):
-    tile = 256
+        total = jnp.zeros((1, 3 * width), F32)
+        for slot, table in enumerate((t0_ref, t1_ref)):
+            for half in range(2):
+                rows = slice(half * BLK // 2, (half + 1) * BLK // 2)
+                lanes = slice(slot * HD, (slot + 1) * HD)
+                q = jnp.concatenate([dq_ref[h, rows, lanes] for h in range(heads)], axis=1)
+                q = turn(q.astype(F32), table[rows, :], heads // 2, False, -1.0).astype(BF)
+                kv = jnp.concatenate([dkv_ref[h, slot, rows] for h in range(heads)], axis=1)
+                kv = turn(kv.astype(F32), table[rows, :], heads, True, -1.0).astype(BF)
+                here = slice(slot * BLK + rows.start, slot * BLK + rows.stop)
+                gj[here, :width] = q
+                gj[here, width:] = kv
+                total += jnp.sum(
+                    jnp.concatenate([q, kv], axis=1).astype(F32), axis=0, keepdims=True
+                )
+        corner = [total[:, r * 128 : (r + 1) * 128] for r in range(3 * width // 128)]
+        corner = jnp.concatenate(corner + [jnp.zeros((2, 128), F32)], axis=0)
+        sums[...] = corner
+
+    both = gj[...]
+    tile, cols = out_ref.shape
+    out_ref[:, : 3 * width] = dot(x_ref[...], both, TN).astype(BF)
+    out_ref[:, 3 * width : 4 * width] = dot(g_ref[...], m_ref[...], TN).astype(BF)
+    zero = jnp.zeros((120, 128), F32)
+    block = jnp.concatenate([sums[...], zero] * (tile // 128), axis=0)
+    out_ref[:, 4 * width :] = block.astype(BF)
+    gs_ref[...] = (s_ref[...].astype(F32) + dot(both, w_ref[...], NT)).astype(BF)
+
+
+def join(places, dq, dkv, table, x, g, mixed, w, partial_grad, heads):
+    tile = 512
     width = 3 * heads * HD
-    table = pl.BlockSpec((2, tile, 2 * HD), lambda i: (0, i, 0))
-    out, sums = pl.pallas_call(
-        functools.partial(unturn_kernel, heads),
-        grid=(BLK // tile,),
+    rows, depth = x.shape
+    cols = width + heads * HD + 128
+    strip = pl.BlockSpec((rows, tile), lambda i, places: (0, i))
+    return pl.pallas_call(
+        functools.partial(join_kernel, heads),
+        grid_spec=pltpu.PrefetchScalarGridSpec(
+            num_scalar_prefetch=1,
+            grid=(depth // tile,),
+            in_specs=[
+                pl.BlockSpec(dq.shape, lambda i, places: (0, 0, 0)),
+                pl.BlockSpec(dkv.shape, lambda i, places: (0, 0, 0, 0)),
+                pl.BlockSpec((None, BLK, 2 * HD), lambda i, places: (places[0], 0, 0)),
+                pl.BlockSpec((None, BLK, 2 * HD), lambda i, places: (places[1], 0, 0)),
+                strip,
+                strip,
+                pl.BlockSpec(mixed.shape, lambda i, places: (0, 0)),
+                pl.BlockSpec((tile, width), lambda i, places: (i, 0)),
+                strip,
+            ],
+            out_specs=(pl.BlockSpec((tile, cols), lambda i, places: (i, 0)), strip),
+            scratch_shapes=[pltpu.VMEM((rows, width), BF), pltpu.VMEM((8, 128), F32)],
+        ),
         out_shape=(
-            jax.ShapeDtypeStruct((2, BLK, width), BF),
-            jax.ShapeDtypeStruct((1, width), F32),
+            jax.ShapeDtypeStruct((depth, cols), BF),
+            jax.ShapeDtypeStruct((rows, depth), BF),
         ),
+        compiler_params=pltpu.CompilerParams(vmem_limit_bytes=60 * 2**20),
+        cost_estimate=SMALL,
+        name="join",
+    )(places, dq, dkv, table, table, x, g, mixed, w, partial_grad)
+
+
+def ff_part(main, down, first, x, g, w_ref, h_ref, s_ref, pause):
+    rows, depth = x.shape[1:]
+    x = x.reshape(2 * rows, depth)
+    g = g.reshape(2 * rows, depth)
+    gate_up = dot(x, w_ref[:, first:], NN)
+    pause(0)
+    gh = dot(g, w_ref[:, :down], NN)
+    ends = gate_up[:, 2 * main :]
+    gate = jnp.concatenate([gate_up[:, :main], ends], axis=1)
+    up = jnp.concatenate([gate_up[:, main : 2 * main], pltpu.roll(ends, HD, 1)], axis=1)
+    sig = jax.nn.sigmoid(gate)
+    silu = gate * sig
+    hidden = (silu * up).astype(BF)
+    d_gate = gh * up * sig * (1.0 + gate * (1.0 - sig))
+    d_up = gh * silu
+    tail = d_gate[:, main:] + pltpu.roll(d_up[:, main:], HD, 1)
+    grads = jnp.concatenate(
+        [d_gate[:, :main].astype(BF), d_up[:, :main].astype(BF), tail.astype(BF)], axis=1
+    )
+    h_ref[...] = hidden.reshape(h_ref.shape)
+    pause(1)
+    s_ref[...] = dot(grads, w_ref[:, first:], NT).astype(BF).reshape(s_ref.shape)
+    return grads, hidden
+
+
+def branches_kernel(heads, h_ref, o_ref, w_ref, mixed_ref, out_ref):
+    rows = h_ref.shape[1]
+    mixed = [
+        jnp.concatenate(
+            [o_ref[head][:, slot * HD : (slot + 1) * HD] for head in range(heads)], axis=1
+        )
+        for slot in range(2)
+    ]
+    hidden = h_ref[...].reshape(2 * rows, -1)
+    mixed = jnp.concatenate(mixed, axis=0)
+    held = jnp.concatenate([hidden, mixed], axis=1)
+    mixed_ref[...] = mixed.reshape(mixed_ref.shape)
+    out_ref[...] = dot(held, w_ref[...], NT).astype(BF).reshape(out_ref.shape)
+
+
+def add_branches(hidden, o, w, heads):
+    depth = w.shape[0]
+    rows = BLK // 2
+    kept = hidden.shape[2] + heads * HD
+
+    def tile(lanes, lead=2):
+        return pl.BlockSpec((lead, rows, lanes), lambda i: (0, i, 0))
+
+    return pl.pallas_call(
+        functools.partial(branches_kernel, heads),
+        grid=(2,),
         in_specs=[
-            pl.BlockSpec((heads, tile, 2 * HD), lambda i: (0, i, 0)),
-            pl.BlockSpec((heads, 2, tile, 2 * HD), lambda i: (0, 0, i, 0)),
-            table,
-            table,
-            table,
-            table,
+            tile(hidden.shape[2]),
+            tile(2 * HD, heads),
+            pl.BlockSpec((depth, kept), lambda i: (0, 0)),
         ],
-        out_specs=(
-            pl.BlockSpec((2, tile, width), lambda i: (0, i, 0)),
-            pl.BlockSpec((1, width), lambda i: (0, 0)),
+        out_specs=(tile(heads * HD), tile(depth)),
+        out_shape=(
+            jax.ShapeDtypeStruct((2, BLK, heads * HD), BF),
+            jax.ShapeDtypeStruct((2, BLK, depth), BF),
         ),
-        compiler_params=pltpu.CompilerParams(vmem_limit_bytes=40 * 2**20),
-        name="unturn",
-    )(dq, dkv, *tables)
-    return out.reshape(2 * BLK, width), sums
+        compiler_params=pltpu.CompilerParams(vmem_limit_bytes=60 * 2**20),
+        cost_estimate=SMALL,
+        name="add_branches",
+    )(hidden, o, w)
 
 
 def coords():
@@ -429,45 +541,6 @@
         yield
     for ticket, ref in passed:
         links.arrived(ticket, ref)
-
-
-def spread_heads(links, joined, queries, pairs):
-    y, z, c, unused_l, unused_x = coords()
-    rows = queries.shape[1]
-    keys = pl.ds(rows, joined.shape[1] - rows)
-    links.local(joined.at[y, pl.ds(0, rows)], queries.at[y])
-    links.local(joined.at[y, keys], pairs.at[y, z, c])
-    order = (1, 3, 2)
-    direct = [
-        links.send(joined.at[(y + d) % 4, keys], pairs.at[y, z, c], dy=d) for d in order
-    ]
-    across = [links.send(joined.at[y, keys], pairs.at[y, z, c], dz=1)]
-    passed = [(links.send(joined.at[y, keys], pairs.at[y, z, c], dc=1), 0, 0)]
-    asked = [
-        links.send(joined.at[(y + d) % 4, pl.ds(0, rows)], queries.at[y], dy=d) for d in order
-    ]
-    yield
-
-    def far(i):
-        dy = 0 if i == 0 else -order[i - 1]
-        ref = pairs.at[(y + dy) % 4, 1 - z, c]
-        links.arrived(across[i], ref)
-        passed.append((links.send(ref, ref, dc=1), dy, 1))
-
-    for i, d in enumerate(order):
-        ref = pairs.at[(y - d) % 4, z, c]
-        links.arrived(direct[i], ref)
-        across.append(links.send(ref, ref, dz=1))
-        passed.append((links.send(ref, ref, dc=1), -d, 0))
-        yield
-        far(i)
-        yield
-    far(3)
-    yield
-    for i, d in enumerate(order):
-        links.arrived(asked[i], queries.at[(y - d) % 4])
-    for ticket, dy, dz in passed:
-        links.arrived(ticket, pairs.at[(y + dy) % 4, (z + dz) % 2, 1 - c])
 
 
 def add_up(target, sources, rows, finish):
@@ -614,55 +687,214 @@
             pltpu.SemaphoreType.DMA((16,)),
         ],
         compiler_params=pltpu.CompilerParams(
-            collective_id=number, has_side_effects=True, vmem_limit_bytes=48 * 2**20
+            collective_id=number, has_side_effects=True, vmem_limit_bytes=60 * 2**20
         ),
+        cost_estimate=SMALL,
         name=name,
     )(*args)
 
 
-def start_kernel(s_ref, w_ref, x_out, w_out, *sems):
+def start_kernel(s_ref, c_ref, w_ref, f_ref, x_out, g_out, w_out, f_out, *sems):
     links = Links(*sems)
     links.greet(BR_NEAR + TOK_NEAR)
-    in_turn([gather_br(links, s_ref, x_out), gather_tok(links, w_ref, w_out)])
+    in_turn(
+        [
+            gather_br(links, s_ref, x_out),
+            gather_tok(links, w_ref, w_out),
+            gather_tok(links, f_ref, f_out),
+            gather_br(links, c_ref, g_out),
+        ]
+    )
     links.close()
 
 
-def start(shifted, weights):
+def start(shifted, cot, weights, ff):
     rows, depth = shifted.shape
-    wrows, cols = weights.shape
+    wrows = weights.shape[0]
+    whole = jax.ShapeDtypeStruct((2, 4, rows, depth), BF)
     return comm_call(
         start_kernel,
         "start",
         0,
-        (shifted, weights),
+        (shifted, cot, weights, ff),
         (
-            jax.ShapeDtypeStruct((2, 4, rows, depth), BF),
-            jax.ShapeDtypeStruct((4, 2, 2, wrows, cols), BF),
+            whole,
+            whole,
+            jax.ShapeDtypeStruct((4, 2, 2, wrows, weights.shape[1]), BF),
+            jax.ShapeDtypeStruct((4, 2, 2, wrows, ff.shape[1]), BF),
         ),
-    )
-
-
-def heads_kernel(joined, cot, queries, pairs, grad_out, *sems):
+        copies=64,
+    )
+
+
+def ff_heads_kernel(
+    main,
+    down,
+    first,
+    x_ref,
+    g_ref,
+    x_strip,
+    g_strip,
+    w_ref,
+    joined,
+    h_ref,
+    s_ref,
+    grad_ref,
+    asked,
+    pairs,
+    held,
+    held_hidden,
+    *sems,
+):
+    y, z, c, unused_l, unused_x = coords()
+    step = pl.program_id(0)
     links = Links(*sems)
-    links.greet(BR_NEAR + TOK_ALL)
-    in_turn([spread_heads(links, joined, queries, pairs), gather_br(links, cot, grad_out)])
-    links.close()
-
-
-def heads_out(joined, cot):
-    rows, depth = cot.shape
-    heads, span, lanes = joined.shape
-    return comm_call(
-        heads_kernel,
-        "heads_out",
-        1,
-        (joined, cot),
-        (
-            jax.ShapeDtypeStruct((4, BLK, lanes), BF),
-            jax.ShapeDtypeStruct((4, 2, 2, span - BLK, lanes), BF),
-            jax.ShapeDtypeStruct((2, 4, rows, depth), BF),
+    order = (1, 3, 2)
+    front, back = pl.ds(0, 2), pl.ds(2, 2)
+
+    def pair(dy, dz=0, dc=0):
+        return pairs.at[(y + dy) % 4, (z + dz) % 2, (c + dc) % 2]
+
+    kept = [
+        pltpu.make_async_copy(joined.at[y, front], asked.at[y], sems[2].at[0]),
+        pltpu.make_async_copy(joined.at[y, back], pair(0), sems[2].at[1]),
+    ]
+    number = iter(range(64))
+
+    def plan(source, target, lands, **offsets):
+        n = next(number)
+        return links.copy(n, source, target, offsets), links.copy(n, lands, lands, offsets)
+
+    keys = [
+        plan(joined.at[(y + d) % 4, back], pair(0), pair(-d), dy=d) for d in order
+    ]
+    rest = [
+        plan(joined.at[(y + d) % 4, front], asked.at[y], asked.at[(y - d) % 4], dy=d)
+        for d in order
+    ]
+    mine = joined.at[y, back]
+    far = [plan(mine, pair(0), pair(0, 1), dz=1)]
+    near = [plan(mine, pair(0), pair(0, 0, 1), dc=1)]
+    for d in order:
+        far.append(plan(pair(-d), pair(-d), pair(-d, 1), dz=1))
+        near.append(plan(pair(-d), pair(-d), pair(-d, 0, 1), dc=1))
+    diagonal = [plan(pair(-d, 1), pair(-d, 1), pair(-d, 1, 1), dc=1) for d in (0,) + order]
+
+    def relay(i):
+        keys[i][1].wait_recv()
+        far[i + 1][0].start()
+        near[i + 1][0].start()
+
+    def cross(i):
+        far[i][1].wait_recv()
+        diagonal[i][0].start()
+
+    @pl.when(step == 0)
+    def _():
+        links.greet(TOK_ALL)
+        for copy in kept:
+            copy.start()
+        for copy, unused in [keys[0], far[0], keys[1], near[0], keys[2]] + rest:
+            copy.start()
+
+    def pause(point):
+        @pl.when(step == 0)
+        def _():
+            if point == 0:
+                relay(0)
+                relay(1)
+            else:
+                relay(2)
+
+        @pl.when(step == 1)
+        def _():
+            if point == 0:
+                cross(0)
+            else:
+                cross(1)
+
+    for i in range(2, 4):
+
+        @pl.when(step == i + 1)
+        def _():
+            cross(i)
+
+    rows = x_ref.shape[1]
+
+    @pl.when(step < 2)
+    def _():
+        grads, hidden = ff_part(
+            main, down, first, x_ref[...], g_ref[...], w_ref, h_ref, s_ref, pause
+        )
+        here = pl.ds(pl.multiple_of(step * rows, rows), rows)
+        held[:, here, :] = grads.reshape(2, rows, -1)
+        held_hidden[:, here, :] = hidden.reshape(2, rows, -1)
+
+    @pl.when(step >= 2)
+    def _():
+        grads = held[...].reshape(-1, held.shape[2])
+        hidden = held_hidden[...].reshape(-1, down)
+        grad_ref[:, :down] = dot(g_strip[...], hidden, TN).astype(BF)
+        grad_ref[:, down:] = dot(x_strip[...], grads, TN).astype(BF)
+
+    @pl.when(step == pl.num_programs(0) - 1)
+    def _():
+        for copy in kept:
+            copy.wait()
+        for unused, landed in rest + near + diagonal:
+            landed.wait_recv()
+        for copy, unused in keys + rest + far + near + diagonal:
+            copy.wait_send()
+
+
+def ff_heads(x, g, w, joined, main, down, first):
+    depth, cols = w.shape
+    heads, unused, span, lanes = joined.shape
+    rows = BLK // 2
+    both = cols - first
+    strip = 512
+
+    def tile(width):
+        return pl.BlockSpec((2, rows, width), lambda i: (0, jnp.minimum(i, 1), 0))
+
+    return pl.pallas_call(
+        functools.partial(ff_heads_kernel, main, down, first),
+        grid=(2 + depth // strip,),
+        in_specs=[
+            tile(depth),
+            tile(depth),
+            pl.BlockSpec((2 * BLK, strip), lambda i: (0, jnp.maximum(i - 2, 0))),
+            pl.BlockSpec((2 * BLK, strip), lambda i: (0, jnp.maximum(i - 2, 0))),
+            pl.BlockSpec((depth, cols), lambda i: (0, 0), pipeline_mode=pl.Buffered(1)),
+            ANY,
+        ],
+        out_specs=(
+            tile(down),
+            tile(depth),
+            pl.BlockSpec((strip, both + down), lambda i: (jnp.maximum(i - 2, 0), 0)),
+            ANY,
+            ANY,
         ),
-    )
+        out_shape=(
+            jax.ShapeDtypeStruct((2, BLK, down), BF),
+            jax.ShapeDtypeStruct((2, BLK, depth), BF),
+            jax.ShapeDtypeStruct((depth, both + down), BF),
+            jax.ShapeDtypeStruct((4, 2, span, lanes), BF),
+            jax.ShapeDtypeStruct((4, 2, 2, 2, span, lanes), BF),
+        ),
+        scratch_shapes=[
+            pltpu.VMEM((2, BLK, both), BF),
+            pltpu.VMEM((2, BLK, down), BF),
+            pltpu.SemaphoreType.DMA((32,)),
+            pltpu.SemaphoreType.DMA((32,)),
+            pltpu.SemaphoreType.DMA((2,)),
+        ],
+        compiler_params=pltpu.CompilerParams(
+            collective_id=1, has_side_effects=True, vmem_limit_bytes=60 * 2**20
+        ),
+        cost_estimate=SMALL,
+        name="ff_heads",
+    )(x, g, x.reshape(2 * BLK, depth), g.reshape(2 * BLK, depth), w, joined)
 
 
 def home_kernel(grads, dq, branches, tokens, dq_home, grads_home, result, *rest):
@@ -710,30 +942,116 @@
     )
 
 
-def last_kernel(grads, weights, shifted, mine_out, *rest):
-    own, side, out, cross, mine, near, edge, wout, wcross = rest[:9]
-    links = Links(*rest[9:])
-    links.greet(BR_ALL + TOK_ALL)
+def turn_back(grads, tokens, cot, gain, parts, result):
+    rows, depth = tokens.shape
+    chunk = 16
+
+    def normal(here):
+        value = tokens[here, :].astype(F32)
+        value = value - jnp.mean(value, axis=-1, keepdims=True)
+        scale = lax.rsqrt(jnp.mean(value * value, axis=-1, keepdims=True) + EPSILON)
+        return value * scale, scale
+
+    def rows_at(i):
+        return pl.ds(pl.multiple_of(i * chunk, chunk), chunk)
+
+    def sums(i, carry):
+        here = rows_at(i)
+        grad = grads[here, :]
+        up = grad * normal(here)[0]
+        return carry[0] + up.reshape(2, 8, depth).sum(0), carry[1] + grad.reshape(
+            2, 8, depth
+        ).sum(0)
+
+    zero = jnp.zeros((8, depth), F32)
+    found = lax.fori_loop(0, rows // chunk, sums, (zero, zero))
+    for k in range(2):
+        line = jnp.sum(found[k], axis=0, keepdims=True)
+        parts[16 * k : 16 * (k + 1), :] = jnp.concatenate(
+            [line[:, t * 128 : (t + 1) * 128] for t in range(depth // 128)], axis=0
+        )
+    yield
+
+    def back(i, unused):
+        here = rows_at(i)
+        normed, scale = normal(here)
+        grad = grads[here, :] * gain[...]
+        grad = grad - jnp.mean(grad, axis=-1, keepdims=True)
+        grad = grad - normed * jnp.mean(grad * normed, axis=-1, keepdims=True)
+        result[here, :] = cot[here, :].astype(F32) + scale * grad
+        return unused
+
+    lax.fori_loop(0, rows // chunk, back, 0)
+
+
+BR_PEERS = [dict(dl=i // 4, dx=i % 4) for i in range(1, 8)]
+TOK_PEERS = [dict(dy=i // 4, dz=(i // 2) % 2, dc=i % 2) for i in range(1, 16)]
+
+
+def last_kernel(
+    heads, grads, weights, tokens, cot, gain, result, qkv_out, out_out, bias_out, sides, *rest
+):
+    own, side, out, cross, mine, near, edge, wout, wcross, summed, wsum = rest[:11]
+    parts, parts_in, lines, lines_in = rest[11:15]
+    links = Links(*rest[15:])
+    links.greet(BR_PEERS + TOK_PEERS)
+    y, z, c, l, x = coords()
     in_turn(
         [
-            reduce_tok(links, weights, mine, near, edge, wout, wcross, mine_out),
-            reduce_br(links, grads, own, side, out, cross, shifted, plain),
+            reduce_tok(links, weights, mine, near, edge, wout, wcross, wsum),
+            reduce_br(links, grads, own, side, out, cross, summed, plain),
         ]
     )
+    through = turn_back(summed, tokens, cot, gain, parts, result)
+    next(through)
+    tickets = [links.send(parts, parts_in.at[i], **o) for i, o in enumerate(BR_PEERS)]
+    for unused in through:
+        pass
+    total = parts[...]
+    for i, ticket in enumerate(tickets):
+        links.arrived(ticket, parts_in.at[i])
+        total = total + parts_in[i]
+    lines[...] = jnp.zeros_like(lines)
+    for t in range(16):
+        lines[t, 0:2, :] = jnp.concatenate([total[t : t + 1], total[16 + t : 17 + t]], axis=0)
+    tickets = []
+    for i, o in enumerate(TOK_PEERS):
+        there = ((y + o["dy"]) % 4) * 4 + ((z + o["dz"]) % 2) * 2 + (c + o["dc"]) % 2
+        tickets.append(links.send(lines.at[there], lines_in.at[i], **o))
+    width = heads * HD
+    qkv_out[0] = wsum[:, :width]
+    for k in range(2):
+        qkv_out[1 + k] = jnp.concatenate(
+            [
+                wsum[:, width + (2 * h + k) * HD : width + (2 * h + k + 1) * HD]
+                for h in range(heads)
+            ],
+            axis=1,
+        )
+    out_out[...] = jnp.transpose(wsum[:, 3 * width : 4 * width])
+    bias_out[...] = wsum[:8, 4 * width :]
+    total = lines[y * 4 + z * 2 + c]
+    for i, ticket in enumerate(tickets):
+        links.arrived(ticket, lines_in.at[i])
+        total = total + lines_in[i]
+    sides[...] = total
     links.close()
 
 
-def last_sums(grads, weights):
+def last_sums(grads, weights, tokens, cot, gain, heads):
     rows, depth = grads.shape[2:]
     wrows, cols = weights.shape[3:]
     return comm_call(
-        last_kernel,
+        functools.partial(last_kernel, heads),
         "last_sums",
         3,
-        (grads, weights),
+        (grads, weights, tokens, cot, gain),
         (
             jax.ShapeDtypeStruct((rows, depth), F32),
-            jax.ShapeDtypeStruct((wrows, cols), F32),
+            jax.ShapeDtypeStruct((3, wrows, heads * HD), F32),
+            jax.ShapeDtypeStruct((heads * HD, wrows), F32),
+            jax.ShapeDtypeStruct((8, 128), F32),
+            jax.ShapeDtypeStruct((8, 128), F32),
         ),
         scratch=[
             pltpu.VMEM((2, rows, depth), BF),
@@ -745,45 +1063,17 @@
             pltpu.VMEM((3, 2, wrows, cols), BF),
             pltpu.VMEM((wrows, cols), BF),
             pltpu.VMEM((wrows, cols), BF),
+            pltpu.VMEM((rows, depth), F32),
+            pltpu.VMEM((wrows, cols), F32),
+            pltpu.VMEM((32, 128), F32),
+            pltpu.VMEM((7, 32, 128), F32),
+            pltpu.VMEM((16, 8, 128), F32),
+            pltpu.VMEM((15, 8, 128), F32),
         ],
-        out_vmem=(0, 1),
-    )
-
-
-def sides_kernel(parts, result, here, side, *sems):
-    y, z, c, l, x = coords()
-    links = Links(*sems)
-    near = [dict(dl=i // 4, dx=i % 4) for i in range(1, 8)]
-    wide = [dict(dy=i // 4, dz=(i // 2) % 2, dc=i % 2) for i in range(1, 16)]
-    links.greet(near + wide)
-    tickets = []
-    for i, o in enumerate(near):
-        there = ((l + o["dl"]) % 2) * 4 + (x + o["dx"]) % 4
-        tickets.append(links.send(parts.at[there], here.at[i], **o))
-    total = parts[l * 4 + x]
-    for i, ticket in enumerate(tickets):
-        links.arrived(ticket, here.at[i])
-        total = total + here[i]
-    here[7] = total
-    tickets = [links.send(here.at[7], side.at[i], **o) for i, o in enumerate(wide)]
-    for i, ticket in enumerate(tickets):
-        links.arrived(ticket, side.at[i])
-        total = total + side[i]
-    result[...] = total
-    links.close()
-
-
-def sum_sides(parts):
-    return comm_call(
-        sides_kernel,
-        "sum_sides",
-        4,
-        (parts,),
-        (jax.ShapeDtypeStruct(parts.shape[1:], F32),),
-        scratch=[pltpu.VMEM(parts.shape, F32), pltpu.VMEM((15,) + parts.shape[1:], F32)],
-        in_vmem=(0,),
-        out_vmem=(0,),
-    )[0]
+        in_vmem=(2, 3, 4),
+        out_vmem=(0, 1, 2, 3, 4),
+        copies=64,
+    )
 
 
 def tok_perm(dy):
@@ -799,23 +1089,14 @@
     return lax.dynamic_slice_in_dim(stacked, (4 - y) % 4, 4, 0)
 
 
-def rotary_tables(positions, long_shape):
+def rotary_table():
     half = ROT // 2
-    frequency = ROPE_BASE ** (-(jnp.arange(half).astype(F32) * 2.0 / ROT))
-    angles = positions.astype(F32)[:, None] * frequency[None, :]
-    cos, sin = jnp.cos(angles), jnp.sin(angles)
-    rows = positions.shape[0]
-    one = jnp.ones((rows, HD - ROT), F32)
-    zero = jnp.zeros((rows, HD - ROT), F32)
-    cos64 = jnp.concatenate([cos, cos, one], axis=1)
-    sin64 = jnp.concatenate([-sin, sin, zero], axis=1)
-    tables = (
-        jnp.concatenate([cos64, cos64], axis=1),
-        jnp.concatenate([sin64, sin64], axis=1),
-        jnp.concatenate([cos64, jnp.ones((rows, HD), F32)], axis=1),
-        jnp.concatenate([sin64, jnp.zeros((rows, HD), F32)], axis=1),
-    )
-    return tuple(t.reshape(2, BLK, 2 * HD) for t in tables)
+    frequency = (ROPE_BASE ** (-(np.arange(half) * 2.0 / ROT))).astype(np.float32)
+    angles = np.arange(LB * BLK, dtype=np.float32)[:, None] * frequency[None, :]
+    cos, sin = np.cos(angles), np.sin(angles)
+    one = np.ones((LB * BLK, HD - ROT), np.float32)
+    table = np.concatenate([cos, cos, one, -sin, sin, 0.0 * one], axis=1)
+    return table.astype(np.float32).reshape(LB, BLK, 2 * HD)
 
 
 def body(
@@ -854,36 +1135,36 @@
     kv_shard = jnp.stack(
         [w.reshape(wrows, heads, HD) for w in (qkv_weight[1], qkv_weight[2])], axis=2
     ).reshape(wrows, 2 * width)
-    bias_row = jnp.pad(qkv_bias.reshape(1, -1), ((0, wrows - 1), (0, 128 - qkv_bias.size)))
+    per = qkv_bias.shape[2]
+    lane_tok = jnp.arange(HD, dtype=jnp.int32) // per
+    bias_lanes = jnp.where(lane_tok == tok, jnp.tile(qkv_bias, (1, 1, HD // per)), 0)
+    bias_rows = jnp.concatenate(
+        [
+            bias_lanes[0].reshape(-1),
+            jnp.stack([bias_lanes[1], bias_lanes[2]], axis=1).reshape(-1),
+        ]
+    ).reshape(-1, 128)
+    bias_row = jnp.pad(bias_rows, ((0, wrows - bias_rows.shape[0]), (0, 0)))
     qkv_shard = jnp.concatenate([qkv_weight[0], kv_shard, bias_row], axis=1)
     ff_shard = jnp.concatenate(
         [
+            jnp.transpose(down_weight),
+            jnp.zeros((wrows, 128 - tail), BF),
+            jnp.transpose(out_weight),
             gate_weight[:, :main],
             up_weight[:, :main],
             gate_weight[:, main:],
             up_weight[:, main:],
-            jnp.transpose(down_weight),
-            jnp.zeros((wrows, 128 - tail), BF),
-            jnp.transpose(out_weight),
         ],
         axis=1,
     )
-    both_width = 2 * hidden_width
     down_width = main + 128
-    ff_full = lax.all_gather(ff_shard, "tok", axis=0, tiled=True)
-    gu_full = ff_full[:, :both_width]
-    down_full = ff_full[:, both_width : both_width + down_width]
-    out_full = ff_full[:, both_width + down_width :]
-    x, qkv_full = start(shifted, qkv_shard)
-    x = x.reshape(2 * BLK, depth)
+    first = down_width + width
+    x, grad, qkv_full, ff_full = start(shifted, cotangent, qkv_shard, ff_shard)
+    x = x.reshape(2, BLK, depth)
+    grad = grad.reshape(2, BLK, depth)
     qkv_full = qkv_full.reshape(16 * wrows, -1)
-
-    bias = qkv_full.reshape(16, wrows, -1)[:, 0, 3 * width : 3 * width + qkv_bias.size]
-    bias = jnp.transpose(bias.reshape(16, 3, heads, 4), (1, 2, 0, 3)).reshape(3, heads, HD)
-    bias = jnp.concatenate(
-        [bias[0].reshape(1, width), jnp.stack([bias[1], bias[2]], axis=1).reshape(1, 2 * width)],
-        axis=1,
-    ).astype(F32)
+    ff_full = ff_full.reshape(16 * wrows, -1)
 
     slot_table = jnp.arange(total_blocks, dtype=jnp.int32)
     slot_of = jnp.sum(
@@ -906,118 +1187,74 @@
     ).astype(jnp.int32)
 
     my_blocks = lax.dynamic_slice_in_dim(block_map, tok * 2, 2)
-    my_start = (
-        jnp.where(my_blocks < long_blocks, my_blocks % LB, (my_blocks - long_blocks) % 2) * BLK
-    )
-    positions = (my_start[:, None] + jnp.arange(BLK, dtype=jnp.int32)[None, :]).reshape(-1)
-    tables = rotary_tables(positions, long_blocks)
-
-    q_heads, kv_heads = project(x, qkv_full, bias, tables, heads)
-    joined = jnp.concatenate([q_heads, kv_heads.reshape(heads, 2 * BLK, 2 * HD)], axis=1)
-    q_all, kv_all, grad = heads_out(joined, cotangent)
+    places = jnp.where(my_blocks < long_blocks, my_blocks % LB, (my_blocks - long_blocks) % 2)
+    table = jnp.asarray(rotary_table())
+
+    joined = project(places, x, grad, qkv_full, ff_full, table, heads)
+    hidden, grad_x, grad_ff, qd_all, kv_all = ff_heads(
+        x, grad, ff_full, joined, main, down_width, first
+    )
+    kv_all = kv_all.reshape(-1, 2 * HD)
+    x = x.reshape(2 * BLK, depth)
     grad = grad.reshape(2 * BLK, depth)
-    kv_all = kv_all.reshape(-1, 2 * HD)
-
-    turned, lse, o_parts = attn_fwd(query_block, query_limit, key_slot, q_all, kv_all, long_blocks)
-
-    def to_heads(flat):
-        split = flat.reshape(2, BLK, heads, HD)
-        return jnp.transpose(split, (2, 1, 0, 3)).reshape(heads, BLK, 2 * HD)
-
-    def from_heads(packed):
-        split = packed.reshape(heads, BLK, 2, HD)
-        return jnp.transpose(split, (2, 1, 0, 3)).reshape(2 * BLK, width)
-
-    mixed = from_heads(swap_heads(o_parts, y))
-
-    grad_mixed = dot(grad, out_full, NN).astype(BF)
-    do_all = swap_heads(to_heads(grad_mixed), y)
-
-    both = dot(x, gu_full, NN)
-    grad_hidden = dot(grad, down_full, NN)
-    ends = both[:, 2 * main :]
-    gate = jnp.concatenate([both[:, :main], ends[:, :tail]], axis=1)
-    up = jnp.concatenate([both[:, main : 2 * main], ends[:, tail:]], axis=1)
-    gh = grad_hidden[:, :hidden_width]
-    sig = jax.nn.sigmoid(gate)
-    hidden = (gate * sig * up).astype(BF)
-    hidden = jnp.pad(hidden, ((0, 0), (0, down_width - hidden_width)))
-    grad_gate = (gh * up * sig * (1.0 + gate * (1.0 - sig))).astype(BF)
-    grad_up = (gh * gate * sig).astype(BF)
-    grad_both = jnp.concatenate(
-        [grad_gate[:, :main], grad_up[:, :main], grad_gate[:, main:], grad_up[:, main:]], axis=1
-    )
-    branches = (dot(hidden, down_full, NT) + dot(mixed, out_full, NT)).astype(BF)
-    grad_ff = jnp.concatenate(
-        [
-            dot(x, grad_both, TN).astype(BF),
-            dot(grad, hidden, TN).astype(BF),
-            dot(grad, mixed, TN).astype(BF),
-        ],
-        axis=1,
-    )
     grad_ff = lax.psum_scatter(grad_ff, "tok", scatter_dimension=0, tiled=True)
 
+    turned, lse, o_parts = attn_fwd(query_block, query_limit, key_slot, qd_all, kv_all, long_blocks)
+    o_heads = swap_heads(o_parts, y)
     dq_parts, dkv_all = attn_bwd(
-        query_block, query_limit, key_slot, q_all, do_all, kv_all, turned, lse, long_blocks
-    )
+        query_block, query_limit, key_slot, qd_all, kv_all, turned, lse, long_blocks
+    )
+    o_heads, dq_parts = lax.optimization_barrier((o_heads, dq_parts))
+    mixed, branches = add_branches(hidden, o_heads, ff_full, heads)
     dq_heads, dkv_heads, result = heads_home(
         dkv_all.reshape(4, 2, 2, 2 * BLK, 2 * HD),
         dq_parts,
         branches.reshape(2, 4, rows, depth),
         tokens,
     )
-    dkv_heads = dkv_heads.reshape(heads, 2, BLK, 2 * HD)
-    grad_joined, bias_sums = unturn(dq_heads, dkv_heads, tables, heads)
-    grad_shifted = (
-        dot(grad_both, gu_full, NT) + dot(grad_joined, qkv_full[:, : 3 * width], NT)
-    ).astype(BF)
-    grad_qkv = dot(x, grad_joined, TN).astype(BF)
-    qsum = bias_sums[0, :width].reshape(1, heads, HD)
-    kvsum = jnp.transpose(bias_sums[0, width:].reshape(heads, 2, HD), (1, 0, 2))
-    bsum = jnp.concatenate([qsum, kvsum], axis=0).reshape(3, heads, 16, 4)
-    bsum = jnp.transpose(bsum, (2, 0, 1, 3)).reshape(16, 1, qkv_bias.size).astype(BF)
-    bsum = jnp.pad(bsum, ((0, 0), (0, wrows - 1), (0, 128 - qkv_bias.size)))
-    grad_qkv = jnp.concatenate([grad_qkv, bsum.reshape(16 * wrows, 128)], axis=1)
-    my_grad_shifted, grad_qkv = last_sums(
-        grad_shifted.reshape(2, 4, rows, depth), grad_qkv.reshape(4, 2, 2, wrows, -1)
-    )
-
-    grad_bias_out = grad_qkv[0, 3 * width : 3 * width + qkv_bias.size].reshape(qkv_bias.shape)
-    gkv = grad_qkv[:, width : 3 * width].reshape(wrows, heads, 2, HD)
-    grad_qkv_out = jnp.stack(
+    grad_ff, dq_heads = lax.optimization_barrier((grad_ff, dq_heads))
+    grad_qkv, grad_shifted = join(
+        places,
+        dq_heads,
+        dkv_heads.reshape(heads, 2, BLK, 2 * HD),
+        table,
+        x,
+        grad,
+        mixed.reshape(2 * BLK, width),
+        qkv_full,
+        grad_x.reshape(2 * BLK, depth),
+        heads,
+    )
+    grad_tokens, grad_qkv, grad_out_out, bias_sums, sides = last_sums(
+        grad_shifted.reshape(2, 4, rows, depth),
+        grad_qkv.reshape(4, 2, 2, wrows, -1),
+        tokens,
+        cotangent,
+        norm_gain.reshape(1, depth),
+        heads,
+    )
+    bias_sums = bias_sums[: 3 * width // 128].reshape(-1)
+    bias_sums = jnp.concatenate(
         [
-            grad_qkv[:, :width],
-            gkv[:, :, 0].reshape(wrows, width),
-            gkv[:, :, 1].reshape(wrows, width),
+            bias_sums[:width].reshape(1, heads, HD),
+            jnp.transpose(bias_sums[width:].reshape(heads, 2, HD), (1, 0, 2)),
         ]
     )
+    grad_bias_out = lax.dynamic_slice_in_dim(bias_sums, tok * per, per, 2)
     grad_ff = grad_ff.astype(F32)
-    ends = grad_ff[:, 2 * main : both_width]
-    grad_gate_out = jnp.concatenate([grad_ff[:, :main], ends[:, :tail]], axis=1)
-    grad_up_out = jnp.concatenate([grad_ff[:, main : 2 * main], ends[:, tail:]], axis=1)
-    grad_down_out = jnp.transpose(grad_ff[:, both_width : both_width + hidden_width])
-    grad_out_out = jnp.transpose(grad_ff[:, both_width + down_width :])
-
-    gain_part = jnp.sum(my_grad_shifted * normed, axis=0)
-    bias_part = jnp.sum(my_grad_shifted, axis=0)
-    grad_normed = my_grad_shifted * norm_gain
-    grad_tokens = cotangent.astype(F32) + inverse * (
-        grad_normed
-        - jnp.mean(grad_normed, axis=-1, keepdims=True)
-        - normed * jnp.mean(grad_normed * normed, axis=-1, keepdims=True)
-    )
-    sides = jnp.stack([gain_part, bias_part]).reshape(2, 16, 8, 16)
-    sides = jnp.transpose(sides, (2, 0, 1, 3)).reshape(8, 2, 256)
-    sides = sum_sides(jnp.pad(sides, ((0, 0), (0, 6), (0, 0))))
-    sides = lax.dynamic_slice_in_dim(sides[:2].reshape(2, 16, 16), tok, 1, 1)[:, 0]
-    grad_gain, grad_bias = sides[0], sides[1]
+    grad_down_out = jnp.transpose(grad_ff[:, :hidden_width])
+    grad_gu = grad_ff[:, down_width:]
+    ends = grad_gu[:, 2 * main :]
+    grad_gate_out = jnp.concatenate([grad_gu[:, :main], ends[:, :tail]], axis=1)
+    grad_up_out = jnp.concatenate([grad_gu[:, main : 2 * main], ends[:, tail:]], axis=1)
+
+    sides = lax.dynamic_slice_in_dim(sides[:2], lax.axis_index("br") * 16, 16, 1)
     return (
         result,
         grad_tokens,
-        grad_gain,
-        grad_bias,
-        grad_qkv_out,
+        sides[0],
+        sides[1],
+        grad_qkv,
         grad_bias_out,
         grad_out_out,
         grad_gate_out,

time: 503 us -> 425 us (0.84)
  matrix products: 71.3 us -> 0 us
  Pallas kernels: 309 us -> 372 us
  local copies, waits for them, and re-layouts: 61.9 us -> 23.3 us
  other arithmetic: 27.1 us -> 7.49 us
  waiting for transfers between devices: 6.15 us -> 0.05 us
    pallas_call x2 -> x4, Pallas kernels: 7.74 us -> 88.9 us  [the longest x1 52.5 us: ff_heads(): pl.pallas_call(functools.partial(ff_heads_kernel, main, down, first), gri...]
    dot_general x11 -> x0, matrix products: 71.3 us -> none  [dot(): return lax.dot_general(left, right, dims, preferred_element_type=F32)]
    pallas_call x5 -> x3, Pallas kernels: 253 us -> 216 us  [comm_call(): pl.pallas_call(kernel, out_shape=tuple(outs), in_specs=[VMEM if i in in_v...]
    unnamed x106 -> x39, local copies, waits for them, and re-layouts: 34.5 us -> 11.8 us
    concatenate x7 -> x3, other arithmetic: 20.7 us -> 0.72 us  [the longest x1 0.67 us: body(): jnp.concatenate([bias_sums[:width].reshape(1, heads, HD), jnp.transpose(b...]
    pallas_call x1, Pallas kernels: 19.9 us -> 29.6 us  [attn_fwd(): pl.pallas_call(functools.partial(attn_fwd_kernel, long_blocks), out_shape...]
    concatenate x12 -> x1, local copies, waits for them, and re-layouts: 10.2 us -> 0.98 us  [body(): jnp.concatenate([jnp.transpose(down_weight), jnp.zeros((wrows, 128 - tail...]
    pallas_call x1, Pallas kernels: 28.3 us -> 36.9 us  [attn_bwd(): pl.pallas_call(functools.partial(attn_bwd_kernel, long_blocks), out_shape...]
  transfers between devices with their start and end apart: 8 -> 4, of which waited for: 3 -> 0; matrix products, arithmetic and copies ran while one was open for 13% -> 1% of each run, Pallas kernels for 62% -> 31%
where the time goes in v4:
time: 425 us; the launch traced here: 420 us
  Pallas kernels  372 us (88%)
  local copies, waits for them, and re-layouts  23.3 us (5%)
  between operations  14.4 us (3%)
  other arithmetic  7.49 us (2%)
    pallas_call x3, Pallas kernels, comm_call(): pl.pallas_call(kernel, out_shape=tuple(outs), in_specs=[VMEM if i in in_v...  216 us
    pallas_call x1, Pallas kernels, ff_heads(): pl.pallas_call(functools.partial(ff_heads_kernel, main, down, first), gri...  52.5 us
    pallas_call x1, Pallas kernels, attn_bwd(): pl.pallas_call(functools.partial(attn_bwd_kernel, long_blocks), out_shape...  36.9 us
    pallas_call x1, Pallas kernels, attn_fwd(): pl.pallas_call(functools.partial(attn_fwd_kernel, long_blocks), out_shape...  29.6 us
    pallas_call x1, Pallas kernels, join(): pl.pallas_call(functools.partial(join_kernel, heads), grid_spec=pltpu.Pre...  16.8 us
    unnamed x39, local copies, waits for them, and re-layouts  11.8 us
    pallas_call x1, Pallas kernels, project(): pl.pallas_call(functools.partial(project_kernel, heads), grid_spec=pltpu....  10.8 us
    pallas_call x1, Pallas kernels, add_branches(): pl.pallas_call(functools.partial(branches_kernel, heads), grid=(2,), in_s...  8.84 us
  transfers between devices with their start and end apart: 4, of which 0 were waited for; matrix products, arithmetic and copies ran while one was open for 1% of the time, Pallas kernels for 31%

profile of v4, /device:TPU:1, one launch (start us, length us, event | category | flops | bytes accessed | tf_op | source)
XLA Modules:
  0.0 420.3 jit_solution(11216080941033108191)
XLA Ops:
  7.3 0.8 slice.80
  8.1 0.9 slice.78
  9.0 0.7 slice.81
  9.7 0.9 slice.79
  10.7 1.2 convert_reduce_fusion
  11.9 1.3 fusion.2
  13.2 0.1 copy.69
  13.3 0.1 copy.70
  13.4 0.7 tile.4
  14.5 0.9 copy.56
  15.4 0.2 copy.67
  15.6 0.2 copy.68
  15.8 1.1 copy.55
  16.8 0.9 slice_bitcast_fusion.1
  17.9 0.1 copy.66
  18.2 0.6 compare_select_fusion.4.places
  18.8 0.7 fusion.7.w_ref
  19.5 1.2 fusion.5.s_ref
  20.7 1.0 concatenate.20.f_ref
  21.7 85.7 %start.1 = (bf16[2,4,128,2048]{3,2,1,0:T(8,128)(2,1)}, bf16[2,4,128,2048]{3,2,1,0:T(8,128)(2,1)}, bf16[4,2,2,128,896]{4,3,2,1,0:T(8,128)(2,1)}, bf16[4,2,2,128,2432]{4,3,2,1,0:T(8,128)(2,1)}) custom-call(bf16[128,2048]{1,0:T(8,128)(2,1)} %fusion.5.s_ref, bf16[128,2048]{1,0:T(8,128)(2,1)} %cot.1, bf16[128,896]{1,0:T(8,128)(2,1)} %fusion.7.w_ref, ...), custom_call_target="tpu_custom_call" | custom-call | flops 1000 | bytes 1000 | tf_op jit(solution)/shard_map/start/pallas_call | solution.py:678
  107.3 10.8 %project.1.joined = bf16[4,4,512,128]{3,2,1,0:T(8,128)(2,1)} custom-call(s32[2]{0:T(128)} %compare_select_fusion.4.places, bf16[2,512,2048]{2,1,0:T(8,128)(2,1)} %bitcast.57, bf16[2,512,2048]{2,1,0:T(8,128)(2,1)} %bitcast.61, bf16[2048,896]{1,0:T(8,128)(2,1)} %bitcast.65, bf16[2048,896]{1,0:T(8,128)(2,1)} %bitcast.66, bf16[2048,2432]{1,0:T(8,128)(2,1)} %bitcast.54, ...), custom_call_target="tpu_custom_call" | custom-call | flops 1000 | bytes 1000 | tf_op jit(solution)/shard_map/project/pallas_call | solution.py:221
  118.1 52.5 %ff_heads.1 = (bf16[2,512,768]{2,1,0:T(8,128)(2,1)}, bf16[2,512,2048]{2,1,0:T(8,128)(2,1)}, bf16[2048,2176]{1,0:T(8,128)(2,1)}, bf16[4,2,512,128]{3,2,1,0:T(8,128)(2,1)}, bf16[4,2,2,2,512,128]{5,4,3,2,1,0:T(8,128)(2,1)}) custom-call(bf16[2,512,2048]{2,1,0:T(8,128)(2,1)} %bitcast.58, bf16[2,512,2048]{2,1,0:T(8,128)(2,1)} %bitcast.62, ...), custom_call_target="tpu_custom_call" | custom-call | flops 1000 | bytes 1000 | tf_op jit(solution)/shard_map/ff_heads/pallas_call | solution.py:860
  170.9 0.6 select_reduce_fusion.kslot
  171.5 0.2 select_reduce_fusion.2.qblk
  171.7 0.7 select_reduce_fusion.1.qlim
  172.4 29.6 %attn_fwd.1 = (f32[4,128,512]{2,1,0:T(8,128)}, f32[8,1,512]{2,1,0:T(1,128)}, bf16[4,512,128]{2,1,0:T(8,128)(2,1)}) custom-call(s32[8]{0:T(128)} %copy-done.6, s32[8]{0:T(128)} %select_reduce_fusion.1.qlim, s32[32]{0:T(128)} %select_reduce_fusion.kslot, bf16[4,2,512,128]{3,2,1,0:T(8,128)(2,1)} %get-tuple-element.44.q_ref, bf16[16384,128]{1,0:T(8,128)(2,1)} %bitcast.68), custom_call_target="tpu_custom_call" | custom-call | flops 1000 | bytes 1000 | tf_op jit(solution)/shard_map/attn_fwd/pallas_call | solution.py:92
  202.0 1.1 dynamic-slice_bitcast_fusion
  203.1 2.2 collective-permute-start
  205.3 1.3 collective-permute-start.1
  206.6 36.9 %attn_bwd.1 = (bf16[4,512,128]{2,1,0:T(8,128)(2,1)}, bf16[16384,128]{1,0:T(8,128)(2,1)}) custom-call(s32[8]{0:T(128)} %copy-done.6, s32[8]{0:T(128)} %select_reduce_fusion.1.qlim, s32[32]{0:T(128)} %select_reduce_fusion.kslot, bf16[4,2,512,128]{3,2,1,0:T(8,128)(2,1)} %get-tuple-element.44.q_ref, bf16[16384,128]{1,0:T(8,128)(2,1)} %bitcast.69, ...), custom_call_target="tpu_custom_call" | custom-call | flops 1000 | bytes 1000 | tf_op jit(solution)/shard_map/attn_bwd/pallas_call | solution.py:159
  243.6 0.9 dynamic-slice_dynamic-update-slice_fusion.1
  244.6 0.8 constant_dynamic-slice_fusion.1.o_ref
  245.4 8.8 %add_branches.1 = (bf16[2,512,256]{2,1,0:T(8,128)(2,1)}, bf16[2,512,2048]{2,1,0:T(8,128)(2,1)}) custom-call(bf16[2,512,768]{2,1,0:T(8,128)(2,1)} %get-tuple-element.52.h_ref, bf16[4,512,128]{2,1,0:T(8,128)(2,1)} %constant_dynamic-slice_fusion.1.o_ref, bf16[2048,2432]{1,0:T(8,128)(2,1)} %bitcast.56), custom_call_target="tpu_custom_call" | custom-call | flops 1000 | bytes 1000 | tf_op jit(solution)/shard_map/add_branches/pallas_call | solution.py:377
  254.3 54.6 %heads_home.1 = (bf16[4,512,128]{2,1,0:T(8,128)(2,1)}, bf16[4,1024,128]{2,1,0:T(8,128)(2,1)}, bf16[128,2048]{1,0:T(8,128)(2,1)}) custom-call(bf16[4,2,2,1024,128]{4,3,2,1,0:T(8,128)(2,1)} %bitcast.72, bf16[4,512,128]{2,1,0:T(8,128)(2,1)} %get-tuple-element.51.dq, bf16[2,4,128,2048]{3,2,1,0:T(8,128)(2,1)} %bitcast.74, bf16[128,2048]{1,0:T(8,128)(2,1)} %tokens.3), custom_call_target="tpu_custom_call" | custom-call | flops 1000 | bytes 1000 | tf_op jit(solution)/shard_map/heads_home/pallas_call | solution.py:678
  308.9 16.8 %join.1 = (bf16[2048,1152]{1,0:T(8,128)(2,1)}, bf16[1024,2048]{1,0:T(8,128)(2,1)}) custom-call(s32[2]{0:T(128)} %compare_select_fusion.4.places, bf16[4,512,128]{2,1,0:T(8,128)(2,1)} %get-tuple-element.58.dq_ref, bf16[4,2,512,128]{3,2,1,0:T(8,128)(2,1)} %bitcast.75, f32[8,512,128]{2,1,0:T(8,128)} %constant.157.clone.t0_ref.t1_ref, ...), custom_call_target="tpu_custom_call" | custom-call | flops 1000 | bytes 1000 | tf_op jit(solution)/shard_map/join/pallas_call | solution.py:300
  325.8 75.8 %last_sums.1 = (f32[128,2048]{1,0:T(8,128)}, f32[3,128,256]{2,1,0:T(8,128)}, f32[256,128]{1,0:T(8,128)}, f32[8,128]{1,0:T(8,128)}, f32[8,128]{1,0:T(8,128)}) custom-call(bf16[2,4,128,2048]{3,2,1,0:T(8,128)(2,1)} %bitcast.73, bf16[4,2,2,128,1152]{4,3,2,1,0:T(8,128)(2,1)} %bitcast.70, bf16[128,2048]{1,0:T(8,128)(2,1)} %tokens.3, bf16[128,2048]{1,0:T(8,128)(2,1)} %cot.1, ...), custom_call_target="tpu_custom_call" | custom-call | flops 1000 | bytes 1000 | tf_op jit(solution)/shard_map/last_sums/pallas_call | solution.py:678
  401.6 0.7 slice.85
  402.3 0.7 slice.86
  403.2 0.7 slice.82
  404.0 0.5 slice_bitcast_fusion.4
  404.7 0.9 copy.63
  405.7 0.9 copy.62
  406.6 0.9 copy.64
  407.5 0.7 dynamic-slice_maximum_fusion
  408.2 1.9 copy.84
  410.1 1.0 copy.85
  411.0 1.8 copy.86
  412.8 0.7 copy.87
  (61 shorter events, 1.6 us)
Async XLA Ops:
  7.2 12.3 %copy-start = (bf16[128,2048]{1,0:T(8,128)(2,1)S(1)}, bf16[128,2048]{1,0:T(8,128)(2,1)}, u32[]{:S(2)}) copy-start(bf16[128,2048]{1,0:T(8,128)(2,1)} %tokens.3) | copy-start | bytes 1572868
  7.2 11.0 %copy-start.7 = (s32[32]{0:T(128)S(1)}, s32[32]{0:T(128)}, u32[]{:S(2)}) copy-start(s32[32]{0:T(128)} %param.23) | copy-start | bytes 388
  7.2 12.3 %copy-start.4 = (f32[2048]{0:T(1024)S(1)}, f32[2048]{0:T(1024)}, u32[]{:S(2)}) copy-start(f32[2048]{0:T(1024)} %param.14) | copy-start | bytes 24580
  7.2 12.3 %copy-start.5 = (f32[2048]{0:T(1024)S(1)}, f32[2048]{0:T(1024)}, u32[]{:S(2)}) copy-start(f32[2048]{0:T(1024)} %param.15) | copy-start | bytes 24580
  7.2 301.7 %reduce-scatter.2.cloned.1.call-start = ((), (), s32[]{:S(2)}) async-start(), calls=%async_computation.1 | async-start | bytes 9469952 | tf_op jit(solution)/shard_map/reduce_scatter | solution.py:1200
  170.6 1.1 copy-start.8
  171.7 0.7 copy-start.6
  203.1 40.4 %collective-permute-start = (bf16[512,128]{1,0:T(8,128)(2,1)S(1)}, bf16[512,128]{1,0:T(8,128)(2,1)S(1)}, u32[]{:S(2)}, u32[]{:S(2)}) collective-permute-start(bf16[512,128]{1,0:T(8,128)(2,1)S(1)} %get-tuple-element.107), channel_id=1, source_target_pairs={{0,96},{8,104},{16,112},{24,120},{32,0},{40,8},{48,16},{56,24},{64... | collective-permute-start | bytes 393224 | tf_op jit(solution)/shard_map/ppermute | solution.py:1087
  205.3 38.2 %collective-permute-start.2 = (bf16[512,128]{1,0:T(8,128)(2,1)S(1)}, bf16[512,128]{1,0:T(8,128)(2,1)S(1)}, u32[]{:S(2)}, u32[]{:S(2)}) collective-permute-start(bf16[512,128]{1,0:T(8,128)(2,1)S(1)} %get-tuple-element.104), channel_id=1, source_target_pairs={{0,32},{8,40},{16,48},{24,56},{32,64},{40,72},{48,80},{56,88},{64,... | collective-permute-start | bytes 393224 | tf_op jit(solution)/shard_map/ppermute | solution.py:1087
  205.3 38.2 %collective-permute-start.1 = (bf16[512,128]{1,0:T(8,128)(2,1)S(1)}, bf16[512,128]{1,0:T(8,128)(2,1)S(1)}, u32[]{:S(2)}, u32[]{:S(2)}) collective-permute-start(bf16[512,128]{1,0:T(8,128)(2,1)S(1)} %get-tuple-element.106), channel_id=1, source_target_pairs={{0,64},{8,72},{16,80},{24,88},{32,96},{40,104},{48,112},{56,120},{... | collective-permute-start | bytes 393224 | tf_op jit(solution)/shard_map/ppermute | solution.py:1087
  325.8 77.2 %copy-start.1 = (bf16[128,2176]{1,0:T(8,128)(2,1)S(1)}, bf16[128,2176]{1,0:T(8,128)(2,1)}, u32[]{:S(2)}) copy-start(bf16[128,2176]{1,0:T(8,128)(2,1)} %reduce-scatter.2.cloned.1.call-done) | copy-start | bytes 1671172
  403.1 7.0 %copy-start.2 = (f32[128,2048]{1,0:T(8,128)S(1)}, f32[128,2048]{1,0:T(8,128)}, u32[]{:S(2)}) copy-start(f32[128,2048]{1,0:T(8,128)} %get-tuple-element.129) | copy-start | bytes 3145732
  404.7 8.1 %copy-start.3 = (f32[256,128]{1,0:T(8,128)S(1)}, f32[256,128]{1,0:T(8,128)}, u32[]{:S(2)}) copy-start(f32[256,128]{1,0:T(8,128)} %get-tuple-element.134) | copy-start | bytes 393220
Sparse Core Ops, SparseCore 0:
  170.8 110.9 reduce-scatter.1

commit v5 on v4

--- a/solution.py
+++ b/solution.py
@@ -241,91 +241,6 @@
     )(places, x, g, w, w, ff, table, table)
 
 
-def join_kernel(
-    heads,
-    places,
-    dq_ref,
-    dkv_ref,
-    t0_ref,
-    t1_ref,
-    x_ref,
-    g_ref,
-    m_ref,
-    w_ref,
-    s_ref,
-    out_ref,
-    gs_ref,
-    gj,
-    sums,
-):
-    width = heads * HD
-
-    @pl.when(pl.program_id(0) == 0)
-    def _():
-        total = jnp.zeros((1, 3 * width), F32)
-        for slot, table in enumerate((t0_ref, t1_ref)):
-            for half in range(2):
-                rows = slice(half * BLK // 2, (half + 1) * BLK // 2)
-                lanes = slice(slot * HD, (slot + 1) * HD)
-                q = jnp.concatenate([dq_ref[h, rows, lanes] for h in range(heads)], axis=1)
-                q = turn(q.astype(F32), table[rows, :], heads // 2, False, -1.0).astype(BF)
-                kv = jnp.concatenate([dkv_ref[h, slot, rows] for h in range(heads)], axis=1)
-                kv = turn(kv.astype(F32), table[rows, :], heads, True, -1.0).astype(BF)
-                here = slice(slot * BLK + rows.start, slot * BLK + rows.stop)
-                gj[here, :width] = q
-                gj[here, width:] = kv
-                total += jnp.sum(
-                    jnp.concatenate([q, kv], axis=1).astype(F32), axis=0, keepdims=True
-                )
-        corner = [total[:, r * 128 : (r + 1) * 128] for r in range(3 * width // 128)]
-        corner = jnp.concatenate(corner + [jnp.zeros((2, 128), F32)], axis=0)
-        sums[...] = corner
-
-    both = gj[...]
-    tile, cols = out_ref.shape
-    out_ref[:, : 3 * width] = dot(x_ref[...], both, TN).astype(BF)
-    out_ref[:, 3 * width : 4 * width] = dot(g_ref[...], m_ref[...], TN).astype(BF)
-    zero = jnp.zeros((120, 128), F32)
-    block = jnp.concatenate([sums[...], zero] * (tile // 128), axis=0)
-    out_ref[:, 4 * width :] = block.astype(BF)
-    gs_ref[...] = (s_ref[...].astype(F32) + dot(both, w_ref[...], NT)).astype(BF)
-
-
-def join(places, dq, dkv, table, x, g, mixed, w, partial_grad, heads):
-    tile = 512
-    width = 3 * heads * HD
-    rows, depth = x.shape
-    cols = width + heads * HD + 128
-    strip = pl.BlockSpec((rows, tile), lambda i, places: (0, i))
-    return pl.pallas_call(
-        functools.partial(join_kernel, heads),
-        grid_spec=pltpu.PrefetchScalarGridSpec(
-            num_scalar_prefetch=1,
-            grid=(depth // tile,),
-            in_specs=[
-                pl.BlockSpec(dq.shape, lambda i, places: (0, 0, 0)),
-                pl.BlockSpec(dkv.shape, lambda i, places: (0, 0, 0, 0)),
-                pl.BlockSpec((None, BLK, 2 * HD), lambda i, places: (places[0], 0, 0)),
-                pl.BlockSpec((None, BLK, 2 * HD), lambda i, places: (places[1], 0, 0)),
-                strip,
-                strip,
-                pl.BlockSpec(mixed.shape, lambda i, places: (0, 0)),
-                pl.BlockSpec((tile, width), lambda i, places: (i, 0)),
-                strip,
-            ],
-            out_specs=(pl.BlockSpec((tile, cols), lambda i, places: (i, 0)), strip),
-            scratch_shapes=[pltpu.VMEM((rows, width), BF), pltpu.VMEM((8, 128), F32)],
-        ),
-        out_shape=(
-            jax.ShapeDtypeStruct((depth, cols), BF),
-            jax.ShapeDtypeStruct((rows, depth), BF),
-        ),
-        compiler_params=pltpu.CompilerParams(vmem_limit_bytes=60 * 2**20),
-        cost_estimate=SMALL,
-        name="join",
-    )(places, dq, dkv, table, table, x, g, mixed, w, partial_grad)
-
-
 def ff_part(main, down, first, x, g, w_ref, h_ref, s_ref, pause):
     rows, depth = x.shape[1:]
     x = x.reshape(2 * rows, depth)
@@ -349,48 +264,6 @@
     pause(1)
     s_ref[...] = dot(grads, w_ref[:, first:], NT).astype(BF).reshape(s_ref.shape)
     return grads, hidden
-
-
-def branches_kernel(heads, h_ref, o_ref, w_ref, mixed_ref, out_ref):
-    rows = h_ref.shape[1]
-    mixed = [
-        jnp.concatenate(
-            [o_ref[head][:, slot * HD : (slot + 1) * HD] for head in range(heads)], axis=1
-        )
-        for slot in range(2)
-    ]
-    hidden = h_ref[...].reshape(2 * rows, -1)
-    mixed = jnp.concatenate(mixed, axis=0)
-    held = jnp.concatenate([hidden, mixed], axis=1)
-    mixed_ref[...] = mixed.reshape(mixed_ref.shape)
-    out_ref[...] = dot(held, w_ref[...], NT).astype(BF).reshape(out_ref.shape)
-
-
-def add_branches(hidden, o, w, heads):
-    depth = w.shape[0]
-    rows = BLK // 2
-    kept = hidden.shape[2] + heads * HD
-
-    def tile(lanes, lead=2):
-        return pl.BlockSpec((lead, rows, lanes), lambda i: (0, i, 0))
-
-    return pl.pallas_call(
-        functools.partial(branches_kernel, heads),
-        grid=(2,),
-        in_specs=[
-            tile(hidden.shape[2]),
-            tile(2 * HD, heads),
-            pl.BlockSpec((depth, kept), lambda i: (0, 0)),
-        ],
-        out_specs=(tile(heads * HD), tile(depth)),
-        out_shape=(
-            jax.ShapeDtypeStruct((2, BLK, heads * HD), BF),
-            jax.ShapeDtypeStruct((2, BLK, depth), BF),
-        ),
-        compiler_params=pltpu.CompilerParams(vmem_limit_bytes=60 * 2**20),
-        cost_estimate=SMALL,
-        name="add_branches",
-    )(hidden, o, w)
 
 
 def coords():
@@ -607,65 +480,102 @@
         links.arrived(home[d], grads_home.at[(y - d) % 4])
 
 
-def reduce_br(links, parts, own, near, out, far, target, finish):
+class ScatterSpace:
+    names = ("pieces", "near", "out", "far", "across", "sums", "side")
+
+    def __init__(self, refs):
+        for name, ref in zip(self.names, refs):
+            setattr(self, name, ref)
+
+    @staticmethod
+    def shapes(rows, depth):
+        half = depth // 2
+        sizes = (
+            (2, 4, rows, depth),
+            (3, 2, rows, half),
+            (rows, half),
+            (rows, half),
+            (4, rows, half),
+            (4, rows, half),
+            (3, rows, half),
+        )
+        return [pltpu.VMEM(size, BF) for size in sizes]
+
+
+def scatter_br(links, make, space, target, finish):
     unused_y, unused_z, unused_c, l, x = coords()
-    order = (1, 3, 2)
-    tickets = {}
-    held = {}
-    for dl in (1, 0):
-        there = (l + dl) % 2
-        held[dl] = links.local(parts.at[there, x], own.at[there])
-        for i, d in enumerate(order):
-            tickets[dl, i] = links.send(
-                parts.at[there, (x + d) % 4], near.at[i, there], dx=d
-            )
+    rows, half = space.out.shape
+    first, second = pl.ds(0, half), pl.ds(half, half)
+    order = (1, 3, 2, 0)
+    direct, folded, onward = {}, {}, {}
+    for i, d in enumerate(order):
+        there = (x + d) % 4
+        make(there)
+        if d:
+            for dl in (1, 0):
+                to = (l + dl) % 2
+                direct[dl, i] = links.send(
+                    space.pieces.at[to, there, :, first], space.near.at[i, to], dx=d
+                )
+        folded[d] = links.send(
+            space.pieces.at[1 - l, there, :, second], space.across.at[there], dl=1
+        )
+        yield
+    for i in range(3):
+        links.arrived(direct[1, i], space.near.at[i, 1 - l])
+        yield
+    mine = space.pieces.at[1 - l, x, :, first]
+    add_up(space.out, [mine] + [space.near.at[i, 1 - l] for i in range(3)], rows, plain)
+    over = links.send(space.out, space.far, dl=1)
+    for i, d in enumerate(order):
+        there = (x + d) % 4
+        links.arrived(folded[d], space.across.at[there])
+        own = space.pieces.at[l, there, :, second]
+        add_up(space.sums.at[there], [own, space.across.at[there]], rows, plain)
+        if d:
+            onward[i] = links.send(space.sums.at[there], space.side.at[i], dx=d)
+        yield
+    for i in range(3):
+        links.arrived(direct[0, i], space.near.at[i, l])
     yield
-    rows = out.shape[0]
-    for i in range(3):
-        links.arrived(tickets[1, i], near.at[i, 1 - l])
-        yield
-    links.settle(held[1])
-    add_up(out, [own.at[1 - l]] + [near.at[i, 1 - l] for i in range(3)], rows, plain)
-    across = links.send(out, far, dl=1)
+    links.arrived(over, space.far)
+    sources = [space.pieces.at[l, x, :, first]] + [space.near.at[i, l] for i in range(3)]
+    add_up(target.at[:, first], sources + [space.far], rows, finish(0))
     yield
     for i in range(3):
-        links.arrived(tickets[0, i], near.at[i, l])
+        links.arrived(onward[i], space.side.at[i])
+    sources = [space.sums.at[x]] + [space.side.at[i] for i in range(3)]
+    add_up(target.at[:, second], sources, rows, finish(half))
+
+
+def reduce_tok(links, make, parts, near, side, out, far, target):
+    y, z, c, unused_l, unused_x = coords()
+    order = (1, 3, 2, 0)
+    tickets = {}
+    for d in order:
+        here = (y + d) % 4
+        make(here)
+        tickets[d] = links.send(parts.at[here, :, 1 - c], near.at[here], dc=1)
         yield
-    links.settle(held[0])
-    links.arrived(across, far)
-    add_up(
-        target, [own.at[l]] + [near.at[i, l] for i in range(3)] + [far], rows, finish
-    )
-
-
-def reduce_tok(links, parts, mine, near, side, out, far, target):
-    y, z, c, unused_l, unused_x = coords()
-    order = (1, 3, 2)
-    tickets, held = {}, {}
-    for d in order + (0,):
-        here = (y + d) % 4
-        tickets[d] = links.send(parts.at[here, :, 1 - c], near.at[here], dc=1)
-        held[d] = links.local(parts.at[here, :, c], mine.at[here])
-    yield
     rows = out.shape[0]
     sent = {}
-    for i, d in enumerate(order + (0,)):
+    for i, d in enumerate(order):
         here = (y + d) % 4
         links.arrived(tickets[d], near.at[here])
-        links.settle(held[d])
         for k in range(2):
-            add_up(mine.at[here, k], [mine.at[here, k], near.at[here, k]], rows, plain)
+            own = parts.at[here, k, c]
+            add_up(own, [own, near.at[here, k]], rows, plain)
         if d:
-            sent[i] = links.send(mine.at[here], side.at[i], dy=d)
+            sent[i] = links.send(parts.at[here, :, c], side.at[i], dy=d)
         yield
     for i in range(3):
         links.arrived(sent[i], side.at[i])
         yield
-    add_up(out, [mine.at[y, 1 - z]] + [side.at[i, 1 - z] for i in range(3)], rows, plain)
+    add_up(out, [parts.at[y, 1 - z, c]] + [side.at[i, 1 - z] for i in range(3)], rows, plain)
     across = links.send(out, far, dz=1)
     yield
     links.arrived(across, far)
-    add_up(target, [mine.at[y, z]] + [side.at[i, z] for i in range(3)] + [far], rows, plain)
+    add_up(target, [parts.at[y, z, c]] + [side.at[i, z] for i in range(3)] + [far], rows, plain)
 
 
 BR_NEAR = [dict(dl=1), dict(dx=1), dict(dx=-1)]
@@ -794,7 +704,7 @@
         links.greet(TOK_ALL)
         for copy in kept:
             copy.start()
-        for copy, unused in [keys[0], far[0], keys[1], near[0], keys[2]] + rest:
+        for copy, unused in [keys[0], keys[1], keys[2], far[0], near[0]]:
             copy.start()
 
     def pause(point):
@@ -805,6 +715,8 @@
                 relay(1)
             else:
                 relay(2)
+                for copy, unused in rest:
+                    copy.start()
 
         @pl.when(step == 1)
         def _():
@@ -897,34 +809,91 @@
     )(x, g, x.reshape(2 * BLK, depth), g.reshape(2 * BLK, depth), w, joined)
 
 
-def home_kernel(grads, dq, branches, tokens, dq_home, grads_home, result, *rest):
-    mine, near, far, total, own, side, out, cross = rest[:8]
-    links = Links(*rest[8:])
+def home_kernel(
+    heads,
+    grads,
+    dq,
+    o_parts,
+    hidden,
+    weights,
+    tokens,
+    dq_home,
+    grads_home,
+    mixed_out,
+    result,
+    *rest,
+):
+    mine, near, far, total, held_w, held_h, held_o = rest[:7]
+    space = ScatterSpace(rest[7:14])
+    links = Links(*rest[14:])
+    y, unused_z, unused_c, unused_l, unused_x = coords()
+    rows, depth = tokens.shape
+    kept = held_w.shape[1]
     links.greet(BR_ALL + TOK_ALL)
-
-    def finish(value, here):
-        return value + tokens[here, :].astype(F32)
+    loads = [
+        links.local(o_parts.at[y], held_o.at[y]),
+        links.local(hidden, held_h),
+        links.local(weights.at[:, pl.ds(0, kept)], held_w),
+    ]
+    returned = [
+        (d, links.send(o_parts.at[(y + d) % 4], held_o.at[y], dy=d)) for d in (1, 3, 2)
+    ]
+
+    def make(there):
+        here = pl.ds(pl.multiple_of(there * rows, rows), rows)
+        mixed = [
+            jnp.concatenate(
+                [held_o[head, here, slot * HD : (slot + 1) * HD] for head in range(heads)],
+                axis=1,
+            )
+            for slot in range(2)
+        ]
+        for slot in range(2):
+            mixed_out[slot, here, :] = mixed[slot]
+        both = jnp.concatenate(
+            [held_h[:, here, :].reshape(2 * rows, -1), jnp.concatenate(mixed, axis=0)], axis=1
+        )
+        branches = dot(both, held_w[...], NT).astype(BF)
+        for slot in range(2):
+            space.pieces[slot, there] = branches[slot * rows : (slot + 1) * rows]
+
+    def finish(column):
+        def add(value, here):
+            return value + tokens[here, column : column + value.shape[1]].astype(F32)
+
+        return add
+
+    def output():
+        yield
+        for d, ticket in returned:
+            links.arrived(ticket, held_o.at[(y - d) % 4])
+        for load in loads:
+            links.settle(load)
+        yield from scatter_br(links, make, space, result, finish)
 
     in_turn(
         [
             reduce_heads(links, grads, dq, dq_home, grads_home, mine, near, far, total),
-            reduce_br(links, branches, own, side, out, cross, result, finish),
+            output(),
         ]
     )
     links.close()
 
 
-def heads_home(grads, dq, branches, tokens):
+def heads_home(grads, dq, o_parts, hidden, weights, tokens, heads):
     rows, depth = tokens.shape
     span, lanes = grads.shape[3:]
+    width = heads * HD
+    kept = hidden.shape[2] + width
     return comm_call(
-        home_kernel,
+        functools.partial(home_kernel, heads),
         "heads_home",
         2,
-        (grads, dq, branches, tokens),
+        (grads, dq, o_parts, hidden, weights, tokens),
         (
             jax.ShapeDtypeStruct(dq.shape, BF),
             jax.ShapeDtypeStruct((4, span, lanes), BF),
+            jax.ShapeDtypeStruct((2, BLK, width), BF),
             jax.ShapeDtypeStruct((rows, depth), BF),
         ),
         scratch=[
@@ -932,25 +901,36 @@
             pltpu.VMEM((4, 2, span, lanes), BF),
             pltpu.VMEM((4, span, lanes), BF),
             pltpu.VMEM((4, span, lanes), BF),
-            pltpu.VMEM((2, rows, depth), BF),
-            pltpu.VMEM((3, 2, rows, depth), BF),
-            pltpu.VMEM((rows, depth), BF),
-            pltpu.VMEM((rows, depth), BF),
-        ],
-        in_vmem=(3,),
-        out_vmem=(2,),
-    )
-
-
-def turn_back(grads, tokens, cot, gain, parts, result):
-    rows, depth = tokens.shape
+            pltpu.VMEM((depth, kept), BF),
+            pltpu.VMEM(hidden.shape, BF),
+            pltpu.VMEM(o_parts.shape, BF),
+        ]
+        + ScatterSpace.shapes(rows, depth),
+        in_vmem=(5,),
+        out_vmem=(2, 3),
+        copies=64,
+    )
+
+
+def normal_rows(tokens, normed, scales):
+    rows = tokens.shape[0]
     chunk = 16
 
-    def normal(here):
+    def step(i, unused):
+        here = pl.ds(pl.multiple_of(i * chunk, chunk), chunk)
         value = tokens[here, :].astype(F32)
         value = value - jnp.mean(value, axis=-1, keepdims=True)
         scale = lax.rsqrt(jnp.mean(value * value, axis=-1, keepdims=True) + EPSILON)
-        return value * scale, scale
+        normed[here, :] = value * scale
+        scales[here, :] = jnp.broadcast_to(scale, (chunk, 128))
+        return unused
+
+    lax.fori_loop(0, rows // chunk, step, 0)
+
+
+def turn_back(grads, normed, scales, cot, gain, parts, result):
+    rows, depth = normed.shape
+    chunk = 16
 
     def rows_at(i):
         return pl.ds(pl.multiple_of(i * chunk, chunk), chunk)
@@ -958,10 +938,8 @@
     def sums(i, carry):
         here = rows_at(i)
         grad = grads[here, :]
-        up = grad * normal(here)[0]
-        return carry[0] + up.reshape(2, 8, depth).sum(0), carry[1] + grad.reshape(
-            2, 8, depth
-        ).sum(0)
+        up = (grad * normed[here, :]).reshape(2, 8, depth)
+        return carry[0] + up.sum(0), carry[1] + grad.reshape(2, 8, depth).sum(0)
 
     zero = jnp.zeros((8, depth), F32)
     found = lax.fori_loop(0, rows // chunk, sums, (zero, zero))
@@ -974,11 +952,11 @@
 
     def back(i, unused):
         here = rows_at(i)
-        normed, scale = normal(here)
+        line = normed[here, :]
         grad = grads[here, :] * gain[...]
-        grad = grad - jnp.mean(grad, axis=-1, keepdims=True)
-        grad = grad - normed * jnp.mean(grad * normed, axis=-1, keepdims=True)
-        result[here, :] = cot[here, :].astype(F32) + scale * grad
+        slope = jnp.mean(grad * line, axis=-1, keepdims=True)
+        grad = grad - jnp.mean(grad, axis=-1, keepdims=True) - line * slope
+        result[here, :] = cot[here, :].astype(F32) + scales[here, :1] * grad
         return unused
 
     lax.fori_loop(0, rows // chunk, back, 0)
@@ -989,36 +967,117 @@
 
 
 def last_kernel(
-    heads, grads, weights, tokens, cot, gain, result, qkv_out, out_out, bias_out, sides, *rest
+    heads,
+    dq,
+    dkv,
+    table,
+    x_in,
+    g_in,
+    m_in,
+    w_in,
+    s_in,
+    tokens,
+    cot,
+    gain,
+    result,
+    qkv_out,
+    out_out,
+    bias_out,
+    sides,
+    *rest,
 ):
-    own, side, out, cross, mine, near, edge, wout, wcross, summed, wsum = rest[:11]
-    parts, parts_in, lines, lines_in = rest[11:15]
-    links = Links(*rest[15:])
+    held_q, held_kv, held_t, held_x, held_g, held_m, held_w, held_s, gj = rest[:9]
+    parts, near, side, out, far, wsum, summed, normed, scales = rest[9:18]
+    lines, lines_in, last, last_in = rest[18:22]
+    space = ScatterSpace(rest[22:29])
+    links = Links(*rest[29:])
+    y, z, c, l, x = coords()
     links.greet(BR_PEERS + TOK_PEERS)
-    y, z, c, l, x = coords()
+    width = heads * HD
+    rows, depth = tokens.shape
+    first = [
+        links.local(dq, held_q),
+        links.local(dkv, held_kv),
+        links.local(table, held_t),
+    ]
+    second = [
+        links.local(x_in, held_x),
+        links.local(g_in, held_g),
+        links.local(m_in, held_m),
+    ]
+    third = [links.local(w_in.at[:, pl.ds(0, 3 * width)], held_w), links.local(s_in, held_s)]
+    for load in first:
+        links.settle(load)
+    total = jnp.zeros((1, 3 * width), F32)
+    for slot in range(2):
+        for half in range(2):
+            here = slice(half * BLK // 2, (half + 1) * BLK // 2)
+            lanes = slice(slot * HD, (slot + 1) * HD)
+            turns = held_t[slot, here, :]
+            q = jnp.concatenate([held_q[h, here, lanes] for h in range(heads)], axis=1)
+            q = turn(q.astype(F32), turns, heads // 2, False, -1.0).astype(BF)
+            kv = jnp.concatenate([held_kv[h, slot, here] for h in range(heads)], axis=1)
+            kv = turn(kv.astype(F32), turns, heads, True, -1.0).astype(BF)
+            both = jnp.concatenate([q, kv], axis=1)
+            gj[slot, here, :] = both
+            total += jnp.sum(both.astype(F32), axis=0, keepdims=True)
+    corner = [total[:, r * 128 : (r + 1) * 128] for r in range(3 * width // 128)]
+    corner = jnp.concatenate(corner + [jnp.zeros((122, 128), F32)], axis=0).astype(BF)
+    for load in second:
+        links.settle(load)
+    wrows = parts.shape[3]
+    strip = 4 * wrows
+
+    def weights_of(there):
+        here = pl.ds(pl.multiple_of(there * strip, strip), strip)
+        qkv = dot(held_x[:, here], gj[...].reshape(2 * BLK, 3 * width), TN).astype(BF)
+        outs = dot(held_g[:, here], held_m[...], TN).astype(BF)
+        for k in range(4):
+            at = slice(k * wrows, (k + 1) * wrows)
+            parts[there, k // 2, k % 2, :, : 3 * width] = qkv[at]
+            parts[there, k // 2, k % 2, :, 3 * width : 4 * width] = outs[at]
+            parts[there, k // 2, k % 2, :, 4 * width :] = corner
+
+    def rows_of(there):
+        if third:
+            for load in third:
+                links.settle(load)
+            third.clear()
+        here = pl.ds(pl.multiple_of(there * rows, rows), rows)
+        both = gj[:, here, :].reshape(2 * rows, 3 * width)
+        grads = dot(both, held_w[...], NT)
+        for slot in range(2):
+            value = grads[slot * rows : (slot + 1) * rows] + held_s[slot, here, :].astype(F32)
+            space.pieces[slot, there] = value.astype(BF)
+
+    def aside():
+        for unused in range(5):
+            yield
+        normal_rows(tokens, normed, scales)
+
     in_turn(
         [
-            reduce_tok(links, weights, mine, near, edge, wout, wcross, wsum),
-            reduce_br(links, grads, own, side, out, cross, summed, plain),
+            reduce_tok(links, weights_of, parts, near, side, out, far, wsum),
+            scatter_br(links, rows_of, space, summed, lambda column: plain),
+            aside(),
         ]
     )
-    through = turn_back(summed, tokens, cot, gain, parts, result)
+    through = turn_back(summed, normed, scales, cot, gain, lines, result)
     next(through)
-    tickets = [links.send(parts, parts_in.at[i], **o) for i, o in enumerate(BR_PEERS)]
+    tickets = [links.send(lines, lines_in.at[i], **o) for i, o in enumerate(BR_PEERS)]
     for unused in through:
         pass
-    total = parts[...]
+    total = lines[...]
     for i, ticket in enumerate(tickets):
-        links.arrived(ticket, parts_in.at[i])
-        total = total + parts_in[i]
-    lines[...] = jnp.zeros_like(lines)
+        links.arrived(ticket, lines_in.at[i])
+        total = total + lines_in[i]
+    last[...] = jnp.zeros_like(last)
     for t in range(16):
-        lines[t, 0:2, :] = jnp.concatenate([total[t : t + 1], total[16 + t : 17 + t]], axis=0)
+        last[t, 0:2, :] = jnp.concatenate([total[t : t + 1], total[16 + t : 17 + t]], axis=0)
     tickets = []
     for i, o in enumerate(TOK_PEERS):
         there = ((y + o["dy"]) % 4) * 4 + ((z + o["dz"]) % 2) * 2 + (c + o["dc"]) % 2
-        tickets.append(links.send(lines.at[there], lines_in.at[i], **o))
-    width = heads * HD
+        tickets.append(links.send(last.at[there], last_in.at[i], **o))
     qkv_out[0] = wsum[:, :width]
     for k in range(2):
         qkv_out[1 + k] = jnp.concatenate(
@@ -1030,63 +1089,60 @@
         )
     out_out[...] = jnp.transpose(wsum[:, 3 * width : 4 * width])
     bias_out[...] = wsum[:8, 4 * width :]
-    total = lines[y * 4 + z * 2 + c]
+    total = last[y * 4 + z * 2 + c]
     for i, ticket in enumerate(tickets):
-        links.arrived(ticket, lines_in.at[i])
-        total = total + lines_in[i]
+        links.arrived(ticket, last_in.at[i])
+        total = total + last_in[i]
     sides[...] = total
     links.close()
 
 
-def last_sums(grads, weights, tokens, cot, gain, heads):
-    rows, depth = grads.shape[2:]
-    wrows, cols = weights.shape[3:]
+def last_sums(dq, dkv, table, x, g, mixed, w, partial_grad, tokens, cot, gain, heads):
+    rows, depth = tokens.shape
+    wrows = depth // 16
+    width = heads * HD
+    cols = 4 * width + 128
     return comm_call(
         functools.partial(last_kernel, heads),
         "last_sums",
         3,
-        (grads, weights, tokens, cot, gain),
+        (dq, dkv, table, x, g, mixed, w, partial_grad, tokens, cot, gain),
         (
             jax.ShapeDtypeStruct((rows, depth), F32),
-            jax.ShapeDtypeStruct((3, wrows, heads * HD), F32),
-            jax.ShapeDtypeStruct((heads * HD, wrows), F32),
+            jax.ShapeDtypeStruct((3, wrows, width), F32),
+            jax.ShapeDtypeStruct((width, wrows), F32),
             jax.ShapeDtypeStruct((8, 128), F32),
             jax.ShapeDtypeStruct((8, 128), F32),
         ),
         scratch=[
-            pltpu.VMEM((2, rows, depth), BF),
-            pltpu.VMEM((3, 2, rows, depth), BF),
-            pltpu.VMEM((rows, depth), BF),
-            pltpu.VMEM((rows, depth), BF),
-            pltpu.VMEM((4, 2, wrows, cols), BF),
+            pltpu.VMEM(dq.shape, BF),
+            pltpu.VMEM(dkv.shape, BF),
+            pltpu.VMEM(table.shape, F32),
+            pltpu.VMEM(x.shape, BF),
+            pltpu.VMEM(g.shape, BF),
+            pltpu.VMEM(mixed.shape, BF),
+            pltpu.VMEM((depth, 3 * width), BF),
+            pltpu.VMEM(partial_grad.shape, BF),
+            pltpu.VMEM((2, BLK, 3 * width), BF),
+            pltpu.VMEM((4, 2, 2, wrows, cols), BF),
             pltpu.VMEM((4, 2, wrows, cols), BF),
             pltpu.VMEM((3, 2, wrows, cols), BF),
             pltpu.VMEM((wrows, cols), BF),
             pltpu.VMEM((wrows, cols), BF),
+            pltpu.VMEM((wrows, cols), F32),
             pltpu.VMEM((rows, depth), F32),
-            pltpu.VMEM((wrows, cols), F32),
+            pltpu.VMEM((rows, depth), F32),
+            pltpu.VMEM((rows, 128), F32),
             pltpu.VMEM((32, 128), F32),
             pltpu.VMEM((7, 32, 128), F32),
             pltpu.VMEM((16, 8, 128), F32),
             pltpu.VMEM((15, 8, 128), F32),
-        ],
-        in_vmem=(2, 3, 4),
+        ]
+        + ScatterSpace.shapes(rows, depth),
+        in_vmem=(8, 9, 10),
         out_vmem=(0, 1, 2, 3, 4),
-        copies=64,
-    )
-
-
-def tok_perm(dy):
-    return [(t, ((t // 4 + dy) % 4) * 4 + t % 4) for t in range(16)]
-
-
-def swap_heads(parts, y):
-    back = [lax.dynamic_index_in_dim(parts, y, 0, keepdims=False)]
-    for d in (3, 2, 1):
-        piece = lax.dynamic_index_in_dim(parts, (y + d) % 4, 0, keepdims=False)
-        back.append(lax.ppermute(piece, "tok", tok_perm(d)))
-    stacked = jnp.stack(back + back)
-    return lax.dynamic_slice_in_dim(stacked, (4 - y) % 4, 4, 0)
+        copies=80,
+    )
 
 
 def rotary_table():
@@ -1200,34 +1256,23 @@
     grad_ff = lax.psum_scatter(grad_ff, "tok", scatter_dimension=0, tiled=True)
 
     turned, lse, o_parts = attn_fwd(query_block, query_limit, key_slot, qd_all, kv_all, long_blocks)
-    o_heads = swap_heads(o_parts, y)
     dq_parts, dkv_all = attn_bwd(
         query_block, query_limit, key_slot, qd_all, kv_all, turned, lse, long_blocks
     )
-    o_heads, dq_parts = lax.optimization_barrier((o_heads, dq_parts))
-    mixed, branches = add_branches(hidden, o_heads, ff_full, heads)
-    dq_heads, dkv_heads, result = heads_home(
-        dkv_all.reshape(4, 2, 2, 2 * BLK, 2 * HD),
-        dq_parts,
-        branches.reshape(2, 4, rows, depth),
-        tokens,
+    dq_heads, dkv_heads, mixed, result = heads_home(
+        dkv_all.reshape(4, 2, 2, 2 * BLK, 2 * HD), dq_parts, o_parts, hidden, ff_full, tokens, heads
     )
     grad_ff, dq_heads = lax.optimization_barrier((grad_ff, dq_heads))
-    grad_qkv, grad_shifted = join(
-        places,
+    turns = jnp.stack([lax.dynamic_index_in_dim(table, places[i], 0, False) for i in range(2)])
+    grad_tokens, grad_qkv, grad_out_out, bias_sums, sides = last_sums(
         dq_heads,
         dkv_heads.reshape(heads, 2, BLK, 2 * HD),
-        table,
+        turns,
         x,
         grad,
         mixed.reshape(2 * BLK, width),
         qkv_full,
-        grad_x.reshape(2 * BLK, depth),
-        heads,
-    )
-    grad_tokens, grad_qkv, grad_out_out, bias_sums, sides = last_sums(
-        grad_shifted.reshape(2, 4, rows, depth),
-        grad_qkv.reshape(4, 2, 2, wrows, -1),
+        grad_x,
         tokens,
         cotangent,
         norm_gain.reshape(1, depth),

time: 425 us -> 411 us (0.967)
  Pallas kernels: 372 us -> 359 us
  between operations: 14.4 us -> 18.7 us
    pallas_call x3, Pallas kernels: 216 us -> 251 us  [comm_call(): pl.pallas_call(kernel, out_shape=tuple(outs), in_specs=[VMEM if i in in_v...]
    pallas_call x2 -> x0, Pallas kernels: 25.7 us -> none  [the longest x1 16.8 us: join(): pl.pallas_call(functools.partial(join_kernel, heads), grid_spec=pltpu.Pre...]
    pallas_call x1, Pallas kernels: 36.9 us -> 25.1 us  [attn_bwd(): pl.pallas_call(functools.partial(attn_bwd_kernel, long_blocks), out_shape...]
    pallas_call x1, Pallas kernels: 29.6 us -> 18.8 us  [attn_fwd(): pl.pallas_call(functools.partial(attn_fwd_kernel, long_blocks), out_shape...]
    unnamed x39 -> x35, local copies, waits for them, and re-layouts: 11.8 us -> 10.8 us
  transfers between devices with their start and end apart: 4 -> 1, of which waited for: 0 -> 0; matrix products, arithmetic and copies ran while one was open for 1% -> 1% of each run, Pallas kernels for 31% -> 34%
where the time goes in v5:
time: 411 us; the launch traced here: 408 us
  Pallas kernels  359 us (87%)
  local copies, waits for them, and re-layouts  22 us (5%)
  between operations  18.7 us (5%)
  other arithmetic  8.32 us (2%)
    pallas_call x3, Pallas kernels, comm_call(): pl.pallas_call(kernel, out_shape=tuple(outs), in_specs=[VMEM if i in in_v...  251 us
    pallas_call x1, Pallas kernels, ff_heads(): pl.pallas_call(functools.partial(ff_heads_kernel, main, down, first), gri...  52.6 us
    pallas_call x1, Pallas kernels, attn_bwd(): pl.pallas_call(functools.partial(attn_bwd_kernel, long_blocks), out_shape...  25.1 us
    pallas_call x1, Pallas kernels, attn_fwd(): pl.pallas_call(functools.partial(attn_fwd_kernel, long_blocks), out_shape...  18.8 us
    unnamed x35, local copies, waits for them, and re-layouts  10.8 us
    pallas_call x1, Pallas kernels, project(): pl.pallas_call(functools.partial(project_kernel, heads), grid_spec=pltpu....  10.7 us
  transfers between devices with their start and end apart: 1, of which 0 were waited for; matrix products, arithmetic and copies ran while one was open for 1% of the time, Pallas kernels for 34%

profile of v5, /device:TPU:1, one launch (start us, length us, event | category | flops | bytes accessed | tf_op | source)
XLA Modules:
  0.0 407.5 jit_solution(8247377276009712113)
XLA Ops:
  7.3 0.8 slice.86
  8.1 0.9 slice.84
  9.0 0.7 slice.87
  9.7 0.9 slice.85
  10.7 1.2 convert_reduce_fusion
  11.9 1.3 fusion.2
  13.2 0.1 copy.69
  13.3 0.1 copy.70
  13.4 0.7 tile.4
  14.1 0.1 tile.10
  14.4 0.1 reshape.143
  14.5 0.9 copy.56
  15.4 0.2 copy.67
  15.6 0.2 copy.68
  15.8 1.1 copy.55
  16.8 0.9 slice_bitcast_fusion.1
  17.7 0.1 copy.65
  17.9 0.1 copy.66
  18.0 0.1 copy.54
  18.2 0.6 compare_select_fusion.4.places
  18.8 0.7 fusion.7.w_ref
  19.5 1.2 fusion.5.s_ref
  20.7 1.0 concatenate.20.f_ref
  21.7 85.7 %start.1 = (bf16[2,4,128,2048]{3,2,1,0:T(8,128)(2,1)}, bf16[2,4,128,2048]{3,2,1,0:T(8,128)(2,1)}, bf16[4,2,2,128,896]{4,3,2,1,0:T(8,128)(2,1)}, bf16[4,2,2,128,2432]{4,3,2,1,0:T(8,128)(2,1)}) custom-call(bf16[128,2048]{1,0:T(8,128)(2,1)} %fusion.5.s_ref, bf16[128,2048]{1,0:T(8,128)(2,1)} %cot.1, bf16[128,896]{1,0:T(8,128)(2,1)} %fusion.7.w_ref, ...), custom_call_target="tpu_custom_call" | custom-call | flops 1000 | bytes 1000 | tf_op jit(solution)/shard_map/start/pallas_call | solution.py:588
  107.3 10.7 %project.1.joined = bf16[4,4,512,128]{3,2,1,0:T(8,128)(2,1)} custom-call(s32[2]{0:T(128)} %compare_select_fusion.4.places, bf16[2,512,2048]{2,1,0:T(8,128)(2,1)} %bitcast.40, bf16[2,512,2048]{2,1,0:T(8,128)(2,1)} %bitcast.44, bf16[2048,896]{1,0:T(8,128)(2,1)} %bitcast.48, bf16[2048,896]{1,0:T(8,128)(2,1)} %bitcast.49, bf16[2048,2432]{1,0:T(8,128)(2,1)} %bitcast.37, ...), custom_call_target="tpu_custom_call" | custom-call | flops 1000 | bytes 1000 | tf_op jit(solution)/shard_map/project/pallas_call | solution.py:221
  118.0 52.6 %ff_heads.1 = (bf16[2,512,768]{2,1,0:T(8,128)(2,1)}, bf16[2,512,2048]{2,1,0:T(8,128)(2,1)}, bf16[2048,2176]{1,0:T(8,128)(2,1)}, bf16[4,2,512,128]{3,2,1,0:T(8,128)(2,1)}, bf16[4,2,2,2,512,128]{5,4,3,2,1,0:T(8,128)(2,1)}) custom-call(bf16[2,512,2048]{2,1,0:T(8,128)(2,1)} %bitcast.41, bf16[2,512,2048]{2,1,0:T(8,128)(2,1)} %bitcast.45, ...), custom_call_target="tpu_custom_call" | custom-call | flops 1000 | bytes 1000 | tf_op jit(solution)/shard_map/ff_heads/pallas_call | solution.py:772
  170.9 0.6 select_reduce_fusion.kslot
  171.5 0.2 select_reduce_fusion.2.qblk
  171.7 0.7 select_reduce_fusion.1.qlim
  172.4 18.8 %attn_fwd.1 = (f32[4,128,512]{2,1,0:T(8,128)}, f32[8,1,512]{2,1,0:T(1,128)}, bf16[4,512,128]{2,1,0:T(8,128)(2,1)}) custom-call(s32[8]{0:T(128)} %copy-done.7, s32[8]{0:T(128)} %select_reduce_fusion.1.qlim, s32[32]{0:T(128)} %select_reduce_fusion.kslot, bf16[4,2,512,128]{3,2,1,0:T(8,128)(2,1)} %get-tuple-element.39.q_ref, bf16[16384,128]{1,0:T(8,128)(2,1)} %bitcast.51), custom_call_target="tpu_custom_call" | custom-call | flops 1000 | bytes 1000 | tf_op jit(solution)/shard_map/attn_fwd/pallas_call | solution.py:92
  191.2 25.1 %attn_bwd.1 = (bf16[4,512,128]{2,1,0:T(8,128)(2,1)}, bf16[16384,128]{1,0:T(8,128)(2,1)}) custom-call(s32[8]{0:T(128)} %copy-done.7, s32[8]{0:T(128)} %select_reduce_fusion.1.qlim, s32[32]{0:T(128)} %select_reduce_fusion.kslot, bf16[4,2,512,128]{3,2,1,0:T(8,128)(2,1)} %get-tuple-element.39.q_ref, bf16[16384,128]{1,0:T(8,128)(2,1)} %bitcast.52, ...), custom_call_target="tpu_custom_call" | custom-call | flops 1000 | bytes 1000 | tf_op jit(solution)/shard_map/attn_bwd/pallas_call | solution.py:159
  216.3 92.9 %heads_home.1 = (bf16[4,512,128]{2,1,0:T(8,128)(2,1)}, bf16[4,1024,128]{2,1,0:T(8,128)(2,1)}, bf16[2,512,256]{2,1,0:T(8,128)(2,1)}, bf16[128,2048]{1,0:T(8,128)(2,1)}) custom-call(bf16[4,2,2,1024,128]{4,3,2,1,0:T(8,128)(2,1)} %bitcast.53, bf16[4,512,128]{2,1,0:T(8,128)(2,1)} %get-tuple-element.44.dq, bf16[4,512,128]{2,1,0:T(8,128)(2,1)} %get-tuple-element.45.o_parts, ...), custom_call_target="tpu_custom_call" | custom-call | flops 1000 | bytes 1000 | tf_op jit(solution)/shard_map/heads_home/pallas_call | solution.py:588
  309.1 0.6 fusion.14
  313.6 1.1 constant_dynamic-slice_fusion.2
  314.7 0.8 pad_maximum_fusion.table
  315.5 72.9 %last_sums.1 = (f32[128,2048]{1,0:T(8,128)}, f32[3,128,256]{2,1,0:T(8,128)}, f32[256,128]{1,0:T(8,128)}, f32[8,128]{1,0:T(8,128)}, f32[8,128]{1,0:T(8,128)}) custom-call(bf16[4,512,128]{2,1,0:T(8,128)(2,1)} %get-tuple-element.50.dq, bf16[4,2,512,128]{3,2,1,0:T(8,128)(2,1)} %bitcast.54, f32[2,512,128]{2,1,0:T(8,128)} %pad_maximum_fusion.table, ...), custom_call_target="tpu_custom_call" | custom-call | flops 1000 | bytes 1000 | tf_op jit(solution)/shard_map/last_sums/pallas_call | solution.py:588
  388.4 0.7 slice.93
  389.1 0.7 slice.94
  390.0 0.7 slice.90
  390.8 0.5 slice_bitcast_fusion.4
  391.5 0.9 copy.63
  392.5 0.9 copy.62
  393.4 0.9 copy.64
  394.3 0.7 dynamic-slice_maximum_fusion
  395.0 1.9 copy.77
  396.9 1.0 copy.78
  397.8 1.8 copy.79
  399.6 0.7 copy.80
  (49 shorter events, 1.0 us)
Async XLA Ops:
  7.2 12.3 %copy-start = (bf16[128,2048]{1,0:T(8,128)(2,1)S(1)}, bf16[128,2048]{1,0:T(8,128)(2,1)}, u32[]{:S(2)}) copy-start(bf16[128,2048]{1,0:T(8,128)(2,1)} %tokens.3) | copy-start | bytes 1572868
  7.2 11.0 %copy-start.8 = (s32[32]{0:T(128)S(1)}, s32[32]{0:T(128)}, u32[]{:S(2)}) copy-start(s32[32]{0:T(128)} %param.23) | copy-start | bytes 388
  7.2 12.3 %copy-start.4 = (f32[2048]{0:T(1024)S(1)}, f32[2048]{0:T(1024)}, u32[]{:S(2)}) copy-start(f32[2048]{0:T(1024)} %param.14) | copy-start | bytes 24580
  7.2 12.3 %copy-start.5 = (f32[2048]{0:T(1024)S(1)}, f32[2048]{0:T(1024)}, u32[]{:S(2)}) copy-start(f32[2048]{0:T(1024)} %param.15) | copy-start | bytes 24580
  7.2 308.3 %reduce-scatter.2.cloned.1.call-start = ((), (), s32[]{:S(2)}) async-start(), calls=%async_computation.1 | async-start | bytes 9469952 | tf_op jit(solution)/shard_map/reduce_scatter | solution.py:1256
  170.6 1.1 copy-start.9
  171.7 0.7 copy-start.7
  216.3 92.9 %copy-start.6 = (s32[2]{0:T(128)S(1)}, s32[2]{0:T(128)}, u32[]{:S(2)}) copy-start(s32[2]{0:T(128)} %compare_select_fusion.4.places) | copy-start | bytes 28
  315.5 74.2 %copy-start.1 = (bf16[128,2176]{1,0:T(8,128)(2,1)S(1)}, bf16[128,2176]{1,0:T(8,128)(2,1)}, u32[]{:S(2)}) copy-start(bf16[128,2176]{1,0:T(8,128)(2,1)} %reduce-scatter.2.cloned.1.call-done) | copy-start | bytes 1671172
  389.9 7.0 %copy-start.2 = (f32[128,2048]{1,0:T(8,128)S(1)}, f32[128,2048]{1,0:T(8,128)}, u32[]{:S(2)}) copy-start(f32[128,2048]{1,0:T(8,128)} %get-tuple-element.119) | copy-start | bytes 3145732
  391.5 8.1 %copy-start.3 = (f32[256,128]{1,0:T(8,128)S(1)}, f32[256,128]{1,0:T(8,128)}, u32[]{:S(2)}) copy-start(f32[256,128]{1,0:T(8,128)} %get-tuple-element.124) | copy-start | bytes 393220
Sparse Core Ops, SparseCore 0:
  170.8 124.9 reduce-scatter.1

commit v6 on v5

--- a/solution.py
+++ b/solution.py
@@ -187,67 +187,15 @@
     return values * cos + partner * sin
 
 
-def project_kernel(
-    heads, places, x_ref, g_ref, w_ref, b_ref, wo_ref, t0_ref, t1_ref, out_ref
-):
-    width = heads * HD
-    rows = w_ref.shape[0] // 16
-    corner = b_ref[:8, :].astype(F32)
-    for t in range(1, 16):
-        corner = corner + b_ref[t * rows : t * rows + 8, :].astype(F32)
-    bias = jnp.concatenate([corner[r : r + 1] for r in range(3 * width // 128)], axis=1)
-    parts, grads = [], []
-    tile, depth = x_ref.shape[1:]
-    products = dot(x_ref[...].reshape(2 * tile, depth), w_ref[...], NN) + bias
-    mixed = dot(g_ref[...].reshape(2 * tile, depth), wo_ref[...], NN).astype(BF)
-    for slot, table in enumerate((t0_ref[...], t1_ref[...])):
-        joined = products[slot * tile : (slot + 1) * tile]
-        parts.append(turn(joined[:, :width], table, heads // 2, False, 1.0).astype(BF))
-        grads.append(mixed[slot * tile : (slot + 1) * tile])
-        kv = turn(joined[:, width:], table, heads, True, 1.0).astype(BF)
-        for head in range(heads):
-            out_ref[head, 2 + slot] = kv[:, head * 2 * HD : (head + 1) * 2 * HD]
-    for head in range(heads):
-        lanes = slice(head * HD, (head + 1) * HD)
-        for i, pair in enumerate((parts, grads)):
-            out_ref[head, i] = jnp.concatenate([pair[0][:, lanes], pair[1][:, lanes]], axis=1)
-
-
-def project(places, x, g, w, ff, table, heads):
-    tile = 256
-    width = 3 * heads * HD
-    depth = x.shape[2]
-    rows = pl.BlockSpec((2, tile, depth), lambda i, places: (0, i, 0))
-    return pl.pallas_call(
-        functools.partial(project_kernel, heads),
-        grid_spec=pltpu.PrefetchScalarGridSpec(
-            num_scalar_prefetch=1,
-            grid=(BLK // tile,),
-            in_specs=[
-                rows,
-                rows,
-                pl.BlockSpec((depth, width), lambda i, places: (0, 0)),
-                pl.BlockSpec((depth, 128), lambda i, places: (0, width // 128)),
-                pl.BlockSpec((depth, heads * HD), lambda i, places: (0, 3)),
-                pl.BlockSpec((None, tile, 2 * HD), lambda i, places: (places[0], i, 0)),
-                pl.BlockSpec((None, tile, 2 * HD), lambda i, places: (places[1], i, 0)),
-            ],
-            out_specs=pl.BlockSpec((heads, 4, tile, 2 * HD), lambda i, places: (0, 0, i, 0)),
-        ),
-        out_shape=jax.ShapeDtypeStruct((heads, 4, BLK, 2 * HD), BF),
-        compiler_params=pltpu.CompilerParams(vmem_limit_bytes=60 * 2**20),
-        cost_estimate=SMALL,
-        name="project",
-    )(places, x, g, w, w, ff, table, table)
-
-
-def ff_part(main, down, first, x, g, w_ref, h_ref, s_ref, pause):
+def ff_part(main, down, first, x, g, w_ref, h_ref, s_ref, mixed_grad, pause):
     rows, depth = x.shape[1:]
     x = x.reshape(2 * rows, depth)
     g = g.reshape(2 * rows, depth)
     gate_up = dot(x, w_ref[:, first:], NN)
     pause(0)
-    gh = dot(g, w_ref[:, :down], NN)
+    gh = dot(g, w_ref[:, :first], NN)
+    mixed_grad(gh[:, down:].astype(BF))
+    gh = gh[:, :down]
     ends = gate_up[:, 2 * main :]
     gate = jnp.concatenate([gate_up[:, :main], ends], axis=1)
     up = jnp.concatenate([gate_up[:, main : 2 * main], pltpu.roll(ends, HD, 1)], axis=1)
@@ -368,7 +316,7 @@
     def place(dl):
         return lambda dx, part: half_of(whole.at[(l + dl) % 2, (x + dx) % 4], part)
 
-    links.local(own, place(0)(0, None))
+    kept = links.local(own, place(0)(0, None))
     across = links.send(own, place(0)(0, None), dl=1)
     near = ring_four(links, own, place(0), "dx", lambda d: None)
     next(near)
@@ -380,6 +328,7 @@
         yield
     for unused in far:
         yield
+    links.settle(kept)
 
 
 def gather_tok(links, own, whole):
@@ -398,7 +347,7 @@
 
         return landed
 
-    links.local(own, place(0)(0, None))
+    kept = links.local(own, place(0)(0, None))
     across = links.send(own, place(0)(0, None), dz=1)
     near = ring_four(links, own, place(0), "dy", passer(0))
     next(near)
@@ -412,6 +361,7 @@
         yield
     for unused in far:
         yield
+    links.settle(kept)
     for ticket, ref in passed:
         links.arrived(ticket, ref)
 
@@ -488,8 +438,11 @@
             setattr(self, name, ref)
 
     @staticmethod
-    def shapes(rows, depth):
-        half = depth // 2
+    def shapes(rows, depth, half):
+        if half == depth:
+            sizes = ((2, 4, rows, depth), (3, 2, rows, depth), (rows, depth), (rows, depth))
+            return [pltpu.VMEM(size, BF) for size in sizes]
+        assert 2 * half == depth
         sizes = (
             (2, 4, rows, depth),
             (3, 2, rows, half),
@@ -505,6 +458,7 @@
 def scatter_br(links, make, space, target, finish):
     unused_y, unused_z, unused_c, l, x = coords()
     rows, half = space.out.shape
+    split = half < target.shape[1]
     first, second = pl.ds(0, half), pl.ds(half, half)
     order = (1, 3, 2, 0)
     direct, folded, onward = {}, {}, {}
@@ -517,9 +471,10 @@
                 direct[dl, i] = links.send(
                     space.pieces.at[to, there, :, first], space.near.at[i, to], dx=d
                 )
-        folded[d] = links.send(
-            space.pieces.at[1 - l, there, :, second], space.across.at[there], dl=1
-        )
+        if split:
+            folded[d] = links.send(
+                space.pieces.at[1 - l, there, :, second], space.across.at[there], dl=1
+            )
         yield
     for i in range(3):
         links.arrived(direct[1, i], space.near.at[i, 1 - l])
@@ -527,7 +482,7 @@
     mine = space.pieces.at[1 - l, x, :, first]
     add_up(space.out, [mine] + [space.near.at[i, 1 - l] for i in range(3)], rows, plain)
     over = links.send(space.out, space.far, dl=1)
-    for i, d in enumerate(order):
+    for i, d in enumerate(order if split else ()):
         there = (x + d) % 4
         links.arrived(folded[d], space.across.at[there])
         own = space.pieces.at[l, there, :, second]
@@ -541,6 +496,8 @@
     links.arrived(over, space.far)
     sources = [space.pieces.at[l, x, :, first]] + [space.near.at[i, l] for i in range(3)]
     add_up(target.at[:, first], sources + [space.far], rows, finish(0))
+    if not split:
+        return
     yield
     for i in range(3):
         links.arrived(onward[i], space.side.at[i])
@@ -584,11 +541,15 @@
 TOK_ALL = TOK_NEAR + [dict(dy=2)]
 
 
-def comm_call(kernel, name, number, args, outs, scratch=(), in_vmem=(), out_vmem=(), copies=48):
+def comm_call(
+    kernel, name, number, args, outs, scratch=(), in_vmem=(), out_vmem=(), in_smem=(), copies=48
+):
     return pl.pallas_call(
         kernel,
         out_shape=tuple(outs),
-        in_specs=[VMEM if i in in_vmem else ANY for i in range(len(args))],
+        in_specs=[
+            VMEM if i in in_vmem else SMEM if i in in_smem else ANY for i in range(len(args))
+        ],
         out_specs=tuple(VMEM if i in out_vmem else ANY for i in range(len(outs))),
         scratch_shapes=list(scratch)
         + [
@@ -604,37 +565,205 @@
     )(*args)
 
 
-def start_kernel(s_ref, c_ref, w_ref, f_ref, x_out, g_out, w_out, f_out, *sems):
-    links = Links(*sems)
-    links.greet(BR_NEAR + TOK_NEAR)
-    in_turn(
-        [
-            gather_br(links, s_ref, x_out),
-            gather_tok(links, w_ref, w_out),
-            gather_tok(links, f_ref, f_out),
-            gather_br(links, c_ref, g_out),
+def table_rows(table, block_map, slot, long_blocks):
+    block = block_map[lax.axis_index("tok") * 2 + slot]
+    place = jnp.where(block < long_blocks, block % LB, (block - long_blocks) % 2)
+    return table[place]
+
+
+def shift_rows(tokens, gain, bias, shifted):
+    rows = tokens.shape[0]
+    chunk = 16
+
+    def step(i, unused):
+        here = pl.ds(pl.multiple_of(i * chunk, chunk), chunk)
+        value = tokens[here, :].astype(F32)
+        value = value - jnp.mean(value, axis=-1, keepdims=True)
+        scale = lax.rsqrt(jnp.mean(value * value, axis=-1, keepdims=True) + EPSILON)
+        shifted[here, :] = (value * scale * gain[...] + bias[...]).astype(BF)
+        return unused
+
+    lax.fori_loop(0, rows // chunk, step, 0)
+
+
+def turned(block):
+    return jnp.transpose(block.astype(F32)).astype(BF)
+
+
+def bias_places(heads, per):
+    width = heads * HD
+    places = np.zeros((128, 3 * width), np.float32)
+    for column in range(3 * width):
+        if column < width:
+            part, head, lane = 0, column // HD, column % HD
+        else:
+            pair, lane = divmod(column - width, HD)
+            part, head = 1 + pair % 2, pair // 2
+        places[(part * heads + head) * per + lane % per, column] = 1.0
+    return places
+
+
+def start_kernel(
+    heads,
+    main,
+    block_map,
+    tokens,
+    gain,
+    bias,
+    cot,
+    qkv,
+    qkv_bias,
+    places,
+    gate,
+    up,
+    down,
+    out,
+    table,
+    x_out,
+    g_out,
+    w_out,
+    f_out,
+    kv_mine,
+    q_heads,
+    *rest,
+):
+    shifted, qkv_shard, ff_shard, held_x, held_w, pairs, queries, held_t = rest[:8]
+    links = Links(*rest[8:])
+    y, z, c, unused_l, unused_x = coords()
+    width = heads * HD
+    links.greet(BR_NEAR + TOK_ALL)
+    rotary = links.local(table, held_t)
+    shift_rows(tokens, gain, bias, shifted)
+    rows, depth = tokens.shape
+    kv = []
+    for head in range(heads):
+        lanes = slice(head * HD, (head + 1) * HD)
+        kv += [qkv[1, :, lanes], qkv[2, :, lanes]]
+    qkv_shard[:, : 3 * width] = jnp.concatenate([qkv[0]] + kv, axis=1)
+    line = dot(qkv_bias[...], places[...], NN)
+    lane = lax.broadcasted_iota(jnp.int32, line.shape, 1) % HD
+    line = jnp.where(lane // (HD // 16) == lax.axis_index("tok"), line, 0.0)[:1]
+    lines = [line[:, r * 128 : (r + 1) * 128] for r in range(3 * width // 128)]
+    zero = jnp.zeros((qkv_shard.shape[0] - len(lines), 128), F32)
+    qkv_shard[:, 3 * width :] = jnp.concatenate(lines + [zero], axis=0).astype(BF)
+
+    def project(half):
+        tile = 2 * rows
+        here = slice(half * tile, (half + 1) * tile)
+        span = held_x[:, 2 * half : 2 * half + 2].reshape(2 * tile, depth)
+        corner = held_w[0, 0, 0, :8, 3 * width :].astype(F32)
+        for t in range(1, 16):
+            corner = corner + held_w[t // 4, t // 2 % 2, t % 2, :8, 3 * width :].astype(F32)
+        added = jnp.concatenate([corner[r : r + 1] for r in range(len(lines))], axis=1)
+        products = dot(span, held_w[...].reshape(depth, -1)[:, : 3 * width], NN) + added
+        parts = []
+        for slot in range(2):
+            turns = table_rows(held_t, block_map, slot, 2 * LB)[here]
+            joined = products[slot * tile : (slot + 1) * tile]
+            parts.append(turn(joined[:, :width], turns, heads // 2, False, 1.0).astype(BF))
+            kv = turn(joined[:, width:], turns, heads, True, 1.0).astype(BF)
+            for head in range(heads):
+                pairs[head, slot, here, :] = kv[:, head * 2 * HD : (head + 1) * 2 * HD]
+        for head in range(heads):
+            lanes = slice(head * HD, (head + 1) * HD)
+            queries[head, here, :] = jnp.concatenate(
+                [parts[0][:, lanes], parts[1][:, lanes]], axis=1
+            )
+
+    def attention():
+        tasks = [gather_br(links, shifted, held_x), gather_tok(links, qkv_shard, held_w)]
+        while tasks:
+            for task in list(tasks):
+                try:
+                    next(task)
+                except StopIteration:
+                    tasks.remove(task)
+            yield
+        links.local(held_x, x_out)
+        links.local(held_w, w_out)
+        links.settle(rotary)
+        for half in range(2):
+            project(half)
+        sent = [
+            (d, links.send(pairs.at[(y + d) % 4], kv_mine.at[y], dy=d)) for d in (1, 3, 2)
         ]
-    )
+        links.local(pairs.at[y], kv_mine.at[y])
+        links.local(queries, q_heads)
+        for unused in range(12):
+            yield
+        for d, ticket in sent:
+            links.arrived(ticket, kv_mine.at[(y - d) % 4])
+
+    def feed_forward():
+        ff_shard[:, :main] = turned(down[:main, :])
+        tail = down.shape[0] - main
+        ends = jnp.concatenate([down[main:, :], jnp.zeros((128 - tail, rows), BF)], axis=0)
+        ff_shard[:, main : main + 128] = turned(ends)
+        at = main + 128
+        ff_shard[:, at : at + width] = turned(out[...])
+        at += width
+        ff_shard[:, at : at + main] = turned(gate[:main, :])
+        ff_shard[:, at + main : at + 2 * main] = turned(up[:main, :])
+        ends = jnp.concatenate([gate[main:, :], up[main:, :]], axis=0)
+        ff_shard[:, at + 2 * main :] = turned(ends)
+        yield
+        yield from gather_tok(links, ff_shard, f_out)
+
+    def gradient():
+        for unused in range(3):
+            yield
+        yield from gather_br(links, cot, g_out)
+
+    in_turn([attention(), feed_forward(), gradient()])
     links.close()
 
 
-def start(shifted, cot, weights, ff):
-    rows, depth = shifted.shape
-    wrows = weights.shape[0]
+def start(
+    block_map, tokens, gain, bias, cot, qkv, qkv_bias, gate, up, down, out, table, heads, main
+):
+    rows, depth = tokens.shape
+    wrows = qkv.shape[1]
+    width = heads * HD
+    cols = main + 128 + width + 2 * gate.shape[0]
     whole = jax.ShapeDtypeStruct((2, 4, rows, depth), BF)
-    return comm_call(
-        start_kernel,
-        "start",
-        0,
-        (shifted, cot, weights, ff),
-        (
-            whole,
-            whole,
-            jax.ShapeDtypeStruct((4, 2, 2, wrows, weights.shape[1]), BF),
-            jax.ShapeDtypeStruct((4, 2, 2, wrows, ff.shape[1]), BF),
+    places = jnp.asarray(bias_places(heads, qkv_bias.shape[2]))
+    flat = jnp.pad(qkv_bias.reshape(1, -1).astype(F32), ((0, 7), (0, 128 - qkv_bias.size)))
+    args = (block_map, tokens, gain, bias, cot, qkv, flat, places, gate, up, down, out, table)
+    copies = 72
+    shapes = (
+        whole,
+        whole,
+        jax.ShapeDtypeStruct((4, 2, 2, wrows, 3 * width + 128), BF),
+        jax.ShapeDtypeStruct((4, 2, 2, wrows, cols), BF),
+        jax.ShapeDtypeStruct((heads, 2, BLK, 2 * HD), BF),
+        jax.ShapeDtypeStruct((heads, BLK, 2 * HD), BF),
+    )
+    specs = [SMEM] + [VMEM] * (len(args) - 1)
+    specs[4] = specs[12] = ANY
+    return pl.pallas_call(
+        functools.partial(start_kernel, heads, main),
+        out_shape=shapes,
+        in_specs=specs,
+        out_specs=(ANY,) * len(shapes),
+        scratch_shapes=[
+            pltpu.VMEM((rows, depth), BF),
+            pltpu.VMEM((wrows, 3 * width + 128), BF),
+            pltpu.VMEM((wrows, cols), BF),
+            pltpu.VMEM(whole.shape, BF),
+            pltpu.VMEM(shapes[2].shape, BF),
+            pltpu.VMEM(shapes[4].shape, BF),
+            pltpu.VMEM(shapes[5].shape, BF),
+            pltpu.VMEM(table.shape, F32),
+            pltpu.SemaphoreType.DMA((copies,)),
+            pltpu.SemaphoreType.DMA((copies,)),
+            pltpu.SemaphoreType.DMA((16,)),
+        ],
+        compiler_params=pltpu.CompilerParams(
+            collective_id=0, has_side_effects=True, vmem_limit_bytes=60 * 2**20
         ),
-        copies=64,
-    )
+        cost_estimate=SMALL,
+        name="start",
+    )(*args)
 
 
 def ff_heads_kernel(
@@ -645,55 +774,52 @@
     g_ref,
     x_strip,
     g_strip,
-    w_ref,
-    joined,
+    weights,
+    kv_mine,
+    q_heads,
     h_ref,
     s_ref,
     grad_ref,
     asked,
     pairs,
+    w_ref,
     held,
     held_hidden,
+    outs,
     *sems,
 ):
     y, z, c, unused_l, unused_x = coords()
     step = pl.program_id(0)
+    final = pl.num_programs(0) - 1
     links = Links(*sems)
     order = (1, 3, 2)
-    front, back = pl.ds(0, 2), pl.ds(2, 2)
-
-    def pair(dy, dz=0, dc=0):
-        return pairs.at[(y + dy) % 4, (z + dz) % 2, (c + dc) % 2]
-
+    rows = x_ref.shape[1]
+
+    load = pltpu.make_async_copy(weights, w_ref, sems[2].at[0])
     kept = [
-        pltpu.make_async_copy(joined.at[y, front], asked.at[y], sems[2].at[0]),
-        pltpu.make_async_copy(joined.at[y, back], pair(0), sems[2].at[1]),
+        pltpu.make_async_copy(kv_mine, pairs.at[:, z, c], sems[2].at[1]),
+        pltpu.make_async_copy(q_heads.at[y], asked.at[y, 0], sems[2].at[2]),
     ]
+    kept_out = pltpu.make_async_copy(outs.at[y], asked.at[y, 1], sems[2].at[3])
     number = iter(range(64))
 
     def plan(source, target, lands, **offsets):
         n = next(number)
         return links.copy(n, source, target, offsets), links.copy(n, lands, lands, offsets)
 
-    keys = [
-        plan(joined.at[(y + d) % 4, back], pair(0), pair(-d), dy=d) for d in order
+    def swap(source, k):
+        return [
+            plan(source.at[(y + d) % 4], asked.at[y, k], asked.at[(y - d) % 4, k], dy=d)
+            for d in order
+        ]
+
+    far = [plan(kv_mine.at[i], pairs.at[i, z, c], pairs.at[i, 1 - z, c], dz=1) for i in range(4)]
+    near = [plan(kv_mine.at[i], pairs.at[i, z, c], pairs.at[i, z, 1 - c], dc=1) for i in range(4)]
+    diagonal = [
+        plan(pairs.at[i, 1 - z, c], pairs.at[i, 1 - z, c], pairs.at[i, 1 - z, 1 - c], dc=1)
+        for i in range(4)
     ]
-    rest = [
-        plan(joined.at[(y + d) % 4, front], asked.at[y], asked.at[(y - d) % 4], dy=d)
-        for d in order
-    ]
-    mine = joined.at[y, back]
-    far = [plan(mine, pair(0), pair(0, 1), dz=1)]
-    near = [plan(mine, pair(0), pair(0, 0, 1), dc=1)]
-    for d in order:
-        far.append(plan(pair(-d), pair(-d), pair(-d, 1), dz=1))
-        near.append(plan(pair(-d), pair(-d), pair(-d, 0, 1), dc=1))
-    diagonal = [plan(pair(-d, 1), pair(-d, 1), pair(-d, 1, 1), dc=1) for d in (0,) + order]
-
-    def relay(i):
-        keys[i][1].wait_recv()
-        far[i + 1][0].start()
-        near[i + 1][0].start()
+    asked_q, asked_o = swap(q_heads, 0), swap(outs, 1)
 
     def cross(i):
         far[i][1].wait_recv()
@@ -701,29 +827,18 @@
 
     @pl.when(step == 0)
     def _():
-        links.greet(TOK_ALL)
+        load.start()
+        links.greet([dict(dz=1), dict(dc=1), dict(dy=1), dict(dy=2), dict(dy=3)])
+        for copy, unused in far + near + asked_q:
+            copy.start()
         for copy in kept:
             copy.start()
-        for copy, unused in [keys[0], keys[1], keys[2], far[0], near[0]]:
-            copy.start()
+        load.wait()
 
     def pause(point):
-        @pl.when(step == 0)
-        def _():
-            if point == 0:
-                relay(0)
-                relay(1)
-            else:
-                relay(2)
-                for copy, unused in rest:
-                    copy.start()
-
         @pl.when(step == 1)
         def _():
-            if point == 0:
-                cross(0)
-            else:
-                cross(1)
+            cross(point)
 
     for i in range(2, 4):
 
@@ -731,16 +846,28 @@
         def _():
             cross(i)
 
-    rows = x_ref.shape[1]
+    here = pl.ds(pl.multiple_of(jnp.minimum(step, 1) * rows, rows), rows)
+
+    def mixed_grad(value):
+        for head in range(outs.shape[0]):
+            lanes = slice(head * HD, (head + 1) * HD)
+            outs[head, here, :] = jnp.concatenate(
+                [value[:rows, lanes], value[rows:, lanes]], axis=1
+            )
 
     @pl.when(step < 2)
     def _():
         grads, hidden = ff_part(
-            main, down, first, x_ref[...], g_ref[...], w_ref, h_ref, s_ref, pause
+            main, down, first, x_ref[...], g_ref[...], w_ref, h_ref, s_ref, mixed_grad, pause
         )
-        here = pl.ds(pl.multiple_of(step * rows, rows), rows)
         held[:, here, :] = grads.reshape(2, rows, -1)
         held_hidden[:, here, :] = hidden.reshape(2, rows, -1)
+
+    @pl.when(step == 1)
+    def _():
+        for copy, unused in asked_o:
+            copy.start()
+        kept_out.start()
 
     @pl.when(step >= 2)
     def _():
@@ -749,19 +876,19 @@
         grad_ref[:, :down] = dot(g_strip[...], hidden, TN).astype(BF)
         grad_ref[:, down:] = dot(x_strip[...], grads, TN).astype(BF)
 
-    @pl.when(step == pl.num_programs(0) - 1)
+    @pl.when(step == final)
     def _():
-        for copy in kept:
+        for copy in kept + [kept_out]:
             copy.wait()
-        for unused, landed in rest + near + diagonal:
+        for unused, landed in near + diagonal + asked_q + asked_o:
             landed.wait_recv()
-        for copy, unused in keys + rest + far + near + diagonal:
+        for copy, unused in far + near + diagonal + asked_q + asked_o:
             copy.wait_send()
 
 
-def ff_heads(x, g, w, joined, main, down, first):
+def ff_heads(x, g, w, kv_mine, q_heads, main, down, first):
     depth, cols = w.shape
-    heads, unused, span, lanes = joined.shape
+    heads, unused, span, lanes = kv_mine.shape
     rows = BLK // 2
     both = cols - first
     strip = 512
@@ -777,7 +904,8 @@
             tile(depth),
             pl.BlockSpec((2 * BLK, strip), lambda i: (0, jnp.maximum(i - 2, 0))),
             pl.BlockSpec((2 * BLK, strip), lambda i: (0, jnp.maximum(i - 2, 0))),
-            pl.BlockSpec((depth, cols), lambda i: (0, 0), pipeline_mode=pl.Buffered(1)),
+            ANY,
+            ANY,
             ANY,
         ],
         out_specs=(
@@ -795,18 +923,20 @@
             jax.ShapeDtypeStruct((4, 2, 2, 2, span, lanes), BF),
         ),
         scratch_shapes=[
+            pltpu.VMEM((depth, cols), BF),
             pltpu.VMEM((2, BLK, both), BF),
             pltpu.VMEM((2, BLK, down), BF),
+            pltpu.VMEM(q_heads.shape, BF),
             pltpu.SemaphoreType.DMA((32,)),
             pltpu.SemaphoreType.DMA((32,)),
-            pltpu.SemaphoreType.DMA((2,)),
+            pltpu.SemaphoreType.DMA((4,)),
         ],
         compiler_params=pltpu.CompilerParams(
             collective_id=1, has_side_effects=True, vmem_limit_bytes=60 * 2**20
         ),
         cost_estimate=SMALL,
         name="ff_heads",
-    )(x, g, x.reshape(2 * BLK, depth), g.reshape(2 * BLK, depth), w, joined)
+    )(x, g, x.reshape(2 * BLK, depth), g.reshape(2 * BLK, depth), w, kv_mine, q_heads)
 
 
 def home_kernel(
@@ -824,8 +954,8 @@
     *rest,
 ):
     mine, near, far, total, held_w, held_h, held_o = rest[:7]
-    space = ScatterSpace(rest[7:14])
-    links = Links(*rest[14:])
+    space = ScatterSpace(rest[7:11])
+    links = Links(*rest[11:])
     y, unused_z, unused_c, unused_l, unused_x = coords()
     rows, depth = tokens.shape
     kept = held_w.shape[1]
@@ -905,7 +1035,7 @@
             pltpu.VMEM(hidden.shape, BF),
             pltpu.VMEM(o_parts.shape, BF),
         ]
-        + ScatterSpace.shapes(rows, depth),
+        + ScatterSpace.shapes(rows, depth, depth),
         in_vmem=(5,),
         out_vmem=(2, 3),
         copies=64,
@@ -979,6 +1109,7 @@
     tokens,
     cot,
     gain,
+    block_map,
     result,
     qkv_out,
     out_out,
@@ -1013,7 +1144,7 @@
         for half in range(2):
             here = slice(half * BLK // 2, (half + 1) * BLK // 2)
             lanes = slice(slot * HD, (slot + 1) * HD)
-            turns = held_t[slot, here, :]
+            turns = table_rows(held_t, block_map, slot, 2 * LB)[here]
             q = jnp.concatenate([held_q[h, here, lanes] for h in range(heads)], axis=1)
             q = turn(q.astype(F32), turns, heads // 2, False, -1.0).astype(BF)
             kv = jnp.concatenate([held_kv[h, slot, here] for h in range(heads)], axis=1)
@@ -1097,7 +1228,9 @@
     links.close()
 
 
-def last_sums(dq, dkv, table, x, g, mixed, w, partial_grad, tokens, cot, gain, heads):
+def last_sums(
+    dq, dkv, table, x, g, mixed, w, partial_grad, tokens, cot, gain, block_map, heads
+):
     rows, depth = tokens.shape
     wrows = depth // 16
     width = heads * HD
@@ -1106,7 +1239,7 @@
         functools.partial(last_kernel, heads),
         "last_sums",
         3,
-        (dq, dkv, table, x, g, mixed, w, partial_grad, tokens, cot, gain),
+        (dq, dkv, table, x, g, mixed, w, partial_grad, tokens, cot, gain, block_map),
         (
             jax.ShapeDtypeStruct((rows, depth), F32),
             jax.ShapeDtypeStruct((3, wrows, width), F32),
@@ -1138,11 +1271,39 @@
             pltpu.VMEM((16, 8, 128), F32),
             pltpu.VMEM((15, 8, 128), F32),
         ]
-        + ScatterSpace.shapes(rows, depth),
+        + ScatterSpace.shapes(rows, depth, depth // 2),
         in_vmem=(8, 9, 10),
+        in_smem=(11,),
         out_vmem=(0, 1, 2, 3, 4),
         copies=80,
     )
+
+
+def unpack_kernel(main, grads, down, gate, up):
+    def lines(start, count):
+        return jnp.transpose(grads[:, start : start + count].astype(F32))
+
+    tail = down.shape[0] - main
+    down[:main, :] = lines(0, main)
+    down[main:, :] = lines(main, 128)[:tail]
+    at = main + 128
+    gate[:main, :] = lines(at, main)
+    up[:main, :] = lines(at + main, main)
+    ends = lines(at + 2 * main, 128)
+    gate[main:, :] = ends[:tail]
+    up[main:, :] = ends[tail:]
+
+
+def unpack(grads, main, hidden_width):
+    shape = jax.ShapeDtypeStruct((hidden_width, grads.shape[0]), F32)
+    return pl.pallas_call(
+        functools.partial(unpack_kernel, main),
+        out_shape=(shape,) * 3,
+        in_specs=[VMEM],
+        out_specs=(VMEM,) * 3,
+        cost_estimate=SMALL,
+        name="unpack",
+    )(grads)
 
 
 def rotary_table():
@@ -1182,41 +1343,25 @@
     main = hidden_width // 128 * 128
     tail = hidden_width - main
 
-    residual = tokens.astype(F32)
-    centred = residual - jnp.mean(residual, axis=-1, keepdims=True)
-    inverse = lax.rsqrt(jnp.mean(centred * centred, axis=-1, keepdims=True) + EPSILON)
-    normed = centred * inverse
-    shifted = (normed * norm_gain + norm_bias).astype(BF)
-
-    kv_shard = jnp.stack(
-        [w.reshape(wrows, heads, HD) for w in (qkv_weight[1], qkv_weight[2])], axis=2
-    ).reshape(wrows, 2 * width)
-    per = qkv_bias.shape[2]
-    lane_tok = jnp.arange(HD, dtype=jnp.int32) // per
-    bias_lanes = jnp.where(lane_tok == tok, jnp.tile(qkv_bias, (1, 1, HD // per)), 0)
-    bias_rows = jnp.concatenate(
-        [
-            bias_lanes[0].reshape(-1),
-            jnp.stack([bias_lanes[1], bias_lanes[2]], axis=1).reshape(-1),
-        ]
-    ).reshape(-1, 128)
-    bias_row = jnp.pad(bias_rows, ((0, wrows - bias_rows.shape[0]), (0, 0)))
-    qkv_shard = jnp.concatenate([qkv_weight[0], kv_shard, bias_row], axis=1)
-    ff_shard = jnp.concatenate(
-        [
-            jnp.transpose(down_weight),
-            jnp.zeros((wrows, 128 - tail), BF),
-            jnp.transpose(out_weight),
-            gate_weight[:, :main],
-            up_weight[:, :main],
-            gate_weight[:, main:],
-            up_weight[:, main:],
-        ],
-        axis=1,
-    )
     down_width = main + 128
     first = down_width + width
-    x, grad, qkv_full, ff_full = start(shifted, cotangent, qkv_shard, ff_shard)
+    table = jnp.asarray(rotary_table())
+    x, grad, qkv_full, ff_full, kv_mine, q_heads = start(
+        block_map,
+        tokens,
+        norm_gain.reshape(1, depth),
+        norm_bias.reshape(1, depth),
+        cotangent,
+        qkv_weight,
+        qkv_bias,
+        jnp.transpose(gate_weight),
+        jnp.transpose(up_weight),
+        down_weight,
+        out_weight,
+        table,
+        heads,
+        main,
+    )
     x = x.reshape(2, BLK, depth)
     grad = grad.reshape(2, BLK, depth)
     qkv_full = qkv_full.reshape(16 * wrows, -1)
@@ -1242,13 +1387,8 @@
         jnp.where(query_row[:, None] == row_table[None, :], lengths[None, :], 0), axis=1
     ).astype(jnp.int32)
 
-    my_blocks = lax.dynamic_slice_in_dim(block_map, tok * 2, 2)
-    places = jnp.where(my_blocks < long_blocks, my_blocks % LB, (my_blocks - long_blocks) % 2)
-    table = jnp.asarray(rotary_table())
-
-    joined = project(places, x, grad, qkv_full, ff_full, table, heads)
     hidden, grad_x, grad_ff, qd_all, kv_all = ff_heads(
-        x, grad, ff_full, joined, main, down_width, first
+        x, grad, ff_full, kv_mine, q_heads, main, down_width, first
     )
     kv_all = kv_all.reshape(-1, 2 * HD)
     x = x.reshape(2 * BLK, depth)
@@ -1263,11 +1403,10 @@
         dkv_all.reshape(4, 2, 2, 2 * BLK, 2 * HD), dq_parts, o_parts, hidden, ff_full, tokens, heads
     )
     grad_ff, dq_heads = lax.optimization_barrier((grad_ff, dq_heads))
-    turns = jnp.stack([lax.dynamic_index_in_dim(table, places[i], 0, False) for i in range(2)])
     grad_tokens, grad_qkv, grad_out_out, bias_sums, sides = last_sums(
         dq_heads,
         dkv_heads.reshape(heads, 2, BLK, 2 * HD),
-        turns,
+        table,
         x,
         grad,
         mixed.reshape(2 * BLK, width),
@@ -1276,6 +1415,7 @@
         tokens,
         cotangent,
         norm_gain.reshape(1, depth),
+        block_map,
         heads,
     )
     bias_sums = bias_sums[: 3 * width // 128].reshape(-1)
@@ -1285,13 +1425,10 @@
             jnp.transpose(bias_sums[width:].reshape(heads, 2, HD), (1, 0, 2)),
         ]
     )
-    grad_bias_out = lax.dynamic_slice_in_dim(bias_sums, tok * per, per, 2)
-    grad_ff = grad_ff.astype(F32)
-    grad_down_out = jnp.transpose(grad_ff[:, :hidden_width])
-    grad_gu = grad_ff[:, down_width:]
-    ends = grad_gu[:, 2 * main :]
-    grad_gate_out = jnp.concatenate([grad_gu[:, :main], ends[:, :tail]], axis=1)
-    grad_up_out = jnp.concatenate([grad_gu[:, main : 2 * main], ends[:, tail:]], axis=1)
+    grad_bias_out = lax.dynamic_slice_in_dim(
+        bias_sums, tok * qkv_bias.shape[2], qkv_bias.shape[2], 2
+    )
+    grad_down, grad_gate, grad_up = unpack(grad_ff, main, hidden_width)
 
     sides = lax.dynamic_slice_in_dim(sides[:2], lax.axis_index("br") * 16, 16, 1)
     return (
@@ -1302,9 +1439,9 @@
         grad_qkv,
         grad_bias_out,
         grad_out_out,
-        grad_gate_out,
-        grad_up_out,
-        grad_down_out,
+        jnp.transpose(grad_gate),
+        jnp.transpose(grad_up),
+        grad_down,
     )
 
 

time: 411 us -> 371 us (0.903)
  Pallas kernels: 359 us -> 339 us
  local copies, waits for them, and re-layouts: 22 us -> 9.61 us
  other arithmetic: 8.32 us -> 2.87 us
    pallas_call x3 -> x2, Pallas kernels: 251 us -> 149 us  [comm_call(): pl.pallas_call(kernel, out_shape=tuple(outs), in_specs=[VMEM if i in in_v...]
    pallas_call x1 -> x2, Pallas kernels: 10.7 us -> 98.3 us  [the longest x1 96.2 us: start(): pl.pallas_call(functools.partial(start_kernel, heads, main), out_shape=sh...]
    pallas_call x1, Pallas kernels: 52.6 us -> 46.3 us  [ff_heads(): pl.pallas_call(functools.partial(ff_heads_kernel, main, down, first), gri...]
    unnamed x35 -> x14, local copies, waits for them, and re-layouts: 10.8 us -> 5.93 us
  transfers between devices with their start and end apart: 1 -> 1, of which waited for: 0 -> 0; matrix products, arithmetic and copies ran while one was open for 1% -> 0% of each run, Pallas kernels for 34% -> 33%
where the time goes in v6:
time: 371 us; the launch traced here: 366 us
  Pallas kernels  339 us (91%)
  between operations  14.6 us (4%)
  local copies, waits for them, and re-layouts  9.61 us (3%)
    pallas_call x2, Pallas kernels, comm_call(): pl.pallas_call(kernel, out_shape=tuple(outs), in_specs=[VMEM if i in in_v...  149 us
    pallas_call x1, Pallas kernels, start(): pl.pallas_call(functools.partial(start_kernel, heads, main), out_shape=sh...  96.2 us
    pallas_call x1, Pallas kernels, ff_heads(): pl.pallas_call(functools.partial(ff_heads_kernel, main, down, first), gri...  46.3 us
    pallas_call x1, Pallas kernels, attn_bwd(): pl.pallas_call(functools.partial(attn_bwd_kernel, long_blocks), out_shape...  26.2 us
    pallas_call x1, Pallas kernels, attn_fwd(): pl.pallas_call(functools.partial(attn_fwd_kernel, long_blocks), out_shape...  19.2 us
  transfers between devices with their start and end apart: 1, of which 0 were waited for; matrix products, arithmetic and copies ran while one was open for 0% of the time, Pallas kernels for 33%

profile of v6, /device:TPU:1, one launch (start us, length us, event | category | flops | bytes accessed | tf_op | source)
XLA Modules:
  0.0 365.8 jit_solution(400186262983496349)
XLA Ops:
  7.2 0.0 reduce-scatter.2.cloned.1.call-start
  7.2 0.8 convert_element_type.14
  8.0 0.6 pad_convert_fusion.qkv_bias
  8.6 96.2 %start.1 = (bf16[2,4,128,2048]{3,2,1,0:T(8,128)(2,1)}, bf16[2,4,128,2048]{3,2,1,0:T(8,128)(2,1)}, bf16[4,2,2,128,896]{4,3,2,1,0:T(8,128)(2,1)}, bf16[4,2,2,128,2...) custom-call(s32[32]{0:T(128)} %block_map.3, bf16[128,2048]{1,0:T(8,128)(2,1)} %tokens.5, ...), custom_call_target="tpu_custom_call" | custom-call | flops 1000 | bytes 1000 | tf_op jit(solution)/shard_map/start/pallas_call | solution.py:743
  104.8 46.3 %ff_heads.1 = (bf16[2,512,768]{2,1,0:T(8,128)(2,1)}, bf16[2,512,2048]{2,1,0:T(8,128)(2,1)}, bf16[2048,2176]{1,0:T(8,128)(2,1)}, bf16[4,2,512,128]{3,2,1,0:T(8,128)(2,1)}, bf16[4,2,2,2,512,128]{5,4,3,2,1,0:T(8,128)(2,1)}) custom-call(bf16[2,512,2048]{2,1,0:T(8,128)(2,1)} %bitcast.25, bf16[2,512,2048]{2,1,0:T(8,128)(2,1)} %bitcast.28, ...), custom_call_target="tpu_custom_call" | custom-call | flops 1000 | bytes 1000 | tf_op jit(solution)/shard_map/ff_heads/pallas_call | solution.py:899
  151.0 0.0 copy-start.3
  151.0 0.0 copy-start.4
  151.1 0.0 reduce-scatter.2.cloned.1.call-update
  151.1 0.1 pad_add_fusion
  151.2 0.1 eq.44
  151.3 0.4 copy-done.3
  151.7 0.6 select_reduce_fusion.kslot
  152.3 0.2 select_reduce_fusion.2.qblk
  152.5 0.0 copy-start.2
  152.5 0.0 copy-done.4
  152.5 0.7 select_reduce_fusion.1.qlim
  153.2 0.0 copy-done.2
  153.2 19.2 %attn_fwd.1 = (f32[4,128,512]{2,1,0:T(8,128)}, f32[8,1,512]{2,1,0:T(1,128)}, bf16[4,512,128]{2,1,0:T(8,128)(2,1)}) custom-call(s32[8]{0:T(128)} %copy-done.2, s32[8]{0:T(128)} %select_reduce_fusion.1.qlim, s32[32]{0:T(128)} %select_reduce_fusion.kslot, bf16[4,2,512,128]{3,2,1,0:T(8,128)(2,1)} %get-tuple-element.45.q_ref, bf16[16384,128]{1,0:T(8,128)(2,1)} %bitcast.31), custom_call_target="tpu_custom_call" | custom-call | flops 1000 | bytes 1000 | tf_op jit(solution)/shard_map/attn_fwd/pallas_call | solution.py:92
  172.4 26.2 %attn_bwd.1 = (bf16[4,512,128]{2,1,0:T(8,128)(2,1)}, bf16[16384,128]{1,0:T(8,128)(2,1)}) custom-call(s32[8]{0:T(128)} %copy-done.2, s32[8]{0:T(128)} %select_reduce_fusion.1.qlim, s32[32]{0:T(128)} %select_reduce_fusion.kslot, bf16[4,2,512,128]{3,2,1,0:T(8,128)(2,1)} %get-tuple-element.45.q_ref, bf16[16384,128]{1,0:T(8,128)(2,1)} %bitcast.32, ...), custom_call_target="tpu_custom_call" | custom-call | flops 1000 | bytes 1000 | tf_op jit(solution)/shard_map/attn_bwd/pallas_call | solution.py:159
  198.6 74.0 %heads_home.1 = (bf16[4,512,128]{2,1,0:T(8,128)(2,1)}, bf16[4,1024,128]{2,1,0:T(8,128)(2,1)}, bf16[2,512,256]{2,1,0:T(8,128)(2,1)}, bf16[128,2048]{1,0:T(8,128)(2,1)}) custom-call(bf16[4,2,2,1024,128]{4,3,2,1,0:T(8,128)(2,1)} %bitcast.33, bf16[4,512,128]{2,1,0:T(8,128)(2,1)} %get-tuple-element.50.dq, bf16[4,512,128]{2,1,0:T(8,128)(2,1)} %get-tuple-element.51.o_parts, ...), custom_call_target="tpu_custom_call" | custom-call | flops 1000 | bytes 1000 | tf_op jit(solution)/shard_map/heads_home/pallas_call | solution.py:547
  272.6 0.0 reduce-scatter.2.cloned.1.call-done.grads
  272.6 0.0 copy-start
  272.6 74.7 %last_sums.1 = (f32[128,2048]{1,0:T(8,128)}, f32[3,128,256]{2,1,0:T(8,128)}, f32[256,128]{1,0:T(8,128)}, f32[8,128]{1,0:T(8,128)}, f32[8,128]{1,0:T(8,128)}) custom-call(bf16[4,512,128]{2,1,0:T(8,128)(2,1)} %get-tuple-element.56.dq, bf16[4,2,512,128]{3,2,1,0:T(8,128)(2,1)} %bitcast.35, f32[8,512,128]{2,1,0:T(8,128)} %constant.80.clone.table, ...), custom_call_target="tpu_custom_call" | custom-call | flops 1000 | bytes 1000 | tf_op jit(solution)/shard_map/last_sums/pallas_call | solution.py:547
  347.4 0.0 copy-start.1
  347.4 0.7 slice.23
  348.1 0.7 slice.24
  348.7 0.7 slice.20
  349.4 0.1 constant_dynamic-slice_fusion
  349.5 0.5 slice_bitcast_fusion
  350.0 0.1 reshape.146
  350.1 0.1 reshape.147
  350.2 2.2 unpack.1
  352.4 0.7 dynamic-slice_maximum_fusion
  353.0 0.0 copy-done
  353.0 0.8 copy.33
  353.8 2.3 copy.34
  356.1 1.8 copy.35
  357.9 0.0 copy-done.1
  357.9 0.7 copy.36
  (3 shorter events, 0.0 us)
Async XLA Ops:
  7.2 265.4 %reduce-scatter.2.cloned.1.call-start = ((), (), s32[]{:S(2)}) async-start(), calls=%async_computation.1 | async-start | bytes 9469952 | tf_op jit(solution)/shard_map/reduce_scatter | solution.py:1396
  151.0 0.7 copy-start.3
  151.0 1.5 copy-start.4
  152.5 0.7 copy-start.2
  272.6 80.4 %copy-start = (bf16[128,2048]{1,0:T(8,128)(2,1)S(1)}, bf16[128,2048]{1,0:T(8,128)(2,1)}, u32[]{:S(2)}) copy-start(bf16[128,2048]{1,0:T(8,128)(2,1)} %get-tuple-element.84) | copy-start | bytes 1572868
  347.4 10.5 %copy-start.1 = (f32[256,128]{1,0:T(8,128)S(1)}, f32[256,128]{1,0:T(8,128)}, u32[]{:S(2)}) copy-start(f32[256,128]{1,0:T(8,128)} %get-tuple-element.90) | copy-start | bytes 393220
Sparse Core Ops, SparseCore 0:
  151.2 113.5 reduce-scatter.1

commit v7 on v6

--- a/solution.py
+++ b/solution.py
@@ -516,20 +516,26 @@
         yield
     rows = out.shape[0]
     sent = {}
-    for i, d in enumerate(order):
-        here = (y + d) % 4
-        links.arrived(tickets[d], near.at[here])
-        for k in range(2):
+    for dz in (1, 0):
+        k = (z + dz) % 2
+        for i, d in enumerate(order):
+            here = (y + d) % 4
+            if dz:
+                links.arrived(tickets[d], near.at[here])
             own = parts.at[here, k, c]
             add_up(own, [own, near.at[here, k]], rows, plain)
-        if d:
-            sent[i] = links.send(parts.at[here, :, c], side.at[i], dy=d)
-        yield
+            if d:
+                sent[dz, i] = links.send(own, side.at[i, k], dy=d)
+            if dz:
+                yield
     for i in range(3):
-        links.arrived(sent[i], side.at[i])
+        links.arrived(sent[1, i], side.at[i, 1 - z])
         yield
     add_up(out, [parts.at[y, 1 - z, c]] + [side.at[i, 1 - z] for i in range(3)], rows, plain)
     across = links.send(out, far, dz=1)
+    yield
+    for i in range(3):
+        links.arrived(sent[0, i], side.at[i, z])
     yield
     links.arrived(across, far)
     add_up(target, [parts.at[y, z, c]] + [side.at[i, z] for i in range(3)] + [far], rows, plain)
@@ -555,7 +561,7 @@
         + [
             pltpu.SemaphoreType.DMA((copies,)),
             pltpu.SemaphoreType.DMA((copies,)),
-            pltpu.SemaphoreType.DMA((16,)),
+            pltpu.SemaphoreType.DMA((32,)),
         ],
         compiler_params=pltpu.CompilerParams(
             collective_id=number, has_side_effects=True, vmem_limit_bytes=60 * 2**20
@@ -756,7 +762,7 @@
             pltpu.VMEM(table.shape, F32),
             pltpu.SemaphoreType.DMA((copies,)),
             pltpu.SemaphoreType.DMA((copies,)),
-            pltpu.SemaphoreType.DMA((16,)),
+            pltpu.SemaphoreType.DMA((32,)),
         ],
         compiler_params=pltpu.CompilerParams(
             collective_id=0, has_side_effects=True, vmem_limit_bytes=60 * 2**20
@@ -939,6 +945,17 @@
     )(x, g, x.reshape(2 * BLK, depth), g.reshape(2 * BLK, depth), w, kv_mine, q_heads)
 
 
+def residual(tokens, first):
+    def finish(column):
+        def add(value, here):
+            at = first + column
+            return value + tokens[here, at : at + value.shape[1]].astype(F32)
+
+        return add
+
+    return finish
+
+
 def home_kernel(
     heads,
     grads,
@@ -951,11 +968,12 @@
     grads_home,
     mixed_out,
     result,
+    later,
     *rest,
 ):
-    mine, near, far, total, held_w, held_h, held_o = rest[:7]
-    space = ScatterSpace(rest[7:11])
-    links = Links(*rest[11:])
+    mine, near, far, total, held_w, held_h, held_o, held_later = rest[:8]
+    space = ScatterSpace(rest[8:12])
+    links = Links(*rest[12:])
     y, unused_z, unused_c, unused_l, unused_x = coords()
     rows, depth = tokens.shape
     kept = held_w.shape[1]
@@ -984,14 +1002,12 @@
             [held_h[:, here, :].reshape(2 * rows, -1), jnp.concatenate(mixed, axis=0)], axis=1
         )
         branches = dot(both, held_w[...], NT).astype(BF)
+        half = space.pieces.shape[3]
         for slot in range(2):
-            space.pieces[slot, there] = branches[slot * rows : (slot + 1) * rows]
-
-    def finish(column):
-        def add(value, here):
-            return value + tokens[here, column : column + value.shape[1]].astype(F32)
-
-        return add
+            piece = branches[slot * rows : (slot + 1) * rows]
+            space.pieces[slot, there] = piece[:, :half]
+            held_later[slot, there] = piece[:, half:]
+        links.local(held_later.at[:, there], later.at[:, there])
 
     def output():
         yield
@@ -999,7 +1015,7 @@
             links.arrived(ticket, held_o.at[(y - d) % 4])
         for load in loads:
             links.settle(load)
-        yield from scatter_br(links, make, space, result, finish)
+        yield from scatter_br(links, make, space, result, residual(tokens, 0))
 
     in_turn(
         [
@@ -1024,7 +1040,8 @@
             jax.ShapeDtypeStruct(dq.shape, BF),
             jax.ShapeDtypeStruct((4, span, lanes), BF),
             jax.ShapeDtypeStruct((2, BLK, width), BF),
-            jax.ShapeDtypeStruct((rows, depth), BF),
+            jax.ShapeDtypeStruct((rows, depth // 2), BF),
+            jax.ShapeDtypeStruct((2, 4, rows, depth // 2), BF),
         ),
         scratch=[
             pltpu.VMEM((4, 2, span, lanes), BF),
@@ -1034,8 +1051,9 @@
             pltpu.VMEM((depth, kept), BF),
             pltpu.VMEM(hidden.shape, BF),
             pltpu.VMEM(o_parts.shape, BF),
+            pltpu.VMEM((2, 4, rows, depth // 2), BF),
         ]
-        + ScatterSpace.shapes(rows, depth, depth),
+        + ScatterSpace.shapes(rows, depth // 2, depth // 2),
         in_vmem=(5,),
         out_vmem=(2, 3),
         copies=64,
@@ -1110,10 +1128,11 @@
     cot,
     gain,
     block_map,
+    later,
     result,
     qkv_out,
     out_out,
-    bias_out,
+    late_out,
     sides,
     *rest,
 ):
@@ -1121,11 +1140,13 @@
     parts, near, side, out, far, wsum, summed, normed, scales = rest[9:18]
     lines, lines_in, last, last_in = rest[18:22]
     space = ScatterSpace(rest[22:29])
-    links = Links(*rest[29:])
+    late = ScatterSpace(rest[29:33])
+    links = Links(*rest[33:])
     y, z, c, l, x = coords()
     links.greet(BR_PEERS + TOK_PEERS)
     width = heads * HD
     rows, depth = tokens.shape
+    branches = [links.local(later, late.pieces)]
     first = [
         links.local(dq, held_q),
         links.local(dkv, held_kv),
@@ -1152,8 +1173,14 @@
             both = jnp.concatenate([q, kv], axis=1)
             gj[slot, here, :] = both
             total += jnp.sum(both.astype(F32), axis=0, keepdims=True)
-    corner = [total[:, r * 128 : (r + 1) * 128] for r in range(3 * width // 128)]
-    corner = jnp.concatenate(corner + [jnp.zeros((122, 128), F32)], axis=0).astype(BF)
+    line = [total[:, :width]]
+    for k in range(2):
+        at = [width + (2 * h + k) * HD for h in range(heads)]
+        line.append(jnp.concatenate([total[:, a : a + HD] for a in at], axis=1))
+    line = jnp.concatenate(line, axis=1)
+    bias_sums = jnp.concatenate(
+        [line[:, r * 128 : (r + 1) * 128] for r in range(3 * width // 128)], axis=0
+    )
     for load in second:
         links.settle(load)
     wrows = parts.shape[3]
@@ -1167,7 +1194,6 @@
             at = slice(k * wrows, (k + 1) * wrows)
             parts[there, k // 2, k % 2, :, : 3 * width] = qkv[at]
             parts[there, k // 2, k % 2, :, 3 * width : 4 * width] = outs[at]
-            parts[there, k // 2, k % 2, :, 4 * width :] = corner
 
     def rows_of(there):
         if third:
@@ -1181,6 +1207,11 @@
             value = grads[slot * rows : (slot + 1) * rows] + held_s[slot, here, :].astype(F32)
             space.pieces[slot, there] = value.astype(BF)
 
+    def loaded(there):
+        for load in branches:
+            links.settle(load)
+        branches.clear()
+
     def aside():
         for unused in range(5):
             yield
@@ -1190,6 +1221,7 @@
         [
             reduce_tok(links, weights_of, parts, near, side, out, far, wsum),
             scatter_br(links, rows_of, space, summed, lambda column: plain),
+            scatter_br(links, loaded, late, late_out, residual(tokens, depth // 2)),
             aside(),
         ]
     )
@@ -1202,9 +1234,8 @@
     for i, ticket in enumerate(tickets):
         links.arrived(ticket, lines_in.at[i])
         total = total + lines_in[i]
-    last[...] = jnp.zeros_like(last)
     for t in range(16):
-        last[t, 0:2, :] = jnp.concatenate([total[t : t + 1], total[16 + t : 17 + t]], axis=0)
+        last[t] = jnp.concatenate([total[t : t + 1], total[16 + t : 17 + t], bias_sums], axis=0)
     tickets = []
     for i, o in enumerate(TOK_PEERS):
         there = ((y + o["dy"]) % 4) * 4 + ((z + o["dz"]) % 2) * 2 + (c + o["dc"]) % 2
@@ -1219,7 +1250,6 @@
             axis=1,
         )
     out_out[...] = jnp.transpose(wsum[:, 3 * width : 4 * width])
-    bias_out[...] = wsum[:8, 4 * width :]
     total = last[y * 4 + z * 2 + c]
     for i, ticket in enumerate(tickets):
         links.arrived(ticket, last_in.at[i])
@@ -1229,22 +1259,22 @@
 
 
 def last_sums(
-    dq, dkv, table, x, g, mixed, w, partial_grad, tokens, cot, gain, block_map, heads
+    dq, dkv, table, x, g, mixed, w, partial_grad, tokens, cot, gain, block_map, later, heads
 ):
     rows, depth = tokens.shape
     wrows = depth // 16
     width = heads * HD
-    cols = 4 * width + 128
+    cols = 4 * width
     return comm_call(
         functools.partial(last_kernel, heads),
         "last_sums",
         3,
-        (dq, dkv, table, x, g, mixed, w, partial_grad, tokens, cot, gain, block_map),
+        (dq, dkv, table, x, g, mixed, w, partial_grad, tokens, cot, gain, block_map, later),
         (
             jax.ShapeDtypeStruct((rows, depth), F32),
             jax.ShapeDtypeStruct((3, wrows, width), F32),
             jax.ShapeDtypeStruct((width, wrows), F32),
-            jax.ShapeDtypeStruct((8, 128), F32),
+            jax.ShapeDtypeStruct((rows, depth // 2), BF),
             jax.ShapeDtypeStruct((8, 128), F32),
         ),
         scratch=[
@@ -1271,18 +1301,26 @@
             pltpu.VMEM((16, 8, 128), F32),
             pltpu.VMEM((15, 8, 128), F32),
         ]
-        + ScatterSpace.shapes(rows, depth, depth // 2),
+        + ScatterSpace.shapes(rows, depth, depth // 2)
+        + ScatterSpace.shapes(rows, depth // 2, depth // 2),
         in_vmem=(8, 9, 10),
         in_smem=(11,),
         out_vmem=(0, 1, 2, 3, 4),
-        copies=80,
-    )
-
-
-def unpack_kernel(main, grads, down, gate, up):
+        copies=96,
+    )
+
+
+def finish_kernel(main, grads, first, second, tokens, qkv, out, *outs):
     def lines(start, count):
         return jnp.transpose(grads[:, start : start + count].astype(F32))
 
+    result, tokens_out, qkv_out, out_out, down, gate, up = outs
+    half = first.shape[1]
+    result[:, :half] = first[...]
+    result[:, half:] = second[...]
+    tokens_out[...] = tokens[...]
+    qkv_out[...] = qkv[...]
+    out_out[...] = out[...]
     tail = down.shape[0] - main
     down[:main, :] = lines(0, main)
     down[main:, :] = lines(main, 128)[:tail]
@@ -1294,16 +1332,23 @@
     up[main:, :] = ends[tail:]
 
 
-def unpack(grads, main, hidden_width):
+def finish(grads, first, second, tokens, qkv, out, main, hidden_width):
+    rows, half = first.shape
     shape = jax.ShapeDtypeStruct((hidden_width, grads.shape[0]), F32)
     return pl.pallas_call(
-        functools.partial(unpack_kernel, main),
-        out_shape=(shape,) * 3,
-        in_specs=[VMEM],
-        out_specs=(VMEM,) * 3,
+        functools.partial(finish_kernel, main),
+        out_shape=(
+            jax.ShapeDtypeStruct((rows, 2 * half), BF),
+            jax.ShapeDtypeStruct(tokens.shape, F32),
+            jax.ShapeDtypeStruct(qkv.shape, F32),
+            jax.ShapeDtypeStruct(out.shape, F32),
+        )
+        + (shape,) * 3,
+        in_specs=[VMEM] * 6,
+        out_specs=(VMEM,) * 7,
         cost_estimate=SMALL,
-        name="unpack",
-    )(grads)
+        name="finish",
+    )(grads, first, second, tokens, qkv, out)
 
 
 def rotary_table():
@@ -1399,11 +1444,11 @@
     dq_parts, dkv_all = attn_bwd(
         query_block, query_limit, key_slot, qd_all, kv_all, turned, lse, long_blocks
     )
-    dq_heads, dkv_heads, mixed, result = heads_home(
+    dq_heads, dkv_heads, mixed, first_half, later = heads_home(
         dkv_all.reshape(4, 2, 2, 2 * BLK, 2 * HD), dq_parts, o_parts, hidden, ff_full, tokens, heads
     )
     grad_ff, dq_heads = lax.optimization_barrier((grad_ff, dq_heads))
-    grad_tokens, grad_qkv, grad_out_out, bias_sums, sides = last_sums(
+    grad_tokens, grad_qkv, grad_out, second_half, sides = last_sums(
         dq_heads,
         dkv_heads.reshape(heads, 2, BLK, 2 * HD),
         table,
@@ -1416,19 +1461,15 @@
         cotangent,
         norm_gain.reshape(1, depth),
         block_map,
+        later,
         heads,
     )
-    bias_sums = bias_sums[: 3 * width // 128].reshape(-1)
-    bias_sums = jnp.concatenate(
-        [
-            bias_sums[:width].reshape(1, heads, HD),
-            jnp.transpose(bias_sums[width:].reshape(heads, 2, HD), (1, 0, 2)),
-        ]
-    )
-    grad_bias_out = lax.dynamic_slice_in_dim(
-        bias_sums, tok * qkv_bias.shape[2], qkv_bias.shape[2], 2
-    )
-    grad_down, grad_gate, grad_up = unpack(grad_ff, main, hidden_width)
+    grad_qkv_bias = lax.dynamic_slice_in_dim(
+        sides[2:].reshape(3, heads, HD), tok * qkv_bias.shape[2], qkv_bias.shape[2], 2
+    )
+    result, grad_tokens, grad_qkv, grad_out, grad_down, grad_gate, grad_up = finish(
+        grad_ff, first_half, second_half, grad_tokens, grad_qkv, grad_out, main, hidden_width
+    )
 
     sides = lax.dynamic_slice_in_dim(sides[:2], lax.axis_index("br") * 16, 16, 1)
     return (
@@ -1437,8 +1478,8 @@
         sides[0],
         sides[1],
         grad_qkv,
-        grad_bias_out,
-        grad_out_out,
+        grad_qkv_bias,
+        grad_out,
         jnp.transpose(grad_gate),
         jnp.transpose(grad_up),
         grad_down,

time: 371 us -> 379 us (1.022)
  Pallas kernels: 339 us -> 348 us
  waiting for transfers between devices: 0.04 us -> 6.85 us
  local copies, waits for them, and re-layouts: 9.61 us -> 3.96 us
    reduce_scatter x1, waiting for transfers between devices: 0.02 us -> 6.83 us  [body(): grad_ff = lax.psum_scatter(grad_ff, 'tok', scatter_dimension=0, tiled=True)]
    unnamed x14 -> x6, local copies, waits for them, and re-layouts: 5.93 us -> 0.41 us
    pallas_call x1, Pallas kernels: 19.2 us -> 24.1 us  [attn_fwd(): pl.pallas_call(functools.partial(attn_fwd_kernel, long_blocks), out_shape...]
    pallas_call x1, Pallas kernels: 26.2 us -> 30.8 us  [attn_bwd(): pl.pallas_call(functools.partial(attn_bwd_kernel, long_blocks), out_shape...]
  transfers between devices with their start and end apart: 1 -> 1, of which waited for: 0 -> 1; matrix products, arithmetic and copies ran while one was open for 0% -> 0% of each run, Pallas kernels for 33% -> 29%
where the time goes in v7:
time: 379 us; the launch traced here: 376 us
  Pallas kernels  348 us (92%)
  between operations  14.6 us (4%)
  waiting for transfers between devices  6.85 us (2%)
  local copies, waits for them, and re-layouts  3.96 us (1%)
    pallas_call x2, Pallas kernels, comm_call(): pl.pallas_call(kernel, out_shape=tuple(outs), in_specs=[VMEM if i in in_v...  147 us
    pallas_call x1, Pallas kernels, start(): pl.pallas_call(functools.partial(start_kernel, heads, main), out_shape=sh...  96.3 us
    pallas_call x1, Pallas kernels, ff_heads(): pl.pallas_call(functools.partial(ff_heads_kernel, main, down, first), gri...  46.2 us
    pallas_call x1, Pallas kernels, attn_bwd(): pl.pallas_call(functools.partial(attn_bwd_kernel, long_blocks), out_shape...  30.8 us
    pallas_call x1, Pallas kernels, attn_fwd(): pl.pallas_call(functools.partial(attn_fwd_kernel, long_blocks), out_shape...  24.1 us
  transfers between devices with their start and end apart: 1, of which 1 were waited for; matrix products, arithmetic and copies ran while one was open for 0% of the time, Pallas kernels for 29%

profile of v7, /device:TPU:1, one launch (start us, length us, event | category | flops | bytes accessed | tf_op | source)
XLA Modules:
  0.0 376.0 jit_solution(10997859560219806438)
XLA Ops:
  7.2 0.0 reduce-scatter.2.cloned.1.call-start
  7.2 0.8 convert_element_type.14
  8.0 0.6 pad_convert_fusion.qkv_bias
  8.6 96.3 %start.1 = (bf16[2,4,128,2048]{3,2,1,0:T(8,128)(2,1)}, bf16[2,4,128,2048]{3,2,1,0:T(8,128)(2,1)}, bf16[4,2,2,128,896]{4,3,2,1,0:T(8,128)(2,1)}, bf16[4,2,2,128,2...) custom-call(s32[32]{0:T(128)} %block_map.3, bf16[128,2048]{1,0:T(8,128)(2,1)} %tokens.5, ...), custom_call_target="tpu_custom_call" | custom-call | flops 1000 | bytes 1000 | tf_op jit(solution)/shard_map/start/pallas_call | solution.py:749
  104.9 46.2 %ff_heads.1 = (bf16[2,512,768]{2,1,0:T(8,128)(2,1)}, bf16[2,512,2048]{2,1,0:T(8,128)(2,1)}, bf16[2048,2176]{1,0:T(8,128)(2,1)}, bf16[4,2,512,128]{3,2,1,0:T(8,128)(2,1)}, bf16[4,2,2,2,512,128]{5,4,3,2,1,0:T(8,128)(2,1)}) custom-call(bf16[2,512,2048]{2,1,0:T(8,128)(2,1)} %bitcast.22, bf16[2,512,2048]{2,1,0:T(8,128)(2,1)} %bitcast.25, ...), custom_call_target="tpu_custom_call" | custom-call | flops 1000 | bytes 1000 | tf_op jit(solution)/shard_map/ff_heads/pallas_call | solution.py:905
  151.1 0.0 copy-start
  151.2 0.0 copy-start.2
  151.2 0.0 reduce-scatter.2.cloned.1.call-update
  151.2 0.1 pad_add_fusion
  151.3 0.1 eq.44
  151.4 0.4 copy-done
  151.8 0.6 select_reduce_fusion.kslot
  152.4 0.2 select_reduce_fusion.2.qblk
  152.6 0.0 copy-start.1
  152.6 0.0 copy-done.2
  152.6 0.7 select_reduce_fusion.1.qlim
  153.3 0.0 copy-done.1
  153.3 24.1 %attn_fwd.1 = (f32[4,128,512]{2,1,0:T(8,128)}, f32[8,1,512]{2,1,0:T(1,128)}, bf16[4,512,128]{2,1,0:T(8,128)(2,1)}) custom-call(s32[8]{0:T(128)} %copy-done.1, s32[8]{0:T(128)} %select_reduce_fusion.1.qlim, s32[32]{0:T(128)} %select_reduce_fusion.kslot, bf16[4,2,512,128]{3,2,1,0:T(8,128)(2,1)} %get-tuple-element.51.q_ref, bf16[16384,128]{1,0:T(8,128)(2,1)} %bitcast.28), custom_call_target="tpu_custom_call" | custom-call | flops 1000 | bytes 1000 | tf_op jit(solution)/shard_map/attn_fwd/pallas_call | solution.py:92
  177.5 30.8 %attn_bwd.1 = (bf16[4,512,128]{2,1,0:T(8,128)(2,1)}, bf16[16384,128]{1,0:T(8,128)(2,1)}) custom-call(s32[8]{0:T(128)} %copy-done.1, s32[8]{0:T(128)} %select_reduce_fusion.1.qlim, s32[32]{0:T(128)} %select_reduce_fusion.kslot, bf16[4,2,512,128]{3,2,1,0:T(8,128)(2,1)} %get-tuple-element.51.q_ref, bf16[16384,128]{1,0:T(8,128)(2,1)} %bitcast.29, ...), custom_call_target="tpu_custom_call" | custom-call | flops 1000 | bytes 1000 | tf_op jit(solution)/shard_map/attn_bwd/pallas_call | solution.py:159
  208.2 54.2 %heads_home.1 = (bf16[4,512,128]{2,1,0:T(8,128)(2,1)}, bf16[4,1024,128]{2,1,0:T(8,128)(2,1)}, bf16[2,512,256]{2,1,0:T(8,128)(2,1)}, bf16[128,1024]{1,0:T(8,128)(2,1)}, bf16[2,4,128,1024]{3,2,1,0:T(8,128)(2,1)}) custom-call(bf16[4,2,2,1024,128]{4,3,2,1,0:T(8,128)(2,1)} %bitcast.30, bf16[4,512,128]{2,1,0:T(8,128)(2,1)} %get-tuple-element.56.dq, ...), custom_call_target="tpu_custom_call" | custom-call | flops 1000 | bytes 1000 | tf_op jit(solution)/shard_map/heads_home/pallas_call | solution.py:553
  262.4 6.8 %reduce-scatter.2.cloned.1.call-done.grads = bf16[128,2176]{1,0:T(8,128)(2,1)} async-done(((bf16[2048,2176]{1,0:T(8,128)(2,1)}), bf16[128,2176]{1,0:T(8,128)(2,1)}) %reduce-scatter.2.cloned.1.call-update) | async-done | bytes 557072 | tf_op jit(solution)/shard_map/reduce_scatter | solution.py:1441
  269.3 93.2 %last_sums.1 = (f32[128,2048]{1,0:T(8,128)}, f32[3,128,256]{2,1,0:T(8,128)}, f32[256,128]{1,0:T(8,128)}, bf16[128,1024]{1,0:T(8,128)(2,1)}, f32[8,128]{1,0:T(8,128)}) custom-call(bf16[4,512,128]{2,1,0:T(8,128)(2,1)} %get-tuple-element.62.dq, bf16[4,2,512,128]{3,2,1,0:T(8,128)(2,1)} %bitcast.32, f32[8,512,128]{2,1,0:T(8,128)} %constant.80.clone.table, ...), custom_call_target="tpu_custom_call" | custom-call | flops 1000 | bytes 1000 | tf_op jit(solution)/shard_map/last_sums/pallas_call | solution.py:553
  362.5 0.7 slice.12
  363.1 0.7 slice.15
  363.8 0.1 constant_dynamic-slice_fusion
  363.9 0.5 slice_bitcast_fusion
  364.4 0.1 reshape.138
  364.5 0.7 constant_dynamic-slice_fusion.1
  365.2 3.6 finish.1
  (2 shorter events, 0.0 us)
Async XLA Ops:
  7.2 262.1 %reduce-scatter.2.cloned.1.call-start = ((), (), s32[]{:S(2)}) async-start(), calls=%async_computation.1 | async-start | bytes 9469952 | tf_op jit(solution)/shard_map/reduce_scatter | solution.py:1441
  151.1 0.7 copy-start
  151.2 1.5 copy-start.2
  152.6 0.7 copy-start.1
Sparse Core Ops, SparseCore 0:
  151.3 117.9 reduce-scatter.1

commit v8 on v7

--- a/solution.py
+++ b/solution.py
@@ -48,19 +48,39 @@
     return (key_pos <= query_pos) & (key_pos < limit)
 
 
-def attn_fwd_kernel(long_blocks, qblk, qlim, kslot, q_ref, kv_ref, ot_ref, lse_ref, o_ref):
-    def pack(i, unused):
+def attn_kernel(
+    block_map, lengths, q_ref, kv_ref, o_ref, dq_ref, dkv_ref, slot_of, ot, lses, acc, dqt
+):
+    total_blocks = block_map.shape[0]
+    long_blocks = total_blocks // 2
+    own = lax.axis_index("tok") % 4
+
+    def note(slot, unused):
+        slot_of[block_map[slot]] = slot
+        return unused
+
+    lax.fori_loop(0, total_blocks, note, 0)
+
+    def about(i, half):
+        block = block_map[2 * (4 * i + own) + half]
+        is_long, place, first = block_info(block, long_blocks)
+        row = jnp.where(
+            is_long, block // LB, long_blocks // LB + (block - long_blocks) // 2
+        )
+        return is_long, place, first, lengths[row]
+
+    def rows_at(block):
+        return pl.ds(pl.multiple_of(slot_of[block] * BLK, BLK), BLK)
+
+    def forward(i, unused):
         packed = q_ref[i, 0]
         for half in range(2):
-            slot = 2 * i + half
-            is_long, place, first = block_info(qblk[slot], long_blocks)
-            limit = qlim[slot]
+            is_long, place, first, limit = about(i, half)
             queries = lane_half(packed, half, False) * jnp.asarray(0.125, BF)
 
             def step(j, carry, masked):
-                top, total, acc = carry
-                rows = pl.ds(pl.multiple_of(kslot[first + j] * BLK, BLK), BLK)
-                kv = kv_ref[rows, :]
+                top, total, summed = carry
+                kv = kv_ref[rows_at(first + j), :]
                 scores = dot(kv, queries, NT)
                 if masked:
                     scores = jnp.where(allowed_pairs(place, j, limit), scores, MASKED)
@@ -68,8 +88,8 @@
                 fade = jnp.exp(top - new_top)
                 probs = jnp.exp(scores - new_top)
                 total = total * fade + jnp.sum(probs, axis=0, keepdims=True)
-                acc = acc * fade + dot(kv, probs.astype(BF), TN)
-                return new_top, total, acc
+                summed = summed * fade + dot(kv, probs.astype(BF), TN)
+                return new_top, total, summed
 
             free = jnp.where(is_long, place, 0)
             carry = (
@@ -78,54 +98,32 @@
                 jnp.zeros((2 * HD, BLK), F32),
             )
             carry = lax.fori_loop(0, free, lambda j, c: step(j, c, False), carry)
-            top, total, acc = lax.fori_loop(free, place + 1, lambda j, c: step(j, c, True), carry)
-            lse_ref[slot] = top + jnp.log(total)
-            ot_ref[i, half * HD : (half + 1) * HD, :] = acc[HD:, :] / total
-        o_ref[i] = jnp.transpose(ot_ref[i]).astype(BF)
+            top, total, summed = lax.fori_loop(
+                free, place + 1, lambda j, c: step(j, c, True), carry
+            )
+            lses[2 * i + half] = top + jnp.log(total)
+            ot[i, half * HD : (half + 1) * HD, :] = summed[HD:, :] / total
+        o_ref[i] = jnp.transpose(ot[i]).astype(BF)
         return unused
 
-    lax.fori_loop(0, q_ref.shape[0], pack, 0)
-
-
-def attn_fwd(qblk, qlim, kslot, q, kv, long_blocks):
-    n = q.shape[0]
-    return pl.pallas_call(
-        functools.partial(attn_fwd_kernel, long_blocks),
-        out_shape=(
-            jax.ShapeDtypeStruct((n, 2 * HD, BLK), F32),
-            jax.ShapeDtypeStruct((2 * n, 1, BLK), F32),
-            jax.ShapeDtypeStruct((n, BLK, 2 * HD), BF),
-        ),
-        in_specs=[SMEM, SMEM, SMEM, VMEM, VMEM],
-        out_specs=(VMEM, VMEM, VMEM),
-        compiler_params=pltpu.CompilerParams(vmem_limit_bytes=60 * 2**20),
-        cost_estimate=SMALL,
-        name="attn_fwd",
-    )(qblk, qlim, kslot, q, kv)
-
-
-def attn_bwd_kernel(
-    long_blocks, qblk, qlim, kslot, q_ref, kv_ref, ot_ref, lse_ref, dq_ref, dkv_ref, acc, dqt
-):
+    lax.fori_loop(0, q_ref.shape[0], forward, 0)
     acc[...] = jnp.zeros_like(acc)
 
-    def pack(i, unused):
+    def backward(i, unused):
         q_packed = q_ref[i, 0]
         d_packed = q_ref[i, 1]
         d_turned = jnp.transpose(d_packed.astype(F32))
         for half in range(2):
-            slot = 2 * i + half
-            is_long, place, first = block_info(qblk[slot], long_blocks)
-            limit = qlim[slot]
+            is_long, place, first, limit = about(i, half)
             queries = lane_half(q_packed, half, False) * jnp.asarray(0.125, BF)
             grads = lane_half(d_packed, half, True)
             both = jnp.concatenate([queries, grads], axis=0)
             lanes = slice(half * HD, (half + 1) * HD)
-            delta = jnp.sum(d_turned[lanes] * ot_ref[i, lanes, :], axis=0, keepdims=True)
-            lse = lse_ref[slot]
+            delta = jnp.sum(d_turned[lanes] * ot[i, lanes, :], axis=0, keepdims=True)
+            lse = lses[2 * i + half]
 
             def step(j, total, masked):
-                rows = pl.ds(pl.multiple_of(kslot[first + j] * BLK, BLK), BLK)
+                rows = rows_at(first + j)
                 kv = kv_ref[rows, :]
                 scores = dot(kv, queries, NT)
                 if masked:
@@ -144,7 +142,7 @@
         dq_ref[i] = jnp.transpose(dqt[...]).astype(BF)
         return unused
 
-    lax.fori_loop(0, q_ref.shape[0], pack, 0)
+    lax.fori_loop(0, q_ref.shape[0], backward, 0)
 
     def finish(i, unused):
         rows = pl.ds(pl.multiple_of(i * BLK, BLK), BLK)
@@ -154,21 +152,25 @@
     lax.fori_loop(0, kv_ref.shape[0] // BLK, finish, 0)
 
 
-def attn_bwd(qblk, qlim, kslot, q, kv, ot, lse, long_blocks):
-    n = q.shape[0]
+def attention(block_map, lengths, qd, kv):
+    n = qd.shape[0]
+    shape = jax.ShapeDtypeStruct((n, BLK, 2 * HD), BF)
     return pl.pallas_call(
-        functools.partial(attn_bwd_kernel, long_blocks),
-        out_shape=(
-            jax.ShapeDtypeStruct((n, BLK, 2 * HD), BF),
-            jax.ShapeDtypeStruct(kv.shape, BF),
-        ),
-        in_specs=[SMEM, SMEM, SMEM, VMEM, VMEM, VMEM, VMEM],
-        out_specs=(VMEM, VMEM),
-        scratch_shapes=[pltpu.VMEM(kv.shape, F32), pltpu.VMEM((2 * HD, BLK), F32)],
+        attn_kernel,
+        out_shape=(shape, shape, jax.ShapeDtypeStruct(kv.shape, BF)),
+        in_specs=[SMEM, SMEM, VMEM, VMEM],
+        out_specs=(VMEM, VMEM, VMEM),
+        scratch_shapes=[
+            pltpu.SMEM(block_map.shape, jnp.int32),
+            pltpu.VMEM((n, 2 * HD, BLK), F32),
+            pltpu.VMEM((2 * n, 1, BLK), F32),
+            pltpu.VMEM(kv.shape, F32),
+            pltpu.VMEM((2 * HD, BLK), F32),
+        ],
         compiler_params=pltpu.CompilerParams(vmem_limit_bytes=60 * 2**20),
         cost_estimate=SMALL,
-        name="attn_bwd",
-    )(qblk, qlim, kslot, q, kv, ot, lse)
+        name="attention",
+    )(block_map, lengths, qd, kv)
 
 
 def turn(values, table, copies, paired, sign):
@@ -431,28 +433,48 @@
 
 
 class ScatterSpace:
-    names = ("pieces", "near", "out", "far", "across", "sums", "side")
-
     def __init__(self, refs):
-        for name, ref in zip(self.names, refs):
-            setattr(self, name, ref)
+        self.pieces, self.ring, self.out, self.far = refs[:4]
+        if len(refs) > 4:
+            self.across, self.sums, self.last = refs[4:]
 
     @staticmethod
     def shapes(rows, depth, half):
-        if half == depth:
-            sizes = ((2, 4, rows, depth), (3, 2, rows, depth), (rows, depth), (rows, depth))
-            return [pltpu.VMEM(size, BF) for size in sizes]
-        assert 2 * half == depth
-        sizes = (
-            (2, 4, rows, depth),
-            (3, 2, rows, half),
-            (rows, half),
-            (rows, half),
-            (4, rows, half),
-            (4, rows, half),
-            (3, rows, half),
+        def ring(parts, columns):
+            return (parts, 2, rows + rows // 2, columns)
+
+        sizes = [(2, 4, rows, depth), ring(2, half), (rows, half), (rows, half)]
+        if half < depth:
+            assert 2 * half == depth
+            sizes += [(4, rows, half), (4, rows, half), ring(1, half)]
+        return [pltpu.VMEM(size, BF) for size in sizes]
+
+
+def ring_sum(links, pieces, ring, total, finish):
+    unused_y, unused_z, unused_c, unused_l, x = coords()
+    rows = total.shape[0]
+    half = rows // 2
+    halves = (pl.ds(0, half), pl.ds(half, half))
+    passing = pl.ds(rows, half)
+    whole = pl.ds(0, rows)
+    opposite = pieces((x + 2) % 4)
+    steps = (1, -1)
+    first = [
+        links.send(opposite.at[halves[k]], ring.at[k, passing], dx=steps[k]) for k in range(2)
+    ]
+    yield
+    second = []
+    for k in range(2):
+        links.arrived(first[k], ring.at[k, passing])
+        piece = pieces((x + steps[k]) % 4)
+        add_up(
+            piece.at[halves[k]], [piece.at[halves[k]], ring.at[k, passing]], half, plain
         )
-        return [pltpu.VMEM(size, BF) for size in sizes]
+        second.append(links.send(piece, ring.at[k, whole], dx=steps[k]))
+        yield
+    for k in range(2):
+        links.arrived(second[k], ring.at[k, whole])
+    add_up(total, [pieces(x), ring.at[0, whole], ring.at[1, whole]], rows, finish)
 
 
 def scatter_br(links, make, space, target, finish):
@@ -460,49 +482,63 @@
     rows, half = space.out.shape
     split = half < target.shape[1]
     first, second = pl.ds(0, half), pl.ds(half, half)
-    order = (1, 3, 2, 0)
-    direct, folded, onward = {}, {}, {}
-    for i, d in enumerate(order):
+    order = (2, 1, 3, 0)
+
+    def part(to):
+        return lambda there: space.pieces.at[to, there, :, first]
+
+    folded = {}
+    outer = ring_sum(links, part(1 - l), space.ring.at[0], space.out, plain)
+    for d in order:
         there = (x + d) % 4
         make(there)
-        if d:
-            for dl in (1, 0):
-                to = (l + dl) % 2
-                direct[dl, i] = links.send(
-                    space.pieces.at[to, there, :, first], space.near.at[i, to], dx=d
-                )
         if split:
             folded[d] = links.send(
                 space.pieces.at[1 - l, there, :, second], space.across.at[there], dl=1
             )
-        yield
-    for i in range(3):
-        links.arrived(direct[1, i], space.near.at[i, 1 - l])
-        yield
-    mine = space.pieces.at[1 - l, x, :, first]
-    add_up(space.out, [mine] + [space.near.at[i, 1 - l] for i in range(3)], rows, plain)
+        if d == 2:
+            next(outer)
+        yield
+    inner = ring_sum(links, part(l), space.ring.at[1], target.at[:, first], finish(0))
+    next(inner)
+    yield from outer
     over = links.send(space.out, space.far, dl=1)
-    for i, d in enumerate(order if split else ()):
+    next(inner)
+    next(inner)
+    yield
+    rest = []
+    for d in order if split else ():
         there = (x + d) % 4
         links.arrived(folded[d], space.across.at[there])
         own = space.pieces.at[l, there, :, second]
         add_up(space.sums.at[there], [own, space.across.at[there]], rows, plain)
-        if d:
-            onward[i] = links.send(space.sums.at[there], space.side.at[i], dx=d)
-        yield
-    for i in range(3):
-        links.arrived(direct[0, i], space.near.at[i, l])
-    yield
-    links.arrived(over, space.far)
-    sources = [space.pieces.at[l, x, :, first]] + [space.near.at[i, l] for i in range(3)]
-    add_up(target.at[:, first], sources + [space.far], rows, finish(0))
-    if not split:
-        return
-    yield
-    for i in range(3):
-        links.arrived(onward[i], space.side.at[i])
-    sources = [space.sums.at[x]] + [space.side.at[i] for i in range(3)]
-    add_up(target.at[:, second], sources, rows, finish(half))
+        if d == 2:
+            late = ring_sum(
+                links,
+                lambda there: space.sums.at[there],
+                space.last.at[0],
+                target.at[:, second],
+                finish(half),
+            )
+            next(late)
+            rest.append(late)
+        yield
+
+    def joined():
+        links.arrived(over, space.far)
+        mine = space.pieces.at[l, x, :, first]
+        add_up(mine, [mine, space.far], rows, plain)
+        yield
+        yield from inner
+
+    rest.append(joined())
+    while rest:
+        for task in list(rest):
+            try:
+                next(task)
+            except StopIteration:
+                rest.remove(task)
+        yield
 
 
 def reduce_tok(links, make, parts, near, side, out, far, target):
@@ -945,11 +981,10 @@
     )(x, g, x.reshape(2 * BLK, depth), g.reshape(2 * BLK, depth), w, kv_mine, q_heads)
 
 
-def residual(tokens, first):
+def residual(tokens):
     def finish(column):
         def add(value, here):
-            at = first + column
-            return value + tokens[here, at : at + value.shape[1]].astype(F32)
+            return value + tokens[here, column : column + value.shape[1]].astype(F32)
 
         return add
 
@@ -968,16 +1003,15 @@
     grads_home,
     mixed_out,
     result,
-    later,
     *rest,
 ):
-    mine, near, far, total, held_w, held_h, held_o, held_later = rest[:8]
-    space = ScatterSpace(rest[8:12])
-    links = Links(*rest[12:])
+    mine, near, far, total, held_w, held_h, held_o = rest[:7]
+    space = ScatterSpace(rest[7:11])
+    links = Links(*rest[11:])
     y, unused_z, unused_c, unused_l, unused_x = coords()
     rows, depth = tokens.shape
     kept = held_w.shape[1]
-    links.greet(BR_ALL + TOK_ALL)
+    links.greet(BR_NEAR + TOK_ALL)
     loads = [
         links.local(o_parts.at[y], held_o.at[y]),
         links.local(hidden, held_h),
@@ -1002,12 +1036,8 @@
             [held_h[:, here, :].reshape(2 * rows, -1), jnp.concatenate(mixed, axis=0)], axis=1
         )
         branches = dot(both, held_w[...], NT).astype(BF)
-        half = space.pieces.shape[3]
         for slot in range(2):
-            piece = branches[slot * rows : (slot + 1) * rows]
-            space.pieces[slot, there] = piece[:, :half]
-            held_later[slot, there] = piece[:, half:]
-        links.local(held_later.at[:, there], later.at[:, there])
+            space.pieces[slot, there] = branches[slot * rows : (slot + 1) * rows]
 
     def output():
         yield
@@ -1015,7 +1045,7 @@
             links.arrived(ticket, held_o.at[(y - d) % 4])
         for load in loads:
             links.settle(load)
-        yield from scatter_br(links, make, space, result, residual(tokens, 0))
+        yield from scatter_br(links, make, space, result, residual(tokens))
 
     in_turn(
         [
@@ -1040,8 +1070,7 @@
             jax.ShapeDtypeStruct(dq.shape, BF),
             jax.ShapeDtypeStruct((4, span, lanes), BF),
             jax.ShapeDtypeStruct((2, BLK, width), BF),
-            jax.ShapeDtypeStruct((rows, depth // 2), BF),
-            jax.ShapeDtypeStruct((2, 4, rows, depth // 2), BF),
+            jax.ShapeDtypeStruct((rows, depth), BF),
         ),
         scratch=[
             pltpu.VMEM((4, 2, span, lanes), BF),
@@ -1051,9 +1080,8 @@
             pltpu.VMEM((depth, kept), BF),
             pltpu.VMEM(hidden.shape, BF),
             pltpu.VMEM(o_parts.shape, BF),
-            pltpu.VMEM((2, 4, rows, depth // 2), BF),
         ]
-        + ScatterSpace.shapes(rows, depth // 2, depth // 2),
+        + ScatterSpace.shapes(rows, depth, depth),
         in_vmem=(5,),
         out_vmem=(2, 3),
         copies=64,
@@ -1128,11 +1156,9 @@
     cot,
     gain,
     block_map,
-    later,
     result,
     qkv_out,
     out_out,
-    late_out,
     sides,
     *rest,
 ):
@@ -1140,13 +1166,11 @@
     parts, near, side, out, far, wsum, summed, normed, scales = rest[9:18]
     lines, lines_in, last, last_in = rest[18:22]
     space = ScatterSpace(rest[22:29])
-    late = ScatterSpace(rest[29:33])
-    links = Links(*rest[33:])
+    links = Links(*rest[29:])
     y, z, c, l, x = coords()
     links.greet(BR_PEERS + TOK_PEERS)
     width = heads * HD
     rows, depth = tokens.shape
-    branches = [links.local(later, late.pieces)]
     first = [
         links.local(dq, held_q),
         links.local(dkv, held_kv),
@@ -1207,59 +1231,51 @@
             value = grads[slot * rows : (slot + 1) * rows] + held_s[slot, here, :].astype(F32)
             space.pieces[slot, there] = value.astype(BF)
 
-    def loaded(there):
-        for load in branches:
-            links.settle(load)
-        branches.clear()
+    def shifted():
+        yield from scatter_br(links, rows_of, space, summed, lambda column: plain)
+        through = turn_back(summed, normed, scales, cot, gain, lines, result)
+        next(through)
+        near_sums = [links.send(lines, lines_in.at[i], **o) for i, o in enumerate(BR_PEERS)]
+        yield
+        for unused in through:
+            pass
+        sums = lines[...]
+        for i, ticket in enumerate(near_sums):
+            links.arrived(ticket, lines_in.at[i])
+            sums = sums + lines_in[i]
+        for t in range(16):
+            last[t] = jnp.concatenate([sums[t : t + 1], sums[16 + t : 17 + t], bias_sums], axis=0)
+        all_sums = []
+        for i, o in enumerate(TOK_PEERS):
+            there = ((y + o["dy"]) % 4) * 4 + ((z + o["dz"]) % 2) * 2 + (c + o["dc"]) % 2
+            all_sums.append(links.send(last.at[there], last_in.at[i], **o))
+        yield
+        yield
+        sums = last[y * 4 + z * 2 + c]
+        for i, ticket in enumerate(all_sums):
+            links.arrived(ticket, last_in.at[i])
+            sums = sums + last_in[i]
+        sides[...] = sums
+
+    def weights():
+        yield from reduce_tok(links, weights_of, parts, near, side, out, far, wsum)
+        qkv_out[0] = wsum[:, :width]
+        for k in range(2):
+            at = [width + (2 * h + k) * HD for h in range(heads)]
+            qkv_out[1 + k] = jnp.concatenate([wsum[:, a : a + HD] for a in at], axis=1)
+        out_out[...] = jnp.transpose(wsum[:, 3 * width :])
 
     def aside():
         for unused in range(5):
             yield
         normal_rows(tokens, normed, scales)
 
-    in_turn(
-        [
-            reduce_tok(links, weights_of, parts, near, side, out, far, wsum),
-            scatter_br(links, rows_of, space, summed, lambda column: plain),
-            scatter_br(links, loaded, late, late_out, residual(tokens, depth // 2)),
-            aside(),
-        ]
-    )
-    through = turn_back(summed, normed, scales, cot, gain, lines, result)
-    next(through)
-    tickets = [links.send(lines, lines_in.at[i], **o) for i, o in enumerate(BR_PEERS)]
-    for unused in through:
-        pass
-    total = lines[...]
-    for i, ticket in enumerate(tickets):
-        links.arrived(ticket, lines_in.at[i])
-        total = total + lines_in[i]
-    for t in range(16):
-        last[t] = jnp.concatenate([total[t : t + 1], total[16 + t : 17 + t], bias_sums], axis=0)
-    tickets = []
-    for i, o in enumerate(TOK_PEERS):
-        there = ((y + o["dy"]) % 4) * 4 + ((z + o["dz"]) % 2) * 2 + (c + o["dc"]) % 2
-        tickets.append(links.send(last.at[there], last_in.at[i], **o))
-    qkv_out[0] = wsum[:, :width]
-    for k in range(2):
-        qkv_out[1 + k] = jnp.concatenate(
-            [
-                wsum[:, width + (2 * h + k) * HD : width + (2 * h + k + 1) * HD]
-                for h in range(heads)
-            ],
-            axis=1,
-        )
-    out_out[...] = jnp.transpose(wsum[:, 3 * width : 4 * width])
-    total = last[y * 4 + z * 2 + c]
-    for i, ticket in enumerate(tickets):
-        links.arrived(ticket, last_in.at[i])
-        total = total + last_in[i]
-    sides[...] = total
+    in_turn([shifted(), weights(), aside()])
     links.close()
 
 
 def last_sums(
-    dq, dkv, table, x, g, mixed, w, partial_grad, tokens, cot, gain, block_map, later, heads
+    dq, dkv, table, x, g, mixed, w, partial_grad, tokens, cot, gain, block_map, heads
 ):
     rows, depth = tokens.shape
     wrows = depth // 16
@@ -1269,12 +1285,11 @@
         functools.partial(last_kernel, heads),
         "last_sums",
         3,
-        (dq, dkv, table, x, g, mixed, w, partial_grad, tokens, cot, gain, block_map, later),
+        (dq, dkv, table, x, g, mixed, w, partial_grad, tokens, cot, gain, block_map),
         (
             jax.ShapeDtypeStruct((rows, depth), F32),
             jax.ShapeDtypeStruct((3, wrows, width), F32),
             jax.ShapeDtypeStruct((width, wrows), F32),
-            jax.ShapeDtypeStruct((rows, depth // 2), BF),
             jax.ShapeDtypeStruct((8, 128), F32),
         ),
         scratch=[
@@ -1301,23 +1316,20 @@
             pltpu.VMEM((16, 8, 128), F32),
             pltpu.VMEM((15, 8, 128), F32),
         ]
-        + ScatterSpace.shapes(rows, depth, depth // 2)
-        + ScatterSpace.shapes(rows, depth // 2, depth // 2),
+        + ScatterSpace.shapes(rows, depth, depth // 2),
         in_vmem=(8, 9, 10),
         in_smem=(11,),
-        out_vmem=(0, 1, 2, 3, 4),
+        out_vmem=(0, 1, 2, 3),
         copies=96,
     )
 
 
-def finish_kernel(main, grads, first, second, tokens, qkv, out, *outs):
+def finish_kernel(main, grads, value, tokens, qkv, out, *outs):
     def lines(start, count):
         return jnp.transpose(grads[:, start : start + count].astype(F32))
 
     result, tokens_out, qkv_out, out_out, down, gate, up = outs
-    half = first.shape[1]
-    result[:, :half] = first[...]
-    result[:, half:] = second[...]
+    result[...] = value[...]
     tokens_out[...] = tokens[...]
     qkv_out[...] = qkv[...]
     out_out[...] = out[...]
@@ -1332,23 +1344,22 @@
     up[main:, :] = ends[tail:]
 
 
-def finish(grads, first, second, tokens, qkv, out, main, hidden_width):
-    rows, half = first.shape
+def finish(grads, value, tokens, qkv, out, main, hidden_width):
     shape = jax.ShapeDtypeStruct((hidden_width, grads.shape[0]), F32)
     return pl.pallas_call(
         functools.partial(finish_kernel, main),
         out_shape=(
-            jax.ShapeDtypeStruct((rows, 2 * half), BF),
+            jax.ShapeDtypeStruct(value.shape, BF),
             jax.ShapeDtypeStruct(tokens.shape, F32),
             jax.ShapeDtypeStruct(qkv.shape, F32),
             jax.ShapeDtypeStruct(out.shape, F32),
         )
         + (shape,) * 3,
-        in_specs=[VMEM] * 6,
+        in_specs=[VMEM] * 5,
         out_specs=(VMEM,) * 7,
         cost_estimate=SMALL,
         name="finish",
-    )(grads, first, second, tokens, qkv, out)
+    )(grads, value, tokens, qkv, out)
 
 
 def rotary_table():
@@ -1376,9 +1387,6 @@
     lengths,
 ):
     tok = lax.axis_index("tok")
-    y, z, c = tok // 4, (tok // 2) % 2, tok % 2
-    total_blocks = block_map.shape[0]
-    long_blocks = total_blocks // 2
     rows = tokens.shape[0]
     depth = tokens.shape[1]
     wrows = qkv_weight.shape[1]
@@ -1412,26 +1420,6 @@
     qkv_full = qkv_full.reshape(16 * wrows, -1)
     ff_full = ff_full.reshape(16 * wrows, -1)
 
-    slot_table = jnp.arange(total_blocks, dtype=jnp.int32)
-    slot_of = jnp.sum(
-        jnp.where(block_map[None, :] == slot_table[:, None], slot_table[None, :], 0), axis=1
-    )
-    key_slot = slot_of.astype(jnp.int32)
-    from_tok = jnp.arange(4, dtype=jnp.int32) * 4 + z * 2 + c
-    my_queries = jnp.stack([2 * from_tok, 2 * from_tok + 1], axis=1).reshape(-1)
-    query_block = jnp.sum(
-        jnp.where(my_queries[:, None] == slot_table[None, :], block_map[None, :], 0), axis=1
-    ).astype(jnp.int32)
-    query_row = jnp.where(
-        query_block < long_blocks,
-        query_block // LB,
-        long_blocks // LB + (query_block - long_blocks) // 2,
-    )
-    row_table = jnp.arange(lengths.shape[0], dtype=jnp.int32)
-    query_limit = jnp.sum(
-        jnp.where(query_row[:, None] == row_table[None, :], lengths[None, :], 0), axis=1
-    ).astype(jnp.int32)
-
     hidden, grad_x, grad_ff, qd_all, kv_all = ff_heads(
         x, grad, ff_full, kv_mine, q_heads, main, down_width, first
     )
@@ -1440,15 +1428,12 @@
     grad = grad.reshape(2 * BLK, depth)
     grad_ff = lax.psum_scatter(grad_ff, "tok", scatter_dimension=0, tiled=True)
 
-    turned, lse, o_parts = attn_fwd(query_block, query_limit, key_slot, qd_all, kv_all, long_blocks)
-    dq_parts, dkv_all = attn_bwd(
-        query_block, query_limit, key_slot, qd_all, kv_all, turned, lse, long_blocks
-    )
-    dq_heads, dkv_heads, mixed, first_half, later = heads_home(
+    o_parts, dq_parts, dkv_all = attention(block_map, lengths, qd_all, kv_all)
+    dq_heads, dkv_heads, mixed, result = heads_home(
         dkv_all.reshape(4, 2, 2, 2 * BLK, 2 * HD), dq_parts, o_parts, hidden, ff_full, tokens, heads
     )
     grad_ff, dq_heads = lax.optimization_barrier((grad_ff, dq_heads))
-    grad_tokens, grad_qkv, grad_out, second_half, sides = last_sums(
+    grad_tokens, grad_qkv, grad_out, sides = last_sums(
         dq_heads,
         dkv_heads.reshape(heads, 2, BLK, 2 * HD),
         table,
@@ -1461,14 +1446,13 @@
         cotangent,
         norm_gain.reshape(1, depth),
         block_map,
-        later,
         heads,
     )
     grad_qkv_bias = lax.dynamic_slice_in_dim(
         sides[2:].reshape(3, heads, HD), tok * qkv_bias.shape[2], qkv_bias.shape[2], 2
     )
     result, grad_tokens, grad_qkv, grad_out, grad_down, grad_gate, grad_up = finish(
-        grad_ff, first_half, second_half, grad_tokens, grad_qkv, grad_out, main, hidden_width
+        grad_ff, result, grad_tokens, grad_qkv, grad_out, main, hidden_width
     )
 
     sides = lax.dynamic_slice_in_dim(sides[:2], lax.axis_index("br") * 16, 16, 1)

time: 379 us -> 359 us (0.947)
  Pallas kernels: 348 us -> 333 us
  waiting for transfers between devices: 6.85 us -> 2.66 us
    pallas_call x2 -> x1, Pallas kernels: 54.9 us -> 40 us  [attention(): pl.pallas_call(attn_kernel, out_shape=(shape, shape, jax.ShapeDtypeStruct...]
    reduce_scatter x1, waiting for transfers between devices: 6.83 us -> 2.64 us  [body(): grad_ff = lax.psum_scatter(grad_ff, 'tok', scatter_dimension=0, tiled=True)]
  transfers between devices with their start and end apart: 1 -> 1, of which waited for: 1 -> 1; matrix products, arithmetic and copies ran while one was open for 0% -> 0% of each run, Pallas kernels for 29% -> 34%
where the time goes in v8:
time: 359 us; the launch traced here: 354 us
  Pallas kernels  333 us (93%)
  between operations  14.5 us (4%)
    pallas_call x2, Pallas kernels, comm_call(): pl.pallas_call(kernel, out_shape=tuple(outs), in_specs=[VMEM if i in in_v...  147 us
    pallas_call x1, Pallas kernels, start(): pl.pallas_call(functools.partial(start_kernel, heads, main), out_shape=sh...  96.3 us
    pallas_call x1, Pallas kernels, ff_heads(): pl.pallas_call(functools.partial(ff_heads_kernel, main, down, first), gri...  46.2 us
    pallas_call x1, Pallas kernels, attention(): pl.pallas_call(attn_kernel, out_shape=(shape, shape, jax.ShapeDtypeStruct...  40 us
  transfers between devices with their start and end apart: 1, of which 1 were waited for; matrix products, arithmetic and copies ran while one was open for 0% of the time, Pallas kernels for 34%

profile of v8, /device:TPU:1, one launch (start us, length us, event | category | flops | bytes accessed | tf_op | source)
XLA Modules:
  0.0 354.4 jit_solution(6996276876204163764)
XLA Ops:
  7.2 0.0 reduce-scatter.2.cloned.1.call-start
  7.2 0.8 convert_element_type.14
  8.0 0.6 pad_convert_fusion.qkv_bias
  8.6 96.3 %start.1 = (bf16[2,4,128,2048]{3,2,1,0:T(8,128)(2,1)}, bf16[2,4,128,2048]{3,2,1,0:T(8,128)(2,1)}, bf16[4,2,2,128,896]{4,3,2,1,0:T(8,128)(2,1)}, bf16[4,2,2,128,2...) custom-call(s32[32]{0:T(128)} %block_map.5, bf16[128,2048]{1,0:T(8,128)(2,1)} %tokens.5, ...), custom_call_target="tpu_custom_call" | custom-call | flops 1000 | bytes 1000 | tf_op jit(solution)/shard_map/start/pallas_call | solution.py:785
  104.9 46.2 %ff_heads.1 = (bf16[2,512,768]{2,1,0:T(8,128)(2,1)}, bf16[2,512,2048]{2,1,0:T(8,128)(2,1)}, bf16[2048,2176]{1,0:T(8,128)(2,1)}, bf16[4,2,512,128]{3,2,1,0:T(8,128)(2,1)}, bf16[4,2,2,2,512,128]{5,4,3,2,1,0:T(8,128)(2,1)}) custom-call(bf16[2,512,2048]{2,1,0:T(8,128)(2,1)} %bitcast.22, bf16[2,512,2048]{2,1,0:T(8,128)(2,1)} %bitcast.25, ...), custom_call_target="tpu_custom_call" | custom-call | flops 1000 | bytes 1000 | tf_op jit(solution)/shard_map/ff_heads/pallas_call | solution.py:941
  151.2 0.0 reduce-scatter.2.cloned.1.call-update
  151.2 40.0 %attention.1 = (bf16[4,512,128]{2,1,0:T(8,128)(2,1)}, bf16[4,512,128]{2,1,0:T(8,128)(2,1)}, bf16[16384,128]{1,0:T(8,128)(2,1)}) custom-call(s32[32]{0:T(128)} %block_map.5, s32[10]{0:T(128)} %lengths.1, bf16[4,2,512,128]{3,2,1,0:T(8,128)(2,1)} %get-tuple-element.47.q_ref, bf16[16384,128]{1,0:T(8,128)(2,1)} %bitcast.28), custom_call_target="tpu_custom_call" | custom-call | flops 1000 | bytes 1000 | tf_op jit(solution)/shard_map/attention/pallas_call | solution.py:158
  191.2 79.5 %heads_home.1 = (bf16[4,512,128]{2,1,0:T(8,128)(2,1)}, bf16[4,1024,128]{2,1,0:T(8,128)(2,1)}, bf16[2,512,256]{2,1,0:T(8,128)(2,1)}, bf16[128,2048]{1,0:T(8,128)(2,1)}) custom-call(bf16[4,2,2,1024,128]{4,3,2,1,0:T(8,128)(2,1)} %bitcast.29, bf16[4,512,128]{2,1,0:T(8,128)(2,1)} %get-tuple-element.50.dq, bf16[4,512,128]{2,1,0:T(8,128)(2,1)} %get-tuple-element.51.o_parts, ...), custom_call_target="tpu_custom_call" | custom-call | flops 1000 | bytes 1000 | tf_op jit(solution)/shard_map/heads_home/pallas_call | solution.py:589
  270.7 2.6 reduce-scatter.2.cloned.1.call-done.grads
  273.4 67.4 %last_sums.1 = (f32[128,2048]{1,0:T(8,128)}, f32[3,128,256]{2,1,0:T(8,128)}, f32[256,128]{1,0:T(8,128)}, f32[8,128]{1,0:T(8,128)}) custom-call(bf16[4,512,128]{2,1,0:T(8,128)(2,1)} %get-tuple-element.56.dq, bf16[4,2,512,128]{3,2,1,0:T(8,128)(2,1)} %bitcast.31, f32[8,512,128]{2,1,0:T(8,128)} %constant.26.clone.table, bf16[1024,2048]{1,0:T(8,128)(2,1)} %bitcast.24, ...), custom_call_target="tpu_custom_call" | custom-call | flops 1000 | bytes 1000 | tf_op jit(solution)/shard_map/last_sums/pallas_call | solution.py:589
  340.8 0.7 slice.12
  341.5 0.7 slice.15
  342.2 0.1 constant_dynamic-slice_fusion.1
  342.2 0.5 slice_bitcast_fusion
  342.8 0.1 reshape.79
  342.8 0.7 constant_dynamic-slice_fusion
  343.5 3.6 %finish.1 = (bf16[128,2048]{1,0:T(8,128)(2,1)}, f32[128,2048]{1,0:T(8,128)}, f32[3,128,256]{2,1,0:T(8,128)}, f32[256,128]{1,0:T(8,128)}, f32[704,128]{1,0:T(8,12...) custom-call(bf16[128,2176]{1,0:T(8,128)(2,1)} %reduce-scatter.2.cloned.1.call-done.grads, ...), custom_call_target="tpu_custom_call" | custom-call | flops 1000 | bytes 1000 | tf_op jit(solution)/shard_map/finish/pallas_call | solution.py:1349
Async XLA Ops:
  7.2 266.2 %reduce-scatter.2.cloned.1.call-start = ((), (), s32[]{:S(2)}) async-start(), calls=%async_computation.1 | async-start | bytes 9469952 | tf_op jit(solution)/shard_map/reduce_scatter | solution.py:1429
Sparse Core Ops, SparseCore 0:
  151.3 122.0 reduce-scatter.1

commit v9 on v8

--- a/solution.py
+++ b/solution.py
@@ -444,9 +444,9 @@
             return (parts, 2, rows + rows // 2, columns)
 
         sizes = [(2, 4, rows, depth), ring(2, half), (rows, half), (rows, half)]
-        if half < depth:
-            assert 2 * half == depth
-            sizes += [(4, rows, half), (4, rows, half), ring(1, half)]
+        rest = depth - half
+        if rest:
+            sizes += [(4, rows, rest), (4, rows, rest), ring(1, rest)]
         return [pltpu.VMEM(size, BF) for size in sizes]
 
 
@@ -481,7 +481,7 @@
     unused_y, unused_z, unused_c, l, x = coords()
     rows, half = space.out.shape
     split = half < target.shape[1]
-    first, second = pl.ds(0, half), pl.ds(half, half)
+    first, second = pl.ds(0, half), pl.ds(half, target.shape[1] - half)
     order = (2, 1, 3, 0)
 
     def part(to):
@@ -607,10 +607,11 @@
     )(*args)
 
 
-def table_rows(table, block_map, slot, long_blocks):
+def table_rows(table, block_map, slot, here):
     block = block_map[lax.axis_index("tok") * 2 + slot]
+    long_blocks = 2 * LB
     place = jnp.where(block < long_blocks, block % LB, (block - long_blocks) % 2)
-    return table[place]
+    return table[place, here, :]
 
 
 def shift_rows(tokens, gain, bias, shifted):
@@ -700,7 +701,7 @@
         products = dot(span, held_w[...].reshape(depth, -1)[:, : 3 * width], NN) + added
         parts = []
         for slot in range(2):
-            turns = table_rows(held_t, block_map, slot, 2 * LB)[here]
+            turns = table_rows(held_t, block_map, slot, here)
             joined = products[slot * tile : (slot + 1) * tile]
             parts.append(turn(joined[:, :width], turns, heads // 2, False, 1.0).astype(BF))
             kv = turn(joined[:, width:], turns, heads, True, 1.0).astype(BF)
@@ -726,6 +727,7 @@
         links.settle(rotary)
         for half in range(2):
             project(half)
+            yield
         sent = [
             (d, links.send(pairs.at[(y + d) % 4], kv_mine.at[y], dy=d)) for d in (1, 3, 2)
         ]
@@ -837,7 +839,10 @@
     order = (1, 3, 2)
     rows = x_ref.shape[1]
 
-    load = pltpu.make_async_copy(weights, w_ref, sems[2].at[0])
+    loads = [
+        pltpu.make_async_copy(weights.at[:, part], w_ref.at[:, part], sems[2].at[n])
+        for n, part in ((0, pl.ds(first, w_ref.shape[1] - first)), (4, pl.ds(0, first)))
+    ]
     kept = [
         pltpu.make_async_copy(kv_mine, pairs.at[:, z, c], sems[2].at[1]),
         pltpu.make_async_copy(q_heads.at[y], asked.at[y, 0], sems[2].at[2]),
@@ -869,15 +874,22 @@
 
     @pl.when(step == 0)
     def _():
-        load.start()
+        for load in loads:
+            load.start()
         links.greet([dict(dz=1), dict(dc=1), dict(dy=1), dict(dy=2), dict(dy=3)])
         for copy, unused in far + near + asked_q:
             copy.start()
         for copy in kept:
             copy.start()
-        load.wait()
+        loads[0].wait()
 
     def pause(point):
+        if point == 0:
+
+            @pl.when(step == 0)
+            def _():
+                loads[1].wait()
+
         @pl.when(step == 1)
         def _():
             cross(point)
@@ -971,7 +983,7 @@
             pltpu.VMEM(q_heads.shape, BF),
             pltpu.SemaphoreType.DMA((32,)),
             pltpu.SemaphoreType.DMA((32,)),
-            pltpu.SemaphoreType.DMA((4,)),
+            pltpu.SemaphoreType.DMA((5,)),
         ],
         compiler_params=pltpu.CompilerParams(
             collective_id=1, has_side_effects=True, vmem_limit_bytes=60 * 2**20
@@ -1135,7 +1147,10 @@
         result[here, :] = cot[here, :].astype(F32) + scales[here, :1] * grad
         return unused
 
-    lax.fori_loop(0, rows // chunk, back, 0)
+    middle = rows // chunk // 2
+    lax.fori_loop(0, middle, back, 0)
+    yield
+    lax.fori_loop(middle, 2 * middle, back, 0)
 
 
 BR_PEERS = [dict(dl=i // 4, dx=i % 4) for i in range(1, 8)]
@@ -1164,9 +1179,9 @@
 ):
     held_q, held_kv, held_t, held_x, held_g, held_m, held_w, held_s, gj = rest[:9]
     parts, near, side, out, far, wsum, summed, normed, scales = rest[9:18]
-    lines, lines_in, last, last_in = rest[18:22]
-    space = ScatterSpace(rest[22:29])
-    links = Links(*rest[29:])
+    lines, lines_in, last, last_in, bias_acc = rest[18:23]
+    space = ScatterSpace(rest[23:30])
+    links = Links(*rest[30:])
     y, z, c, l, x = coords()
     links.greet(BR_PEERS + TOK_PEERS)
     width = heads * HD
@@ -1176,41 +1191,48 @@
         links.local(dkv, held_kv),
         links.local(table, held_t),
     ]
+    third = [links.local(w_in.at[:, pl.ds(0, 3 * width)], held_w), links.local(s_in, held_s)]
     second = [
         links.local(x_in, held_x),
         links.local(g_in, held_g),
         links.local(m_in, held_m),
     ]
-    third = [links.local(w_in.at[:, pl.ds(0, 3 * width)], held_w), links.local(s_in, held_s)]
-    for load in first:
-        links.settle(load)
-    total = jnp.zeros((1, 3 * width), F32)
-    for slot in range(2):
-        for half in range(2):
-            here = slice(half * BLK // 2, (half + 1) * BLK // 2)
+    wrows = parts.shape[3]
+    strip = 4 * wrows
+    bias_acc[...] = jnp.zeros_like(bias_acc)
+
+    def settle(loads):
+        for load in loads:
+            links.settle(load)
+        loads.clear()
+
+    def turn_rows(here):
+        for slot in range(2):
             lanes = slice(slot * HD, (slot + 1) * HD)
-            turns = table_rows(held_t, block_map, slot, 2 * LB)[here]
+            turns = table_rows(held_t, block_map, slot, here)
             q = jnp.concatenate([held_q[h, here, lanes] for h in range(heads)], axis=1)
             q = turn(q.astype(F32), turns, heads // 2, False, -1.0).astype(BF)
-            kv = jnp.concatenate([held_kv[h, slot, here] for h in range(heads)], axis=1)
+            kv = jnp.concatenate([held_kv[h, slot, here, :] for h in range(heads)], axis=1)
             kv = turn(kv.astype(F32), turns, heads, True, -1.0).astype(BF)
             both = jnp.concatenate([q, kv], axis=1)
             gj[slot, here, :] = both
-            total += jnp.sum(both.astype(F32), axis=0, keepdims=True)
-    line = [total[:, :width]]
-    for k in range(2):
-        at = [width + (2 * h + k) * HD for h in range(heads)]
-        line.append(jnp.concatenate([total[:, a : a + HD] for a in at], axis=1))
-    line = jnp.concatenate(line, axis=1)
-    bias_sums = jnp.concatenate(
-        [line[:, r * 128 : (r + 1) * 128] for r in range(3 * width // 128)], axis=0
-    )
-    for load in second:
-        links.settle(load)
-    wrows = parts.shape[3]
-    strip = 4 * wrows
+            bias_acc[...] += jnp.sum(
+                both.astype(F32).reshape(rows // 8, 8, 3 * width), axis=0
+            )
+
+    def bias_lines():
+        total = jnp.sum(bias_acc[...], axis=0, keepdims=True)
+        line = [total[:, :width]]
+        for k in range(2):
+            at = [width + (2 * h + k) * HD for h in range(heads)]
+            line.append(jnp.concatenate([total[:, a : a + HD] for a in at], axis=1))
+        line = jnp.concatenate(line, axis=1)
+        return jnp.concatenate(
+            [line[:, r * 128 : (r + 1) * 128] for r in range(3 * width // 128)], axis=0
+        )
 
     def weights_of(there):
+        settle(second)
         here = pl.ds(pl.multiple_of(there * strip, strip), strip)
         qkv = dot(held_x[:, here], gj[...].reshape(2 * BLK, 3 * width), TN).astype(BF)
         outs = dot(held_g[:, here], held_m[...], TN).astype(BF)
@@ -1220,11 +1242,10 @@
             parts[there, k // 2, k % 2, :, 3 * width : 4 * width] = outs[at]
 
     def rows_of(there):
-        if third:
-            for load in third:
-                links.settle(load)
-            third.clear()
+        settle(first)
         here = pl.ds(pl.multiple_of(there * rows, rows), rows)
+        turn_rows(here)
+        settle(third)
         both = gj[:, here, :].reshape(2 * rows, 3 * width)
         grads = dot(both, held_w[...], NT)
         for slot in range(2):
@@ -1237,8 +1258,8 @@
         next(through)
         near_sums = [links.send(lines, lines_in.at[i], **o) for i, o in enumerate(BR_PEERS)]
         yield
-        for unused in through:
-            pass
+        next(through)
+        bias_sums = bias_lines()
         sums = lines[...]
         for i, ticket in enumerate(near_sums):
             links.arrived(ticket, lines_in.at[i])
@@ -1250,6 +1271,8 @@
             there = ((y + o["dy"]) % 4) * 4 + ((z + o["dz"]) % 2) * 2 + (c + o["dc"]) % 2
             all_sums.append(links.send(last.at[there], last_in.at[i], **o))
         yield
+        for unused in through:
+            pass
         yield
         sums = last[y * 4 + z * 2 + c]
         for i, ticket in enumerate(all_sums):
@@ -1258,6 +1281,8 @@
         sides[...] = sums
 
     def weights():
+        for unused in range(4):
+            yield
         yield from reduce_tok(links, weights_of, parts, near, side, out, far, wsum)
         qkv_out[0] = wsum[:, :width]
         for k in range(2):
@@ -1315,8 +1340,9 @@
             pltpu.VMEM((7, 32, 128), F32),
             pltpu.VMEM((16, 8, 128), F32),
             pltpu.VMEM((15, 8, 128), F32),
+            pltpu.VMEM((8, 3 * width), F32),
         ]
-        + ScatterSpace.shapes(rows, depth, depth // 2),
+        + ScatterSpace.shapes(rows, depth, depth // 4 * 3),
         in_vmem=(8, 9, 10),
         in_smem=(11,),
         out_vmem=(0, 1, 2, 3),
@@ -1432,7 +1458,6 @@
     dq_heads, dkv_heads, mixed, result = heads_home(
         dkv_all.reshape(4, 2, 2, 2 * BLK, 2 * HD), dq_parts, o_parts, hidden, ff_full, tokens, heads
     )
-    grad_ff, dq_heads = lax.optimization_barrier((grad_ff, dq_heads))
     grad_tokens, grad_qkv, grad_out, sides = last_sums(
         dq_heads,
         dkv_heads.reshape(heads, 2, BLK, 2 * HD),
@@ -1451,6 +1476,7 @@
     grad_qkv_bias = lax.dynamic_slice_in_dim(
         sides[2:].reshape(3, heads, HD), tok * qkv_bias.shape[2], qkv_bias.shape[2], 2
     )
+    grad_ff, grad_tokens = lax.optimization_barrier((grad_ff, grad_tokens))
     result, grad_tokens, grad_qkv, grad_out, grad_down, grad_gate, grad_up = finish(
         grad_ff, result, grad_tokens, grad_qkv, grad_out, main, hidden_width
     )

time: 359 us -> 360 us (level)
    pallas_call x2, Pallas kernels: 147 us -> 134 us  [comm_call(): pl.pallas_call(kernel, out_shape=tuple(outs), in_specs=[VMEM if i in in_v...]
    pallas_call x1, Pallas kernels: 40 us -> 50.1 us  [attention(): pl.pallas_call(attn_kernel, out_shape=(shape, shape, jax.ShapeDtypeStruct...]
    pallas_call x1, Pallas kernels: 96.3 us -> 101 us  [start(): pl.pallas_call(functools.partial(start_kernel, heads, main), out_shape=sh...]
  transfers between devices with their start and end apart: 1 -> 1, of which waited for: 1 -> 0; matrix products, arithmetic and copies ran while one was open for 0% -> 1% of each run, Pallas kernels for 34% -> 52%
where the time goes in v9:
time: 360 us; the launch traced here: 355 us
  Pallas kernels  336 us (93%)
  between operations  14.5 us (4%)
    pallas_call x2, Pallas kernels, comm_call(): pl.pallas_call(kernel, out_shape=tuple(outs), in_specs=[VMEM if i in in_v...  134 us
    pallas_call x1, Pallas kernels, start(): pl.pallas_call(functools.partial(start_kernel, heads, main), out_shape=sh...  101 us
    pallas_call x1, Pallas kernels, attention(): pl.pallas_call(attn_kernel, out_shape=(shape, shape, jax.ShapeDtypeStruct...  50.1 us
    pallas_call x1, Pallas kernels, ff_heads(): pl.pallas_call(functools.partial(ff_heads_kernel, main, down, first), gri...  47.9 us
  transfers between devices with their start and end apart: 1, of which 0 were waited for; matrix products, arithmetic and copies ran while one was open for 1% of the time, Pallas kernels for 52%

profile of v9, /device:TPU:1, one launch (start us, length us, event | category | flops | bytes accessed | tf_op | source)
XLA Modules:
  0.0 354.9 jit_solution(16244451009672231000)
XLA Ops:
  7.2 0.0 reduce-scatter.2.cloned.1.call-start
  7.2 0.8 convert_element_type.14
  8.0 0.6 pad_convert_fusion.qkv_bias
  8.6 100.7 %start.1 = (bf16[2,4,128,2048]{3,2,1,0:T(8,128)(2,1)}, bf16[2,4,128,2048]{3,2,1,0:T(8,128)(2,1)}, bf16[4,2,2,128,896]{4,3,2,1,0:T(8,128)(2,1)}, bf16[4,2,2,128,2...) custom-call(s32[32]{0:T(128)} %block_map.5, bf16[128,2048]{1,0:T(8,128)(2,1)} %tokens.5, ...), custom_call_target="tpu_custom_call" | custom-call | flops 1000 | bytes 1000 | tf_op jit(solution)/shard_map/start/pallas_call | solution.py:787
  109.3 47.9 %ff_heads.1 = (bf16[2,512,768]{2,1,0:T(8,128)(2,1)}, bf16[2,512,2048]{2,1,0:T(8,128)(2,1)}, bf16[2048,2176]{1,0:T(8,128)(2,1)}, bf16[4,2,512,128]{3,2,1,0:T(8,128)(2,1)}, bf16[4,2,2,2,512,128]{5,4,3,2,1,0:T(8,128)(2,1)}) custom-call(bf16[2,512,2048]{2,1,0:T(8,128)(2,1)} %bitcast.22, bf16[2,512,2048]{2,1,0:T(8,128)(2,1)} %bitcast.25, ...), custom_call_target="tpu_custom_call" | custom-call | flops 1000 | bytes 1000 | tf_op jit(solution)/shard_map/ff_heads/pallas_call | solution.py:953
  157.2 0.0 reduce-scatter.2.cloned.1.call-update
  157.2 50.1 %attention.1 = (bf16[4,512,128]{2,1,0:T(8,128)(2,1)}, bf16[4,512,128]{2,1,0:T(8,128)(2,1)}, bf16[16384,128]{1,0:T(8,128)(2,1)}) custom-call(s32[32]{0:T(128)} %block_map.5, s32[10]{0:T(128)} %lengths.1, bf16[4,2,512,128]{3,2,1,0:T(8,128)(2,1)} %get-tuple-element.47.q_ref, bf16[16384,128]{1,0:T(8,128)(2,1)} %bitcast.28), custom_call_target="tpu_custom_call" | custom-call | flops 1000 | bytes 1000 | tf_op jit(solution)/shard_map/attention/pallas_call | solution.py:158
  207.3 70.3 %heads_home.1 = (bf16[4,512,128]{2,1,0:T(8,128)(2,1)}, bf16[4,1024,128]{2,1,0:T(8,128)(2,1)}, bf16[2,512,256]{2,1,0:T(8,128)(2,1)}, bf16[128,2048]{1,0:T(8,128)(2,1)}) custom-call(bf16[4,2,2,1024,128]{4,3,2,1,0:T(8,128)(2,1)} %bitcast.29, bf16[4,512,128]{2,1,0:T(8,128)(2,1)} %get-tuple-element.50.dq, bf16[4,512,128]{2,1,0:T(8,128)(2,1)} %get-tuple-element.51.o_parts, ...), custom_call_target="tpu_custom_call" | custom-call | flops 1000 | bytes 1000 | tf_op jit(solution)/shard_map/heads_home/pallas_call | solution.py:589
  277.7 63.6 %last_sums.1 = (f32[128,2048]{1,0:T(8,128)}, f32[3,128,256]{2,1,0:T(8,128)}, f32[256,128]{1,0:T(8,128)}, f32[8,128]{1,0:T(8,128)}) custom-call(bf16[4,512,128]{2,1,0:T(8,128)(2,1)} %get-tuple-element.53.dq, bf16[4,2,512,128]{3,2,1,0:T(8,128)(2,1)} %bitcast.31, f32[8,512,128]{2,1,0:T(8,128)} %constant.26.clone.table, bf16[1024,2048]{1,0:T(8,128)(2,1)} %bitcast.24, ...), custom_call_target="tpu_custom_call" | custom-call | flops 1000 | bytes 1000 | tf_op jit(solution)/shard_map/last_sums/pallas_call | solution.py:589
  341.3 0.7 slice.12
  342.0 0.7 slice.15
  342.7 0.1 reshape.79
  342.7 0.1 constant_dynamic-slice_fusion.1
  342.8 0.7 constant_dynamic-slice_fusion
  343.5 0.5 slice_bitcast_fusion
  344.0 0.0 reduce-scatter.2.cloned.1.call-done.grads
  344.0 3.6 %finish.1 = (bf16[128,2048]{1,0:T(8,128)(2,1)}, f32[128,2048]{1,0:T(8,128)}, f32[3,128,256]{2,1,0:T(8,128)}, f32[256,128]{1,0:T(8,128)}, f32[704,128]{1,0:T(8,12...) custom-call(bf16[128,2176]{1,0:T(8,128)(2,1)} %reduce-scatter.2.cloned.1.call-done.grads, ...), custom_call_target="tpu_custom_call" | custom-call | flops 1000 | bytes 1000 | tf_op jit(solution)/shard_map/finish/pallas_call | solution.py:1375
Async XLA Ops:
  7.2 336.8 %reduce-scatter.2.cloned.1.call-start = ((), (), s32[]{:S(2)}) async-start(), calls=%async_computation.1 | async-start | bytes 9469952 | tf_op jit(solution)/shard_map/reduce_scatter | solution.py:1455
Sparse Core Ops, SparseCore 0:
  157.4 122.8 reduce-scatter.1
